TPU v7x, 32 devices: a whole 2x2x4 slice. The times are simulated.
32 devices in a mesh: seq: 8 (over z, y), batch: 4 (over x, core).
Axes of the slice: x: 2, y: 2, z: 4, core: 2. Of those that a mesh axis runs over, the one named last changes fastest.
Arguments:
- inputs: bfloat16 [4, 8192, 2048], P('batch', 'seq'), may hold values from -6 to 6
- input_map: bfloat16 [4, 8192, 128], P('batch', 'seq'), may hold values from -0.5 to 0.5
- output_map: bfloat16 [4, 8192, 128], P('batch', 'seq'), may hold values from -0.5 to 0.5
- step_raw: float32 [4, 32, 8192], P('batch', None, 'seq'), may hold values from -4.5 to 4.5
- step_bias: float32 [32], replicated, may hold values from -2 to 0
- decay_rate: float32 [32], replicated, may hold values from 3.0517578e-05 to 0.05
- skip_gain: float32 [32], replicated, may hold values from 0.5 to 1.5
- cotangent: bfloat16 [4, 8192, 2048], P('batch', 'seq'), may hold values from -6 to 6
Outputs:
- grad_inputs: bfloat16 [4, 8192, 2048], P('batch', 'seq')
- grad_input_map: float32 [4, 8192, 128], P('batch', 'seq')
- grad_output_map: float32 [4, 8192, 128], P('batch', 'seq')
- grad_step_raw: float32 [4, 32, 8192], P('batch', None, 'seq')
- grad_params: float32 [2, 32], replicated
- grad_decay_rate: float32 [32], replicated
All inputs are finite; a program needn't handle non-finite values.
Results may differ from a plain program's by a relative error of at most 0.034.
Values sent between devices are 32-bit elements; how exact they have to be, the bound alone decides.
No kernel may reach another device: no remote copies, remote signals or barrier semaphores. Data moves between devices by JAX's collectives and lax.ppermute only.
A program may use at most 192 MiB of HBM per device.

v0:
```python
import functools
import math

import jax
import jax.numpy as jnp
from jax import lax
from jax.experimental import pallas as pl
from jax.experimental.pallas import tpu as pltpu
from jax.sharding import PartitionSpec as P

GROUP = 256
PARTS = 2
VMEM_LIMIT = 61 * 1024 * 1024
F32 = jnp.float32
BF16 = jnp.bfloat16


def dot(a, b, dims):
    return lax.dot_general(a, b, (dims, ((), ())), preferred_element_type=F32)


NN = ((1,), (0,))
NT = ((1,), (1,))
TN = ((0,), (0,))


def split2(a):
    hi = a.astype(BF16).astype(F32)
    return hi, a - hi


def head_matrix(heads, width):
    size = width // heads
    row = lax.broadcasted_iota(jnp.int32, (heads, width), 0)
    col = lax.broadcasted_iota(jnp.int32, (heads, width), 1)
    return ((col >= row * size) & (col < (row + 1) * size)).astype(F32)


def spread(rows, twice):
    hi, lo = split2(rows)
    return dot(jnp.concatenate([hi, lo], axis=0).astype(BF16), twice, TN)


def head_sums(values, member):
    hi, lo = split2(values)
    return dot(member, hi.astype(BF16), NT) + dot(member, lo.astype(BF16), NT)


def running(rows, upper):
    hi, rest = split2(rows)
    mid, lo = split2(rest)
    k = rows.shape[0]
    out = dot(jnp.concatenate([hi, mid, lo], axis=0).astype(BF16), upper, NN)
    return out[:k] + out[k : 2 * k] + out[2 * k :]


def triangle(width, lower):
    row = lax.broadcasted_iota(jnp.int32, (width, width), 0)
    col = lax.broadcasted_iota(jnp.int32, (width, width), 1)
    return (row >= col) if lower else (row <= col)


def softplus(v):
    return jnp.maximum(v, 0.0) + jnp.log1p(jnp.exp(-jnp.abs(v)))


def column(line, piece, heads):
    shape = (heads, line.shape[1])
    row = lax.broadcasted_iota(jnp.int32, shape, 0)
    col = lax.broadcasted_iota(jnp.int32, shape, 1)
    return jnp.sum(jnp.where(col == row + piece * heads, line, 0.0), axis=1, keepdims=True)


def block_sums(logs, blocks):
    heads = logs.shape[0]
    ones = triangle(GROUP, False).astype(BF16)
    stacked = jnp.concatenate([logs[:, n * GROUP : (n + 1) * GROUP] for n in range(blocks)], axis=0)
    cums = running(stacked, ones)
    return [cums[n * heads : (n + 1) * heads] for n in range(blocks)]


def local_kernel(
    at_ref, x_ref, dy_ref, b_ref, c_ref, raw_ref, bias_ref, rate_ref, *refs
):
    outs, (bt, ct) = refs[:-2], refs[-2:]
    g = pl.program_id(0)
    heads = raw_ref.shape[1]
    length, width = x_ref.shape
    states = b_ref.shape[1]
    blocks = length // GROUP
    piece = at_ref[0] + g
    member = head_matrix(heads, width)
    twice = jnp.concatenate([member, member], axis=0).astype(BF16)

    @pl.when(g == 0)
    def _():
        bt[...] = b_ref[...].T
        ct[...] = c_ref[...].T

    step = softplus(raw_ref[0] + column(bias_ref[...], piece, heads))
    cums = block_sums(-column(rate_ref[...], piece, heads) * step, blocks)
    total = jnp.zeros((heads, 1), F32)
    for n in range(blocks):
        cums[n] = cums[n] + total
        total = cums[n][:, GROUP - 1 :]
    state = jnp.zeros((states, width), F32)
    grad = jnp.zeros((states, width), F32)
    for n in range(blocks):
        rows = slice(n * GROUP, (n + 1) * GROUP)
        weight = spread(jnp.exp(total - cums[n]) * step[:, rows], twice)
        scaled_x = (x_ref[rows, :].astype(F32) * weight).astype(BF16)
        state = state + dot(bt[:, rows], scaled_x, NN)
        scaled_dy = (dy_ref[rows, :].astype(F32) * spread(jnp.exp(cums[n]), twice)).astype(BF16)
        grad = grad + dot(ct[:, rows], scaled_dy, NN)
    decay = spread(jnp.broadcast_to(jnp.exp(total), (heads, 8)), twice)
    for k, out_ref in enumerate(outs):

        @pl.when(g == k)
        def _():
            out_ref[:states] = state
            out_ref[states : 2 * states] = grad
            out_ref[2 * states :] = decay


def local_states(at, x, dy, b, c, raw, bias, rate):
    length, channels = x.shape
    pieces, heads, _ = raw.shape
    width = channels // pieces
    states = b.shape[1]
    columns = pl.BlockSpec((length, width), lambda g, at: (0, at[0] + g))
    maps = pl.BlockSpec((length, states), lambda g, at: (0, 0))
    line = pl.BlockSpec(bias.shape, lambda g, at: (0, 0))
    grid_spec = pltpu.PrefetchScalarGridSpec(
        num_scalar_prefetch=1,
        grid=(PARTS,),
        in_specs=[
            columns,
            columns,
            maps,
            maps,
            pl.BlockSpec((1, heads, length), lambda g, at: (at[0] + g, 0, 0)),
            line,
            line,
        ],
        out_specs=[pl.BlockSpec((2 * states + 8, width), lambda g, at: (0, 0))] * PARTS,
        scratch_shapes=[
            pltpu.VMEM((states, length), BF16),
            pltpu.VMEM((states, length), BF16),
        ],
    )
    return pl.pallas_call(
        local_kernel,
        grid_spec=grid_spec,
        out_shape=[jax.ShapeDtypeStruct((2 * states + 8, width), F32)] * PARTS,
        compiler_params=pltpu.CompilerParams(vmem_limit_bytes=VMEM_LIMIT),
        cost_estimate=pl.CostEstimate(
            flops=8 * PARTS * length * width * states,
            bytes_accessed=4 * PARTS * length * width,
            transcendentals=0,
        ),
        name="local_states",
    )(at, x, dy, b, c, raw, bias, rate)


def grads_kernel(first, scale, part, half, *refs):
    y_ref, x_ref, dy_ref, b_ref, c_ref, raw_ref, bias_ref, rate_ref, skip_ref, mine_ref, other_ref = refs[:11]
    refs = refs[11:]
    if not first:
        dc_in, db_in, par_in = refs[:3]
        refs = refs[5:]
    dx_ref, dc_ref, db_ref, draw_ref, par_ref, left, right, carried, gains, sums, tail, bt, ct = refs
    g = pl.program_id(0)
    heads = raw_ref.shape[1]
    width = x_ref.shape[1]
    states = b_ref.shape[1]
    length = x_ref.shape[0]
    blocks = length // GROUP
    piece = g * half + part
    member = head_matrix(heads, width)
    twice = jnp.concatenate([member, member], axis=0).astype(BF16)
    row = lax.broadcasted_iota(jnp.int32, (3 * width, 128), 0)
    col = lax.broadcasted_iota(jnp.int32, (3 * width, 128), 1)
    size = width // heads
    low = jnp.where(row < width, row, jnp.where(row < 2 * width, row - width, row - 2 * width))
    want = jnp.where(row < 2 * width, col, col - heads)
    adder = ((low >= want * size) & (low < (want + 1) * size)).astype(BF16)
    upper = triangle(GROUP, False)
    lower = triangle(GROUP, True)
    lower_ones = lower.astype(BF16)
    rows = [slice(n * GROUP, (n + 1) * GROUP) for n in range(blocks)]

    @pl.when(g == 0)
    def _():
        bt[...] = b_ref[...].T
        ct[...] = c_ref[...].T
        for n in range(blocks):
            b, c = b_ref[rows[n], :], c_ref[rows[n], :]
            left[n, :, :GROUP] = jnp.where(lower, dot(c, b, NT), 0.0).astype(BF16)
            left[n, :, GROUP:] = c
            right[n, :, :GROUP] = jnp.where(upper, dot(b, c, NT), 0.0).astype(BF16)
            right[n, :, GROUP:] = b
        sums[...] = jnp.zeros_like(sums)
        tail[...] = jnp.zeros_like(tail)
        par_ref[...] = jnp.zeros_like(par_ref) if first else par_in[...]

    raw = raw_ref[0] + column(bias_ref[...], piece, heads)
    rate = column(rate_ref[...], piece, heads)
    step = softplus(raw)
    gate = 1.0 / (1.0 + jnp.exp(-raw))
    cums = block_sums(-rate * step, blocks)
    totals = [cum[:, GROUP - 1 :] for cum in cums]
    own = g == y_ref[0]
    state = jnp.where(own, mine_ref[:states], other_ref[:states])
    grad = jnp.where(own, mine_ref[states:], other_ref[states:])
    gathered = jnp.concatenate(
        [jnp.exp(t) for t in totals] + [column(skip_ref[...], piece, heads)] * (8 - blocks), axis=1
    )
    gathered = spread(gathered, twice)
    wholes = [gathered[n : n + 1] for n in range(blocks)]
    skip = gathered[blocks : blocks + 1]
    ends = []
    for n in range(blocks):
        weight = spread(jnp.exp(totals[n] - cums[n]) * step[:, rows[n]], twice)
        gains[n] = weight
        scaled = (x_ref[rows[n], :].astype(F32) * weight).astype(BF16)
        carried[n, :GROUP] = scaled
        state = wholes[n] * state
        carried[n, GROUP:] = state.astype(BF16)
        state = state + dot(bt[:, rows[n]], scaled, NN)
        ends.append(state)
    direct = jnp.zeros((8, width), F32)
    bias_sum = jnp.zeros((heads, 1), F32)
    rate_sum = jnp.zeros((heads, 1), F32)
    for n in reversed(range(blocks)):
        dy = dy_ref[rows[n], :].astype(F32)
        x = x_ref[rows[n], :].astype(F32)
        direct = direct + jnp.sum((dy * x).reshape(GROUP // 8, 8, width), axis=0)
        scaled_dy = (dy * spread(jnp.exp(cums[n] - totals[n]), twice)).astype(BF16)
        scaled_x = carried[n, :GROUP]
        grad_low = grad.astype(BF16)
        forward = dot(left[n], carried[n], NN)
        backward = dot(right[n], jnp.concatenate([scaled_dy, grad_low], axis=0), NN)
        dx_ref[rows[n], :] = (gains[n] * backward + skip * dy).astype(dx_ref.dtype)
        v = scaled_x.astype(F32) * backward
        difference = scaled_dy.astype(F32) * forward - v
        hi = difference.astype(BF16)
        lo = (difference - hi.astype(F32)).astype(BF16)
        added = dot(jnp.concatenate([hi, lo, v.astype(BF16)], axis=1), adder, NN).T
        edge = head_sums(
            jnp.broadcast_to(jnp.sum(ends[n] * grad, axis=0, keepdims=True), (8, width)),
            member.astype(BF16),
        )
        slope = running(added[:heads], lower_ones) + edge[:, :1]
        here = step[:, rows[n]]
        draw = (added[heads : 2 * heads] / here - rate * slope) * gate[:, rows[n]]
        draw_ref[0, :, rows[n]] = draw
        bias_sum = bias_sum + jnp.sum(draw, axis=1, keepdims=True)
        rate_sum = rate_sum - jnp.sum(here * slope, axis=1, keepdims=True)
        sums[n] += dot(scaled_dy, carried[n], NT)
        tail[n] += dot(scaled_x, grad_low, NT)
        grad = wholes[n] * (grad + dot(ct[:, rows[n]], scaled_dy, NN))
    skip_sum = jnp.sum(head_sums(direct, member.astype(BF16)), axis=1, keepdims=True)
    shape = (heads, par_ref.shape[1])
    spot = lax.broadcasted_iota(jnp.int32, shape, 1) == (
        lax.broadcasted_iota(jnp.int32, shape, 0) + piece * heads
    )
    for k, value in enumerate((bias_sum, skip_sum, rate_sum)):
        par_ref[k : k + 1] += jnp.sum(jnp.where(spot, value * scale, 0.0), axis=0, keepdims=True)

    @pl.when(g == pl.num_programs(0) - 1)
    def _():
        for n in range(blocks):
            pair = jnp.where(lower, sums[n, :, :GROUP], 0.0).astype(BF16)
            dc = dot(pair, b_ref[rows[n], :], NN) + sums[n, :, GROUP:]
            db = dot(pair, c_ref[rows[n], :], TN) + tail[n]
            if not first:
                dc = dc + dc_in[rows[n], :]
                db = db + db_in[rows[n], :]
            dc_ref[rows[n], :] = dc
            db_ref[rows[n], :] = db


def local_grads(part, scale, y, x, dy, b, c, raw, bias, rate, skip, mine, other, before):
    length, channels = x.shape
    pieces, heads, _ = raw.shape
    width = channels // pieces
    states = b.shape[1]
    blocks = length // GROUP
    half = pieces // 2
    first = before is None
    place = lambda g, y: g * half + part
    columns = pl.BlockSpec((length, width), lambda g, y: (0, place(g, y)))
    maps = pl.BlockSpec((length, states), lambda g, y: (0, 0))
    line = pl.BlockSpec(bias.shape, lambda g, y: (0, 0))
    lines = pl.BlockSpec((1, heads, length), lambda g, y: (place(g, y), 0, 0))
    held = pl.BlockSpec((2 * states, width), lambda g, y: (0, 0))
    params = pl.BlockSpec((8, 128), lambda g, y: (0, 0))
    anywhere = pl.BlockSpec(memory_space=pl.ANY)
    in_specs = [columns, columns, maps, maps, lines, line, line, line, held, held]
    args = [x, dy, b, c, raw, bias, rate, skip, mine, other]
    aliases = {}
    if not first:
        dx, dc, db, draw, par = before
        args += [dc, db, par, dx, draw]
        in_specs += [maps, maps, params, anywhere, anywhere]
        aliases = {14: 0, 15: 3}
    grid_spec = pltpu.PrefetchScalarGridSpec(
        num_scalar_prefetch=1,
        grid=(2,),
        in_specs=in_specs,
        out_specs=[columns, maps, maps, lines, params],
        scratch_shapes=[
            pltpu.VMEM((blocks, GROUP, GROUP + states), BF16),
            pltpu.VMEM((blocks, GROUP, GROUP + states), BF16),
            pltpu.VMEM((blocks, GROUP + states, width), BF16),
            pltpu.VMEM((blocks, GROUP, width), F32),
            pltpu.VMEM((blocks, GROUP, GROUP + states), F32),
            pltpu.VMEM((blocks, GROUP, states), F32),
            pltpu.VMEM((states, length), BF16),
            pltpu.VMEM((states, length), BF16),
        ],
    )
    return pl.pallas_call(
        functools.partial(grads_kernel, first, scale, part, half),
        grid_spec=grid_spec,
        out_shape=[
            jax.ShapeDtypeStruct((length, channels), BF16),
            jax.ShapeDtypeStruct((length, states), F32),
            jax.ShapeDtypeStruct((length, states), F32),
            jax.ShapeDtypeStruct((pieces, heads, length), F32),
            jax.ShapeDtypeStruct((8, 128), F32),
        ],
        input_output_aliases=aliases,
        compiler_params=pltpu.CompilerParams(vmem_limit_bytes=VMEM_LIMIT),
        cost_estimate=pl.CostEstimate(
            flops=24 * length * width * (GROUP + states),
            bytes_accessed=12 * length * width,
            transcendentals=0,
        ),
        name="local_grads",
    )(y, *args)


def summed_over(value, axis):
    size = lax.axis_size(axis)
    if size & (size - 1):
        return lax.psum(value, axis)
    bit = 1
    while bit < size:
        steps = (bit, 2 * bit, 3 * bit) if 4 * bit <= size else (bit,)
        got = [lax.ppermute(value, axis, [(i, i ^ s) for i in range(size)]) for s in steps]
        value = value + got[0]
        if len(got) == 3:
            value = value + (got[1] + got[2])
        bit *= 4 if len(got) == 3 else 2
    return value


def entering(sent, kept, states):
    size = lax.axis_size("seq")
    pairs = size // 2
    index = lax.axis_index("seq")
    place, second = index // 2, index % 2 == 1
    swap = [(i, i ^ 1) for i in range(size)]
    got = lax.ppermute(sent, "seq", swap)

    def parts(a):
        return a[:states], a[states : 2 * states], a[2 * states : 2 * states + 1]

    (own_l, own_k, own_d), (got_l, got_k, got_d) = parts(kept), parts(got)
    l1, k1, d1 = [jnp.where(second, b, a) for a, b in ((own_l, got_l), (own_k, got_k), (own_d, got_d))]
    l2, k2, d2 = [jnp.where(second, a, b) for a, b in ((own_l, got_l), (own_k, got_k), (own_d, got_d))]
    whole_l = d2 * l1 + l2
    whole_k = k1 + d1 * k2
    whole_d = d1 * d2
    start = jnp.zeros_like(whole_l)
    end = jnp.zeros_like(whole_k)
    for hop in range(1, pairs):
        message = jnp.where(place == hop - 1, whole_d * start + whole_l, whole_d * end + whole_k)
        route = []
        for y in range(2):
            route.append((2 * (hop - 1) + y, 2 * hop + y))
            route.append((2 * (pairs - hop) + y, 2 * (pairs - hop - 1) + y))
        arrived = lax.ppermute(message, "seq", route)
        start = jnp.where(place == hop, arrived, start)
        end = jnp.where(place == pairs - 1 - hop, arrived, end)
    for_first = jnp.concatenate([start, k2 + d2 * end], axis=0)
    for_second = jnp.concatenate([d1 * start + l1, end], axis=0)
    mine = jnp.where(second, for_second, for_first)
    other = lax.ppermute(jnp.where(second, for_first, for_second), "seq", swap)
    return mine, other


def shards(inputs, input_map, output_map, step_raw, step_bias, decay_rate, skip_gain, cotangent):
    length, channels = inputs.shape[1:]
    heads = step_raw.shape[1]
    states = input_map.shape[2]
    pieces = 2 * PARTS
    group = heads // pieces
    x, b, c, dy = inputs[0], input_map[0], output_map[0], cotangent[0]
    raw = step_raw[0].reshape(pieces, group, length)
    bias = step_bias.reshape(1, heads)
    rate = decay_rate.reshape(1, heads)
    skip = skip_gain.reshape(1, heads)
    y = lax.axis_index("seq") % 2
    scale = 1.0 / math.sqrt(length * lax.axis_size("seq") * lax.axis_size("batch"))

    def local(half):
        at = jnp.reshape(half * PARTS, (1,)).astype(jnp.int32)
        return local_states(at, x, dy, b, c, raw, bias, rate)

    sent, kept = local(1 - y), local(y)
    met = [entering(sent[part], kept[part], states) for part in range(PARTS)]
    here = jnp.reshape(y, (1,)).astype(jnp.int32)
    before = None
    for part in range(PARTS):
        mine, other = met[part]
        before = local_grads(
            part, scale, here, x, dy, b, c, raw, bias, rate, skip, mine, other, before
        )
    dx, dc, db, draw, params = before
    summed = summed_over(summed_over(params, "batch"), "seq")
    return (
        dx[None],
        db[None],
        dc[None],
        draw.reshape(heads, length)[None],
        summed[:2, :heads],
        summed[2, :heads],
    )


def solution(mesh):
    in_specs = (
        P("batch", "seq", None),
        P("batch", "seq", None),
        P("batch", "seq", None),
        P("batch", None, "seq"),
        P(),
        P(),
        P(),
        P("batch", "seq", None),
    )
    out_specs = (
        P("batch", "seq", None),
        P("batch", "seq", None),
        P("batch", "seq", None),
        P("batch", None, "seq"),
        P(),
        P(),
    )
    return jax.shard_map(shards, mesh=mesh, in_specs=in_specs, out_specs=out_specs, check_vma=False)
```

profile of v0, /device:TPU:0, one launch (start us, length us, event | category | flops | bytes accessed | tf_op | source)
XLA Modules:
  0.0 130.8 jit_solution(6028881604047874437)
XLA Ops:
  0.6 7.1 %local_states.2 = (f32[264,512]{1,0:T(8,128)}, f32[264,512]{1,0:T(8,128)}) custom-call(s32[1]{0:T(128)} %bitcast.9.at_ref, bf16[1024,2048]{1,0:T(8,128)(2,1)} %bitcast.23, bf16[1024,2048]{1,0:T(8,128)(2,1)} %bitcast.27, bf16[1024,128]{1,0:T(8,128)(2,1)} %bitcast.31, bf16[1024,128]{1,0:T(8,128)(2,1)} %bitcast.35, f32[4,8,1024]{2,1,0:T(8,128)} %bitcast.39, ...), custom_call_target="tpu_custom_call" | custom-call | flops 1073741824 | bytes 4194304 | tf_op jit(solution)/shard_map/local_states/pallas_call | solution.py:151
  7.8 3.0 %collective-permute-start.5 = (f32[264,512]{1,0:T(8,128)}, f32[264,512]{1,0:T(8,128)S(1)}, u32[]{:S(2)}, u32[]{:S(2)}) collective-permute-start(f32[264,512]{1,0:T(8,128)} %get-tuple-element.22), channel_id=1, source_target_pairs={{0,4},{4,0},{8,12},{12,8},{16,20},{20,16},{24,28},{28,24},{1,5},{5... | collective-permute-start | bytes 1622024 | tf_op jit(solution)/shard_map/ppermute | solution.py:365
  10.7 0.0 collective-permute-start
  10.8 7.1 %local_states.3 = (f32[264,512]{1,0:T(8,128)}, f32[264,512]{1,0:T(8,128)}) custom-call(s32[1]{0:T(128)} %bitcast.10.at_ref, bf16[1024,2048]{1,0:T(8,128)(2,1)} %bitcast.24, bf16[1024,2048]{1,0:T(8,128)(2,1)} %bitcast.28, bf16[1024,128]{1,0:T(8,128)(2,1)} %bitcast.32, bf16[1024,128]{1,0:T(8,128)(2,1)} %bitcast.36, f32[4,8,1024]{2,1,0:T(8,128)} %bitcast.40, ...), custom_call_target="tpu_custom_call" | custom-call | flops 1073741824 | bytes 4194304 | tf_op jit(solution)/shard_map/local_states/pallas_call | solution.py:151
  17.9 6.1 %collective-permute-done.5 = f32[264,512]{1,0:T(8,128)S(1)} collective-permute-done((f32[264,512]{1,0:T(8,128)}, f32[264,512]{1,0:T(8,128)S(1)}, u32[]{:S(2)}, u32[]{:S(2)}) %collective-permute-start.5) | collective-permute-done | bytes 540704 | tf_op jit(solution)/shard_map/ppermute | solution.py:365
  24.0 0.7 fusion.4
  24.8 1.2 add_select_fusion.2
  26.0 4.0 %collective-permute-start.6 = (f32[128,512]{1,0:T(8,128)S(1)}, f32[128,512]{1,0:T(8,128)S(1)}, u32[]{:S(2)}, u32[]{:S(2)}) collective-permute-start(f32[128,512]{1,0:T(8,128)S(1)} %get-tuple-element.38), channel_id=1, source_target_pairs={{0,8},{24,16},{4,12},{28,20},{1,9},{25,17},{5,13},{29,21},{2,10},{... | collective-permute-start | bytes 786440 | tf_op jit(solution)/shard_map/ppermute | solution.py:384
  30.0 4.7 %collective-permute-done = f32[264,512]{1,0:T(8,128)S(1)} collective-permute-done((f32[264,512]{1,0:T(8,128)}, f32[264,512]{1,0:T(8,128)S(1)}, u32[]{:S(2)}, u32[]{:S(2)}) %collective-permute-start) | collective-permute-done | bytes 540704 | tf_op jit(solution)/shard_map/ppermute | solution.py:365
  34.8 0.7 fusion.5
  35.5 1.2 add_select_fusion.5
  36.7 3.7 %collective-permute-start.1 = (f32[128,512]{1,0:T(8,128)S(1)}, f32[128,512]{1,0:T(8,128)S(1)}, u32[]{:S(2)}, u32[]{:S(2)}) collective-permute-start(f32[128,512]{1,0:T(8,128)S(1)} %get-tuple-element.48), channel_id=1, source_target_pairs={{0,8},{24,16},{4,12},{28,20},{1,9},{25,17},{5,13},{29,21},{2,10},{... | collective-permute-start | bytes 786440 | tf_op jit(solution)/shard_map/ppermute | solution.py:384
  40.4 0.1 add_select_fusion.1
  40.5 0.7 collective-permute-start.7
  41.2 3.9 %collective-permute-done.1 = f32[128,512]{1,0:T(8,128)S(1)} collective-permute-done((f32[128,512]{1,0:T(8,128)S(1)}, f32[128,512]{1,0:T(8,128)S(1)}, u32[]{:S(2)}, u32[]{:S(2)}) %collective-permute-start.1) | collective-permute-done | bytes 262176 | tf_op jit(solution)/shard_map/ppermute | solution.py:384
  45.1 0.8 add_select_fusion.4
  45.9 0.7 collective-permute-start.2
  46.6 0.8 add_select_fusion
  47.4 1.3 collective-permute-start.8
  48.7 0.1 add_select_fusion.3
  48.8 1.5 %collective-permute-start.3 = (f32[128,512]{1,0:T(8,128)S(1)}, f32[128,512]{1,0:T(8,128)S(1)}, u32[]{:S(2)}, u32[]{:S(2)}) collective-permute-start(f32[128,512]{1,0:T(8,128)S(1)} %add_select_fusion.3), channel_id=1, source_target_pairs={{16,24},{8,0},{20,28},{12,4},{17,25},{9,1},{21,29},{13,5},{18,26},... | collective-permute-start | bytes 786440 | tf_op jit(solution)/shard_map/ppermute | solution.py:384
  50.3 10.9 %collective-permute-done.8 = f32[128,512]{1,0:T(8,128)} collective-permute-done((f32[128,512]{1,0:T(8,128)}, f32[128,512]{1,0:T(8,128)}, u32[]{:S(2)}, u32[]{:S(2)}) %collective-permute-start.8) | collective-permute-done | bytes 262176 | tf_op jit(solution)/shard_map/ppermute | solution.py:384
  61.2 1.3 multiply_add_fusion.1
  62.4 0.9 fusion
  63.4 1.5 %collective-permute-start.9 = (f32[256,512]{1,0:T(8,128)S(1)}, f32[256,512]{1,0:T(8,128)S(1)}, u32[]{:S(2)}, u32[]{:S(2)}) collective-permute-start(f32[256,512]{1,0:T(8,128)S(1)} %get-tuple-element.58), channel_id=1, source_target_pairs={{0,4},{4,0},{8,12},{12,8},{16,20},{20,16},{24,28},{28,24},{1,5},{5... | collective-permute-start | bytes 1572872 | tf_op jit(solution)/shard_map/ppermute | solution.py:390
  64.9 0.2 multiply_add_fusion.4
  65.1 0.9 fusion.2
  66.0 0.7 collective-permute-start.4
  66.8 10.4 %collective-permute-done.9.refs_10_ = f32[256,512]{1,0:T(8,128)S(1)} collective-permute-done((f32[256,512]{1,0:T(8,128)S(1)}, f32[256,512]{1,0:T(8,128)S(1)}, u32[]{:S(2)}, u32[]{:S(2)}) %collective-permute-start.9) | collective-permute-done | bytes 524320 | tf_op jit(solution)/shard_map/ppermute | solution.py:390
  77.1 0.8 copy-done.3
  77.9 17.3 %local_grads.2 = (bf16[1024,2048]{1,0:T(8,128)(2,1)}, f32[1024,128]{1,0:T(8,128)}, f32[1024,128]{1,0:T(8,128)}, f32[4,8,1024]{2,1,0:T(8,128)}, f32[8,128]{1,0:T(8,128)}) custom-call(s32[1]{0:T(128)} %bitcast.refs_0_, bf16[1024,2048]{1,0:T(8,128)(2,1)} %bitcast.25, bf16[1024,2048]{1,0:T(8,128)(2,1)} %bitcast.29, bf16[1024,128]{1,0:T(8,128)(2,1)} %bitcast.33, ...), custom_call_target="tpu_custom_call" | custom-call | flops 4831838208 | bytes 6291456 | tf_op jit(solution)/shard_map/local_grads/pallas_call | solution.py:323
  95.3 0.8 copy-done.4
  96.1 17.8 %local_grads.3 = (bf16[1024,2048]{1,0:T(8,128)(2,1)}, f32[1024,128]{1,0:T(8,128)}, f32[1024,128]{1,0:T(8,128)}, f32[4,8,1024]{2,1,0:T(8,128)}, f32[8,128]{1,0:T(8,128)}) custom-call(s32[1]{0:T(128)} %bitcast.refs_0_, bf16[1024,2048]{1,0:T(8,128)(2,1)} %bitcast.26, bf16[1024,2048]{1,0:T(8,128)(2,1)} %bitcast.30, ...), custom_call_target="tpu_custom_call", output_to_operand_aliasing={{0}: (14, {}), {3}: (15, {})} | custom-call | flops 4831838208 | bytes 6291456 | tf_op jit(solution)/shard_map/local_grads/pallas_call | solution.py:323
  113.9 0.1 collective-permute-start.12
  114.0 1.6 %collective-permute-start.11 = (f32[8,128]{1,0:T(8,128)}, f32[8,128]{1,0:T(8,128)S(1)}, u32[]{:S(2)}, u32[]{:S(2)}) collective-permute-start(f32[8,128]{1,0:T(8,128)} %get-tuple-element.33), channel_id=1, source_target_pairs={{0,2},{1,3},{2,0},{3,1},{4,6},{5,7},{6,4},{7,5},{8,10},{9,11},{10,... | collective-permute-start | bytes 12296 | tf_op jit(solution)/shard_map/ppermute | solution.py:351
  115.5 0.3 collective-permute-start.10
  115.8 1.4 %collective-permute-done.12 = f32[8,128]{1,0:T(8,128)S(1)} collective-permute-done((f32[8,128]{1,0:T(8,128)}, f32[8,128]{1,0:T(8,128)S(1)}, u32[]{:S(2)}, u32[]{:S(2)}) %collective-permute-start.12) | collective-permute-done | bytes 4128 | tf_op jit(solution)/shard_map/ppermute | solution.py:351
  117.2 0.7 collective-permute-done.11
  117.9 0.7 add_add_fusion.1
  118.5 0.8 collective-permute-start.15
  119.4 2.2 %collective-permute-start.14 = (f32[8,128]{1,0:T(8,128)S(1)}, f32[8,128]{1,0:T(8,128)S(1)}, u32[]{:S(2)}, u32[]{:S(2)}) collective-permute-start(f32[8,128]{1,0:T(8,128)S(1)} %add_add_fusion.1), channel_id=1, source_target_pairs={{0,8},{4,12},{8,0},{12,4},{16,24},{20,28},{24,16},{28,20},{1,9},{5... | collective-permute-start | bytes 12296 | tf_op jit(solution)/shard_map/ppermute | solution.py:351
  121.5 0.5 collective-permute-start.13
  122.1 1.0 collective-permute-done.15
  123.1 0.1 collective-permute-done.14
  123.2 2.0 %collective-permute-done.13 = f32[8,128]{1,0:T(8,128)S(1)} collective-permute-done((f32[8,128]{1,0:T(8,128)S(1)}, f32[8,128]{1,0:T(8,128)S(1)}, u32[]{:S(2)}, u32[]{:S(2)}) %collective-permute-start.13) | collective-permute-done | bytes 4128 | tf_op jit(solution)/shard_map/ppermute | solution.py:351
  125.2 4.5 %collective-permute-done.16 = f32[8,128]{1,0:T(8,128)S(1)} collective-permute-done((f32[8,128]{1,0:T(8,128)S(1)}, f32[8,128]{1,0:T(8,128)S(1)}, u32[]{:S(2)}, u32[]{:S(2)}) %collective-permute-start.16) | collective-permute-done | bytes 4128 | tf_op jit(solution)/shard_map/ppermute | solution.py:351
  129.7 0.5 slice_bitcast_fusion
  130.2 0.6 slice.54
  (19 shorter events, 0.1 us)
Async XLA Ops:
  7.8 16.3 %collective-permute-start.5 = (f32[264,512]{1,0:T(8,128)}, f32[264,512]{1,0:T(8,128)S(1)}, u32[]{:S(2)}, u32[]{:S(2)}) collective-permute-start(f32[264,512]{1,0:T(8,128)} %get-tuple-element.22), channel_id=1, source_target_pairs={{0,4},{4,0},{8,12},{12,8},{16,20},{20,16},{24,28},{28,24},{1,5},{5... | collective-permute-start | bytes 1622024 | tf_op jit(solution)/shard_map/ppermute | solution.py:365
  10.7 24.1 %collective-permute-start = (f32[264,512]{1,0:T(8,128)}, f32[264,512]{1,0:T(8,128)S(1)}, u32[]{:S(2)}, u32[]{:S(2)}) collective-permute-start(f32[264,512]{1,0:T(8,128)} %get-tuple-element.20), channel_id=1, source_target_pairs={{0,4},{4,0},{8,12},{12,8},{16,20},{20,16},{24,28},{28,24},{1,5},{5... | collective-permute-start | bytes 1622024 | tf_op jit(solution)/shard_map/ppermute | solution.py:365
  24.8 36.4 %copy-start.1 = (f32[264,512]{1,0:T(8,128)S(1)}, f32[264,512]{1,0:T(8,128)}, u32[]{:S(2)}) copy-start(f32[264,512]{1,0:T(8,128)} %get-tuple-element.23) | copy-start | bytes 1622020
  26.0 14.4 %collective-permute-start.6 = (f32[128,512]{1,0:T(8,128)S(1)}, f32[128,512]{1,0:T(8,128)S(1)}, u32[]{:S(2)}, u32[]{:S(2)}) collective-permute-start(f32[128,512]{1,0:T(8,128)S(1)} %get-tuple-element.38), channel_id=1, source_target_pairs={{0,8},{24,16},{4,12},{28,20},{1,9},{25,17},{5,13},{29,21},{2,10},{... | collective-permute-start | bytes 786440 | tf_op jit(solution)/shard_map/ppermute | solution.py:384
  36.7 8.4 %collective-permute-start.1 = (f32[128,512]{1,0:T(8,128)S(1)}, f32[128,512]{1,0:T(8,128)S(1)}, u32[]{:S(2)}, u32[]{:S(2)}) collective-permute-start(f32[128,512]{1,0:T(8,128)S(1)} %get-tuple-element.48), channel_id=1, source_target_pairs={{0,8},{24,16},{4,12},{28,20},{1,9},{25,17},{5,13},{29,21},{2,10},{... | collective-permute-start | bytes 786440 | tf_op jit(solution)/shard_map/ppermute | solution.py:384
  40.5 6.0 %collective-permute-start.7 = (f32[128,512]{1,0:T(8,128)S(1)}, f32[128,512]{1,0:T(8,128)S(1)}, u32[]{:S(2)}, u32[]{:S(2)}) collective-permute-start(f32[128,512]{1,0:T(8,128)S(1)} %add_select_fusion.1), channel_id=1, source_target_pairs={{8,16},{16,8},{12,20},{20,12},{9,17},{17,9},{13,21},{21,13},{10,18... | collective-permute-start | bytes 786440 | tf_op jit(solution)/shard_map/ppermute | solution.py:384
  45.1 19.8 %copy-start = (f32[264,512]{1,0:T(8,128)S(1)}, f32[264,512]{1,0:T(8,128)}, u32[]{:S(2)}) copy-start(f32[264,512]{1,0:T(8,128)} %get-tuple-element.21) | copy-start | bytes 1622020
  45.9 2.8 %collective-permute-start.2 = (f32[128,512]{1,0:T(8,128)}, f32[128,512]{1,0:T(8,128)S(1)}, u32[]{:S(2)}, u32[]{:S(2)}) collective-permute-start(f32[128,512]{1,0:T(8,128)} %add_select_fusion.4), channel_id=1, source_target_pairs={{8,16},{16,8},{12,20},{20,12},{9,17},{17,9},{13,21},{21,13},{10,18... | collective-permute-start | bytes 786440 | tf_op jit(solution)/shard_map/ppermute | solution.py:384
  46.5 0.8 copy-start.2
  47.4 13.8 %collective-permute-start.8 = (f32[128,512]{1,0:T(8,128)}, f32[128,512]{1,0:T(8,128)}, u32[]{:S(2)}, u32[]{:S(2)}) collective-permute-start(f32[128,512]{1,0:T(8,128)} %add_select_fusion), channel_id=1, source_target_pairs={{16,24},{8,0},{20,28},{12,4},{17,25},{9,1},{21,29},{13,5},{18,26},... | collective-permute-start | bytes 786440 | tf_op jit(solution)/shard_map/ppermute | solution.py:384
  48.8 16.1 %collective-permute-start.3 = (f32[128,512]{1,0:T(8,128)S(1)}, f32[128,512]{1,0:T(8,128)S(1)}, u32[]{:S(2)}, u32[]{:S(2)}) collective-permute-start(f32[128,512]{1,0:T(8,128)S(1)} %add_select_fusion.3), channel_id=1, source_target_pairs={{16,24},{8,0},{20,28},{12,4},{17,25},{9,1},{21,29},{13,5},{18,26},... | collective-permute-start | bytes 786440 | tf_op jit(solution)/shard_map/ppermute | solution.py:384
  63.4 13.8 %collective-permute-start.9 = (f32[256,512]{1,0:T(8,128)S(1)}, f32[256,512]{1,0:T(8,128)S(1)}, u32[]{:S(2)}, u32[]{:S(2)}) collective-permute-start(f32[256,512]{1,0:T(8,128)S(1)} %get-tuple-element.58), channel_id=1, source_target_pairs={{0,4},{4,0},{8,12},{12,8},{16,20},{20,16},{24,28},{28,24},{1,5},{5... | collective-permute-start | bytes 1572872 | tf_op jit(solution)/shard_map/ppermute | solution.py:390
  66.0 29.2 %collective-permute-start.4 = (f32[256,512]{1,0:T(8,128)S(1)}, f32[256,512]{1,0:T(8,128)S(1)}, u32[]{:S(2)}, u32[]{:S(2)}) collective-permute-start(f32[256,512]{1,0:T(8,128)S(1)} %get-tuple-element.60), channel_id=1, source_target_pairs={{0,4},{4,0},{8,12},{12,8},{16,20},{20,16},{24,28},{28,24},{1,5},{5... | collective-permute-start | bytes 1572872 | tf_op jit(solution)/shard_map/ppermute | solution.py:390
  77.1 0.8 copy-start.3
  95.2 0.8 copy-start.4
  113.9 3.3 %collective-permute-start.12 = (f32[8,128]{1,0:T(8,128)}, f32[8,128]{1,0:T(8,128)S(1)}, u32[]{:S(2)}, u32[]{:S(2)}) collective-permute-start(f32[8,128]{1,0:T(8,128)} %get-tuple-element.33), channel_id=1, source_target_pairs={{0,3},{1,2},{2,1},{3,0},{4,7},{5,6},{6,5},{7,4},{8,11},{9,10},{10,... | collective-permute-start | bytes 12296 | tf_op jit(solution)/shard_map/ppermute | solution.py:351
  114.0 3.9 %collective-permute-start.11 = (f32[8,128]{1,0:T(8,128)}, f32[8,128]{1,0:T(8,128)S(1)}, u32[]{:S(2)}, u32[]{:S(2)}) collective-permute-start(f32[8,128]{1,0:T(8,128)} %get-tuple-element.33), channel_id=1, source_target_pairs={{0,2},{1,3},{2,0},{3,1},{4,6},{5,7},{6,4},{7,5},{8,10},{9,11},{10,... | collective-permute-start | bytes 12296 | tf_op jit(solution)/shard_map/ppermute | solution.py:351
  115.5 2.3 %collective-permute-start.10 = (f32[8,128]{1,0:T(8,128)}, f32[8,128]{1,0:T(8,128)S(1)}, u32[]{:S(2)}, u32[]{:S(2)}) collective-permute-start(f32[8,128]{1,0:T(8,128)} %get-tuple-element.33), channel_id=1, source_target_pairs={{0,1},{1,0},{2,3},{3,2},{4,5},{5,4},{6,7},{7,6},{8,9},{9,8},{10,11... | collective-permute-start | bytes 12296 | tf_op jit(solution)/shard_map/ppermute | solution.py:351
  118.5 4.5 %collective-permute-start.15 = (f32[8,128]{1,0:T(8,128)S(1)}, f32[8,128]{1,0:T(8,128)S(1)}, u32[]{:S(2)}, u32[]{:S(2)}) collective-permute-start(f32[8,128]{1,0:T(8,128)S(1)} %add_add_fusion.1), channel_id=1, source_target_pairs={{0,12},{4,8},{8,4},{12,0},{16,28},{20,24},{24,20},{28,16},{1,13},{... | collective-permute-start | bytes 12296 | tf_op jit(solution)/shard_map/ppermute | solution.py:351
  119.4 3.8 %collective-permute-start.14 = (f32[8,128]{1,0:T(8,128)S(1)}, f32[8,128]{1,0:T(8,128)S(1)}, u32[]{:S(2)}, u32[]{:S(2)}) collective-permute-start(f32[8,128]{1,0:T(8,128)S(1)} %add_add_fusion.1), channel_id=1, source_target_pairs={{0,8},{4,12},{8,0},{12,4},{16,24},{20,28},{24,16},{28,20},{1,9},{5... | collective-permute-start | bytes 12296 | tf_op jit(solution)/shard_map/ppermute | solution.py:351
  121.5 3.6 %collective-permute-start.13 = (f32[8,128]{1,0:T(8,128)S(1)}, f32[8,128]{1,0:T(8,128)S(1)}, u32[]{:S(2)}, u32[]{:S(2)}) collective-permute-start(f32[8,128]{1,0:T(8,128)S(1)} %add_add_fusion.1), channel_id=1, source_target_pairs={{0,4},{4,0},{8,12},{12,8},{16,20},{20,16},{24,28},{28,24},{1,5},{5... | collective-permute-start | bytes 12296 | tf_op jit(solution)/shard_map/ppermute | solution.py:351
  125.2 4.5 %collective-permute-start.16 = (f32[8,128]{1,0:T(8,128)S(1)}, f32[8,128]{1,0:T(8,128)S(1)}, u32[]{:S(2)}, u32[]{:S(2)}) collective-permute-start(f32[8,128]{1,0:T(8,128)S(1)} %add_add_fusion), channel_id=1, source_target_pairs={{0,16},{4,20},{8,24},{12,28},{16,0},{20,4},{24,8},{28,12},{1,17},{... | collective-permute-start | bytes 12296 | tf_op jit(solution)/shard_map/ppermute | solution.py:351
where the time goes:
time: 131 us
  Pallas kernels  49.4 us (38%)
  waiting for transfers between devices  45.7 us (35%)
  starting transfers between devices  22.5 us (17%)
  other arithmetic  9.61 us (7%)
  local copies, waits for them, and re-layouts  2.69 us (2%)
    pallas_call x2, Pallas kernels, local_grads(): pl.pallas_call(functools.partial(grads_kernel, first, scale, part, half),...  35.1 us
    ppermute x6, waiting for transfers between devices, entering(): arrived = lax.ppermute(message, 'seq', route)  14.8 us
    pallas_call x2, Pallas kernels, local_states(): pl.pallas_call(local_kernel, grid_spec=grid_spec, out_shape=[jax.ShapeDty...  14.2 us
    ppermute x6, starting transfers between devices, entering(): arrived = lax.ppermute(message, 'seq', route)  11.9 us
    ppermute x2, waiting for transfers between devices, entering(): got = lax.ppermute(sent, 'seq', swap)  10.9 us
    ppermute x2, waiting for transfers between devices, entering(): other = lax.ppermute(jnp.where(second, for_first, for_second), 'seq', swap)  10.4 us
    ppermute x7, waiting for transfers between devices, summed_over(): lax.ppermute(value, axis, [(i, i ^ s) for i in range(size)])  9.63 us
    ppermute x7, starting transfers between devices, summed_over(): lax.ppermute(value, axis, [(i, i ^ s) for i in range(size)])  5.43 us
  transfers between devices with their start and end apart: 17, of which 11 were waited for; matrix products, arithmetic and copies ran while one was open for 7% of the time, Pallas kernels for 19%

commit v1 on v0

v1 whole, which is shorter than its diff:
```python
import functools
import math

import jax
import jax.numpy as jnp
from jax import lax
from jax.experimental import pallas as pl
from jax.experimental.pallas import tpu as pltpu
from jax.sharding import PartitionSpec as P

GROUP = 256
PARTS = 2
VMEM_LIMIT = 61 * 1024 * 1024
F32 = jnp.float32
BF16 = jnp.bfloat16


def dot(a, b, dims):
    return lax.dot_general(a, b, (dims, ((), ())), preferred_element_type=F32)


NN = ((1,), (0,))
NT = ((1,), (1,))
TN = ((0,), (0,))


def split2(a):
    hi = a.astype(BF16).astype(F32)
    return hi, a - hi


def head_matrix(heads, width):
    size = width // heads
    row = lax.broadcasted_iota(jnp.int32, (heads, width), 0)
    col = lax.broadcasted_iota(jnp.int32, (heads, width), 1)
    return ((col >= row * size) & (col < (row + 1) * size)).astype(F32)


def head_sums(values, member):
    hi, lo = split2(values)
    return dot(member, hi.astype(BF16), NT) + dot(member, lo.astype(BF16), NT)


def running(rows, upper):
    hi, rest = split2(rows)
    mid, lo = split2(rest)
    k = rows.shape[0]
    out = dot(jnp.concatenate([hi, mid, lo], axis=0).astype(BF16), upper, NN)
    return out[:k] + out[k : 2 * k] + out[2 * k :]


def triangle(width, lower):
    row = lax.broadcasted_iota(jnp.int32, (width, width), 0)
    col = lax.broadcasted_iota(jnp.int32, (width, width), 1)
    return (row >= col) if lower else (row <= col)


def softplus(v):
    return jnp.maximum(v, 0.0) + jnp.log1p(jnp.exp(-jnp.abs(v)))


def column(line, piece, heads):
    shape = (heads, line.shape[1])
    row = lax.broadcasted_iota(jnp.int32, shape, 0)
    col = lax.broadcasted_iota(jnp.int32, shape, 1)
    return jnp.sum(jnp.where(col == row + piece * heads, line, 0.0), axis=1, keepdims=True)


def block_sums(logs, blocks):
    heads = logs.shape[0]
    ones = triangle(GROUP, False).astype(BF16)
    stacked = jnp.concatenate([logs[:, n * GROUP : (n + 1) * GROUP] for n in range(blocks)], axis=0)
    cums = running(stacked, ones)
    return [cums[n * heads : (n + 1) * heads] for n in range(blocks)]


def factors(raw, bias, rate, skip, columns_ref, table_ref):
    heads, length = raw.shape
    width = table_ref.shape[1]
    blocks = length // GROUP
    step = softplus(raw + bias)
    cums = block_sums(-rate * step, blocks)
    totals = [cum[:, GROUP - 1 :] for cum in cums]
    before = [jnp.zeros((heads, 1), F32)]
    for total in totals:
        before.append(before[-1] + total)
    for n in range(blocks):
        rows = slice(n * GROUP, (n + 1) * GROUP)
        gain = split2(jnp.exp(totals[n] - cums[n]) * step[:, rows])
        lift = split2(jnp.exp(cums[n] - totals[n]))
        columns_ref[rows, :] = jnp.concatenate([*gain, *lift], axis=0).T.astype(BF16)
    whole = before[-1]
    lines = [jnp.exp(t) for t in totals]
    lines += [jnp.exp(whole - before[n + 1]) for n in range(blocks)]
    lines += [jnp.exp(before[n + 1]) for n in range(blocks)]
    lines += [jnp.exp(whole), skip]
    lines += [skip] * (-len(lines) % 8)
    hi, lo = split2(jnp.concatenate(lines, axis=1).T)
    member = head_matrix(heads, width).astype(BF16)
    table_ref[...] = dot(hi.astype(BF16), member, NN) + dot(lo.astype(BF16), member, NN)


def picker(piece, heads, all_heads, width, first):
    shape = (4 * all_heads, width)
    row = lax.broadcasted_iota(jnp.int32, shape, 0)
    col = lax.broadcasted_iota(jnp.int32, shape, 1)
    size = width // heads
    base = (0 if first else 2 * all_heads) + piece * heads
    hit = None
    for term in range(2):
        low = (row - (base + term * all_heads)) * size
        one = (col >= low) & (col < low + size)
        hit = one if hit is None else hit | one
    return hit.astype(BF16)


def local_kernel(first, *refs):
    at_ref, x_ref, dy_ref, b_ref, c_ref = refs[:5]
    if first:
        raw_ref, bias_ref, rate_ref, skip_ref = refs[5:9]
        outs = refs[9 : 9 + PARTS]
        xs_ref, ys_ref, direct_ref, columns_ref, table_ref, bt, ct = refs[9 + PARTS :]
    else:
        columns_ref, table_ref = refs[5:7]
        outs = refs[10 : 10 + PARTS]
        xs_ref, ys_ref, direct_ref, bt, ct = refs[10 + PARTS :]
    g = pl.program_id(0)
    length, width = x_ref.shape
    states = b_ref.shape[1]
    blocks = length // GROUP
    piece = at_ref[0] + g
    all_heads = columns_ref.shape[1] // 4
    heads = all_heads * width // table_ref.shape[1]

    @pl.when(g == 0)
    def _():
        bt[...] = b_ref[...].T
        ct[...] = c_ref[...].T
        if first:
            factors(
                raw_ref[0],
                column(bias_ref[...], 0, all_heads),
                column(rate_ref[...], 0, all_heads),
                column(skip_ref[...], 0, all_heads),
                columns_ref,
                table_ref,
            )

    gain = picker(piece, heads, all_heads, width, True)
    lift = picker(piece, heads, all_heads, width, False)
    table = table_ref[:, pl.ds(pl.multiple_of(piece * width, width), width)]
    state = jnp.zeros((states, width), F32)
    grad = jnp.zeros((states, width), F32)
    direct = jnp.zeros((8, width), F32)
    for n in range(blocks):
        rows = slice(n * GROUP, (n + 1) * GROUP)
        x = x_ref[rows, :].astype(F32)
        dy = dy_ref[rows, :].astype(F32)
        direct = direct + jnp.sum((dy * x).reshape(GROUP // 8, 8, width), axis=0)
        scaled_x = (x * dot(columns_ref[rows, :], gain, NN)).astype(BF16)
        scaled_dy = (dy * dot(columns_ref[rows, :], lift, NN)).astype(BF16)
        xs_ref[rows, :] = scaled_x
        ys_ref[rows, :] = scaled_dy
        later = table[blocks + n : blocks + n + 1]
        earlier = table[2 * blocks + n : 2 * blocks + n + 1]
        state = state + later * dot(bt[:, rows], scaled_x, NN)
        grad = grad + earlier * dot(ct[:, rows], scaled_dy, NN)
    direct_ref[...] = direct
    decay = jnp.broadcast_to(table[3 * blocks : 3 * blocks + 1], (8, width))
    for k, out_ref in enumerate(outs):

        @pl.when(g == k)
        def _():
            out_ref[:states] = state
            out_ref[states : 2 * states] = grad
            out_ref[2 * states :] = decay


def local_states(at, x, dy, b, c, vectors, before):
    length, channels = x.shape
    states = b.shape[1]
    pieces = 2 * PARTS
    width = channels // pieces
    lines = 3 * (length // GROUP) + 2
    lines += -lines % 8
    first = before is None
    whole = lambda g, at: (0, 0)
    columns = pl.BlockSpec((length, width), lambda g, at: (0, at[0] + g))
    strip = pl.BlockSpec((8, width), lambda g, at: (0, at[0] + g))
    maps = pl.BlockSpec((length, states), whole)
    anywhere = pl.BlockSpec(memory_space=pl.ANY)
    in_specs = [columns, columns, maps, maps]
    out_specs = [pl.BlockSpec((2 * states + 8, width), whole)] * PARTS + [columns, columns, strip]
    out_shape = [jax.ShapeDtypeStruct((2 * states + 8, width), F32)] * PARTS + [
        jax.ShapeDtypeStruct((length, channels), BF16),
        jax.ShapeDtypeStruct((length, channels), BF16),
        jax.ShapeDtypeStruct((8, channels), F32),
    ]
    aliases = {}
    if first:
        raw, bias, rate, skip = vectors
        heads = raw.shape[1]
        args = [raw, bias, rate, skip]
        in_specs += [pl.BlockSpec(raw.shape, lambda g, at: (0, 0, 0))]
        in_specs += [pl.BlockSpec(bias.shape, whole)] * 3
        tables = [
            jax.ShapeDtypeStruct((length, 4 * heads), BF16),
            jax.ShapeDtypeStruct((lines, channels), F32),
        ]
        out_shape += tables
        out_specs += [pl.BlockSpec(t.shape, whole) for t in tables]
    else:
        xs, ys, direct, factor_columns, table = before
        args = [factor_columns, table, xs, ys, direct]
        in_specs += [pl.BlockSpec(factor_columns.shape, whole), pl.BlockSpec(table.shape, whole)]
        in_specs += [anywhere] * 3
        aliases = {7: PARTS, 8: PARTS + 1, 9: PARTS + 2}
    grid_spec = pltpu.PrefetchScalarGridSpec(
        num_scalar_prefetch=1,
        grid=(PARTS,),
        in_specs=in_specs,
        out_specs=out_specs,
        scratch_shapes=[
            pltpu.VMEM((states, length), BF16),
            pltpu.VMEM((states, length), BF16),
        ],
    )
    out = pl.pallas_call(
        functools.partial(local_kernel, first),
        grid_spec=grid_spec,
        out_shape=out_shape,
        input_output_aliases=aliases,
        compiler_params=pltpu.CompilerParams(vmem_limit_bytes=VMEM_LIMIT),
        cost_estimate=pl.CostEstimate(
            flops=8 * PARTS * length * width * states,
            bytes_accessed=8 * PARTS * length * width,
            transcendentals=0,
        ),
        name="local_states",
    )(at, x, dy, b, c, *args)
    return out[:PARTS], list(out[PARTS:])


def grads_kernel(first, scale, part, half, *refs):
    y_ref, xs_ref, ys_ref, dy_ref, direct_ref, b_ref, c_ref, columns_ref, table_ref = refs[:9]
    raw_ref, bias_ref, rate_ref, mine_ref, other_ref = refs[9:14]
    refs = refs[14:]
    if not first:
        dc_in, db_in, par_in = refs[:3]
        refs = refs[5:]
    dx_ref, dc_ref, db_ref, draw_ref, par_ref = refs[:5]
    left, right, sums, dc_sum, db_sum, bt, ct, adder = refs[5:]
    g = pl.program_id(0)
    heads = raw_ref.shape[1]
    length, width = xs_ref.shape
    states = b_ref.shape[1]
    blocks = length // GROUP
    piece = g * half + part
    all_heads = columns_ref.shape[1] // 4
    member = head_matrix(heads, width).astype(BF16)
    lower = triangle(GROUP, True)
    rows = [slice(n * GROUP, (n + 1) * GROUP) for n in range(blocks)]

    @pl.when(g == 0)
    def _():
        bt[...] = b_ref[...].T
        ct[...] = c_ref[...].T
        upper = triangle(GROUP, False)
        for n in range(blocks):
            b, c = b_ref[rows[n], :], c_ref[rows[n], :]
            left[n] = jnp.where(lower, dot(c, b, NT), 0.0).astype(BF16)
            right[n] = jnp.where(upper, dot(b, c, NT), 0.0).astype(BF16)
        sums[...] = jnp.zeros_like(sums)
        dc_sum[...] = jnp.zeros_like(dc_sum)
        db_sum[...] = jnp.zeros_like(db_sum)
        par_ref[...] = jnp.zeros_like(par_ref) if first else par_in[...]
        row = lax.broadcasted_iota(jnp.int32, (width, 128), 0)
        col = lax.broadcasted_iota(jnp.int32, (width, 128), 1)
        size = width // heads
        one = ((row >= col * size) & (row < (col + 1) * size)).astype(BF16)
        col = col - heads
        two = ((row >= col * size) & (row < (col + 1) * size)).astype(BF16)
        adder[:width] = one
        adder[width : 2 * width] = one
        adder[2 * width :] = two

    own = g == y_ref[0]
    state = jnp.where(own, mine_ref[:states], other_ref[:states])
    grad = jnp.where(own, mine_ref[states:], other_ref[states:])
    table = table_ref[...]
    skip = table[3 * blocks + 1 : 3 * blocks + 2]
    entering_low, ends = [], []
    for n in range(blocks):
        state = table[n : n + 1] * state
        entering_low.append(state.astype(BF16))
        state = state + dot(bt[:, rows[n]], xs_ref[rows[n], :], NN)
        ends.append(state)
    leaving_low, edges = [None] * blocks, [None] * blocks
    for n in reversed(range(blocks)):
        leaving_low[n] = grad.astype(BF16)
        edges[n] = jnp.sum(ends[n] * grad, axis=0, keepdims=True)
        grad = table[n : n + 1] * (grad + dot(ct[:, rows[n]], ys_ref[rows[n], :], NN))
    gain = picker(piece, heads, all_heads, width, True)
    added = []
    for n in range(blocks):
        scaled_x, scaled_dy = xs_ref[rows[n], :], ys_ref[rows[n], :]
        forward = dot(left[n], scaled_x, NN) + dot(c_ref[rows[n], :], entering_low[n], NN)
        backward = dot(right[n], scaled_dy, NN) + dot(b_ref[rows[n], :], leaving_low[n], NN)
        weight = dot(columns_ref[rows[n], :], gain, NN)
        dx_ref[rows[n], :] = (weight * backward + skip * dy_ref[rows[n], :].astype(F32)).astype(
            dx_ref.dtype
        )
        v = scaled_x.astype(F32) * backward
        difference = scaled_dy.astype(F32) * forward - v
        hi = difference.astype(BF16)
        lo = (difference - hi.astype(F32)).astype(BF16)
        added.append(dot(jnp.concatenate([hi, lo, v.astype(BF16)], axis=1), adder[...], NN))
        sums[n] += dot(scaled_dy, scaled_x, NT)
        dc_sum[n] += dot(scaled_dy, entering_low[n], NT)
        db_sum[n] += dot(scaled_x, leaving_low[n], NT)
    added = [a.T for a in added]
    edge = head_sums(jnp.concatenate(edges + [edges[0]] * (8 - blocks), axis=0), member)
    slopes = running(
        jnp.concatenate([a[:heads] for a in added], axis=0), lower.astype(BF16)
    )
    slope = jnp.concatenate(
        [slopes[n * heads : (n + 1) * heads] + edge[:, n : n + 1] for n in range(blocks)], axis=1
    )
    v = jnp.concatenate([a[heads : 2 * heads] for a in added], axis=1)
    raw = raw_ref[0] + column(bias_ref[...], piece, heads)
    step = softplus(raw)
    draw = (v / step - column(rate_ref[...], piece, heads) * slope) / (1.0 + jnp.exp(-raw))
    draw_ref[0] = draw
    values = (
        jnp.sum(draw, axis=1, keepdims=True),
        jnp.sum(head_sums(direct_ref[...], member), axis=1, keepdims=True),
        -jnp.sum(step * slope, axis=1, keepdims=True),
    )
    shape = (heads, par_ref.shape[1])
    spot = lax.broadcasted_iota(jnp.int32, shape, 1) == (
        lax.broadcasted_iota(jnp.int32, shape, 0) + piece * heads
    )
    for k, value in enumerate(values):
        par_ref[k : k + 1] += jnp.sum(jnp.where(spot, value * scale, 0.0), axis=0, keepdims=True)

    @pl.when(g == pl.num_programs(0) - 1)
    def _():
        for n in range(blocks):
            pair = jnp.where(lower, sums[n], 0.0).astype(BF16)
            dc = dot(pair, b_ref[rows[n], :], NN) + dc_sum[n]
            db = dot(pair, c_ref[rows[n], :], TN) + db_sum[n]
            if not first:
                dc = dc + dc_in[rows[n], :]
                db = db + db_in[rows[n], :]
            dc_ref[rows[n], :] = dc
            db_ref[rows[n], :] = db


def local_grads(part, scale, y, saved, dy, b, c, vectors, mine, other, before):
    xs, ys, direct, factor_columns, table = saved
    raw, bias, rate, _ = vectors
    length, channels = xs.shape
    pieces = 2 * PARTS
    heads = raw.shape[1] // pieces
    raw = raw.reshape(pieces, heads, length)
    width = channels // pieces
    states = b.shape[1]
    blocks = length // GROUP
    half = pieces // 2
    first = before is None
    whole = lambda g, y: (0, 0)
    place = lambda g, y: (0, g * half + part)
    columns = pl.BlockSpec((length, width), place)
    maps = pl.BlockSpec((length, states), whole)
    line = pl.BlockSpec(bias.shape, whole)
    lines = pl.BlockSpec((1, heads, length), lambda g, y: (g * half + part, 0, 0))
    held = pl.BlockSpec((2 * states, width), whole)
    params = pl.BlockSpec((8, 128), whole)
    anywhere = pl.BlockSpec(memory_space=pl.ANY)
    in_specs = [columns, columns, columns, pl.BlockSpec((8, width), place), maps, maps]
    in_specs += [
        pl.BlockSpec(factor_columns.shape, whole),
        pl.BlockSpec((table.shape[0], width), place),
    ]
    in_specs += [lines, line, line, held, held]
    args = [xs, ys, dy, direct, b, c, factor_columns, table, raw, bias, rate, mine, other]
    aliases = {}
    if not first:
        dx, dc, db, draw, par = before
        args += [dc, db, par, dx, draw]
        in_specs += [maps, maps, params, anywhere, anywhere]
        aliases = {17: 0, 18: 3}
    grid_spec = pltpu.PrefetchScalarGridSpec(
        num_scalar_prefetch=1,
        grid=(2,),
        in_specs=in_specs,
        out_specs=[columns, maps, maps, lines, params],
        scratch_shapes=[
            pltpu.VMEM((blocks, GROUP, GROUP), BF16),
            pltpu.VMEM((blocks, GROUP, GROUP), BF16),
            pltpu.VMEM((blocks, GROUP, GROUP), F32),
            pltpu.VMEM((blocks, GROUP, states), F32),
            pltpu.VMEM((blocks, GROUP, states), F32),
            pltpu.VMEM((states, length), BF16),
            pltpu.VMEM((states, length), BF16),
            pltpu.VMEM((3 * width, 128), BF16),
        ],
    )
    return pl.pallas_call(
        functools.partial(grads_kernel, first, scale, part, half),
        grid_spec=grid_spec,
        out_shape=[
            jax.ShapeDtypeStruct((length, channels), BF16),
            jax.ShapeDtypeStruct((length, states), F32),
            jax.ShapeDtypeStruct((length, states), F32),
            jax.ShapeDtypeStruct((pieces, heads, length), F32),
            jax.ShapeDtypeStruct((8, 128), F32),
        ],
        input_output_aliases=aliases,
        compiler_params=pltpu.CompilerParams(vmem_limit_bytes=VMEM_LIMIT),
        cost_estimate=pl.CostEstimate(
            flops=24 * length * width * (GROUP + states),
            bytes_accessed=12 * length * width,
            transcendentals=0,
        ),
        name="local_grads",
    )(y, *args)


def summed_over(value, axis):
    size = lax.axis_size(axis)
    if size & (size - 1):
        return lax.psum(value, axis)
    bit = 1
    while bit < size:
        steps = (bit, 2 * bit, 3 * bit) if 4 * bit <= size else (bit,)
        got = [lax.ppermute(value, axis, [(i, i ^ s) for i in range(size)]) for s in steps]
        value = value + got[0]
        if len(got) == 3:
            value = value + (got[1] + got[2])
        bit *= 4 if len(got) == 3 else 2
    return value


def entering(got, kept, states):
    size = lax.axis_size("seq")
    pairs = size // 2
    index = lax.axis_index("seq")
    place, second = index // 2, index % 2 == 1
    swap = [(i, i ^ 1) for i in range(size)]

    def parts(a):
        return a[:states], a[states : 2 * states], a[2 * states : 2 * states + 1]

    (own_l, own_k, own_d), (got_l, got_k, got_d) = parts(kept), parts(got)
    l1, k1, d1 = [jnp.where(second, b, a) for a, b in ((own_l, got_l), (own_k, got_k), (own_d, got_d))]
    l2, k2, d2 = [jnp.where(second, a, b) for a, b in ((own_l, got_l), (own_k, got_k), (own_d, got_d))]
    whole_l = d2 * l1 + l2
    whole_k = k1 + d1 * k2
    whole_d = d1 * d2
    start = jnp.zeros_like(whole_l)
    end = jnp.zeros_like(whole_k)
    for hop in range(1, pairs):
        message = jnp.where(place == hop - 1, whole_d * start + whole_l, whole_d * end + whole_k)
        route = []
        for y in range(2):
            route.append((2 * (hop - 1) + y, 2 * hop + y))
            route.append((2 * (pairs - hop) + y, 2 * (pairs - hop - 1) + y))
        arrived = lax.ppermute(message, "seq", route)
        start = jnp.where(place == hop, arrived, start)
        end = jnp.where(place == pairs - 1 - hop, arrived, end)
    for_first = jnp.concatenate([start, k2 + d2 * end], axis=0)
    for_second = jnp.concatenate([d1 * start + l1, end], axis=0)
    mine = jnp.where(second, for_second, for_first)
    other = lax.ppermute(jnp.where(second, for_first, for_second), "seq", swap)
    return mine, other


def shards(inputs, input_map, output_map, step_raw, step_bias, decay_rate, skip_gain, cotangent):
    length, channels = inputs.shape[1:]
    heads = step_raw.shape[1]
    states = input_map.shape[2]
    x, b, c, dy = inputs[0], input_map[0], output_map[0], cotangent[0]
    vectors = (
        step_raw,
        step_bias.reshape(1, heads),
        decay_rate.reshape(1, heads),
        skip_gain.reshape(1, heads),
    )
    size = lax.axis_size("seq")
    y = lax.axis_index("seq") % 2
    scale = 1.0 / math.sqrt(length * size * lax.axis_size("batch"))
    at = lambda half: jnp.reshape(half * PARTS, (1,)).astype(jnp.int32)
    sent, saved = local_states(at(1 - y), x, dy, b, c, vectors, None)
    kept, saved[:3] = local_states(at(y), x, dy, b, c, vectors, saved)
    got = []
    for part in range(PARTS):
        message = sent[part]
        if got:
            message, got[-1] = lax.optimization_barrier((message, got[-1]))
        got.append(lax.ppermute(message, "seq", [(i, i ^ 1) for i in range(size)]))
    met = [entering(got[part], kept[part], states) for part in range(PARTS)]
    here = jnp.reshape(y, (1,)).astype(jnp.int32)
    before = None
    for part in range(PARTS):
        mine, other = met[part]
        before = local_grads(part, scale, here, saved, dy, b, c, vectors, mine, other, before)
    dx, dc, db, draw, params = before
    summed = summed_over(summed_over(params, "batch"), "seq")
    return (
        dx[None],
        db[None],
        dc[None],
        draw.reshape(heads, length)[None],
        summed[:2, :heads],
        summed[2, :heads],
    )


def solution(mesh):
    in_specs = (
        P("batch", "seq", None),
        P("batch", "seq", None),
        P("batch", "seq", None),
        P("batch", None, "seq"),
        P(),
        P(),
        P(),
        P("batch", "seq", None),
    )
    out_specs = (
        P("batch", "seq", None),
        P("batch", "seq", None),
        P("batch", "seq", None),
        P("batch", None, "seq"),
        P(),
        P(),
    )
    return jax.shard_map(shards, mesh=mesh, in_specs=in_specs, out_specs=out_specs, check_vma=False)
```

time: 131 us -> 124 us (0.947)
  Pallas kernels: 49.4 us -> 42.8 us
  waiting for transfers between devices: 45.7 us -> 43.9 us
  starting transfers between devices: 22.5 us -> 24.1 us
    pallas_call x2, Pallas kernels: 35.1 us -> 27.9 us  [local_grads(): pl.pallas_call(functools.partial(grads_kernel, first, scale, part, half),...]
    ppermute x2, starting transfers between devices: 3 us -> 4.77 us  [shards(): got.append(lax.ppermute(message, 'seq', [(i, i ^ 1) for i in range(size)]))]
    ppermute x6, waiting for transfers between devices: 14.8 us -> 13.3 us  [entering(): arrived = lax.ppermute(message, 'seq', route)]
  transfers between devices with their start and end apart: 17 -> 17, of which waited for: 11 -> 11; matrix products, arithmetic and copies ran while one was open for 7% -> 7% of each run, Pallas kernels for 19% -> 17%
where the time goes in v1:
time: 124 us
  waiting for transfers between devices  43.9 us (35%)
  Pallas kernels  42.8 us (35%)
  starting transfers between devices  24.1 us (19%)
  other arithmetic  9.68 us (8%)
  local copies, waits for them, and re-layouts  2.68 us (2%)
    pallas_call x2, Pallas kernels, local_grads(): pl.pallas_call(functools.partial(grads_kernel, first, scale, part, half),...  27.9 us
    pallas_call x2, Pallas kernels, local_states(): pl.pallas_call(functools.partial(local_kernel, first), grid_spec=grid_spe...  14.9 us
    ppermute x6, waiting for transfers between devices, entering(): arrived = lax.ppermute(message, 'seq', route)  13.3 us
    ppermute x2, waiting for transfers between devices, shards(): got.append(lax.ppermute(message, 'seq', [(i, i ^ 1) for i in range(size)]))  11.8 us
    ppermute x6, starting transfers between devices, entering(): arrived = lax.ppermute(message, 'seq', route)  11 us
    ppermute x2, waiting for transfers between devices, entering(): other = lax.ppermute(jnp.where(second, for_first, for_second), 'seq', swap)  10.1 us
    ppermute x7, waiting for transfers between devices, summed_over(): lax.ppermute(value, axis, [(i, i ^ s) for i in range(size)])  8.8 us
    ppermute x7, starting transfers between devices, summed_over(): lax.ppermute(value, axis, [(i, i ^ s) for i in range(size)])  6.25 us
  transfers between devices with their start and end apart: 17, of which 11 were waited for; matrix products, arithmetic and copies ran while one was open for 7% of the time, Pallas kernels for 17%

profile of v1, /device:TPU:0, one launch (start us, length us, event | category | flops | bytes accessed | tf_op | source)
XLA Modules:
  0.0 124.0 jit_solution(10352070610739016196)
XLA Ops:
  0.6 7.8 %local_states.2 = (f32[264,512]{1,0:T(8,128)}, f32[264,512]{1,0:T(8,128)}, bf16[1024,2048]{1,0:T(8,128)(2,1)}, bf16[1024,2048]{1,0:T(8,128)(2,1)}, f32[8,2048]{1...) custom-call(s32[1]{0:T(128)} %bitcast.6.refs_0_, bf16[1024,2048]{1,0:T(8,128)(2,1)} %bitcast.27, ...), custom_call_target="tpu_custom_call" | custom-call | flops 1073741824 | bytes 8388608 | tf_op jit(solution)/shard_map/local_states/pallas_call | solution.py:228
  8.4 3.0 %collective-permute-start = (f32[264,512]{1,0:T(8,128)}, f32[264,512]{1,0:T(8,128)S(1)}, u32[]{:S(2)}, u32[]{:S(2)}) collective-permute-start(f32[264,512]{1,0:T(8,128)} %get-tuple-element.39), channel_id=1, source_target_pairs={{0,4},{4,0},{8,12},{12,8},{16,20},{20,16},{24,28},{28,24},{1,5},{5... | collective-permute-start | bytes 1622024 | tf_op jit(solution)/shard_map/ppermute | solution.py:501
  11.4 7.2 %local_states.3 = (f32[264,512]{1,0:T(8,128)}, f32[264,512]{1,0:T(8,128)}, bf16[1024,2048]{1,0:T(8,128)(2,1)}, bf16[1024,2048]{1,0:T(8,128)(2,1)}, f32[8,2048]{1,0:T(8,128)}) custom-call(s32[1]{0:T(128)} %bitcast.1.refs_0_, bf16[1024,2048]{1,0:T(8,128)(2,1)} %bitcast.28, ...), custom_call_target="tpu_custom_call", output_to_operand_aliasing={{2}: (7, {}), {3}: (8, {}), {4}: (9, {})} | custom-call | flops 1073741824 | bytes 8388608 | tf_op jit(solution)/shard_map/local_states/pallas_call | solution.py:228
  18.6 5.3 %collective-permute-done = f32[264,512]{1,0:T(8,128)S(1)} collective-permute-done((f32[264,512]{1,0:T(8,128)}, f32[264,512]{1,0:T(8,128)S(1)}, u32[]{:S(2)}, u32[]{:S(2)}) %collective-permute-start) | collective-permute-done | bytes 540704 | tf_op jit(solution)/shard_map/ppermute | solution.py:501
  23.9 1.7 %collective-permute-start.1 = (f32[264,512]{1,0:T(8,128)}, f32[264,512]{1,0:T(8,128)S(1)}, u32[]{:S(2)}, u32[]{:S(2)}) collective-permute-start(f32[264,512]{1,0:T(8,128)} %get-tuple-element.40), channel_id=1, source_target_pairs={{0,4},{4,0},{8,12},{12,8},{16,20},{20,16},{24,28},{28,24},{1,5},{5... | collective-permute-start | bytes 1622024 | tf_op jit(solution)/shard_map/ppermute | solution.py:501
  25.7 0.7 fusion.4
  26.4 1.2 add_select_fusion.2
  27.6 3.5 %collective-permute-start.6 = (f32[128,512]{1,0:T(8,128)S(1)}, f32[128,512]{1,0:T(8,128)S(1)}, u32[]{:S(2)}, u32[]{:S(2)}) collective-permute-start(f32[128,512]{1,0:T(8,128)S(1)} %get-tuple-element.58), channel_id=1, source_target_pairs={{0,8},{24,16},{4,12},{28,20},{1,9},{25,17},{5,13},{29,21},{2,10},{... | collective-permute-start | bytes 786440 | tf_op jit(solution)/shard_map/ppermute | solution.py:469
  31.1 6.5 %collective-permute-done.1 = f32[264,512]{1,0:T(8,128)S(1)} collective-permute-done((f32[264,512]{1,0:T(8,128)}, f32[264,512]{1,0:T(8,128)S(1)}, u32[]{:S(2)}, u32[]{:S(2)}) %collective-permute-start.1) | collective-permute-done | bytes 540704 | tf_op jit(solution)/shard_map/ppermute | solution.py:501
  37.6 0.7 fusion.5
  38.3 1.2 add_select_fusion.5
  39.5 3.4 %collective-permute-start.2 = (f32[128,512]{1,0:T(8,128)S(1)}, f32[128,512]{1,0:T(8,128)S(1)}, u32[]{:S(2)}, u32[]{:S(2)}) collective-permute-start(f32[128,512]{1,0:T(8,128)S(1)} %get-tuple-element.68), channel_id=1, source_target_pairs={{0,8},{24,16},{4,12},{28,20},{1,9},{25,17},{5,13},{29,21},{2,10},{... | collective-permute-start | bytes 786440 | tf_op jit(solution)/shard_map/ppermute | solution.py:469
  42.9 0.1 add_select_fusion.1
  43.0 0.7 collective-permute-start.7
  43.7 3.1 %collective-permute-done.2 = f32[128,512]{1,0:T(8,128)S(1)} collective-permute-done((f32[128,512]{1,0:T(8,128)S(1)}, f32[128,512]{1,0:T(8,128)S(1)}, u32[]{:S(2)}, u32[]{:S(2)}) %collective-permute-start.2) | collective-permute-done | bytes 262176 | tf_op jit(solution)/shard_map/ppermute | solution.py:469
  46.8 0.8 add_select_fusion.4
  47.5 0.7 collective-permute-start.3
  48.2 0.8 add_select_fusion
  49.1 1.3 %collective-permute-start.8 = (f32[128,512]{1,0:T(8,128)}, f32[128,512]{1,0:T(8,128)}, u32[]{:S(2)}, u32[]{:S(2)}) collective-permute-start(f32[128,512]{1,0:T(8,128)} %add_select_fusion), channel_id=1, source_target_pairs={{16,24},{8,0},{20,28},{12,4},{17,25},{9,1},{21,29},{13,5},{18,26},... | collective-permute-start | bytes 786440 | tf_op jit(solution)/shard_map/ppermute | solution.py:469
  50.4 0.1 add_select_fusion.3
  50.5 1.5 %collective-permute-start.4 = (f32[128,512]{1,0:T(8,128)S(1)}, f32[128,512]{1,0:T(8,128)S(1)}, u32[]{:S(2)}, u32[]{:S(2)}) collective-permute-start(f32[128,512]{1,0:T(8,128)S(1)} %add_select_fusion.3), channel_id=1, source_target_pairs={{16,24},{8,0},{20,28},{12,4},{17,25},{9,1},{21,29},{13,5},{18,26},... | collective-permute-start | bytes 786440 | tf_op jit(solution)/shard_map/ppermute | solution.py:469
  52.0 10.2 %collective-permute-done.8 = f32[128,512]{1,0:T(8,128)} collective-permute-done((f32[128,512]{1,0:T(8,128)}, f32[128,512]{1,0:T(8,128)}, u32[]{:S(2)}, u32[]{:S(2)}) %collective-permute-start.8) | collective-permute-done | bytes 262176 | tf_op jit(solution)/shard_map/ppermute | solution.py:469
  62.2 1.3 %multiply_add_fusion.1 = (f32[128,512]{1,0:T(8,128)S(1)}, f32[128,512]{1,0:T(8,128)S(1)}, f32[128,512]{1,0:T(8,128)S(1)}, f32[128,512]{1,0:T(8,128)S(1)}) fusion(f32[512]{0:T(512)S(1)} %bitcast.54, f32[264,512]{1,0:T(8,128)S(1)} %copy-done.1, f32[264,512]{1,0:T(8,128)S(1)} %collective-permute-done, pred[]{:T(512)S(6)} %eq.14, ...), kind=kLoop, calls=%fused_computation.9 | loop fusion | flops 786432 | bytes 2887685 | tf_op jit(solution)/shard_map/add | solution.py:473
  63.5 0.9 fusion
  64.4 1.5 %collective-permute-start.9 = (f32[256,512]{1,0:T(8,128)S(1)}, f32[256,512]{1,0:T(8,128)S(1)}, u32[]{:S(2)}, u32[]{:S(2)}) collective-permute-start(f32[256,512]{1,0:T(8,128)S(1)} %get-tuple-element.78), channel_id=1, source_target_pairs={{0,4},{4,0},{8,12},{12,8},{16,20},{20,16},{24,28},{28,24},{1,5},{5... | collective-permute-start | bytes 1572872 | tf_op jit(solution)/shard_map/ppermute | solution.py:475
  65.9 0.2 multiply_add_fusion.4
  66.1 0.9 fusion.2
  67.1 0.5 collective-permute-start.5
  67.6 10.1 %collective-permute-done.9.refs_13_ = f32[256,512]{1,0:T(8,128)S(1)} collective-permute-done((f32[256,512]{1,0:T(8,128)S(1)}, f32[256,512]{1,0:T(8,128)S(1)}, u32[]{:S(2)}, u32[]{:S(2)}) %collective-permute-start.9) | collective-permute-done | bytes 524320 | tf_op jit(solution)/shard_map/ppermute | solution.py:475
  77.7 0.8 copy-done.4
  78.5 13.8 %local_grads.2 = (bf16[1024,2048]{1,0:T(8,128)(2,1)}, f32[1024,128]{1,0:T(8,128)}, f32[1024,128]{1,0:T(8,128)}, f32[4,8,1024]{2,1,0:T(8,128)}, f32[8,128]{1,0:T(8,128)}) custom-call(s32[1]{0:T(128)} %bitcast.refs_0_, bf16[1024,2048]{1,0:T(8,128)(2,1)} %get-tuple-element.35.refs_1_, bf16[1024,2048]{1,0:T(8,128)(2,1)} %get-tuple-element.36.refs_2_, ...), custom_call_target="tpu_custom_call" | custom-call | flops 4831838208 | bytes 6291456 | tf_op jit(solution)/shard_map/local_grads/pallas_call | solution.py:409
  92.3 0.8 copy-done.3
  93.1 14.1 %local_grads.3 = (bf16[1024,2048]{1,0:T(8,128)(2,1)}, f32[1024,128]{1,0:T(8,128)}, f32[1024,128]{1,0:T(8,128)}, f32[4,8,1024]{2,1,0:T(8,128)}, f32[8,128]{1,0:T(8,128)}) custom-call(s32[1]{0:T(128)} %bitcast.refs_0_, bf16[1024,2048]{1,0:T(8,128)(2,1)} %get-tuple-element.35.refs_1_, ...), custom_call_target="tpu_custom_call", output_to_operand_aliasing={{0}: (17, {}), {3}: (18, {})} | custom-call | flops 4831838208 | bytes 6291456 | tf_op jit(solution)/shard_map/local_grads/pallas_call | solution.py:409
  107.3 1.5 %collective-permute-start.11 = (f32[8,128]{1,0:T(8,128)}, f32[8,128]{1,0:T(8,128)S(1)}, u32[]{:S(2)}, u32[]{:S(2)}) collective-permute-start(f32[8,128]{1,0:T(8,128)} %get-tuple-element.53), channel_id=1, source_target_pairs={{0,2},{1,3},{2,0},{3,1},{4,6},{5,7},{6,4},{7,5},{8,10},{9,11},{10,... | collective-permute-start | bytes 12296 | tf_op jit(solution)/shard_map/ppermute | solution.py:437
  108.8 0.3 collective-permute-start.10
  109.1 1.4 %collective-permute-done.12 = f32[8,128]{1,0:T(8,128)S(1)} collective-permute-done((f32[8,128]{1,0:T(8,128)}, f32[8,128]{1,0:T(8,128)S(1)}, u32[]{:S(2)}, u32[]{:S(2)}) %collective-permute-start.12) | collective-permute-done | bytes 4128 | tf_op jit(solution)/shard_map/ppermute | solution.py:437
  110.5 0.6 collective-permute-done.11
  111.2 0.7 add_add_fusion.1
  111.9 0.8 collective-permute-start.15
  112.7 2.2 %collective-permute-start.14 = (f32[8,128]{1,0:T(8,128)S(1)}, f32[8,128]{1,0:T(8,128)S(1)}, u32[]{:S(2)}, u32[]{:S(2)}) collective-permute-start(f32[8,128]{1,0:T(8,128)S(1)} %add_add_fusion.1), channel_id=1, source_target_pairs={{0,8},{4,12},{8,0},{12,4},{16,24},{20,28},{24,16},{28,20},{1,9},{5... | collective-permute-start | bytes 12296 | tf_op jit(solution)/shard_map/ppermute | solution.py:437
  114.8 0.5 collective-permute-start.13
  115.3 1.0 collective-permute-done.15
  116.4 0.1 collective-permute-done.14
  116.5 2.0 %collective-permute-done.13 = f32[8,128]{1,0:T(8,128)S(1)} collective-permute-done((f32[8,128]{1,0:T(8,128)S(1)}, f32[8,128]{1,0:T(8,128)S(1)}, u32[]{:S(2)}, u32[]{:S(2)}) %collective-permute-start.13) | collective-permute-done | bytes 4128 | tf_op jit(solution)/shard_map/ppermute | solution.py:437
  118.5 0.8 collective-permute-start.16
  119.3 3.7 %collective-permute-done.16 = f32[8,128]{1,0:T(8,128)S(1)} collective-permute-done((f32[8,128]{1,0:T(8,128)S(1)}, f32[8,128]{1,0:T(8,128)S(1)}, u32[]{:S(2)}, u32[]{:S(2)}) %collective-permute-start.16) | collective-permute-done | bytes 4128 | tf_op jit(solution)/shard_map/ppermute | solution.py:437
  123.0 0.5 slice_bitcast_fusion
  123.5 0.6 slice.54
  (19 shorter events, 0.1 us)
Async XLA Ops:
  8.4 15.5 %collective-permute-start = (f32[264,512]{1,0:T(8,128)}, f32[264,512]{1,0:T(8,128)S(1)}, u32[]{:S(2)}, u32[]{:S(2)}) collective-permute-start(f32[264,512]{1,0:T(8,128)} %get-tuple-element.39), channel_id=1, source_target_pairs={{0,4},{4,0},{8,12},{12,8},{16,20},{20,16},{24,28},{28,24},{1,5},{5... | collective-permute-start | bytes 1622024 | tf_op jit(solution)/shard_map/ppermute | solution.py:501
  23.9 13.7 %collective-permute-start.1 = (f32[264,512]{1,0:T(8,128)}, f32[264,512]{1,0:T(8,128)S(1)}, u32[]{:S(2)}, u32[]{:S(2)}) collective-permute-start(f32[264,512]{1,0:T(8,128)} %get-tuple-element.40), channel_id=1, source_target_pairs={{0,4},{4,0},{8,12},{12,8},{16,20},{20,16},{24,28},{28,24},{1,5},{5... | collective-permute-start | bytes 1622024 | tf_op jit(solution)/shard_map/ppermute | solution.py:501
  26.4 35.8 %copy-start.1 = (f32[264,512]{1,0:T(8,128)S(1)}, f32[264,512]{1,0:T(8,128)}, u32[]{:S(2)}) copy-start(f32[264,512]{1,0:T(8,128)} %get-tuple-element.43) | copy-start | bytes 1622020
  27.6 15.3 %collective-permute-start.6 = (f32[128,512]{1,0:T(8,128)S(1)}, f32[128,512]{1,0:T(8,128)S(1)}, u32[]{:S(2)}, u32[]{:S(2)}) collective-permute-start(f32[128,512]{1,0:T(8,128)S(1)} %get-tuple-element.58), channel_id=1, source_target_pairs={{0,8},{24,16},{4,12},{28,20},{1,9},{25,17},{5,13},{29,21},{2,10},{... | collective-permute-start | bytes 786440 | tf_op jit(solution)/shard_map/ppermute | solution.py:469
  39.5 7.3 %collective-permute-start.2 = (f32[128,512]{1,0:T(8,128)S(1)}, f32[128,512]{1,0:T(8,128)S(1)}, u32[]{:S(2)}, u32[]{:S(2)}) collective-permute-start(f32[128,512]{1,0:T(8,128)S(1)} %get-tuple-element.68), channel_id=1, source_target_pairs={{0,8},{24,16},{4,12},{28,20},{1,9},{25,17},{5,13},{29,21},{2,10},{... | collective-permute-start | bytes 786440 | tf_op jit(solution)/shard_map/ppermute | solution.py:469
  43.0 5.2 %collective-permute-start.7 = (f32[128,512]{1,0:T(8,128)S(1)}, f32[128,512]{1,0:T(8,128)S(1)}, u32[]{:S(2)}, u32[]{:S(2)}) collective-permute-start(f32[128,512]{1,0:T(8,128)S(1)} %add_select_fusion.1), channel_id=1, source_target_pairs={{8,16},{16,8},{12,20},{20,12},{9,17},{17,9},{13,21},{21,13},{10,18... | collective-permute-start | bytes 786440 | tf_op jit(solution)/shard_map/ppermute | solution.py:469
  46.8 19.1 %copy-start = (f32[264,512]{1,0:T(8,128)S(1)}, f32[264,512]{1,0:T(8,128)}, u32[]{:S(2)}) copy-start(f32[264,512]{1,0:T(8,128)} %get-tuple-element.41) | copy-start | bytes 1622020
  47.5 2.8 %collective-permute-start.3 = (f32[128,512]{1,0:T(8,128)}, f32[128,512]{1,0:T(8,128)S(1)}, u32[]{:S(2)}, u32[]{:S(2)}) collective-permute-start(f32[128,512]{1,0:T(8,128)} %add_select_fusion.4), channel_id=1, source_target_pairs={{8,16},{16,8},{12,20},{20,12},{9,17},{17,9},{13,21},{21,13},{10,18... | collective-permute-start | bytes 786440 | tf_op jit(solution)/shard_map/ppermute | solution.py:469
  48.2 0.8 copy-start.2
  49.1 13.1 %collective-permute-start.8 = (f32[128,512]{1,0:T(8,128)}, f32[128,512]{1,0:T(8,128)}, u32[]{:S(2)}, u32[]{:S(2)}) collective-permute-start(f32[128,512]{1,0:T(8,128)} %add_select_fusion), channel_id=1, source_target_pairs={{16,24},{8,0},{20,28},{12,4},{17,25},{9,1},{21,29},{13,5},{18,26},... | collective-permute-start | bytes 786440 | tf_op jit(solution)/shard_map/ppermute | solution.py:469
  50.5 15.4 %collective-permute-start.4 = (f32[128,512]{1,0:T(8,128)S(1)}, f32[128,512]{1,0:T(8,128)S(1)}, u32[]{:S(2)}, u32[]{:S(2)}) collective-permute-start(f32[128,512]{1,0:T(8,128)S(1)} %add_select_fusion.3), channel_id=1, source_target_pairs={{16,24},{8,0},{20,28},{12,4},{17,25},{9,1},{21,29},{13,5},{18,26},... | collective-permute-start | bytes 786440 | tf_op jit(solution)/shard_map/ppermute | solution.py:469
  64.4 13.3 %collective-permute-start.9 = (f32[256,512]{1,0:T(8,128)S(1)}, f32[256,512]{1,0:T(8,128)S(1)}, u32[]{:S(2)}, u32[]{:S(2)}) collective-permute-start(f32[256,512]{1,0:T(8,128)S(1)} %get-tuple-element.78), channel_id=1, source_target_pairs={{0,4},{4,0},{8,12},{12,8},{16,20},{20,16},{24,28},{28,24},{1,5},{5... | collective-permute-start | bytes 1572872 | tf_op jit(solution)/shard_map/ppermute | solution.py:475
  67.1 25.2 %collective-permute-start.5 = (f32[256,512]{1,0:T(8,128)S(1)}, f32[256,512]{1,0:T(8,128)S(1)}, u32[]{:S(2)}, u32[]{:S(2)}) collective-permute-start(f32[256,512]{1,0:T(8,128)S(1)} %get-tuple-element.80), channel_id=1, source_target_pairs={{0,4},{4,0},{8,12},{12,8},{16,20},{20,16},{24,28},{28,24},{1,5},{5... | collective-permute-start | bytes 1572872 | tf_op jit(solution)/shard_map/ppermute | solution.py:475
  77.7 0.8 copy-start.4
  92.3 0.8 copy-start.3
  107.2 3.3 %collective-permute-start.12 = (f32[8,128]{1,0:T(8,128)}, f32[8,128]{1,0:T(8,128)S(1)}, u32[]{:S(2)}, u32[]{:S(2)}) collective-permute-start(f32[8,128]{1,0:T(8,128)} %get-tuple-element.53), channel_id=1, source_target_pairs={{0,3},{1,2},{2,1},{3,0},{4,7},{5,6},{6,5},{7,4},{8,11},{9,10},{10,... | collective-permute-start | bytes 12296 | tf_op jit(solution)/shard_map/ppermute | solution.py:437
  107.3 3.9 %collective-permute-start.11 = (f32[8,128]{1,0:T(8,128)}, f32[8,128]{1,0:T(8,128)S(1)}, u32[]{:S(2)}, u32[]{:S(2)}) collective-permute-start(f32[8,128]{1,0:T(8,128)} %get-tuple-element.53), channel_id=1, source_target_pairs={{0,2},{1,3},{2,0},{3,1},{4,6},{5,7},{6,4},{7,5},{8,10},{9,11},{10,... | collective-permute-start | bytes 12296 | tf_op jit(solution)/shard_map/ppermute | solution.py:437
  108.8 2.4 %collective-permute-start.10 = (f32[8,128]{1,0:T(8,128)}, f32[8,128]{1,0:T(8,128)S(1)}, u32[]{:S(2)}, u32[]{:S(2)}) collective-permute-start(f32[8,128]{1,0:T(8,128)} %get-tuple-element.53), channel_id=1, source_target_pairs={{0,1},{1,0},{2,3},{3,2},{4,5},{5,4},{6,7},{7,6},{8,9},{9,8},{10,11... | collective-permute-start | bytes 12296 | tf_op jit(solution)/shard_map/ppermute | solution.py:437
  111.9 4.5 %collective-permute-start.15 = (f32[8,128]{1,0:T(8,128)S(1)}, f32[8,128]{1,0:T(8,128)S(1)}, u32[]{:S(2)}, u32[]{:S(2)}) collective-permute-start(f32[8,128]{1,0:T(8,128)S(1)} %add_add_fusion.1), channel_id=1, source_target_pairs={{0,12},{4,8},{8,4},{12,0},{16,28},{20,24},{24,20},{28,16},{1,13},{... | collective-permute-start | bytes 12296 | tf_op jit(solution)/shard_map/ppermute | solution.py:437
  112.7 3.8 %collective-permute-start.14 = (f32[8,128]{1,0:T(8,128)S(1)}, f32[8,128]{1,0:T(8,128)S(1)}, u32[]{:S(2)}, u32[]{:S(2)}) collective-permute-start(f32[8,128]{1,0:T(8,128)S(1)} %add_add_fusion.1), channel_id=1, source_target_pairs={{0,8},{4,12},{8,0},{12,4},{16,24},{20,28},{24,16},{28,20},{1,9},{5... | collective-permute-start | bytes 12296 | tf_op jit(solution)/shard_map/ppermute | solution.py:437
  114.8 3.6 %collective-permute-start.13 = (f32[8,128]{1,0:T(8,128)S(1)}, f32[8,128]{1,0:T(8,128)S(1)}, u32[]{:S(2)}, u32[]{:S(2)}) collective-permute-start(f32[8,128]{1,0:T(8,128)S(1)} %add_add_fusion.1), channel_id=1, source_target_pairs={{0,4},{4,0},{8,12},{12,8},{16,20},{20,16},{24,28},{28,24},{1,5},{5... | collective-permute-start | bytes 12296 | tf_op jit(solution)/shard_map/ppermute | solution.py:437
  118.5 4.5 %collective-permute-start.16 = (f32[8,128]{1,0:T(8,128)S(1)}, f32[8,128]{1,0:T(8,128)S(1)}, u32[]{:S(2)}, u32[]{:S(2)}) collective-permute-start(f32[8,128]{1,0:T(8,128)S(1)} %add_add_fusion), channel_id=1, source_target_pairs={{0,16},{4,20},{8,24},{12,28},{16,0},{20,4},{24,8},{28,12},{1,17},{... | collective-permute-start | bytes 12296 | tf_op jit(solution)/shard_map/ppermute | solution.py:437

commit v2 on v1

--- a/solution.py
+++ b/solution.py
@@ -10,7 +10,7 @@
 
 GROUP = 256
 PARTS = 2
-VMEM_LIMIT = 61 * 1024 * 1024
+VMEM_LIMIT = 60 * 1024 * 1024
 F32 = jnp.float32
 BF16 = jnp.bfloat16
 
@@ -118,12 +118,12 @@
     at_ref, x_ref, dy_ref, b_ref, c_ref = refs[:5]
     if first:
         raw_ref, bias_ref, rate_ref, skip_ref = refs[5:9]
-        outs = refs[9 : 9 + PARTS]
-        xs_ref, ys_ref, direct_ref, columns_ref, table_ref, bt, ct = refs[9 + PARTS :]
+        outs = refs[9:-7]
+        xs_ref, ys_ref, direct_ref, columns_ref, table_ref, bt, ct = refs[-7:]
     else:
         columns_ref, table_ref = refs[5:7]
-        outs = refs[10 : 10 + PARTS]
-        xs_ref, ys_ref, direct_ref, bt, ct = refs[10 + PARTS :]
+        outs = refs[10:-5]
+        xs_ref, ys_ref, direct_ref, bt, ct = refs[-5:]
     g = pl.program_id(0)
     length, width = x_ref.shape
     states = b_ref.shape[1]
@@ -176,7 +176,7 @@
             out_ref[2 * states :] = decay
 
 
-def local_states(at, x, dy, b, c, vectors, before):
+def local_states(at, count, x, dy, b, c, vectors, before):
     length, channels = x.shape
     states = b.shape[1]
     pieces = 2 * PARTS
@@ -190,8 +190,8 @@
     maps = pl.BlockSpec((length, states), whole)
     anywhere = pl.BlockSpec(memory_space=pl.ANY)
     in_specs = [columns, columns, maps, maps]
-    out_specs = [pl.BlockSpec((2 * states + 8, width), whole)] * PARTS + [columns, columns, strip]
-    out_shape = [jax.ShapeDtypeStruct((2 * states + 8, width), F32)] * PARTS + [
+    out_specs = [pl.BlockSpec((2 * states + 8, width), whole)] * count + [columns, columns, strip]
+    out_shape = [jax.ShapeDtypeStruct((2 * states + 8, width), F32)] * count + [
         jax.ShapeDtypeStruct((length, channels), BF16),
         jax.ShapeDtypeStruct((length, channels), BF16),
         jax.ShapeDtypeStruct((8, channels), F32),
@@ -214,10 +214,10 @@
         args = [factor_columns, table, xs, ys, direct]
         in_specs += [pl.BlockSpec(factor_columns.shape, whole), pl.BlockSpec(table.shape, whole)]
         in_specs += [anywhere] * 3
-        aliases = {7: PARTS, 8: PARTS + 1, 9: PARTS + 2}
+        aliases = {7: count, 8: count + 1, 9: count + 2}
     grid_spec = pltpu.PrefetchScalarGridSpec(
         num_scalar_prefetch=1,
-        grid=(PARTS,),
+        grid=(count,),
         in_specs=in_specs,
         out_specs=out_specs,
         scratch_shapes=[
@@ -232,13 +232,13 @@
         input_output_aliases=aliases,
         compiler_params=pltpu.CompilerParams(vmem_limit_bytes=VMEM_LIMIT),
         cost_estimate=pl.CostEstimate(
-            flops=8 * PARTS * length * width * states,
-            bytes_accessed=8 * PARTS * length * width,
+            flops=8 * count * length * width * states,
+            bytes_accessed=8 * count * length * width,
             transcendentals=0,
         ),
         name="local_states",
     )(at, x, dy, b, c, *args)
-    return out[:PARTS], list(out[PARTS:])
+    return out[:count], list(out[count:])
 
 
 def grads_kernel(first, scale, part, half, *refs):
@@ -417,7 +417,7 @@
             jax.ShapeDtypeStruct((8, 128), F32),
         ],
         input_output_aliases=aliases,
-        compiler_params=pltpu.CompilerParams(vmem_limit_bytes=VMEM_LIMIT),
+        compiler_params=pltpu.CompilerParams(vmem_limit_bytes=40 * 1024 * 1024),
         cost_estimate=pl.CostEstimate(
             flops=24 * length * width * (GROUP + states),
             bytes_accessed=12 * length * width,
@@ -442,7 +442,11 @@
     return value
 
 
-def entering(got, kept, states):
+def after(value, *earlier):
+    return lax.optimization_barrier((value, *earlier))[0]
+
+
+def entering(sent, kept, states, token):
     size = lax.axis_size("seq")
     pairs = size // 2
     index = lax.axis_index("seq")
@@ -452,7 +456,10 @@
     def parts(a):
         return a[:states], a[states : 2 * states], a[2 * states : 2 * states + 1]
 
-    (own_l, own_k, own_d), (got_l, got_k, got_d) = parts(kept), parts(got)
+    message = sent if token is None else after(sent, token)
+    arrived = lax.ppermute(message, "seq", swap)
+    token = yield message, arrived
+    (own_l, own_k, own_d), (got_l, got_k, got_d) = parts(kept), parts(after(arrived, token))
     l1, k1, d1 = [jnp.where(second, b, a) for a, b in ((own_l, got_l), (own_k, got_k), (own_d, got_d))]
     l2, k2, d2 = [jnp.where(second, a, b) for a, b in ((own_l, got_l), (own_k, got_k), (own_d, got_d))]
     whole_l = d2 * l1 + l2
@@ -467,17 +474,21 @@
             route.append((2 * (hop - 1) + y, 2 * hop + y))
             route.append((2 * (pairs - hop) + y, 2 * (pairs - hop - 1) + y))
         arrived = lax.ppermute(message, "seq", route)
+        token = yield message, arrived
+        arrived = after(arrived, token)
         start = jnp.where(place == hop, arrived, start)
         end = jnp.where(place == pairs - 1 - hop, arrived, end)
     for_first = jnp.concatenate([start, k2 + d2 * end], axis=0)
     for_second = jnp.concatenate([d1 * start + l1, end], axis=0)
     mine = jnp.where(second, for_second, for_first)
-    other = lax.ppermute(jnp.where(second, for_first, for_second), "seq", swap)
-    return mine, other
+    message = jnp.where(second, for_first, for_second)
+    other = lax.ppermute(message, "seq", swap)
+    yield message, other
+    yield mine, other
 
 
 def shards(inputs, input_map, output_map, step_raw, step_bias, decay_rate, skip_gain, cotangent):
-    length, channels = inputs.shape[1:]
+    length = inputs.shape[1]
     heads = step_raw.shape[1]
     states = input_map.shape[2]
     x, b, c, dy = inputs[0], input_map[0], output_map[0], cotangent[0]
@@ -490,20 +501,37 @@
     size = lax.axis_size("seq")
     y = lax.axis_index("seq") % 2
     scale = 1.0 / math.sqrt(length * size * lax.axis_size("batch"))
-    at = lambda half: jnp.reshape(half * PARTS, (1,)).astype(jnp.int32)
-    sent, saved = local_states(at(1 - y), x, dy, b, c, vectors, None)
-    kept, saved[:3] = local_states(at(y), x, dy, b, c, vectors, saved)
-    got = []
+
+    def local(half, part, count, before):
+        at = jnp.reshape(half * PARTS + part, (1,)).astype(jnp.int32)
+        out, saved = local_states(at, count, x, dy, b, c, vectors, before)
+        return out, saved + list(before[3:] if before else [])
+
+    sent, kept = [], []
+    saved = None
     for part in range(PARTS):
-        message = sent[part]
-        if got:
-            message, got[-1] = lax.optimization_barrier((message, got[-1]))
-        got.append(lax.ppermute(message, "seq", [(i, i ^ 1) for i in range(size)]))
-    met = [entering(got[part], kept[part], states) for part in range(PARTS)]
+        out, saved = local(1 - y, part, 1, saved)
+        sent += out
+    kept, saved = local(y, 0, PARTS, saved)
+
+    transfers = size // 2 + 1
+    order = [(0, 0), (1, 0)] + [
+        pick for k in range(1, transfers) for pick in ((0, k), (1, k - 1)) if pick != (1, 0)
+    ]
+    order.append((1, transfers - 1))
+    flows, token = {}, None
+    for part, k in order:
+        if k == 0:
+            flows[part] = entering(sent[part], kept[part], states, token)
+            message, arrived = next(flows[part])
+            token = arrived if part == 0 else message
+        else:
+            token = flows[part].send(token)[0]
     here = jnp.reshape(y, (1,)).astype(jnp.int32)
     before = None
     for part in range(PARTS):
-        mine, other = met[part]
+        mine, other = next(flows[part])
+        other = after(other, token)
         before = local_grads(part, scale, here, saved, dy, b, c, vectors, mine, other, before)
     dx, dc, db, draw, params = before
     summed = summed_over(summed_over(params, "batch"), "seq")

time: 124 us -> 113 us (0.911)
  waiting for transfers between devices: 43.9 us -> 32.4 us
  starting transfers between devices: 24.1 us -> 29.1 us
  other arithmetic: 9.68 us -> 7.3 us
  local copies, waits for them, and re-layouts: 2.68 us -> 1.13 us
  Pallas kernels: 42.8 us -> 41.5 us
    ppermute x4, waiting for transfers between devices: 21.8 us -> 7.56 us  [the longest x2 5.74 us: entering(): other = lax.ppermute(message, 'seq', swap)]
    ppermute x6, waiting for transfers between devices: 13.3 us -> 18.2 us  [entering(): arrived = lax.ppermute(message, 'seq', route)]
    pallas_call x2, Pallas kernels: 27.9 us -> 24.5 us  [local_grads(): pl.pallas_call(functools.partial(grads_kernel, first, scale, part, half),...]
    ppermute x6, starting transfers between devices: 11 us -> 14 us  [entering(): arrived = lax.ppermute(message, 'seq', route)]
    ppermute x7, starting transfers between devices: 6.25 us -> 9.22 us  [summed_over(): lax.ppermute(value, axis, [(i, i ^ s) for i in range(size)])]
    pallas_call x2 -> x3, Pallas kernels: 14.9 us -> 17 us  [local_states(): pl.pallas_call(functools.partial(local_kernel, first), grid_spec=grid_spe...]
    ppermute x7, waiting for transfers between devices: 8.8 us -> 6.72 us  [summed_over(): lax.ppermute(value, axis, [(i, i ^ s) for i in range(size)])]
    select_n x2, other arithmetic: 1.85 us -> 0.18 us  [the longest x1 0.09 us: entering(): mine = jnp.where(second, for_second, for_first)]
  transfers between devices with their start and end apart: 17 -> 17, of which waited for: 11 -> 12; matrix products, arithmetic and copies ran while one was open for 7% -> 6% of each run, Pallas kernels for 17% -> 21%
where the time goes in v2:
time: 113 us; the launch traced here: 112 us
  Pallas kernels  41.5 us (37%)
  waiting for transfers between devices  32.4 us (29%)
  starting transfers between devices  29.1 us (26%)
  other arithmetic  7.3 us (6%)
    pallas_call x2, Pallas kernels, local_grads(): pl.pallas_call(functools.partial(grads_kernel, first, scale, part, half),...  24.5 us
    ppermute x6, waiting for transfers between devices, entering(): arrived = lax.ppermute(message, 'seq', route)  18.2 us
    pallas_call x3, Pallas kernels, local_states(): pl.pallas_call(functools.partial(local_kernel, first), grid_spec=grid_spe...  17 us
    ppermute x6, starting transfers between devices, entering(): arrived = lax.ppermute(message, 'seq', route)  14 us
    ppermute x7, starting transfers between devices, summed_over(): lax.ppermute(value, axis, [(i, i ^ s) for i in range(size)])  9.22 us
    ppermute x7, waiting for transfers between devices, summed_over(): lax.ppermute(value, axis, [(i, i ^ s) for i in range(size)])  6.72 us
    ppermute x2, waiting for transfers between devices, entering(): other = lax.ppermute(message, 'seq', swap)  5.74 us
    ppermute x2, starting transfers between devices, entering(): arrived = lax.ppermute(message, 'seq', swap)  4.71 us
  transfers between devices with their start and end apart: 17, of which 12 were waited for; matrix products, arithmetic and copies ran while one was open for 6% of the time, Pallas kernels for 21%

profile of v2, /device:TPU:0, one launch (start us, length us, event | category | flops | bytes accessed | tf_op | source)
XLA Modules:
  0.0 112.4 jit_solution(346695838076140497)
XLA Ops:
  0.6 5.2 %local_states.3 = (f32[264,512]{1,0:T(8,128)}, bf16[1024,2048]{1,0:T(8,128)(2,1)}, bf16[1024,2048]{1,0:T(8,128)(2,1)}, f32[8,2048]{1,0:T(8,128)}, bf16[1024,128]{1,0:T(8,128)(2,1)}, /*index=5*/f32[16,2048]{1,0:T(8,128)}) custom-call(s32[1]{0:T(128)} %bitcast.6.refs_0_, bf16[1024,2048]{1,0:T(8,128)(2,1)} %bitcast.47, bf16[1024,2048]{1,0:T(8,128)(2,1)} %bitcast.42, ...), custom_call_target="tpu_custom_call" | custom-call | flops 536870912 | bytes 4194304 | tf_op jit(solution)/shard_map/local_states/pallas_call | solution.py:228
  5.9 3.0 %collective-permute-start = (f32[264,512]{1,0:T(8,128)}, f32[264,512]{1,0:T(8,128)S(1)}, u32[]{:S(2)}, u32[]{:S(2)}) collective-permute-start(f32[264,512]{1,0:T(8,128)} %get-tuple-element.54), channel_id=1, source_target_pairs={{0,4},{4,0},{8,12},{12,8},{16,20},{20,16},{24,28},{28,24},{1,5},{5... | collective-permute-start | bytes 1622024 | tf_op jit(solution)/shard_map/ppermute | solution.py:460
  8.8 4.7 %local_states.4 = (f32[264,512]{1,0:T(8,128)}, bf16[1024,2048]{1,0:T(8,128)(2,1)}, bf16[1024,2048]{1,0:T(8,128)(2,1)}, f32[8,2048]{1,0:T(8,128)}) custom-call(s32[1]{0:T(128)} %bitcast.10.refs_0_, bf16[1024,2048]{1,0:T(8,128)(2,1)} %bitcast.48, bf16[1024,2048]{1,0:T(8,128)(2,1)} %bitcast.43, ...), custom_call_target="tpu_custom_call", output_to_operand_aliasing={{1}: (7, {}), {2}: (8, {}), {3}: (9, {})} | custom-call | flops 536870912 | bytes 4194304 | tf_op jit(solution)/shard_map/local_states/pallas_call | solution.py:228
  13.5 7.1 %local_states.5 = (f32[264,512]{1,0:T(8,128)}, f32[264,512]{1,0:T(8,128)}, bf16[1024,2048]{1,0:T(8,128)(2,1)}, bf16[1024,2048]{1,0:T(8,128)(2,1)}, f32[8,2048]{1,0:T(8,128)}) custom-call(s32[1]{0:T(128)} %bitcast.1.refs_0_, bf16[1024,2048]{1,0:T(8,128)(2,1)} %bitcast.49, ...), custom_call_target="tpu_custom_call", output_to_operand_aliasing={{2}: (7, {}), {3}: (8, {}), {4}: (9, {})} | custom-call | flops 1073741824 | bytes 8388608 | tf_op jit(solution)/shard_map/local_states/pallas_call | solution.py:228
  20.7 0.6 collective-permute-done
  21.3 1.7 %collective-permute-start.1 = (f32[264,512]{1,0:T(8,128)S(1)}, f32[264,512]{1,0:T(8,128)S(1)}, u32[]{:S(2)}, u32[]{:S(2)}) collective-permute-start(f32[264,512]{1,0:T(8,128)S(1)} %copy-done.11), channel_id=1, source_target_pairs={{0,4},{4,0},{8,12},{12,8},{16,20},{20,16},{24,28},{28,24},{1,5},{5... | collective-permute-start | bytes 1622024 | tf_op jit(solution)/shard_map/ppermute | solution.py:460
  23.1 0.7 fusion.5
  23.8 1.2 %add_select_fusion.5 = (f32[128,512]{1,0:T(8,128)S(1)}, f32[128,512]{1,0:T(8,128)S(1)}, f32[128,512]{1,0:T(8,128)S(1)}) fusion(f32[512]{0:T(512)S(1)} %broadcast_multiply_fusion.1, pred[]{:T(512)S(6)} %eq.16, f32[264,512]{1,0:T(8,128)} %get-tuple-element.57, f32[264,512]{1,0:T(8,128)S(1)} %collective-permute-done, pred[]{:T(512)S(6)} %eq.14, ...), kind=kLoop, calls=%fused_computation.19 | loop fusion | flops 720896 | bytes 1841154 | tf_op jit(solution)/shard_map/jit(_where)/select_n | solution.py:471
  25.0 3.5 %collective-permute-start.2 = (f32[128,512]{1,0:T(8,128)S(1)}, f32[128,512]{1,0:T(8,128)S(1)}, u32[]{:S(2)}, u32[]{:S(2)}) collective-permute-start(f32[128,512]{1,0:T(8,128)S(1)} %get-tuple-element.92), channel_id=1, source_target_pairs={{0,8},{24,16},{4,12},{28,20},{1,9},{25,17},{5,13},{29,21},{2,10},{... | collective-permute-start | bytes 786440 | tf_op jit(solution)/shard_map/ppermute | solution.py:476
  28.5 4.4 %collective-permute-done.2 = f32[128,512]{1,0:T(8,128)S(1)} collective-permute-done((f32[128,512]{1,0:T(8,128)S(1)}, f32[128,512]{1,0:T(8,128)S(1)}, u32[]{:S(2)}, u32[]{:S(2)}) %collective-permute-start.2) | collective-permute-done | bytes 262176 | tf_op jit(solution)/shard_map/ppermute | solution.py:476
  32.8 0.1 add_select_fusion.4
  32.9 0.7 collective-permute-start.4
  33.6 1.2 %collective-permute-done.1 = f32[264,512]{1,0:T(8,128)S(1)} collective-permute-done((f32[264,512]{1,0:T(8,128)S(1)}, f32[264,512]{1,0:T(8,128)S(1)}, u32[]{:S(2)}, u32[]{:S(2)}) %collective-permute-start.1) | collective-permute-done | bytes 540704 | tf_op jit(solution)/shard_map/ppermute | solution.py:460
  34.8 0.7 fusion.4
  35.5 1.9 %add_select_fusion.3 = (f32[128,512]{1,0:T(8,128)}, f32[128,512]{1,0:T(8,128)S(1)}, f32[128,512]{1,0:T(8,128)S(1)}) fusion(f32[512]{0:T(512)S(1)} %broadcast_multiply_fusion, pred[]{:T(512)S(6)} %eq.16, f32[264,512]{1,0:T(8,128)} %get-tuple-element.60, f32[264,512]{1,0:T(8,128)S(1)} %collective-permute-done.1, pred[]{:T(512)S(6)} %eq.14, ...), kind=kLoop, calls=%fused_computation.15 | loop fusion | flops 720896 | bytes 1841154 | tf_op jit(solution)/shard_map/jit(_where)/select_n | solution.py:471
  37.4 6.2 %collective-permute-start.3 = (f32[128,512]{1,0:T(8,128)}, f32[128,512]{1,0:T(8,128)S(1)}, u32[]{:S(2)}, u32[]{:S(2)}) collective-permute-start(f32[128,512]{1,0:T(8,128)} %get-tuple-element.86), channel_id=1, source_target_pairs={{0,8},{24,16},{4,12},{28,20},{1,9},{25,17},{5,13},{29,21},{2,10},{... | collective-permute-start | bytes 786440 | tf_op jit(solution)/shard_map/ppermute | solution.py:476
  43.6 0.8 add_select_fusion.2
  44.4 1.3 %collective-permute-start.6 = (f32[128,512]{1,0:T(8,128)}, f32[128,512]{1,0:T(8,128)S(1)}, u32[]{:S(2)}, u32[]{:S(2)}) collective-permute-start(f32[128,512]{1,0:T(8,128)} %add_select_fusion.2), channel_id=1, source_target_pairs={{16,24},{8,0},{20,28},{12,4},{17,25},{9,1},{21,29},{13,5},{18,26},... | collective-permute-start | bytes 786440 | tf_op jit(solution)/shard_map/ppermute | solution.py:476
  45.7 2.1 %collective-permute-done.3 = f32[128,512]{1,0:T(8,128)S(1)} collective-permute-done((f32[128,512]{1,0:T(8,128)}, f32[128,512]{1,0:T(8,128)S(1)}, u32[]{:S(2)}, u32[]{:S(2)}) %collective-permute-start.3) | collective-permute-done | bytes 262176 | tf_op jit(solution)/shard_map/ppermute | solution.py:476
  47.7 0.1 add_select_fusion.1
  47.8 0.7 collective-permute-start.5
  48.5 4.4 %collective-permute-done.6 = f32[128,512]{1,0:T(8,128)S(1)} collective-permute-done((f32[128,512]{1,0:T(8,128)}, f32[128,512]{1,0:T(8,128)S(1)}, u32[]{:S(2)}, u32[]{:S(2)}) %collective-permute-start.6) | collective-permute-done | bytes 262176 | tf_op jit(solution)/shard_map/ppermute | solution.py:476
  52.9 1.3 %multiply_add_fusion.2 = (f32[128,512]{1,0:T(8,128)S(1)}, f32[128,512]{1,0:T(8,128)S(1)}, f32[128,512]{1,0:T(8,128)S(1)}, f32[128,512]{1,0:T(8,128)S(1)}) fusion(f32[512]{0:T(512)S(1)} %bitcast.65, f32[264,512]{1,0:T(8,128)} %get-tuple-element.57, f32[264,512]{1,0:T(8,128)S(1)} %collective-permute-done, pred[]{:T(512)S(6)} %eq.14, ...), kind=kLoop, calls=%fused_computation.11 | loop fusion | flops 786432 | bytes 2887685 | tf_op jit(solution)/shard_map/add | solution.py:482
  54.3 0.1 fusion.2
  54.4 0.1 add_select_fusion
  54.5 1.7 %collective-permute-start.7 = (f32[128,512]{1,0:T(8,128)S(1)}, f32[128,512]{1,0:T(8,128)S(1)}, u32[]{:S(2)}, u32[]{:S(2)}) collective-permute-start(f32[128,512]{1,0:T(8,128)S(1)} %add_select_fusion), channel_id=1, source_target_pairs={{16,24},{8,0},{20,28},{12,4},{17,25},{9,1},{21,29},{13,5},{18,26},... | collective-permute-start | bytes 786440 | tf_op jit(solution)/shard_map/ppermute | solution.py:476
  56.2 0.6 collective-permute-start.9
  56.8 7.4 %collective-permute-done.7 = f32[128,512]{1,0:T(8,128)S(1)} collective-permute-done((f32[128,512]{1,0:T(8,128)S(1)}, f32[128,512]{1,0:T(8,128)S(1)}, u32[]{:S(2)}, u32[]{:S(2)}) %collective-permute-start.7) | collective-permute-done | bytes 262176 | tf_op jit(solution)/shard_map/ppermute | solution.py:476
  64.2 0.2 multiply_add_fusion.1
  64.4 0.1 fusion
  64.5 0.6 collective-permute-start.8
  65.1 5.7 %collective-permute-done.9.refs_13_ = f32[256,512]{1,0:T(8,128)S(1)} collective-permute-done((f32[256,512]{1,0:T(8,128)S(1)}, f32[256,512]{1,0:T(8,128)S(1)}, u32[]{:S(2)}, u32[]{:S(2)}) %collective-permute-start.9) | collective-permute-done | bytes 524320 | tf_op jit(solution)/shard_map/ppermute | solution.py:485
  70.9 12.1 %local_grads.2 = (bf16[1024,2048]{1,0:T(8,128)(2,1)}, f32[1024,128]{1,0:T(8,128)S(1)}, f32[1024,128]{1,0:T(8,128)S(1)}, f32[4,8,1024]{2,1,0:T(8,128)}, f32[8,128]{1,0:T(8,128)S(1)}) custom-call(s32[1]{0:T(128)} %bitcast.refs_0_, bf16[1024,2048]{1,0:T(8,128)(2,1)S(1)} %copy-done, bf16[1024,2048]{1,0:T(8,128)(2,1)S(1)} %copy-done.1, ...), custom_call_target="tpu_custom_call" | custom-call | flops 4831838208 | bytes 6291456 | tf_op jit(solution)/shard_map/local_grads/pallas_call | solution.py:409
  83.0 12.4 %local_grads.3 = (bf16[1024,2048]{1,0:T(8,128)(2,1)}, f32[1024,128]{1,0:T(8,128)}, f32[1024,128]{1,0:T(8,128)}, f32[4,8,1024]{2,1,0:T(8,128)}, f32[8,128]{1,0:T(8,128)S(1)}) custom-call(s32[1]{0:T(128)} %bitcast.refs_0_, bf16[1024,2048]{1,0:T(8,128)(2,1)S(1)} %copy-done, ...), custom_call_target="tpu_custom_call", output_to_operand_aliasing={{0}: (17, {}), {3}: (18, {})} | custom-call | flops 4831838208 | bytes 6291456 | tf_op jit(solution)/shard_map/local_grads/pallas_call | solution.py:409
  95.4 0.1 collective-permute-start.12
  95.4 1.5 %collective-permute-start.11 = (f32[8,128]{1,0:T(8,128)S(1)}, f32[8,128]{1,0:T(8,128)S(1)}, u32[]{:S(2)}, u32[]{:S(2)}) collective-permute-start(f32[8,128]{1,0:T(8,128)S(1)} %get-tuple-element.77), channel_id=1, source_target_pairs={{0,2},{1,3},{2,0},{3,1},{4,6},{5,7},{6,4},{7,5},{8,10},{9,11},{10,... | collective-permute-start | bytes 12296 | tf_op jit(solution)/shard_map/ppermute | solution.py:437
  97.0 0.3 collective-permute-start.10
  97.3 1.2 %collective-permute-done.12 = f32[8,128]{1,0:T(8,128)S(1)} collective-permute-done((f32[8,128]{1,0:T(8,128)S(1)}, f32[8,128]{1,0:T(8,128)S(1)}, u32[]{:S(2)}, u32[]{:S(2)}) %collective-permute-start.12) | collective-permute-done | bytes 4128 | tf_op jit(solution)/shard_map/ppermute | solution.py:437
  98.5 0.6 collective-permute-done.11
  99.1 4.0 %collective-permute-start.15 = (f32[8,128]{1,0:T(8,128)S(1)}, f32[8,128]{1,0:T(8,128)S(1)}, u32[]{:S(2)}, u32[]{:S(2)}) collective-permute-start(f32[8,128]{1,0:T(8,128)S(1)} %add_add_fusion.1), channel_id=1, source_target_pairs={{0,12},{4,8},{8,4},{12,0},{16,28},{20,24},{24,20},{28,16},{1,13},{... | collective-permute-start | bytes 12296 | tf_op jit(solution)/shard_map/ppermute | solution.py:437
  103.1 0.1 collective-permute-start.14
  103.2 1.4 %collective-permute-start.13 = (f32[8,128]{1,0:T(8,128)S(1)}, f32[8,128]{1,0:T(8,128)S(1)}, u32[]{:S(2)}, u32[]{:S(2)}) collective-permute-start(f32[8,128]{1,0:T(8,128)S(1)} %add_add_fusion.1), channel_id=1, source_target_pairs={{0,4},{4,0},{8,12},{12,8},{16,20},{20,16},{24,28},{28,24},{1,5},{5... | collective-permute-start | bytes 12296 | tf_op jit(solution)/shard_map/ppermute | solution.py:437
  104.6 2.0 %collective-permute-done.14 = f32[8,128]{1,0:T(8,128)S(1)} collective-permute-done((f32[8,128]{1,0:T(8,128)S(1)}, f32[8,128]{1,0:T(8,128)S(1)}, u32[]{:S(2)}, u32[]{:S(2)}) %collective-permute-start.14) | collective-permute-done | bytes 4128 | tf_op jit(solution)/shard_map/ppermute | solution.py:437
  106.7 0.1 collective-permute-done.13
  106.8 1.8 %collective-permute-start.16 = (f32[8,128]{1,0:T(8,128)S(1)}, f32[8,128]{1,0:T(8,128)S(1)}, u32[]{:S(2)}, u32[]{:S(2)}) collective-permute-start(f32[8,128]{1,0:T(8,128)S(1)} %add_add_fusion), channel_id=1, source_target_pairs={{0,16},{4,20},{8,24},{12,28},{16,0},{20,4},{24,8},{28,12},{1,17},{... | collective-permute-start | bytes 12296 | tf_op jit(solution)/shard_map/ppermute | solution.py:437
  108.6 2.7 %collective-permute-done.16 = f32[8,128]{1,0:T(8,128)S(1)} collective-permute-done((f32[8,128]{1,0:T(8,128)S(1)}, f32[8,128]{1,0:T(8,128)S(1)}, u32[]{:S(2)}, u32[]{:S(2)}) %collective-permute-start.16) | collective-permute-done | bytes 4128 | tf_op jit(solution)/shard_map/ppermute | solution.py:437
  111.3 0.5 slice_bitcast_fusion
  111.8 0.6 slice.54
  (34 shorter events, 0.1 us)
Async XLA Ops:
  5.9 15.4 %collective-permute-start = (f32[264,512]{1,0:T(8,128)}, f32[264,512]{1,0:T(8,128)S(1)}, u32[]{:S(2)}, u32[]{:S(2)}) collective-permute-start(f32[264,512]{1,0:T(8,128)} %get-tuple-element.54), channel_id=1, source_target_pairs={{0,4},{4,0},{8,12},{12,8},{16,20},{20,16},{24,28},{28,24},{1,5},{5... | collective-permute-start | bytes 1622024 | tf_op jit(solution)/shard_map/ppermute | solution.py:460
  13.5 7.8 %copy-start.11 = (f32[264,512]{1,0:T(8,128)S(1)}, f32[264,512]{1,0:T(8,128)}, u32[]{:S(2)}) copy-start(f32[264,512]{1,0:T(8,128)} %get-tuple-element.55) | copy-start | bytes 1622020
  21.3 13.5 %collective-permute-start.1 = (f32[264,512]{1,0:T(8,128)S(1)}, f32[264,512]{1,0:T(8,128)S(1)}, u32[]{:S(2)}, u32[]{:S(2)}) collective-permute-start(f32[264,512]{1,0:T(8,128)S(1)} %copy-done.11), channel_id=1, source_target_pairs={{0,4},{4,0},{8,12},{12,8},{16,20},{20,16},{24,28},{28,24},{1,5},{5... | collective-permute-start | bytes 1622024 | tf_op jit(solution)/shard_map/ppermute | solution.py:460
  25.0 7.9 %collective-permute-start.2 = (f32[128,512]{1,0:T(8,128)S(1)}, f32[128,512]{1,0:T(8,128)S(1)}, u32[]{:S(2)}, u32[]{:S(2)}) collective-permute-start(f32[128,512]{1,0:T(8,128)S(1)} %get-tuple-element.92), channel_id=1, source_target_pairs={{0,8},{24,16},{4,12},{28,20},{1,9},{25,17},{5,13},{29,21},{2,10},{... | collective-permute-start | bytes 786440 | tf_op jit(solution)/shard_map/ppermute | solution.py:476
  32.9 10.6 %collective-permute-start.4 = (f32[128,512]{1,0:T(8,128)S(1)}, f32[128,512]{1,0:T(8,128)S(1)}, u32[]{:S(2)}, u32[]{:S(2)}) collective-permute-start(f32[128,512]{1,0:T(8,128)S(1)} %add_select_fusion.4), channel_id=1, source_target_pairs={{8,16},{16,8},{12,20},{20,12},{9,17},{17,9},{13,21},{21,13},{10,18... | collective-permute-start | bytes 786440 | tf_op jit(solution)/shard_map/ppermute | solution.py:476
  37.4 26.8 %copy-start.10 = (f32[264,512]{1,0:T(8,128)S(1)}, f32[264,512]{1,0:T(8,128)}, u32[]{:S(2)}) copy-start(f32[264,512]{1,0:T(8,128)} %get-tuple-element.60) | copy-start | bytes 1622020
  37.4 10.3 %collective-permute-start.3 = (f32[128,512]{1,0:T(8,128)}, f32[128,512]{1,0:T(8,128)S(1)}, u32[]{:S(2)}, u32[]{:S(2)}) collective-permute-start(f32[128,512]{1,0:T(8,128)} %get-tuple-element.86), channel_id=1, source_target_pairs={{0,8},{24,16},{4,12},{28,20},{1,9},{25,17},{5,13},{29,21},{2,10},{... | collective-permute-start | bytes 786440 | tf_op jit(solution)/shard_map/ppermute | solution.py:476
  44.4 8.5 %collective-permute-start.6 = (f32[128,512]{1,0:T(8,128)}, f32[128,512]{1,0:T(8,128)S(1)}, u32[]{:S(2)}, u32[]{:S(2)}) collective-permute-start(f32[128,512]{1,0:T(8,128)} %add_select_fusion.2), channel_id=1, source_target_pairs={{16,24},{8,0},{20,28},{12,4},{17,25},{9,1},{21,29},{13,5},{18,26},... | collective-permute-start | bytes 786440 | tf_op jit(solution)/shard_map/ppermute | solution.py:476
  47.8 6.6 %collective-permute-start.5 = (f32[128,512]{1,0:T(8,128)S(1)}, f32[128,512]{1,0:T(8,128)S(1)}, u32[]{:S(2)}, u32[]{:S(2)}) collective-permute-start(f32[128,512]{1,0:T(8,128)S(1)} %add_select_fusion.1), channel_id=1, source_target_pairs={{8,16},{16,8},{12,20},{20,12},{9,17},{17,9},{13,21},{21,13},{10,18... | collective-permute-start | bytes 786440 | tf_op jit(solution)/shard_map/ppermute | solution.py:476
  52.9 18.0 %copy-start.2 = (bf16[1,1024,128]{2,1,0:T(8,128)(2,1)S(1)}, bf16[1,1024,128]{2,1,0:T(8,128)(2,1)}, u32[]{:S(2)}) copy-start(bf16[1,1024,128]{2,1,0:T(8,128)(2,1)} %param.9) | copy-start | bytes 786436
  52.9 18.0 %copy-start.3 = (bf16[1,1024,128]{2,1,0:T(8,128)(2,1)S(1)}, bf16[1,1024,128]{2,1,0:T(8,128)(2,1)}, u32[]{:S(2)}) copy-start(bf16[1,1024,128]{2,1,0:T(8,128)(2,1)} %param.10) | copy-start | bytes 786436
  52.9 18.0 %copy-start.4 = (bf16[1024,128]{1,0:T(8,128)(2,1)S(1)}, bf16[1024,128]{1,0:T(8,128)(2,1)}, u32[]{:S(2)}) copy-start(bf16[1024,128]{1,0:T(8,128)(2,1)} %get-tuple-element.42.refs_5_.refs_7_) | copy-start | bytes 786436
  52.9 18.0 %copy-start.5 = (f32[16,2048]{1,0:T(8,128)S(1)}, f32[16,2048]{1,0:T(8,128)}, u32[]{:S(2)}) copy-start(f32[16,2048]{1,0:T(8,128)} %get-tuple-element.43.refs_6_.refs_8_) | copy-start | bytes 393220
  52.9 18.0 %copy-start.6 = (f32[8,2048]{1,0:T(8,128)S(1)}, f32[8,2048]{1,0:T(8,128)}, u32[]{:S(2)}) copy-start(f32[8,2048]{1,0:T(8,128)} %get-tuple-element.52.refs_4_) | copy-start | bytes 196612
  52.9 18.0 %copy-start.7 = (f32[1,32,1024]{2,1,0:T(8,128)S(1)}, f32[1,32,1024]{2,1,0:T(8,128)}, u32[]{:S(2)}) copy-start(f32[1,32,1024]{2,1,0:T(8,128)} %refs_5_.1) | copy-start | bytes 393220
  54.2 16.6 %copy-start = (bf16[1024,2048]{1,0:T(8,128)(2,1)S(1)}, bf16[1024,2048]{1,0:T(8,128)(2,1)}, u32[]{:S(2)}) copy-start(bf16[1024,2048]{1,0:T(8,128)(2,1)} %get-tuple-element.50.refs_1_) | copy-start | bytes 12582916
  54.2 16.6 %copy-start.1 = (bf16[1024,2048]{1,0:T(8,128)(2,1)S(1)}, bf16[1024,2048]{1,0:T(8,128)(2,1)}, u32[]{:S(2)}) copy-start(bf16[1024,2048]{1,0:T(8,128)(2,1)} %get-tuple-element.51.refs_2_) | copy-start | bytes 12582916
  54.2 16.6 %copy-start.8 = (f32[32]{0:T(128)S(1)}, f32[32]{0:T(128)}, u32[]{:S(2)}) copy-start(f32[32]{0:T(128)} %param.12) | copy-start | bytes 388
  54.3 16.6 %copy-start.9 = (f32[32]{0:T(128)S(1)}, f32[32]{0:T(128)}, u32[]{:S(2)}) copy-start(f32[32]{0:T(128)} %param.13) | copy-start | bytes 388
  54.5 9.7 %collective-permute-start.7 = (f32[128,512]{1,0:T(8,128)S(1)}, f32[128,512]{1,0:T(8,128)S(1)}, u32[]{:S(2)}, u32[]{:S(2)}) collective-permute-start(f32[128,512]{1,0:T(8,128)S(1)} %add_select_fusion), channel_id=1, source_target_pairs={{16,24},{8,0},{20,28},{12,4},{17,25},{9,1},{21,29},{13,5},{18,26},... | collective-permute-start | bytes 786440 | tf_op jit(solution)/shard_map/ppermute | solution.py:476
  56.2 14.6 %collective-permute-start.9 = (f32[256,512]{1,0:T(8,128)S(1)}, f32[256,512]{1,0:T(8,128)S(1)}, u32[]{:S(2)}, u32[]{:S(2)}) collective-permute-start(f32[256,512]{1,0:T(8,128)S(1)} %get-tuple-element.103), channel_id=1, source_target_pairs={{0,4},{4,0},{8,12},{12,8},{16,20},{20,16},{24,28},{28,24},{1,5},{5... | collective-permute-start | bytes 1572872 | tf_op jit(solution)/shard_map/ppermute | solution.py:485
  64.5 18.4 %collective-permute-start.8 = (f32[256,512]{1,0:T(8,128)S(1)}, f32[256,512]{1,0:T(8,128)S(1)}, u32[]{:S(2)}, u32[]{:S(2)}) collective-permute-start(f32[256,512]{1,0:T(8,128)S(1)} %get-tuple-element.104), channel_id=1, source_target_pairs={{0,4},{4,0},{8,12},{12,8},{16,20},{20,16},{24,28},{28,24},{1,5},{5... | collective-permute-start | bytes 1572872 | tf_op jit(solution)/shard_map/ppermute | solution.py:485
  95.4 3.1 %collective-permute-start.12 = (f32[8,128]{1,0:T(8,128)S(1)}, f32[8,128]{1,0:T(8,128)S(1)}, u32[]{:S(2)}, u32[]{:S(2)}) collective-permute-start(f32[8,128]{1,0:T(8,128)S(1)} %get-tuple-element.77), channel_id=1, source_target_pairs={{0,3},{1,2},{2,1},{3,0},{4,7},{5,6},{6,5},{7,4},{8,11},{9,10},{10,... | collective-permute-start | bytes 12296 | tf_op jit(solution)/shard_map/ppermute | solution.py:437
  95.4 3.7 %collective-permute-start.11 = (f32[8,128]{1,0:T(8,128)S(1)}, f32[8,128]{1,0:T(8,128)S(1)}, u32[]{:S(2)}, u32[]{:S(2)}) collective-permute-start(f32[8,128]{1,0:T(8,128)S(1)} %get-tuple-element.77), channel_id=1, source_target_pairs={{0,2},{1,3},{2,0},{3,1},{4,6},{5,7},{6,4},{7,5},{8,10},{9,11},{10,... | collective-permute-start | bytes 12296 | tf_op jit(solution)/shard_map/ppermute | solution.py:437
  97.0 2.1 %collective-permute-start.10 = (f32[8,128]{1,0:T(8,128)S(1)}, f32[8,128]{1,0:T(8,128)S(1)}, u32[]{:S(2)}, u32[]{:S(2)}) collective-permute-start(f32[8,128]{1,0:T(8,128)S(1)} %get-tuple-element.77), channel_id=1, source_target_pairs={{0,1},{1,0},{2,3},{3,2},{4,5},{5,4},{6,7},{7,6},{8,9},{9,8},{10,11... | collective-permute-start | bytes 12296 | tf_op jit(solution)/shard_map/ppermute | solution.py:437
  99.1 5.5 %collective-permute-start.15 = (f32[8,128]{1,0:T(8,128)S(1)}, f32[8,128]{1,0:T(8,128)S(1)}, u32[]{:S(2)}, u32[]{:S(2)}) collective-permute-start(f32[8,128]{1,0:T(8,128)S(1)} %add_add_fusion.1), channel_id=1, source_target_pairs={{0,12},{4,8},{8,4},{12,0},{16,28},{20,24},{24,20},{28,16},{1,13},{... | collective-permute-start | bytes 12296 | tf_op jit(solution)/shard_map/ppermute | solution.py:437
  103.1 3.6 %collective-permute-start.14 = (f32[8,128]{1,0:T(8,128)S(1)}, f32[8,128]{1,0:T(8,128)S(1)}, u32[]{:S(2)}, u32[]{:S(2)}) collective-permute-start(f32[8,128]{1,0:T(8,128)S(1)} %add_add_fusion.1), channel_id=1, source_target_pairs={{0,8},{4,12},{8,0},{12,4},{16,24},{20,28},{24,16},{28,20},{1,9},{5... | collective-permute-start | bytes 12296 | tf_op jit(solution)/shard_map/ppermute | solution.py:437
  103.2 3.6 %collective-permute-start.13 = (f32[8,128]{1,0:T(8,128)S(1)}, f32[8,128]{1,0:T(8,128)S(1)}, u32[]{:S(2)}, u32[]{:S(2)}) collective-permute-start(f32[8,128]{1,0:T(8,128)S(1)} %add_add_fusion.1), channel_id=1, source_target_pairs={{0,4},{4,0},{8,12},{12,8},{16,20},{20,16},{24,28},{28,24},{1,5},{5... | collective-permute-start | bytes 12296 | tf_op jit(solution)/shard_map/ppermute | solution.py:437
  106.8 4.5 %collective-permute-start.16 = (f32[8,128]{1,0:T(8,128)S(1)}, f32[8,128]{1,0:T(8,128)S(1)}, u32[]{:S(2)}, u32[]{:S(2)}) collective-permute-start(f32[8,128]{1,0:T(8,128)S(1)} %add_add_fusion), channel_id=1, source_target_pairs={{0,16},{4,20},{8,24},{12,28},{16,0},{20,4},{24,8},{28,12},{1,17},{... | collective-permute-start | bytes 12296 | tf_op jit(solution)/shard_map/ppermute | solution.py:437

commit v3 on v2

--- a/solution.py
+++ b/solution.py
@@ -3,6 +3,7 @@
 
 import jax
 import jax.numpy as jnp
+import numpy as np
 from jax import lax
 from jax.experimental import pallas as pl
 from jax.experimental.pallas import tpu as pltpu
@@ -11,6 +12,7 @@
 GROUP = 256
 PARTS = 2
 VMEM_LIMIT = 60 * 1024 * 1024
+SMALL_LIMIT = 40 * 1024 * 1024
 F32 = jnp.float32
 BF16 = jnp.bfloat16
 
@@ -114,7 +116,7 @@
     return hit.astype(BF16)
 
 
-def local_kernel(first, *refs):
+def local_kernel(first, last, count, *refs):
     at_ref, x_ref, dy_ref, b_ref, c_ref = refs[:5]
     if first:
         raw_ref, bias_ref, rate_ref, skip_ref = refs[5:9]
@@ -122,8 +124,12 @@
         xs_ref, ys_ref, direct_ref, columns_ref, table_ref, bt, ct = refs[-7:]
     else:
         columns_ref, table_ref = refs[5:7]
-        outs = refs[10:-5]
-        xs_ref, ys_ref, direct_ref, bt, ct = refs[-5:]
+        outs = refs[10 : 10 + count]
+        xs_ref, ys_ref, direct_ref = refs[10 + count : 13 + count]
+        if last:
+            left, right, bt, ct = refs[13 + count :]
+        else:
+            bt, ct = refs[13 + count :]
     g = pl.program_id(0)
     length, width = x_ref.shape
     states = b_ref.shape[1]
@@ -145,6 +151,13 @@
                 columns_ref,
                 table_ref,
             )
+        if last:
+            for n in range(blocks):
+                rows = slice(n * GROUP, (n + 1) * GROUP)
+                scores = dot(c_ref[rows, :], b_ref[rows, :], NT)
+                left[n] = jnp.where(triangle(GROUP, True), scores, 0.0).astype(BF16)
+                scores = dot(b_ref[rows, :], c_ref[rows, :], NT)
+                right[n] = jnp.where(triangle(GROUP, False), scores, 0.0).astype(BF16)
 
     gain = picker(piece, heads, all_heads, width, True)
     lift = picker(piece, heads, all_heads, width, False)
@@ -176,7 +189,7 @@
             out_ref[2 * states :] = decay
 
 
-def local_states(at, count, x, dy, b, c, vectors, before):
+def local_states(at, count, last, x, dy, b, c, vectors, before):
     length, channels = x.shape
     states = b.shape[1]
     pieces = 2 * PARTS
@@ -215,18 +228,23 @@
         in_specs += [pl.BlockSpec(factor_columns.shape, whole), pl.BlockSpec(table.shape, whole)]
         in_specs += [anywhere] * 3
         aliases = {7: count, 8: count + 1, 9: count + 2}
+    scratch = [pltpu.VMEM((states, length), BF16)] * 2
+    if last:
+        blocks = length // GROUP
+        extra = [jax.ShapeDtypeStruct((blocks, GROUP, GROUP), BF16)] * 2
+        extra += [jax.ShapeDtypeStruct((states, length), BF16)] * 2
+        out_shape += extra
+        out_specs += [pl.BlockSpec(e.shape, lambda g, at, n=len(e.shape): (0,) * n) for e in extra]
+        scratch = []
     grid_spec = pltpu.PrefetchScalarGridSpec(
         num_scalar_prefetch=1,
         grid=(count,),
         in_specs=in_specs,
         out_specs=out_specs,
-        scratch_shapes=[
-            pltpu.VMEM((states, length), BF16),
-            pltpu.VMEM((states, length), BF16),
-        ],
+        scratch_shapes=scratch,
     )
     out = pl.pallas_call(
-        functools.partial(local_kernel, first),
+        functools.partial(local_kernel, first, last, count),
         grid_spec=grid_spec,
         out_shape=out_shape,
         input_output_aliases=aliases,
@@ -241,71 +259,69 @@
     return out[:count], list(out[count:])
 
 
-def grads_kernel(first, scale, part, half, *refs):
-    y_ref, xs_ref, ys_ref, dy_ref, direct_ref, b_ref, c_ref, columns_ref, table_ref = refs[:9]
-    raw_ref, bias_ref, rate_ref, mine_ref, other_ref = refs[9:14]
-    refs = refs[14:]
+def adding(width, heads, places):
+    out = np.zeros((len(places) * width, 128), np.float32)
+    size = width // heads
+    for k, place in enumerate(places):
+        for channel in range(width):
+            out[k * width + channel, place * heads + channel // size] = 1.0
+    return jnp.asarray(out, BF16)
+
+
+def lanes_of(values, piece, shape):
+    row = lax.broadcasted_iota(jnp.int32, shape, 0)
+    col = lax.broadcasted_iota(jnp.int32, shape, 1)
+    return jnp.sum(jnp.where(col == row + piece * shape[0], values, 0.0), axis=0, keepdims=True)
+
+
+def inner_kernel(first, scale, piece, *refs):
+    xs_ref, ys_ref, dy_ref, direct_ref, b_ref, c_ref, bt, ct, left, right = refs[:10]
+    adder, columns_ref, table_ref, raw_ref, bias_ref, rate_ref = refs[10:16]
+    refs = refs[16:]
     if not first:
         dc_in, db_in, par_in = refs[:3]
         refs = refs[5:]
-    dx_ref, dc_ref, db_ref, draw_ref, par_ref = refs[:5]
-    left, right, sums, dc_sum, db_sum, bt, ct, adder = refs[5:]
-    g = pl.program_id(0)
+    dx_ref, dc_ref, db_ref, draw_ref, par_ref = refs
     heads = raw_ref.shape[1]
     length, width = xs_ref.shape
     states = b_ref.shape[1]
     blocks = length // GROUP
-    piece = g * half + part
     all_heads = columns_ref.shape[1] // 4
     member = head_matrix(heads, width).astype(BF16)
     lower = triangle(GROUP, True)
     rows = [slice(n * GROUP, (n + 1) * GROUP) for n in range(blocks)]
-
-    @pl.when(g == 0)
-    def _():
-        bt[...] = b_ref[...].T
-        ct[...] = c_ref[...].T
-        upper = triangle(GROUP, False)
-        for n in range(blocks):
-            b, c = b_ref[rows[n], :], c_ref[rows[n], :]
-            left[n] = jnp.where(lower, dot(c, b, NT), 0.0).astype(BF16)
-            right[n] = jnp.where(upper, dot(b, c, NT), 0.0).astype(BF16)
-        sums[...] = jnp.zeros_like(sums)
-        dc_sum[...] = jnp.zeros_like(dc_sum)
-        db_sum[...] = jnp.zeros_like(db_sum)
-        par_ref[...] = jnp.zeros_like(par_ref) if first else par_in[...]
-        row = lax.broadcasted_iota(jnp.int32, (width, 128), 0)
-        col = lax.broadcasted_iota(jnp.int32, (width, 128), 1)
-        size = width // heads
-        one = ((row >= col * size) & (row < (col + 1) * size)).astype(BF16)
-        col = col - heads
-        two = ((row >= col * size) & (row < (col + 1) * size)).astype(BF16)
-        adder[:width] = one
-        adder[width : 2 * width] = one
-        adder[2 * width :] = two
-
-    own = g == y_ref[0]
-    state = jnp.where(own, mine_ref[:states], other_ref[:states])
-    grad = jnp.where(own, mine_ref[states:], other_ref[states:])
     table = table_ref[...]
     skip = table[3 * blocks + 1 : 3 * blocks + 2]
+    state = grad = None
     entering_low, ends = [], []
     for n in range(blocks):
-        state = table[n : n + 1] * state
-        entering_low.append(state.astype(BF16))
-        state = state + dot(bt[:, rows[n]], xs_ref[rows[n], :], NN)
+        fresh = dot(bt[:, rows[n]], xs_ref[rows[n], :], NN)
+        if state is not None:
+            state = table[n : n + 1] * state
+            entering_low.append(state.astype(BF16))
+            state = state + fresh
+        else:
+            entering_low.append(None)
+            state = fresh
         ends.append(state)
-    leaving_low, edges = [None] * blocks, [None] * blocks
+    leaving_low, edges = [None] * blocks, [jnp.zeros((1, width), F32)] * blocks
     for n in reversed(range(blocks)):
-        leaving_low[n] = grad.astype(BF16)
-        edges[n] = jnp.sum(ends[n] * grad, axis=0, keepdims=True)
-        grad = table[n : n + 1] * (grad + dot(ct[:, rows[n]], ys_ref[rows[n], :], NN))
+        if grad is not None:
+            leaving_low[n] = grad.astype(BF16)
+            edges[n] = jnp.sum(ends[n] * grad, axis=0, keepdims=True)
+        if n:
+            fresh = dot(ct[:, rows[n]], ys_ref[rows[n], :], NN)
+            grad = table[n : n + 1] * (fresh if grad is None else grad + fresh)
     gain = picker(piece, heads, all_heads, width, True)
     added = []
     for n in range(blocks):
         scaled_x, scaled_dy = xs_ref[rows[n], :], ys_ref[rows[n], :]
-        forward = dot(left[n], scaled_x, NN) + dot(c_ref[rows[n], :], entering_low[n], NN)
-        backward = dot(right[n], scaled_dy, NN) + dot(b_ref[rows[n], :], leaving_low[n], NN)
+        forward = dot(left[n], scaled_x, NN)
+        if entering_low[n] is not None:
+            forward = forward + dot(c_ref[rows[n], :], entering_low[n], NN)
+        backward = dot(right[n], scaled_dy, NN)
+        if leaving_low[n] is not None:
+            backward = backward + dot(b_ref[rows[n], :], leaving_low[n], NN)
         weight = dot(columns_ref[rows[n], :], gain, NN)
         dx_ref[rows[n], :] = (weight * backward + skip * dy_ref[rows[n], :].astype(F32)).astype(
             dx_ref.dtype
@@ -315,14 +331,18 @@
         hi = difference.astype(BF16)
         lo = (difference - hi.astype(F32)).astype(BF16)
         added.append(dot(jnp.concatenate([hi, lo, v.astype(BF16)], axis=1), adder[...], NN))
-        sums[n] += dot(scaled_dy, scaled_x, NT)
-        dc_sum[n] += dot(scaled_dy, entering_low[n], NT)
-        db_sum[n] += dot(scaled_x, leaving_low[n], NT)
+        pair = jnp.where(lower, dot(scaled_dy, scaled_x, NT), 0.0).astype(BF16)
+        dc = dot(pair, b_ref[rows[n], :], NN)
+        db = dot(pair, c_ref[rows[n], :], TN)
+        if entering_low[n] is not None:
+            dc = dc + dot(scaled_dy, entering_low[n], NT)
+        if leaving_low[n] is not None:
+            db = db + dot(scaled_x, leaving_low[n], NT)
+        dc_ref[rows[n], :] = dc if first else dc + dc_in[rows[n], :]
+        db_ref[rows[n], :] = db if first else db + db_in[rows[n], :]
     added = [a.T for a in added]
     edge = head_sums(jnp.concatenate(edges + [edges[0]] * (8 - blocks), axis=0), member)
-    slopes = running(
-        jnp.concatenate([a[:heads] for a in added], axis=0), lower.astype(BF16)
-    )
+    slopes = running(jnp.concatenate([a[:heads] for a in added], axis=0), lower.astype(BF16))
     slope = jnp.concatenate(
         [slopes[n * heads : (n + 1) * heads] + edge[:, n : n + 1] for n in range(blocks)], axis=1
     )
@@ -336,28 +356,13 @@
         jnp.sum(head_sums(direct_ref[...], member), axis=1, keepdims=True),
         -jnp.sum(step * slope, axis=1, keepdims=True),
     )
-    shape = (heads, par_ref.shape[1])
-    spot = lax.broadcasted_iota(jnp.int32, shape, 1) == (
-        lax.broadcasted_iota(jnp.int32, shape, 0) + piece * heads
-    )
+    par_ref[...] = jnp.zeros_like(par_ref) if first else par_in[...]
     for k, value in enumerate(values):
-        par_ref[k : k + 1] += jnp.sum(jnp.where(spot, value * scale, 0.0), axis=0, keepdims=True)
-
-    @pl.when(g == pl.num_programs(0) - 1)
-    def _():
-        for n in range(blocks):
-            pair = jnp.where(lower, sums[n], 0.0).astype(BF16)
-            dc = dot(pair, b_ref[rows[n], :], NN) + dc_sum[n]
-            db = dot(pair, c_ref[rows[n], :], TN) + db_sum[n]
-            if not first:
-                dc = dc + dc_in[rows[n], :]
-                db = db + db_in[rows[n], :]
-            dc_ref[rows[n], :] = dc
-            db_ref[rows[n], :] = db
-
-
-def local_grads(part, scale, y, saved, dy, b, c, vectors, mine, other, before):
-    xs, ys, direct, factor_columns, table = saved
+        par_ref[k : k + 1] += lanes_of(value * scale, piece, (heads, par_ref.shape[1]))
+
+
+def inner_grads(piece, scale, saved, dy, b, c, vectors, before):
+    xs, ys, direct, factor_columns, table, left, right, bt, ct = saved
     raw, bias, rate, _ = vectors
     length, channels = xs.shape
     pieces = 2 * PARTS
@@ -365,50 +370,31 @@
     raw = raw.reshape(pieces, heads, length)
     width = channels // pieces
     states = b.shape[1]
-    blocks = length // GROUP
-    half = pieces // 2
     first = before is None
-    whole = lambda g, y: (0, 0)
-    place = lambda g, y: (0, g * half + part)
+    adder = adding(width, heads, (0, 0, 1))
+    place = lambda g: (0, piece)
+    all_of = lambda a: pl.BlockSpec(a.shape, lambda g, n=len(a.shape): (0,) * n)
     columns = pl.BlockSpec((length, width), place)
-    maps = pl.BlockSpec((length, states), whole)
-    line = pl.BlockSpec(bias.shape, whole)
-    lines = pl.BlockSpec((1, heads, length), lambda g, y: (g * half + part, 0, 0))
-    held = pl.BlockSpec((2 * states, width), whole)
-    params = pl.BlockSpec((8, 128), whole)
+    maps = pl.BlockSpec((length, states), lambda g: (0, 0))
+    lines = pl.BlockSpec((1, heads, length), lambda g: (piece, 0, 0))
+    params = pl.BlockSpec((8, 128), lambda g: (0, 0))
     anywhere = pl.BlockSpec(memory_space=pl.ANY)
-    in_specs = [columns, columns, columns, pl.BlockSpec((8, width), place), maps, maps]
-    in_specs += [
-        pl.BlockSpec(factor_columns.shape, whole),
-        pl.BlockSpec((table.shape[0], width), place),
-    ]
-    in_specs += [lines, line, line, held, held]
-    args = [xs, ys, dy, direct, b, c, factor_columns, table, raw, bias, rate, mine, other]
+    args = [xs, ys, dy, direct, b, c, bt, ct, left, right]
+    args += [adder, factor_columns, table, raw, bias, rate]
+    in_specs = [columns, columns, columns, pl.BlockSpec((8, width), place)]
+    in_specs += [all_of(a) for a in (b, c, bt, ct, left, right, adder, factor_columns)]
+    in_specs += [pl.BlockSpec((table.shape[0], width), place), lines, all_of(bias), all_of(rate)]
     aliases = {}
     if not first:
         dx, dc, db, draw, par = before
         args += [dc, db, par, dx, draw]
         in_specs += [maps, maps, params, anywhere, anywhere]
-        aliases = {17: 0, 18: 3}
-    grid_spec = pltpu.PrefetchScalarGridSpec(
-        num_scalar_prefetch=1,
-        grid=(2,),
+        aliases = {19: 0, 20: 3}
+    return pl.pallas_call(
+        functools.partial(inner_kernel, first, scale, piece),
+        grid=(1,),
         in_specs=in_specs,
         out_specs=[columns, maps, maps, lines, params],
-        scratch_shapes=[
-            pltpu.VMEM((blocks, GROUP, GROUP), BF16),
-            pltpu.VMEM((blocks, GROUP, GROUP), BF16),
-            pltpu.VMEM((blocks, GROUP, GROUP), F32),
-            pltpu.VMEM((blocks, GROUP, states), F32),
-            pltpu.VMEM((blocks, GROUP, states), F32),
-            pltpu.VMEM((states, length), BF16),
-            pltpu.VMEM((states, length), BF16),
-            pltpu.VMEM((3 * width, 128), BF16),
-        ],
-    )
-    return pl.pallas_call(
-        functools.partial(grads_kernel, first, scale, part, half),
-        grid_spec=grid_spec,
         out_shape=[
             jax.ShapeDtypeStruct((length, channels), BF16),
             jax.ShapeDtypeStruct((length, states), F32),
@@ -417,14 +403,170 @@
             jax.ShapeDtypeStruct((8, 128), F32),
         ],
         input_output_aliases=aliases,
-        compiler_params=pltpu.CompilerParams(vmem_limit_bytes=40 * 1024 * 1024),
+        compiler_params=pltpu.CompilerParams(vmem_limit_bytes=VMEM_LIMIT),
         cost_estimate=pl.CostEstimate(
             flops=24 * length * width * (GROUP + states),
-            bytes_accessed=12 * length * width,
+            bytes_accessed=10 * length * width,
             transcendentals=0,
         ),
-        name="local_grads",
-    )(y, *args)
+        name="inner_grads",
+    )(*args)
+
+
+def entering_kernel(scale, part, half, *refs):
+    y_ref, xs_ref, ys_ref, b_ref, c_ref, adder, columns_ref, table_ref = refs[:8]
+    raw_ref, bias_ref, rate_ref, mine_ref, other_ref, dx_in, draw_in, par_in = refs[8:16]
+    dx_ref, draw_ref, par_ref = refs[16:]
+    g = pl.program_id(0)
+    heads = raw_ref.shape[1]
+    length, width = xs_ref.shape
+    states = b_ref.shape[1]
+    blocks = length // GROUP
+    piece = g * half + part
+    all_heads = columns_ref.shape[1] // 4
+    member = head_matrix(heads, width).astype(BF16)
+    rows = [slice(n * GROUP, (n + 1) * GROUP) for n in range(blocks)]
+
+    @pl.when(g == 0)
+    def _():
+        par_ref[...] = par_in[...]
+
+    own = g == y_ref[0]
+    state = jnp.where(own, mine_ref[:states], other_ref[:states])
+    grad = jnp.where(own, mine_ref[states:], other_ref[states:])
+    table = table_ref[...]
+    gain = picker(piece, heads, all_heads, width, True)
+    added = []
+    for n in range(blocks):
+        entered = (table[2 * blocks + n : 2 * blocks + n + 1] * state).astype(BF16)
+        leaving = (table[blocks + n : blocks + n + 1] * grad).astype(BF16)
+        forward = dot(c_ref[rows[n], :], entered, NN)
+        backward = dot(b_ref[rows[n], :], leaving, NN)
+        weight = dot(columns_ref[rows[n], :], gain, NN)
+        dx_ref[rows[n], :] = (dx_in[rows[n], :].astype(F32) + weight * backward).astype(
+            dx_ref.dtype
+        )
+        p = (xs_ref[rows[n], :].astype(F32) * backward).astype(BF16)
+        q = (ys_ref[rows[n], :].astype(F32) * forward).astype(BF16)
+        added.append(dot(jnp.concatenate([p, q], axis=1), adder[...], NN))
+    added = [a.T for a in added]
+    cross = jnp.sum(state * grad, axis=0, keepdims=True) * table[3 * blocks : 3 * blocks + 1]
+    cross = head_sums(jnp.broadcast_to(cross, (8, width)), member)[:, :1]
+    ps, qs = [a[:heads] for a in added], [a[heads : 2 * heads] for a in added]
+    p_sums = running(jnp.concatenate(ps, axis=0), triangle(GROUP, False).astype(BF16))
+    q_sums = running(jnp.concatenate(qs, axis=0), triangle(GROUP, True).astype(BF16))
+    p_sums = [p_sums[n * heads : (n + 1) * heads] for n in range(blocks)]
+    q_sums = [q_sums[n * heads : (n + 1) * heads] for n in range(blocks)]
+    slopes = [None] * blocks
+    before = cross
+    for n in range(blocks):
+        slopes[n] = p_sums[n] - ps[n] + before
+        before = before + p_sums[n][:, GROUP - 1 :]
+    later = jnp.zeros_like(cross)
+    for n in reversed(range(blocks)):
+        slopes[n] = slopes[n] + q_sums[n] + later
+        later = later + q_sums[n][:, :1]
+    slope = jnp.concatenate(slopes, axis=1)
+    raw = raw_ref[0] + column(bias_ref[...], piece, heads)
+    step = softplus(raw)
+    more = jnp.concatenate(ps, axis=1) / step - column(rate_ref[...], piece, heads) * slope
+    more = more / (1.0 + jnp.exp(-raw))
+    draw_ref[0] = draw_in[0] + more
+    shape = (heads, par_ref.shape[1])
+    par_ref[:1] += lanes_of(jnp.sum(more, axis=1, keepdims=True) * scale, piece, shape)
+    par_ref[2:3] -= lanes_of(jnp.sum(step * slope, axis=1, keepdims=True) * scale, piece, shape)
+
+
+def entering_grads(part, scale, y, saved, b, c, vectors, mine, other, dx, draw, par):
+    xs, ys, _, factor_columns, table = saved[:5]
+    raw, bias, rate, _ = vectors
+    length, channels = xs.shape
+    pieces = 2 * PARTS
+    heads = raw.shape[1] // pieces
+    raw = raw.reshape(pieces, heads, length)
+    width = channels // pieces
+    half = pieces // 2
+    adder = adding(width, heads, (0, 1))
+    place = lambda g, y: (0, g * half + part)
+    all_of = lambda a: pl.BlockSpec(a.shape, lambda g, y, n=len(a.shape): (0,) * n)
+    columns = pl.BlockSpec((length, width), place)
+    lines = pl.BlockSpec((1, heads, length), lambda g, y: (g * half + part, 0, 0))
+    in_specs = [columns, columns] + [all_of(a) for a in (b, c, adder, factor_columns)]
+    in_specs += [pl.BlockSpec((table.shape[0], width), place), lines]
+    in_specs += [all_of(a) for a in (bias, rate, mine, other)] + [columns, lines, all_of(par)]
+    return pl.pallas_call(
+        functools.partial(entering_kernel, scale, part, half),
+        grid_spec=pltpu.PrefetchScalarGridSpec(
+            num_scalar_prefetch=1,
+            grid=(2,),
+            in_specs=in_specs,
+            out_specs=[columns, lines, all_of(par)],
+        ),
+        out_shape=[jax.ShapeDtypeStruct(a.shape, a.dtype) for a in (dx, draw, par)],
+        input_output_aliases={13: 0, 14: 1},
+        compiler_params=pltpu.CompilerParams(vmem_limit_bytes=SMALL_LIMIT),
+        cost_estimate=pl.CostEstimate(
+            flops=24 * length * width * GROUP, bytes_accessed=16 * length * width, transcendentals=0
+        ),
+        name="entering_grads",
+    )(y, xs, ys, b, c, adder, factor_columns, table, raw, bias, rate, mine, other, dx, draw, par)
+
+
+def maps_kernel(*refs):
+    y_ref, xs_ref, ys_ref, table_ref, dc_in, db_in = refs[:6]
+    held, (dc_ref, db_ref) = refs[6:-2], refs[-2:]
+    g = pl.program_id(0)
+    length = xs_ref.shape[0]
+    states = dc_in.shape[1]
+    blocks = length // GROUP
+
+    @pl.when(g == 0)
+    def _():
+        dc_ref[...] = dc_in[...]
+        db_ref[...] = db_in[...]
+
+    own = g // PARTS == y_ref[0]
+    both = None
+    for part in range(PARTS):
+        mine, other = held[2 * part], held[2 * part + 1]
+        one = jnp.where(own, mine[...], other[...])
+        both = one if both is None else jnp.where(g % PARTS == part, one, both)
+    state, grad = both[:states], both[states:]
+    table = table_ref[...]
+    for n in range(blocks):
+        rows = slice(n * GROUP, (n + 1) * GROUP)
+        entered = (table[2 * blocks + n : 2 * blocks + n + 1] * state).astype(BF16)
+        leaving = (table[blocks + n : blocks + n + 1] * grad).astype(BF16)
+        dc_ref[rows, :] += dot(ys_ref[rows, :], entered, NT)
+        db_ref[rows, :] += dot(xs_ref[rows, :], leaving, NT)
+
+
+def maps_grads(y, saved, dc, db, held):
+    xs, ys, _, _, table = saved[:5]
+    length, channels = xs.shape
+    pieces = 2 * PARTS
+    width = channels // pieces
+    place = lambda g, y: (0, g)
+    all_of = lambda a: pl.BlockSpec(a.shape, lambda g, y: (0, 0))
+    columns = pl.BlockSpec((length, width), place)
+    return pl.pallas_call(
+        maps_kernel,
+        grid_spec=pltpu.PrefetchScalarGridSpec(
+            num_scalar_prefetch=1,
+            grid=(pieces,),
+            in_specs=[columns, columns, pl.BlockSpec((table.shape[0], width), place)]
+            + [all_of(a) for a in (dc, db, *held)],
+            out_specs=[all_of(dc), all_of(db)],
+        ),
+        out_shape=[jax.ShapeDtypeStruct(a.shape, a.dtype) for a in (dc, db)],
+        compiler_params=pltpu.CompilerParams(vmem_limit_bytes=SMALL_LIMIT),
+        cost_estimate=pl.CostEstimate(
+            flops=16 * length * channels * dc.shape[1],
+            bytes_accessed=4 * length * channels,
+            transcendentals=0,
+        ),
+        name="maps_grads",
+    )(y, xs, ys, table, dc, db, *held)
 
 
 def summed_over(value, axis):
@@ -433,12 +575,16 @@
         return lax.psum(value, axis)
     bit = 1
     while bit < size:
-        steps = (bit, 2 * bit, 3 * bit) if 4 * bit <= size else (bit,)
-        got = [lax.ppermute(value, axis, [(i, i ^ s) for i in range(size)]) for s in steps]
-        value = value + got[0]
-        if len(got) == 3:
-            value = value + (got[1] + got[2])
-        bit *= 4 if len(got) == 3 else 2
+        count = min(8, size // bit)
+        got = [
+            lax.ppermute(value, axis, [(i, i ^ (k * bit)) for i in range(size)])
+            for k in range(1, count)
+        ]
+        terms = [value] + got
+        while len(terms) > 1:
+            terms = [terms[k] + terms[k + 1] for k in range(0, len(terms), 2)]
+        value = terms[0]
+        bit *= count
     return value
 
 
@@ -504,8 +650,9 @@
 
     def local(half, part, count, before):
         at = jnp.reshape(half * PARTS + part, (1,)).astype(jnp.int32)
-        out, saved = local_states(at, count, x, dy, b, c, vectors, before)
-        return out, saved + list(before[3:] if before else [])
+        last = count == PARTS
+        out, saved = local_states(at, count, last, x, dy, b, c, vectors, before)
+        return out, saved[:3] + list(before[3:] if before else []) + saved[3:]
 
     sent, kept = [], []
     saved = None
@@ -520,6 +667,13 @@
     ]
     order.append((1, transfers - 1))
     flows, token = {}, None
+    inner, piece = None, 0
+
+    def inner_piece(token):
+        bias = vectors[1] if token is None else after(vectors[1], token)
+        moved = (vectors[0], bias, *vectors[2:])
+        return inner_grads(piece, scale, saved, dy, b, c, moved, inner)
+
     for part, k in order:
         if k == 0:
             flows[part] = entering(sent[part], kept[part], states, token)
@@ -527,13 +681,26 @@
             token = arrived if part == 0 else message
         else:
             token = flows[part].send(token)[0]
+        if (part, k) == (0, 1) or (part == 1 and 0 < k < transfers - 1):
+            if piece < 2 * PARTS:
+                inner = inner_piece(token)
+                token = inner[-1]
+                piece += 1
+    while piece < 2 * PARTS:
+        inner = inner_piece(token)
+        token = inner[-1]
+        piece += 1
     here = jnp.reshape(y, (1,)).astype(jnp.int32)
-    before = None
+    dx, dc, db, draw, params = inner
+    held = []
     for part in range(PARTS):
         mine, other = next(flows[part])
         other = after(other, token)
-        before = local_grads(part, scale, here, saved, dy, b, c, vectors, mine, other, before)
-    dx, dc, db, draw, params = before
+        held += [mine, other]
+        dx, draw, params = entering_grads(
+            part, scale, here, saved, b, c, vectors, mine, other, dx, draw, params
+        )
+    dc, db = maps_grads(after(here, params), saved, dc, db, held)
     summed = summed_over(summed_over(params, "batch"), "seq")
     return (
         dx[None],

time: 113 us -> 119 us (1.053)
  waiting for transfers between devices: 32.4 us -> 3.89 us
  Pallas kernels: 41.5 us -> 68.2 us
  starting transfers between devices: 29.1 us -> 32.3 us
  local copies, waits for them, and re-layouts: 1.13 us -> 4.03 us
  other arithmetic: 7.3 us -> 9.07 us
    pallas_call x5 -> x10, Pallas kernels: 41.5 us -> 68.2 us  [the longest x4 32.5 us: inner_grads(): pl.pallas_call(functools.partial(inner_kernel, first, scale, piece), grid...]
    ppermute x6, waiting for transfers between devices: 18.2 us -> 0.02 us  [entering(): arrived = lax.ppermute(message, 'seq', route)]
    ppermute x7 -> x10, waiting for transfers between devices: 6.72 us -> 1.83 us  [summed_over(): lax.ppermute(value, axis, [(i, i ^ k * bit) for i in range(size)])]
    ppermute x7 -> x10, starting transfers between devices: 9.22 us -> 13.1 us  [summed_over(): lax.ppermute(value, axis, [(i, i ^ k * bit) for i in range(size)])]
    ppermute x2, waiting for transfers between devices: 5.74 us -> 2.04 us  [entering(): other = lax.ppermute(message, 'seq', swap)]
    unnamed x24 -> x34, local copies, waits for them, and re-layouts: 0.06 us -> 2.96 us
    ppermute x2, waiting for transfers between devices: 1.82 us -> 0.01 us  [entering(): arrived = lax.ppermute(message, 'seq', swap)]
    ppermute x6, starting transfers between devices: 14 us -> 12.6 us  [entering(): arrived = lax.ppermute(message, 'seq', route)]
  transfers between devices with their start and end apart: 17 -> 20, of which waited for: 12 -> 3; matrix products, arithmetic and copies ran while one was open for 6% -> 8% of each run, Pallas kernels for 21% -> 48%
where the time goes in v3:
time: 119 us; the launch traced here: 118 us
  Pallas kernels  68.2 us (57%)
  starting transfers between devices  32.3 us (27%)
  other arithmetic  9.07 us (8%)
  local copies, waits for them, and re-layouts  4.03 us (3%)
  waiting for transfers between devices  3.89 us (3%)
    pallas_call x4, Pallas kernels, inner_grads(): pl.pallas_call(functools.partial(inner_kernel, first, scale, piece), grid...  32.5 us
    pallas_call x3, Pallas kernels, local_states(): pl.pallas_call(functools.partial(local_kernel, first, last, count), grid_...  17.9 us
    ppermute x10, starting transfers between devices, summed_over(): lax.ppermute(value, axis, [(i, i ^ k * bit) for i in range(size)])  13.1 us
    pallas_call x2, Pallas kernels, entering_grads(): pl.pallas_call(functools.partial(entering_kernel, scale, part, half), gri...  13 us
    ppermute x6, starting transfers between devices, entering(): arrived = lax.ppermute(message, 'seq', route)  12.6 us
    select_n x6, other arithmetic, entering(): jnp.where(place == hop - 1, whole_d * start + whole_l, whole_d * end + wh...  5.45 us
    pallas_call x1, Pallas kernels, maps_grads(): pl.pallas_call(maps_kernel, grid_spec=pltpu.PrefetchScalarGridSpec(num_sc...  4.73 us
    ppermute x2, starting transfers between devices, entering(): arrived = lax.ppermute(message, 'seq', swap)  4.51 us
  transfers between devices with their start and end apart: 20, of which 3 were waited for; matrix products, arithmetic and copies ran while one was open for 8% of the time, Pallas kernels for 48%

profile of v3, /device:TPU:0, one launch (start us, length us, event | category | flops | bytes accessed | tf_op | source)
XLA Modules:
  0.0 118.5 jit_solution(403641365634949953)
XLA Ops:
  0.6 5.2 %local_states.3 = (f32[264,512]{1,0:T(8,128)}, bf16[1024,2048]{1,0:T(8,128)(2,1)}, bf16[1024,2048]{1,0:T(8,128)(2,1)}, f32[8,2048]{1,0:T(8,128)}, bf16[1024,128]{1,0:T(8,128)(2,1)}, /*index=5*/f32[16,2048]{1,0:T(8,128)}) custom-call(s32[1]{0:T(128)} %bitcast.6.refs_0_, bf16[1024,2048]{1,0:T(8,128)(2,1)} %bitcast.70, bf16[1024,2048]{1,0:T(8,128)(2,1)} %bitcast.62, ...), custom_call_target="tpu_custom_call" | custom-call | flops 536870912 | bytes 4194304 | tf_op jit(solution)/shard_map/local_states/pallas_call | solution.py:246
  5.9 3.0 %collective-permute-start = (f32[264,512]{1,0:T(8,128)}, f32[264,512]{1,0:T(8,128)S(1)}, u32[]{:S(2)}, u32[]{:S(2)}) collective-permute-start(f32[264,512]{1,0:T(8,128)} %get-tuple-element.80), channel_id=1, source_target_pairs={{0,4},{4,0},{8,12},{12,8},{16,20},{20,16},{24,28},{28,24},{1,5},{5... | collective-permute-start | bytes 1622024 | tf_op jit(solution)/shard_map/ppermute | solution.py:606
  8.8 4.8 %local_states.4 = (f32[264,512]{1,0:T(8,128)}, bf16[1024,2048]{1,0:T(8,128)(2,1)}, bf16[1024,2048]{1,0:T(8,128)(2,1)}, f32[8,2048]{1,0:T(8,128)}) custom-call(s32[1]{0:T(128)} %bitcast.10.refs_0_, bf16[1024,2048]{1,0:T(8,128)(2,1)} %bitcast.71, bf16[1024,2048]{1,0:T(8,128)(2,1)} %bitcast.63, ...), custom_call_target="tpu_custom_call", output_to_operand_aliasing={{1}: (7, {}), {2}: (8, {}), {3}: (9, {})} | custom-call | flops 536870912 | bytes 4194304 | tf_op jit(solution)/shard_map/local_states/pallas_call | solution.py:246
  13.6 7.9 %local_states.5 = (f32[264,512]{1,0:T(8,128)}, f32[264,512]{1,0:T(8,128)}, bf16[1024,2048]{1,0:T(8,128)(2,1)}, bf16[1024,2048]{1,0:T(8,128)(2,1)}, f32[8,2048]{1...) custom-call(s32[1]{0:T(128)} %bitcast.1.refs_0_, ...), custom_call_target="tpu_custom_call", output_to_operand_aliasing={{2}: (7, {}), {3}: (8, {}), {4}: (9, {})} | custom-call | flops 1073741824 | bytes 8388608 | tf_op jit(solution)/shard_map/local_states/pallas_call | solution.py:246
  21.5 1.5 %collective-permute-start.1 = (f32[264,512]{1,0:T(8,128)}, f32[264,512]{1,0:T(8,128)S(1)}, u32[]{:S(2)}, u32[]{:S(2)}) collective-permute-start(f32[264,512]{1,0:T(8,128)} %get-tuple-element.81), channel_id=1, source_target_pairs={{0,4},{4,0},{8,12},{12,8},{16,20},{20,16},{24,28},{28,24},{1,5},{5... | collective-permute-start | bytes 1622024 | tf_op jit(solution)/shard_map/ppermute | solution.py:606
  23.1 0.7 fusion.5
  23.8 1.2 add_select_fusion.5
  25.0 3.5 %collective-permute-start.2 = (f32[128,512]{1,0:T(8,128)S(1)}, f32[128,512]{1,0:T(8,128)S(1)}, u32[]{:S(2)}, u32[]{:S(2)}) collective-permute-start(f32[128,512]{1,0:T(8,128)S(1)} %get-tuple-element.146), channel_id=1, source_target_pairs={{0,8},{24,16},{4,12},{28,20},{1,9},{25,17},{5,13},{29,21},{2,10},{... | collective-permute-start | bytes 786440 | tf_op jit(solution)/shard_map/ppermute | solution.py:622
  28.5 7.9 %inner_grads.4 = (bf16[1024,2048]{1,0:T(8,128)(2,1)}, f32[1024,128]{1,0:T(8,128)}, f32[1024,128]{1,0:T(8,128)}, f32[4,8,1024]{2,1,0:T(8,128)}, f32[8,128]{1,0:T(8,128)}) custom-call(bf16[1024,2048]{1,0:T(8,128)(2,1)} %get-tuple-element.77.refs_0_.refs_1_, bf16[1024,2048]{1,0:T(8,128)(2,1)} %get-tuple-element.78.refs_1_.refs_2_, bf16[1024,2048]{1,0:T(8,128)(2,1)} %bitcast.65, ...), custom_call_target="tpu_custom_call" | custom-call | flops 4831838208 | bytes 5242880 | tf_op jit(solution)/shard_map/inner_grads/pallas_call | solution.py:393
  36.4 0.1 add_select_fusion.4
  36.5 0.7 collective-permute-start.4
  37.2 0.8 add_select_fusion.3
  38.0 4.3 %collective-permute-start.3 = (f32[128,512]{1,0:T(8,128)}, f32[128,512]{1,0:T(8,128)S(1)}, u32[]{:S(2)}, u32[]{:S(2)}) collective-permute-start(f32[128,512]{1,0:T(8,128)} %get-tuple-element.140), channel_id=1, source_target_pairs={{0,8},{24,16},{4,12},{28,20},{1,9},{25,17},{5,13},{29,21},{2,10},{... | collective-permute-start | bytes 786440 | tf_op jit(solution)/shard_map/ppermute | solution.py:622
  42.3 8.2 %inner_grads.5 = (bf16[1024,2048]{1,0:T(8,128)(2,1)}, f32[1024,128]{1,0:T(8,128)}, f32[1024,128]{1,0:T(8,128)}, f32[4,8,1024]{2,1,0:T(8,128)}, f32[8,128]{1,0:T(8,128)}) custom-call(bf16[1024,2048]{1,0:T(8,128)(2,1)} %get-tuple-element.77.refs_0_.refs_1_, ...), custom_call_target="tpu_custom_call", output_to_operand_aliasing={{0}: (19, {}), {3}: (20, {})} | custom-call | flops 4831838208 | bytes 5242880 | tf_op jit(solution)/shard_map/inner_grads/pallas_call | solution.py:393
  50.5 0.8 add_select_fusion.2
  51.3 1.3 %collective-permute-start.6 = (f32[128,512]{1,0:T(8,128)}, f32[128,512]{1,0:T(8,128)S(1)}, u32[]{:S(2)}, u32[]{:S(2)}) collective-permute-start(f32[128,512]{1,0:T(8,128)} %add_select_fusion.2), channel_id=1, source_target_pairs={{16,24},{8,0},{20,28},{12,4},{17,25},{9,1},{21,29},{13,5},{18,26},... | collective-permute-start | bytes 786440 | tf_op jit(solution)/shard_map/ppermute | solution.py:622
  52.6 0.8 add_select_fusion.1
  53.4 1.3 %collective-permute-start.5 = (f32[128,512]{1,0:T(8,128)}, f32[128,512]{1,0:T(8,128)}, u32[]{:S(2)}, u32[]{:S(2)}) collective-permute-start(f32[128,512]{1,0:T(8,128)} %add_select_fusion.1), channel_id=1, source_target_pairs={{8,16},{16,8},{12,20},{20,12},{9,17},{17,9},{13,21},{21,13},{10,18... | collective-permute-start | bytes 786440 | tf_op jit(solution)/shard_map/ppermute | solution.py:622
  54.8 8.2 %inner_grads.6 = (bf16[1024,2048]{1,0:T(8,128)(2,1)}, f32[1024,128]{1,0:T(8,128)}, f32[1024,128]{1,0:T(8,128)}, f32[4,8,1024]{2,1,0:T(8,128)}, f32[8,128]{1,0:T(8,128)}) custom-call(bf16[1024,2048]{1,0:T(8,128)(2,1)} %get-tuple-element.77.refs_0_.refs_1_, ...), custom_call_target="tpu_custom_call", output_to_operand_aliasing={{0}: (19, {}), {3}: (20, {})} | custom-call | flops 4831838208 | bytes 5242880 | tf_op jit(solution)/shard_map/inner_grads/pallas_call | solution.py:393
  63.0 0.7 copy-done.16
  63.7 1.2 %multiply_add_fusion.2 = (f32[128,512]{1,0:T(8,128)S(1)}, f32[128,512]{1,0:T(8,128)S(1)}, f32[128,512]{1,0:T(8,128)S(1)}, f32[128,512]{1,0:T(8,128)S(1)}) fusion(f32[512]{0:T(512)S(1)} %bitcast.87, f32[264,512]{1,0:T(8,128)S(1)} %copy-done.14, f32[264,512]{1,0:T(8,128)S(1)} %collective-permute-done, pred[]{:T(512)S(6)} %eq.14, f32[128,512]{1,0:T(8,128)} %copy-done.16, ...), kind=kLoop, calls=%fused_computation.11 | loop fusion | flops 786432 | bytes 2887685 | tf_op jit(solution)/shard_map/add | solution.py:628
  65.0 0.1 fusion.2
  65.1 0.8 collective-permute-start.9
  65.9 1.8 %add_select_fusion = f32[128,512]{1,0:T(8,128)} fusion(f32[128,512]{1,0:T(8,128)S(1)} %get-tuple-element.142, f32[128,512]{1,0:T(8,128)S(1)} %get-tuple-element.141, f32[512]{0:T(512)S(1)} %bitcast.76, pred[]{:T(512)S(6)} %eq.17, f32[128,512]{1,0:T(8,128)} %collective-permute-done.5, f32[128,512]{1,0:T(8,128)S(1)} %collective-permute-done.3, pred[]{:T(512)S(6)} %eq.15), kind=kLoop, calls=%fused_computation.10 | loop fusion | flops 589824 | bytes 1312770 | tf_op jit(solution)/shard_map/jit(_where)/select_n | solution.py:617
  67.6 1.5 %collective-permute-start.7 = (f32[128,512]{1,0:T(8,128)}, f32[128,512]{1,0:T(8,128)}, u32[]{:S(2)}, u32[]{:S(2)}) collective-permute-start(f32[128,512]{1,0:T(8,128)} %add_select_fusion), channel_id=1, source_target_pairs={{16,24},{8,0},{20,28},{12,4},{17,25},{9,1},{21,29},{13,5},{18,26},... | collective-permute-start | bytes 786440 | tf_op jit(solution)/shard_map/ppermute | solution.py:622
  69.1 0.0 copy-start.6
  69.2 8.2 %inner_grads.7 = (bf16[1024,2048]{1,0:T(8,128)(2,1)}, f32[1024,128]{1,0:T(8,128)}, f32[1024,128]{1,0:T(8,128)}, f32[4,8,1024]{2,1,0:T(8,128)}, f32[8,128]{1,0:T(8,128)}) custom-call(bf16[1024,2048]{1,0:T(8,128)(2,1)} %get-tuple-element.77.refs_0_.refs_1_, ...), custom_call_target="tpu_custom_call", output_to_operand_aliasing={{0}: (19, {}), {3}: (20, {})} | custom-call | flops 4831838208 | bytes 5242880 | tf_op jit(solution)/shard_map/inner_grads/pallas_call | solution.py:393
  77.5 1.4 %multiply_add_fusion.1 = (f32[128,512]{1,0:T(8,128)S(1)}, f32[128,512]{1,0:T(8,128)S(1)}, f32[128,512]{1,0:T(8,128)S(1)}, f32[128,512]{1,0:T(8,128)S(1)}) fusion(f32[512]{0:T(512)S(1)} %bitcast.83, f32[264,512]{1,0:T(8,128)S(1)} %copy-done.13, f32[264,512]{1,0:T(8,128)S(1)} %collective-permute-done.1, pred[]{:T(512)S(6)} %eq.14, ...), kind=kLoop, calls=%fused_computation.9 | loop fusion | flops 786432 | bytes 2887685 | tf_op jit(solution)/shard_map/add | solution.py:628
  78.9 0.1 fusion
  79.0 1.4 %collective-permute-start.8 = (f32[256,512]{1,0:T(8,128)S(1)}, f32[256,512]{1,0:T(8,128)S(1)}, u32[]{:S(2)}, u32[]{:S(2)}) collective-permute-start(f32[256,512]{1,0:T(8,128)S(1)} %get-tuple-element.158), channel_id=1, source_target_pairs={{0,4},{4,0},{8,12},{12,8},{16,20},{20,16},{24,28},{28,24},{1,5},{5... | collective-permute-start | bytes 1572872 | tf_op jit(solution)/shard_map/ppermute | solution.py:631
  80.5 2.2 %copy-done.1 = bf16[1024,2048]{1,0:T(8,128)(2,1)S(1)} copy-done((bf16[1024,2048]{1,0:T(8,128)(2,1)S(1)}, bf16[1024,2048]{1,0:T(8,128)(2,1)}, u32[]{:S(2)}) %copy-start.1) | copy-done | bytes 4194328
  82.7 6.5 %entering_grads.2 = (bf16[1024,2048]{1,0:T(8,128)(2,1)}, f32[4,8,1024]{2,1,0:T(8,128)}, f32[8,128]{1,0:T(8,128)S(1)}) custom-call(s32[1]{0:T(128)} %bitcast.refs_0_, bf16[1024,2048]{1,0:T(8,128)(2,1)S(1)} %copy-done, bf16[1024,2048]{1,0:T(8,128)(2,1)S(1)} %copy-done.1, ...), custom_call_target="tpu_custom_call", output_to_operand_aliasing={{0}: (13, {}), {1}: (14, {})} | custom-call | flops 3221225472 | bytes 8388608 | tf_op jit(solution)/shard_map/entering_grads/pallas_call | solution.py:497
  89.1 2.0 %collective-permute-done.8.refs_12_.refs_9_ = f32[256,512]{1,0:T(8,128)S(1)} collective-permute-done((f32[256,512]{1,0:T(8,128)S(1)}, f32[256,512]{1,0:T(8,128)S(1)}, u32[]{:S(2)}, u32[]{:S(2)}) %collective-permute-start.8) | collective-permute-done | bytes 524320 | tf_op jit(solution)/shard_map/ppermute | solution.py:631
  91.2 6.6 %entering_grads.3 = (bf16[1024,2048]{1,0:T(8,128)(2,1)}, f32[4,8,1024]{2,1,0:T(8,128)}, f32[8,128]{1,0:T(8,128)S(1)}) custom-call(s32[1]{0:T(128)} %bitcast.refs_0_, bf16[1024,2048]{1,0:T(8,128)(2,1)S(1)} %copy-done, bf16[1024,2048]{1,0:T(8,128)(2,1)S(1)} %copy-done.1, ...), custom_call_target="tpu_custom_call", output_to_operand_aliasing={{0}: (13, {}), {1}: (14, {})} | custom-call | flops 3221225472 | bytes 8388608 | tf_op jit(solution)/shard_map/entering_grads/pallas_call | solution.py:497
  97.7 1.6 %collective-permute-start.11 = (f32[8,128]{1,0:T(8,128)S(1)}, f32[8,128]{1,0:T(8,128)S(1)}, u32[]{:S(2)}, u32[]{:S(2)}) collective-permute-start(f32[8,128]{1,0:T(8,128)S(1)} %get-tuple-element.125), channel_id=1, source_target_pairs={{0,2},{1,3},{2,0},{3,1},{4,6},{5,7},{6,4},{7,5},{8,10},{9,11},{10,... | collective-permute-start | bytes 12296 | tf_op jit(solution)/shard_map/ppermute | solution.py:580
  99.3 0.3 collective-permute-start.10
  99.6 1.2 collective-permute-done.12
  100.8 0.6 collective-permute-done.11
  101.4 1.7 %collective-permute-start.19 = (f32[8,128]{1,0:T(8,128)S(1)}, f32[8,128]{1,0:T(8,128)S(1)}, u32[]{:S(2)}, u32[]{:S(2)}) collective-permute-start(f32[8,128]{1,0:T(8,128)S(1)} %add_add_fusion.1), channel_id=1, source_target_pairs={{0,28},{4,24},{8,20},{12,16},{16,12},{20,8},{24,4},{28,0},{1,29},{... | collective-permute-start | bytes 12296 | tf_op jit(solution)/shard_map/ppermute | solution.py:580
  103.1 2.5 %collective-permute-start.18 = (f32[8,128]{1,0:T(8,128)S(1)}, f32[8,128]{1,0:T(8,128)S(1)}, u32[]{:S(2)}, u32[]{:S(2)}) collective-permute-start(f32[8,128]{1,0:T(8,128)S(1)} %add_add_fusion.1), channel_id=1, source_target_pairs={{0,24},{4,28},{8,16},{12,20},{16,8},{20,12},{24,0},{28,4},{1,25},{... | collective-permute-start | bytes 12296 | tf_op jit(solution)/shard_map/ppermute | solution.py:580
  105.6 3.3 %collective-permute-start.17 = (f32[8,128]{1,0:T(8,128)S(1)}, f32[8,128]{1,0:T(8,128)S(1)}, u32[]{:S(2)}, u32[]{:S(2)}) collective-permute-start(f32[8,128]{1,0:T(8,128)S(1)} %add_add_fusion.1), channel_id=1, source_target_pairs={{0,20},{4,16},{8,28},{12,24},{16,4},{20,0},{24,12},{28,8},{1,21},{... | collective-permute-start | bytes 12296 | tf_op jit(solution)/shard_map/ppermute | solution.py:580
  109.0 0.2 collective-permute-start.16
  109.1 2.1 %collective-permute-start.15 = (f32[8,128]{1,0:T(8,128)S(1)}, f32[8,128]{1,0:T(8,128)S(1)}, u32[]{:S(2)}, u32[]{:S(2)}) collective-permute-start(f32[8,128]{1,0:T(8,128)S(1)} %add_add_fusion.1), channel_id=1, source_target_pairs={{0,12},{4,8},{8,4},{12,0},{16,28},{20,24},{24,20},{28,16},{1,13},{... | collective-permute-start | bytes 12296 | tf_op jit(solution)/shard_map/ppermute | solution.py:580
  111.2 0.3 collective-permute-start.14
  111.5 1.1 collective-permute-start.13
  112.6 4.7 %maps_grads.1 = (f32[1024,128]{1,0:T(8,128)}, f32[1024,128]{1,0:T(8,128)}) custom-call(s32[1]{0:T(128)} %bitcast.refs_0_, bf16[1024,2048]{1,0:T(8,128)(2,1)S(1)} %copy-done, bf16[1024,2048]{1,0:T(8,128)(2,1)S(1)} %copy-done.1, f32[16,2048]{1,0:T(8,128)S(1)} %copy-done.5, f32[1024,128]{1,0:T(8,128)S(1)} %copy-done.11, f32[1024,128]{1,0:T(8,128)S(1)} %copy-done.12, ...), custom_call_target="tpu_custom_call" | custom-call | flops 4294967296 | bytes 8388608 | tf_op jit(solution)/shard_map/maps_grads/pallas_call | solution.py:552
  117.4 0.5 slice_bitcast_fusion
  117.9 0.6 slice.54
  (54 shorter events, 0.2 us)
Async XLA Ops:
  5.9 15.7 %collective-permute-start = (f32[264,512]{1,0:T(8,128)}, f32[264,512]{1,0:T(8,128)S(1)}, u32[]{:S(2)}, u32[]{:S(2)}) collective-permute-start(f32[264,512]{1,0:T(8,128)} %get-tuple-element.80), channel_id=1, source_target_pairs={{0,4},{4,0},{8,12},{12,8},{16,20},{20,16},{24,28},{28,24},{1,5},{5... | collective-permute-start | bytes 1622024 | tf_op jit(solution)/shard_map/ppermute | solution.py:606
  21.5 15.6 %collective-permute-start.1 = (f32[264,512]{1,0:T(8,128)}, f32[264,512]{1,0:T(8,128)S(1)}, u32[]{:S(2)}, u32[]{:S(2)}) collective-permute-start(f32[264,512]{1,0:T(8,128)} %get-tuple-element.81), channel_id=1, source_target_pairs={{0,4},{4,0},{8,12},{12,8},{16,20},{20,16},{24,28},{28,24},{1,5},{5... | collective-permute-start | bytes 1622024 | tf_op jit(solution)/shard_map/ppermute | solution.py:606
  25.0 11.4 %collective-permute-start.2 = (f32[128,512]{1,0:T(8,128)S(1)}, f32[128,512]{1,0:T(8,128)S(1)}, u32[]{:S(2)}, u32[]{:S(2)}) collective-permute-start(f32[128,512]{1,0:T(8,128)S(1)} %get-tuple-element.146), channel_id=1, source_target_pairs={{0,8},{24,16},{4,12},{28,20},{1,9},{25,17},{5,13},{29,21},{2,10},{... | collective-permute-start | bytes 786440 | tf_op jit(solution)/shard_map/ppermute | solution.py:622
  28.5 8.7 %copy-start.13 = (f32[264,512]{1,0:T(8,128)S(1)}, f32[264,512]{1,0:T(8,128)}, u32[]{:S(2)}) copy-start(f32[264,512]{1,0:T(8,128)} %get-tuple-element.93) | copy-start | bytes 1622020
  36.5 14.0 %collective-permute-start.4 = (f32[128,512]{1,0:T(8,128)S(1)}, f32[128,512]{1,0:T(8,128)S(1)}, u32[]{:S(2)}, u32[]{:S(2)}) collective-permute-start(f32[128,512]{1,0:T(8,128)S(1)} %add_select_fusion.4), channel_id=1, source_target_pairs={{8,16},{16,8},{12,20},{20,12},{9,17},{17,9},{13,21},{21,13},{10,18... | collective-permute-start | bytes 786440 | tf_op jit(solution)/shard_map/ppermute | solution.py:622
  38.0 14.6 %collective-permute-start.3 = (f32[128,512]{1,0:T(8,128)}, f32[128,512]{1,0:T(8,128)S(1)}, u32[]{:S(2)}, u32[]{:S(2)}) collective-permute-start(f32[128,512]{1,0:T(8,128)} %get-tuple-element.140), channel_id=1, source_target_pairs={{0,8},{24,16},{4,12},{28,20},{1,9},{25,17},{5,13},{29,21},{2,10},{... | collective-permute-start | bytes 786440 | tf_op jit(solution)/shard_map/ppermute | solution.py:622
  50.5 4.3 %copy-start.15 = (f32[128,512]{1,0:T(8,128)}, f32[128,512]{1,0:T(8,128)S(1)}, u32[]{:S(2)}) copy-start(f32[128,512]{1,0:T(8,128)S(1)} %collective-permute-done.4) | copy-start | bytes 786436
  51.3 11.7 %collective-permute-start.6 = (f32[128,512]{1,0:T(8,128)}, f32[128,512]{1,0:T(8,128)S(1)}, u32[]{:S(2)}, u32[]{:S(2)}) collective-permute-start(f32[128,512]{1,0:T(8,128)} %add_select_fusion.2), channel_id=1, source_target_pairs={{16,24},{8,0},{20,28},{12,4},{17,25},{9,1},{21,29},{13,5},{18,26},... | collective-permute-start | bytes 786440 | tf_op jit(solution)/shard_map/ppermute | solution.py:622
  53.4 12.4 %collective-permute-start.5 = (f32[128,512]{1,0:T(8,128)}, f32[128,512]{1,0:T(8,128)}, u32[]{:S(2)}, u32[]{:S(2)}) collective-permute-start(f32[128,512]{1,0:T(8,128)} %add_select_fusion.1), channel_id=1, source_target_pairs={{8,16},{16,8},{12,20},{20,12},{9,17},{17,9},{13,21},{21,13},{10,18... | collective-permute-start | bytes 786440 | tf_op jit(solution)/shard_map/ppermute | solution.py:622
  54.8 8.9 %copy-start.14 = (f32[264,512]{1,0:T(8,128)S(1)}, f32[264,512]{1,0:T(8,128)}, u32[]{:S(2)}) copy-start(f32[264,512]{1,0:T(8,128)} %get-tuple-element.83) | copy-start | bytes 1622020
  63.0 0.7 copy-start.16
  65.1 15.3 %collective-permute-start.9 = (f32[256,512]{1,0:T(8,128)S(1)}, f32[256,512]{1,0:T(8,128)S(1)}, u32[]{:S(2)}, u32[]{:S(2)}) collective-permute-start(f32[256,512]{1,0:T(8,128)S(1)} %get-tuple-element.157), channel_id=1, source_target_pairs={{0,4},{4,0},{8,12},{12,8},{16,20},{20,16},{24,28},{28,24},{1,5},{5... | collective-permute-start | bytes 1572872 | tf_op jit(solution)/shard_map/ppermute | solution.py:631
  67.6 9.8 %collective-permute-start.7 = (f32[128,512]{1,0:T(8,128)}, f32[128,512]{1,0:T(8,128)}, u32[]{:S(2)}, u32[]{:S(2)}) collective-permute-start(f32[128,512]{1,0:T(8,128)} %add_select_fusion), channel_id=1, source_target_pairs={{16,24},{8,0},{20,28},{12,4},{17,25},{9,1},{21,29},{13,5},{18,26},... | collective-permute-start | bytes 786440 | tf_op jit(solution)/shard_map/ppermute | solution.py:622
  69.1 11.3 %copy-start.5 = (f32[16,2048]{1,0:T(8,128)S(1)}, f32[16,2048]{1,0:T(8,128)}, u32[]{:S(2)}) copy-start(f32[16,2048]{1,0:T(8,128)} %get-tuple-element.70.refs_6_.refs_12_.refs_7_.refs_3_) | copy-start | bytes 393220
  69.1 11.3 %copy-start.6 = (f32[1,32,1024]{2,1,0:T(8,128)S(1)}, f32[1,32,1024]{2,1,0:T(8,128)}, u32[]{:S(2)}) copy-start(f32[1,32,1024]{2,1,0:T(8,128)} %refs_5_.3) | copy-start | bytes 393220
  69.1 11.2 %copy-start.7 = (bf16[1024,128]{1,0:T(8,128)(2,1)S(1)}, bf16[1024,128]{1,0:T(8,128)(2,1)}, u32[]{:S(2)}) copy-start(bf16[1024,128]{1,0:T(8,128)(2,1)} %constant.47.clone.refs_5_) | copy-start | bytes 786436
  77.4 3.0 %copy-start = (bf16[1024,2048]{1,0:T(8,128)(2,1)S(1)}, bf16[1024,2048]{1,0:T(8,128)(2,1)}, u32[]{:S(2)}) copy-start(bf16[1024,2048]{1,0:T(8,128)(2,1)} %get-tuple-element.77.refs_0_.refs_1_) | copy-start | bytes 12582916
  77.4 3.0 %copy-start.2 = (bf16[1,1024,128]{2,1,0:T(8,128)(2,1)S(1)}, bf16[1,1024,128]{2,1,0:T(8,128)(2,1)}, u32[]{:S(2)}) copy-start(bf16[1,1024,128]{2,1,0:T(8,128)(2,1)} %param.15) | copy-start | bytes 786436
  77.4 3.0 %copy-start.3 = (bf16[1,1024,128]{2,1,0:T(8,128)(2,1)S(1)}, bf16[1,1024,128]{2,1,0:T(8,128)(2,1)}, u32[]{:S(2)}) copy-start(bf16[1,1024,128]{2,1,0:T(8,128)(2,1)} %param.16) | copy-start | bytes 786436
  77.4 3.0 %copy-start.4 = (bf16[1024,128]{1,0:T(8,128)(2,1)S(1)}, bf16[1024,128]{1,0:T(8,128)(2,1)}, u32[]{:S(2)}) copy-start(bf16[1024,128]{1,0:T(8,128)(2,1)} %get-tuple-element.69.refs_5_.refs_11_.refs_6_) | copy-start | bytes 786436
  77.4 3.0 %copy-start.8 = (f32[32]{0:T(128)S(1)}, f32[32]{0:T(128)}, u32[]{:S(2)}) copy-start(f32[32]{0:T(128)} %param.18) | copy-start | bytes 388
  77.4 3.0 %copy-start.9 = (f32[32]{0:T(128)S(1)}, f32[32]{0:T(128)}, u32[]{:S(2)}) copy-start(f32[32]{0:T(128)} %param.19) | copy-start | bytes 388
  77.4 3.0 %copy-start.10 = (f32[8,128]{1,0:T(8,128)S(1)}, f32[8,128]{1,0:T(8,128)}, u32[]{:S(2)}) copy-start(f32[8,128]{1,0:T(8,128)} %get-tuple-element.115.refs_15_) | copy-start | bytes 12292
  79.0 12.2 %collective-permute-start.8 = (f32[256,512]{1,0:T(8,128)S(1)}, f32[256,512]{1,0:T(8,128)S(1)}, u32[]{:S(2)}, u32[]{:S(2)}) collective-permute-start(f32[256,512]{1,0:T(8,128)S(1)} %get-tuple-element.158), channel_id=1, source_target_pairs={{0,4},{4,0},{8,12},{12,8},{16,20},{20,16},{24,28},{28,24},{1,5},{5... | collective-permute-start | bytes 1572872 | tf_op jit(solution)/shard_map/ppermute | solution.py:631
  80.5 2.2 %copy-start.1 = (bf16[1024,2048]{1,0:T(8,128)(2,1)S(1)}, bf16[1024,2048]{1,0:T(8,128)(2,1)}, u32[]{:S(2)}) copy-start(bf16[1024,2048]{1,0:T(8,128)(2,1)} %get-tuple-element.78.refs_1_.refs_2_) | copy-start | bytes 12582916
  91.2 21.5 %copy-start.11 = (f32[1024,128]{1,0:T(8,128)S(1)}, f32[1024,128]{1,0:T(8,128)}, u32[]{:S(2)}) copy-start(f32[1024,128]{1,0:T(8,128)} %get-tuple-element.127.refs_4_) | copy-start | bytes 1572868
  91.2 21.5 %copy-start.12 = (f32[1024,128]{1,0:T(8,128)S(1)}, f32[1024,128]{1,0:T(8,128)}, u32[]{:S(2)}) copy-start(f32[1024,128]{1,0:T(8,128)} %get-tuple-element.128.refs_5_) | copy-start | bytes 1572868
  97.7 3.0 %collective-permute-start.12 = (f32[8,128]{1,0:T(8,128)S(1)}, f32[8,128]{1,0:T(8,128)S(1)}, u32[]{:S(2)}, u32[]{:S(2)}) collective-permute-start(f32[8,128]{1,0:T(8,128)S(1)} %get-tuple-element.125), channel_id=1, source_target_pairs={{0,3},{1,2},{2,1},{3,0},{4,7},{5,6},{6,5},{7,4},{8,11},{9,10},{10,... | collective-permute-start | bytes 12296 | tf_op jit(solution)/shard_map/ppermute | solution.py:580
  97.7 3.7 %collective-permute-start.11 = (f32[8,128]{1,0:T(8,128)S(1)}, f32[8,128]{1,0:T(8,128)S(1)}, u32[]{:S(2)}, u32[]{:S(2)}) collective-permute-start(f32[8,128]{1,0:T(8,128)S(1)} %get-tuple-element.125), channel_id=1, source_target_pairs={{0,2},{1,3},{2,0},{3,1},{4,6},{5,7},{6,4},{7,5},{8,10},{9,11},{10,... | collective-permute-start | bytes 12296 | tf_op jit(solution)/shard_map/ppermute | solution.py:580
  99.3 2.1 %collective-permute-start.10 = (f32[8,128]{1,0:T(8,128)S(1)}, f32[8,128]{1,0:T(8,128)S(1)}, u32[]{:S(2)}, u32[]{:S(2)}) collective-permute-start(f32[8,128]{1,0:T(8,128)S(1)} %get-tuple-element.125), channel_id=1, source_target_pairs={{0,1},{1,0},{2,3},{3,2},{4,5},{5,4},{6,7},{7,6},{8,9},{9,8},{10,11... | collective-permute-start | bytes 12296 | tf_op jit(solution)/shard_map/ppermute | solution.py:580
  101.4 9.8 %collective-permute-start.19 = (f32[8,128]{1,0:T(8,128)S(1)}, f32[8,128]{1,0:T(8,128)S(1)}, u32[]{:S(2)}, u32[]{:S(2)}) collective-permute-start(f32[8,128]{1,0:T(8,128)S(1)} %add_add_fusion.1), channel_id=1, source_target_pairs={{0,28},{4,24},{8,20},{12,16},{16,12},{20,8},{24,4},{28,0},{1,29},{... | collective-permute-start | bytes 12296 | tf_op jit(solution)/shard_map/ppermute | solution.py:580
  103.1 8.4 %collective-permute-start.18 = (f32[8,128]{1,0:T(8,128)S(1)}, f32[8,128]{1,0:T(8,128)S(1)}, u32[]{:S(2)}, u32[]{:S(2)}) collective-permute-start(f32[8,128]{1,0:T(8,128)S(1)} %add_add_fusion.1), channel_id=1, source_target_pairs={{0,24},{4,28},{8,16},{12,20},{16,8},{20,12},{24,0},{28,4},{1,25},{... | collective-permute-start | bytes 12296 | tf_op jit(solution)/shard_map/ppermute | solution.py:580
  105.6 11.7 %collective-permute-start.17 = (f32[8,128]{1,0:T(8,128)S(1)}, f32[8,128]{1,0:T(8,128)S(1)}, u32[]{:S(2)}, u32[]{:S(2)}) collective-permute-start(f32[8,128]{1,0:T(8,128)S(1)} %add_add_fusion.1), channel_id=1, source_target_pairs={{0,20},{4,16},{8,28},{12,24},{16,4},{20,0},{24,12},{28,8},{1,21},{... | collective-permute-start | bytes 12296 | tf_op jit(solution)/shard_map/ppermute | solution.py:580
  109.0 8.4 %collective-permute-start.16 = (f32[8,128]{1,0:T(8,128)S(1)}, f32[8,128]{1,0:T(8,128)S(1)}, u32[]{:S(2)}, u32[]{:S(2)}) collective-permute-start(f32[8,128]{1,0:T(8,128)S(1)} %add_add_fusion.1), channel_id=1, source_target_pairs={{0,16},{4,20},{8,24},{12,28},{16,0},{20,4},{24,8},{28,12},{1,17},{... | collective-permute-start | bytes 12296 | tf_op jit(solution)/shard_map/ppermute | solution.py:580
  109.1 8.2 %collective-permute-start.15 = (f32[8,128]{1,0:T(8,128)S(1)}, f32[8,128]{1,0:T(8,128)S(1)}, u32[]{:S(2)}, u32[]{:S(2)}) collective-permute-start(f32[8,128]{1,0:T(8,128)S(1)} %add_add_fusion.1), channel_id=1, source_target_pairs={{0,12},{4,8},{8,4},{12,0},{16,28},{20,24},{24,20},{28,16},{1,13},{... | collective-permute-start | bytes 12296 | tf_op jit(solution)/shard_map/ppermute | solution.py:580
  111.2 6.2 %collective-permute-start.14 = (f32[8,128]{1,0:T(8,128)S(1)}, f32[8,128]{1,0:T(8,128)S(1)}, u32[]{:S(2)}, u32[]{:S(2)}) collective-permute-start(f32[8,128]{1,0:T(8,128)S(1)} %add_add_fusion.1), channel_id=1, source_target_pairs={{0,8},{4,12},{8,0},{12,4},{16,24},{20,28},{24,16},{28,20},{1,9},{5... | collective-permute-start | bytes 12296 | tf_op jit(solution)/shard_map/ppermute | solution.py:580
  111.5 5.9 %collective-permute-start.13 = (f32[8,128]{1,0:T(8,128)S(1)}, f32[8,128]{1,0:T(8,128)S(1)}, u32[]{:S(2)}, u32[]{:S(2)}) collective-permute-start(f32[8,128]{1,0:T(8,128)S(1)} %add_add_fusion.1), channel_id=1, source_target_pairs={{0,4},{4,0},{8,12},{12,8},{16,20},{20,16},{24,28},{28,24},{1,5},{5... | collective-permute-start | bytes 12296 | tf_op jit(solution)/shard_map/ppermute | solution.py:580

commit v4 on v2

--- a/solution.py
+++ b/solution.py
@@ -146,8 +146,8 @@
                 table_ref,
             )
 
-    gain = picker(piece, heads, all_heads, width, True)
-    lift = picker(piece, heads, all_heads, width, False)
+    gain = dot(columns_ref[...], picker(piece, heads, all_heads, width, True), NN)
+    lift = dot(columns_ref[...], picker(piece, heads, all_heads, width, False), NN)
     table = table_ref[:, pl.ds(pl.multiple_of(piece * width, width), width)]
     state = jnp.zeros((states, width), F32)
     grad = jnp.zeros((states, width), F32)
@@ -157,8 +157,8 @@
         x = x_ref[rows, :].astype(F32)
         dy = dy_ref[rows, :].astype(F32)
         direct = direct + jnp.sum((dy * x).reshape(GROUP // 8, 8, width), axis=0)
-        scaled_x = (x * dot(columns_ref[rows, :], gain, NN)).astype(BF16)
-        scaled_dy = (dy * dot(columns_ref[rows, :], lift, NN)).astype(BF16)
+        scaled_x = (x * gain[rows]).astype(BF16)
+        scaled_dy = (dy * lift[rows]).astype(BF16)
         xs_ref[rows, :] = scaled_x
         ys_ref[rows, :] = scaled_dy
         later = table[blocks + n : blocks + n + 1]
@@ -249,7 +249,7 @@
         dc_in, db_in, par_in = refs[:3]
         refs = refs[5:]
     dx_ref, dc_ref, db_ref, draw_ref, par_ref = refs[:5]
-    left, right, sums, dc_sum, db_sum, bt, ct, adder = refs[5:]
+    left, right, sums, dc_sum, db_sum, bt, ct, adder, terms = refs[5:]
     g = pl.program_id(0)
     heads = raw_ref.shape[1]
     length, width = xs_ref.shape
@@ -300,13 +300,12 @@
         leaving_low[n] = grad.astype(BF16)
         edges[n] = jnp.sum(ends[n] * grad, axis=0, keepdims=True)
         grad = table[n : n + 1] * (grad + dot(ct[:, rows[n]], ys_ref[rows[n], :], NN))
-    gain = picker(piece, heads, all_heads, width, True)
-    added = []
+    gain = dot(columns_ref[...], picker(piece, heads, all_heads, width, True), NN)
     for n in range(blocks):
         scaled_x, scaled_dy = xs_ref[rows[n], :], ys_ref[rows[n], :]
         forward = dot(left[n], scaled_x, NN) + dot(c_ref[rows[n], :], entering_low[n], NN)
         backward = dot(right[n], scaled_dy, NN) + dot(b_ref[rows[n], :], leaving_low[n], NN)
-        weight = dot(columns_ref[rows[n], :], gain, NN)
+        weight = gain[rows[n]]
         dx_ref[rows[n], :] = (weight * backward + skip * dy_ref[rows[n], :].astype(F32)).astype(
             dx_ref.dtype
         )
@@ -314,11 +313,14 @@
         difference = scaled_dy.astype(F32) * forward - v
         hi = difference.astype(BF16)
         lo = (difference - hi.astype(F32)).astype(BF16)
-        added.append(dot(jnp.concatenate([hi, lo, v.astype(BF16)], axis=1), adder[...], NN))
+        terms[rows[n], :width] = hi
+        terms[rows[n], width : 2 * width] = lo
+        terms[rows[n], 2 * width :] = v.astype(BF16)
         sums[n] += dot(scaled_dy, scaled_x, NT)
         dc_sum[n] += dot(scaled_dy, entering_low[n], NT)
         db_sum[n] += dot(scaled_x, leaving_low[n], NT)
-    added = [a.T for a in added]
+    added = dot(terms[...], adder[...], NN).T
+    added = [added[:, rows[n]] for n in range(blocks)]
     edge = head_sums(jnp.concatenate(edges + [edges[0]] * (8 - blocks), axis=0), member)
     slopes = running(
         jnp.concatenate([a[:heads] for a in added], axis=0), lower.astype(BF16)
@@ -404,6 +406,7 @@
             pltpu.VMEM((states, length), BF16),
             pltpu.VMEM((states, length), BF16),
             pltpu.VMEM((3 * width, 128), BF16),
+            pltpu.VMEM((length, 3 * width), BF16),
         ],
     )
     return pl.pallas_call(
@@ -452,38 +455,70 @@
     index = lax.axis_index("seq")
     place, second = index // 2, index % 2 == 1
     swap = [(i, i ^ 1) for i in range(size)]
-
-    def parts(a):
-        return a[:states], a[states : 2 * states], a[2 * states : 2 * states + 1]
-
-    message = sent if token is None else after(sent, token)
-    arrived = lax.ppermute(message, "seq", swap)
-    token = yield message, arrived
-    (own_l, own_k, own_d), (got_l, got_k, got_d) = parts(kept), parts(after(arrived, token))
-    l1, k1, d1 = [jnp.where(second, b, a) for a, b in ((own_l, got_l), (own_k, got_k), (own_d, got_d))]
-    l2, k2, d2 = [jnp.where(second, a, b) for a, b in ((own_l, got_l), (own_k, got_k), (own_d, got_d))]
-    whole_l = d2 * l1 + l2
-    whole_k = k1 + d1 * k2
-    whole_d = d1 * d2
-    start = jnp.zeros_like(whole_l)
-    end = jnp.zeros_like(whole_k)
-    for hop in range(1, pairs):
-        message = jnp.where(place == hop - 1, whole_d * start + whole_l, whole_d * end + whole_k)
-        route = []
-        for y in range(2):
-            route.append((2 * (hop - 1) + y, 2 * hop + y))
-            route.append((2 * (pairs - hop) + y, 2 * (pairs - hop - 1) + y))
-        arrived = lax.ppermute(message, "seq", route)
-        token = yield message, arrived
-        arrived = after(arrived, token)
-        start = jnp.where(place == hop, arrived, start)
-        end = jnp.where(place == pairs - 1 - hop, arrived, end)
-    for_first = jnp.concatenate([start, k2 + d2 * end], axis=0)
-    for_second = jnp.concatenate([d1 * start + l1, end], axis=0)
-    mine = jnp.where(second, for_second, for_first)
-    message = jnp.where(second, for_first, for_second)
+    both = lambda moves: [(2 * a + y, 2 * b + y) for a, b in moves for y in range(2)]
+    if pairs == 4:
+        steps = [([(0, 1), (1, 0), (2, 3), (3, 2)],), ([(1, 2), (2, 1)], [(1, 3), (2, 0)])]
+        up = [(place == 0) | (place == 2), place == 1]
+    else:
+        steps = [([(k - 1, k), (pairs - k, pairs - k - 1)],) for k in range(1, pairs)]
+        up = [place == k - 1 for k in range(1, pairs)]
+
+    def halves(got, copy):
+        spans = ((0, states), (states, 2 * states), (2 * states + copy, 2 * states + copy + 1))
+        for low, high in spans:
+            own, other = kept[low:high], got[low:high]
+            yield jnp.where(second, other, own), jnp.where(second, own, other)
+
+    message = sent if token is None else after(sent, *token)
+    got = lax.ppermute(message, "seq", swap)
+    token = yield message, got
+    arrived = []
+    for k, routes in enumerate(steps):
+        if arrived:
+            arrived[-1] = after(arrived[-1], token)
+        else:
+            got = after(got, token)
+        (l1, l2), (k1, k2), (d1, d2) = halves(got, min(k, 3))
+        message = jnp.where(up[k], d2 * l1 + l2, k1 + d1 * k2)
+        if arrived:
+            message = message + d1 * d2 * arrived[-1][:states]
+        if len(steps) == 2 and k == 0:
+            message = jnp.concatenate([message, jnp.broadcast_to(d1 * d2, (8, message.shape[1]))])
+        arrived += [lax.ppermute(message, "seq", both(route)) for route in routes]
+        token = yield message, arrived[-1]
+    arrived[-1] = after(arrived[-1], token)
+
+    def leaving(copy):
+        (l1, _), (_, k2), (d1, d2) = halves(got, copy)
+        zero = jnp.zeros_like(l1)
+        if pairs == 4:
+            near, middle, far = [a[:states] for a in arrived]
+            outer = arrived[0][states + copy : states + copy + 1] * far + near
+            starts, ends = [zero, near, middle, outer], [outer, middle, near, zero]
+        else:
+            starts, ends = [zero] + arrived, arrived[::-1] + [zero]
+        start, end = starts[0], ends[0]
+        for k in range(1, pairs):
+            start = jnp.where(place == k, starts[k], start)
+            end = jnp.where(place == k, ends[k], end)
+        return start, d1 * start + l1, k2 + d2 * end, end
+
+    first_start, second_start, first_end, second_end = leaving(4)
+    message = jnp.concatenate(
+        [
+            jnp.where(second, first_start, second_start),
+            jnp.where(second, first_end, second_end),
+        ]
+    )
     other = lax.ppermute(message, "seq", swap)
     yield message, other
+    first_start, second_start, first_end, second_end = leaving(5)
+    mine = jnp.concatenate(
+        [
+            jnp.where(second, second_start, first_start),
+            jnp.where(second, second_end, first_end),
+        ]
+    )
     yield mine, other
 
 
@@ -514,7 +549,7 @@
         sent += out
     kept, saved = local(y, 0, PARTS, saved)
 
-    transfers = size // 2 + 1
+    transfers = 4 if size == 8 else size // 2 + 1
     order = [(0, 0), (1, 0)] + [
         pick for k in range(1, transfers) for pick in ((0, k), (1, k - 1)) if pick != (1, 0)
     ]
@@ -524,7 +559,7 @@
         if k == 0:
             flows[part] = entering(sent[part], kept[part], states, token)
             message, arrived = next(flows[part])
-            token = arrived if part == 0 else message
+            token = None if part == 0 else message
         else:
             token = flows[part].send(token)[0]
     here = jnp.reshape(y, (1,)).astype(jnp.int32)

time: 113 us -> 104 us (0.920)
  starting transfers between devices: 29.1 us -> 21.4 us
  waiting for transfers between devices: 32.4 us -> 37.7 us
  Pallas kernels: 41.5 us -> 38.4 us
  other arithmetic: 7.3 us -> 4.28 us
    ppermute x8, waiting for transfers between devices: 20 us -> 30.4 us  [the longest x6 24.4 us: entering(): arrived += [lax.ppermute(message, 'seq', both(route)) for route in routes]]
    ppermute x8, starting transfers between devices: 18.7 us -> 11.7 us  [the longest x6 7.17 us: entering(): arrived += [lax.ppermute(message, 'seq', both(route)) for route in routes]]
    ppermute x2, waiting for transfers between devices: 5.74 us -> 0.01 us  [entering(): other = lax.ppermute(message, 'seq', swap)]
    ppermute x7, starting transfers between devices: 9.22 us -> 6.62 us  [summed_over(): lax.ppermute(value, axis, [(i, i ^ s) for i in range(size)])]
    pallas_call x3, Pallas kernels: 17 us -> 14.6 us  [local_states(): pl.pallas_call(functools.partial(local_kernel, first), grid_spec=grid_spe...]
    ppermute x2, starting transfers between devices: 1.14 us -> 3.14 us  [entering(): other = lax.ppermute(message, 'seq', swap)]
    select_n x8 -> x5, other arithmetic: 4.29 us -> 2.62 us  [the longest x2 1.27 us: entering(): message = jnp.where(up[k], d2 * l1 + l2, k1 + d1 * k2)]
    mul x4 -> x1, other arithmetic: 1.46 us -> 0.02 us  [entering(): message = message + d1 * d2 * arrived[-1][:states]]
  transfers between devices with their start and end apart: 17 -> 17, of which waited for: 12 -> 11; matrix products, arithmetic and copies ran while one was open for 6% -> 2% of each run, Pallas kernels for 21% -> 21%
where the time goes in v4:
time: 104 us
  Pallas kernels  38.4 us (37%)
  waiting for transfers between devices  37.7 us (36%)
  starting transfers between devices  21.4 us (21%)
  other arithmetic  4.28 us (4%)
  local copies, waits for them, and re-layouts  1.16 us (1%)
    ppermute x6, waiting for transfers between devices, entering(): arrived += [lax.ppermute(message, 'seq', both(route)) for route in routes]  24.4 us
    pallas_call x2, Pallas kernels, local_grads(): pl.pallas_call(functools.partial(grads_kernel, first, scale, part, half),...  23.9 us
    pallas_call x3, Pallas kernels, local_states(): pl.pallas_call(functools.partial(local_kernel, first), grid_spec=grid_spe...  14.6 us
    ppermute x7, waiting for transfers between devices, summed_over(): lax.ppermute(value, axis, [(i, i ^ s) for i in range(size)])  7.28 us
    ppermute x6, starting transfers between devices, entering(): arrived += [lax.ppermute(message, 'seq', both(route)) for route in routes]  7.17 us
    ppermute x7, starting transfers between devices, summed_over(): lax.ppermute(value, axis, [(i, i ^ s) for i in range(size)])  6.62 us
    ppermute x2, waiting for transfers between devices, entering(): got = lax.ppermute(message, 'seq', swap)  6.06 us
    ppermute x2, starting transfers between devices, entering(): got = lax.ppermute(message, 'seq', swap)  4.48 us
  transfers between devices with their start and end apart: 17, of which 11 were waited for; matrix products, arithmetic and copies ran while one was open for 2% of the time, Pallas kernels for 21%

profile of v4, /device:TPU:0, one launch (start us, length us, event | category | flops | bytes accessed | tf_op | source)
XLA Modules:
  0.0 104.0 jit_solution(4249505267290018657)
XLA Ops:
  0.6 4.6 %local_states.3 = (f32[264,512]{1,0:T(8,128)}, bf16[1024,2048]{1,0:T(8,128)(2,1)}, bf16[1024,2048]{1,0:T(8,128)(2,1)}, f32[8,2048]{1,0:T(8,128)}, bf16[1024,128]{1,0:T(8,128)(2,1)}, /*index=5*/f32[16,2048]{1,0:T(8,128)}) custom-call(s32[1]{0:T(128)} %bitcast.6.refs_0_, bf16[1024,2048]{1,0:T(8,128)(2,1)} %bitcast.65, bf16[1024,2048]{1,0:T(8,128)(2,1)} %bitcast.60, ...), custom_call_target="tpu_custom_call" | custom-call | flops 536870912 | bytes 4194304 | tf_op jit(solution)/shard_map/local_states/pallas_call | solution.py:228
  5.2 3.0 %collective-permute-start.1 = (f32[264,512]{1,0:T(8,128)}, f32[264,512]{1,0:T(8,128)S(1)}, u32[]{:S(2)}, u32[]{:S(2)}) collective-permute-start(f32[264,512]{1,0:T(8,128)} %get-tuple-element.52), channel_id=1, source_target_pairs={{0,4},{4,0},{8,12},{12,8},{16,20},{20,16},{24,28},{28,24},{1,5},{5... | collective-permute-start | bytes 1622024 | tf_op jit(solution)/shard_map/ppermute | solution.py:473
  8.2 3.9 %local_states.4 = (f32[264,512]{1,0:T(8,128)}, bf16[1024,2048]{1,0:T(8,128)(2,1)}, bf16[1024,2048]{1,0:T(8,128)(2,1)}, f32[8,2048]{1,0:T(8,128)}) custom-call(s32[1]{0:T(128)} %bitcast.10.refs_0_, bf16[1024,2048]{1,0:T(8,128)(2,1)} %bitcast.66, bf16[1024,2048]{1,0:T(8,128)(2,1)} %bitcast.61, ...), custom_call_target="tpu_custom_call", output_to_operand_aliasing={{1}: (7, {}), {2}: (8, {}), {3}: (9, {})} | custom-call | flops 536870912 | bytes 4194304 | tf_op jit(solution)/shard_map/local_states/pallas_call | solution.py:228
  12.1 6.1 %local_states.5 = (f32[264,512]{1,0:T(8,128)}, f32[264,512]{1,0:T(8,128)}, bf16[1024,2048]{1,0:T(8,128)(2,1)}, bf16[1024,2048]{1,0:T(8,128)(2,1)}, f32[8,2048]{1,0:T(8,128)}) custom-call(s32[1]{0:T(128)} %bitcast.1.refs_0_, bf16[1024,2048]{1,0:T(8,128)(2,1)} %bitcast.67, ...), custom_call_target="tpu_custom_call", output_to_operand_aliasing={{2}: (7, {}), {3}: (8, {}), {4}: (9, {})} | custom-call | flops 1073741824 | bytes 8388608 | tf_op jit(solution)/shard_map/local_states/pallas_call | solution.py:228
  18.2 2.5 %collective-permute-done.1 = f32[264,512]{1,0:T(8,128)S(1)} collective-permute-done((f32[264,512]{1,0:T(8,128)}, f32[264,512]{1,0:T(8,128)S(1)}, u32[]{:S(2)}, u32[]{:S(2)}) %collective-permute-start.1) | collective-permute-done | bytes 540704 | tf_op jit(solution)/shard_map/ppermute | solution.py:473
  20.7 0.9 broadcast_select_fusion.1
  21.6 1.2 %add_select_fusion.9 = (f32[128,512]{1,0:T(8,128)S(1)}, f32[128,512]{1,0:T(8,128)S(1)}, f32[128,512]{1,0:T(8,128)S(1)}) fusion(f32[512]{0:T(512)S(1)} %bitcast.79, f32[512]{0:T(512)S(1)} %bitcast.78, pred[]{:T(512)S(6)} %or.4, f32[264,512]{1,0:T(8,128)S(1)} %collective-permute-done.1, f32[264,512]{1,0:T(8,128)} %get-tuple-element.51, pred[]{:T(512)S(6)} %eq.14), kind=kLoop, calls=%fused_computation.23 | loop fusion | flops 589824 | bytes 1839106 | tf_op jit(solution)/shard_map/jit(_where)/select_n | solution.py:482
  22.8 1.9 %collective-permute-start.2 = (f32[136,512]{1,0:T(8,128)S(1)}, f32[136,512]{1,0:T(8,128)S(1)}, u32[]{:S(2)}, u32[]{:S(2)}) collective-permute-start(f32[136,512]{1,0:T(8,128)S(1)} %pad_maximum_fusion.4), channel_id=1, source_target_pairs={{0,8},{4,12},{8,0},{12,4},{16,24},{20,28},{24,16},{28,20},{1,9},{5... | collective-permute-start | bytes 835592 | tf_op jit(solution)/shard_map/ppermute | solution.py:487
  24.6 1.5 %collective-permute-start = (f32[264,512]{1,0:T(8,128)S(1)}, f32[264,512]{1,0:T(8,128)S(1)}, u32[]{:S(2)}, u32[]{:S(2)}) collective-permute-start(f32[264,512]{1,0:T(8,128)S(1)} %copy-done.11), channel_id=1, source_target_pairs={{0,4},{4,0},{8,12},{12,8},{16,20},{20,16},{24,28},{28,24},{1,5},{5... | collective-permute-start | bytes 1622024 | tf_op jit(solution)/shard_map/ppermute | solution.py:473
  26.1 4.5 %collective-permute-done.2 = f32[136,512]{1,0:T(8,128)S(1)} collective-permute-done((f32[136,512]{1,0:T(8,128)S(1)}, f32[136,512]{1,0:T(8,128)S(1)}, u32[]{:S(2)}, u32[]{:S(2)}) %collective-permute-start.2) | collective-permute-done | bytes 278560 | tf_op jit(solution)/shard_map/ppermute | solution.py:487
  30.7 1.2 %multiply_add_fusion.5 = f32[128,512]{1,0:T(8,128)S(1)} fusion(f32[128,512]{1,0:T(8,128)S(1)} %get-tuple-element.86, f32[128,512]{1,0:T(8,128)S(1)} %get-tuple-element.85, f32[136,512]{1,0:T(8,128)S(1)} %collective-permute-done.2, f32[512]{0:T(512)S(1)} %bitcast.73, f32[512]{0:T(512)S(1)} %bitcast.75, f32[512]{0:T(512)S(1)} %bitcast.74, pred[]{:T(512)S(6)} %eq.15, ...), kind=kLoop, calls=%fused_computation.22 | loop fusion | flops 589824 | bytes 2103298 | tf_op jit(solution)/shard_map/add | solution.py:484
  31.9 0.7 collective-permute-start.5
  32.6 1.3 %collective-permute-start.4 = (f32[128,512]{1,0:T(8,128)S(1)}, f32[128,512]{1,0:T(8,128)S(1)}, u32[]{:S(2)}, u32[]{:S(2)}) collective-permute-start(f32[128,512]{1,0:T(8,128)S(1)} %multiply_add_fusion.5), channel_id=1, source_target_pairs={{8,24},{12,28},{16,0},{20,4},{9,25},{13,29},{17,1},{21,5},{10,26},... | collective-permute-start | bytes 786440 | tf_op jit(solution)/shard_map/ppermute | solution.py:487
  33.9 3.6 %collective-permute-done = f32[264,512]{1,0:T(8,128)S(1)} collective-permute-done((f32[264,512]{1,0:T(8,128)S(1)}, f32[264,512]{1,0:T(8,128)S(1)}, u32[]{:S(2)}, u32[]{:S(2)}) %collective-permute-start) | collective-permute-done | bytes 540704 | tf_op jit(solution)/shard_map/ppermute | solution.py:473
  37.5 0.1 add_select_fusion.8
  37.7 1.2 %collective-permute-start.3 = (f32[136,512]{1,0:T(8,128)S(1)}, f32[136,512]{1,0:T(8,128)S(1)}, u32[]{:S(2)}, u32[]{:S(2)}) collective-permute-start(f32[136,512]{1,0:T(8,128)S(1)} %pad_maximum_fusion.5), channel_id=1, source_target_pairs={{0,8},{4,12},{8,0},{12,4},{16,24},{20,28},{24,16},{28,20},{1,9},{5... | collective-permute-start | bytes 835592 | tf_op jit(solution)/shard_map/ppermute | solution.py:487
  38.9 7.8 %collective-permute-done.4 = f32[128,512]{1,0:T(8,128)S(1)} collective-permute-done((f32[128,512]{1,0:T(8,128)S(1)}, f32[128,512]{1,0:T(8,128)S(1)}, u32[]{:S(2)}, u32[]{:S(2)}) %collective-permute-start.4) | collective-permute-done | bytes 262176 | tf_op jit(solution)/shard_map/ppermute | solution.py:487
  46.7 0.0 copy-start.7
  46.7 0.2 add_select_fusion
  46.9 0.0 copy-start
  46.9 0.0 copy-start.2
  47.0 0.0 copy-start.6
  47.0 0.0 copy-start.8
  47.0 0.0 copy-start.9
  47.0 1.6 %collective-permute-start.9 = (f32[256,512]{1,0:T(8,128)S(1)}, f32[256,512]{1,0:T(8,128)S(1)}, u32[]{:S(2)}, u32[]{:S(2)}) collective-permute-start(f32[256,512]{1,0:T(8,128)S(1)} %pad_maximum_fusion), channel_id=1, source_target_pairs={{0,4},{4,0},{8,12},{12,8},{16,20},{20,16},{24,28},{28,24},{1,5},{5... | collective-permute-start | bytes 1572872 | tf_op jit(solution)/shard_map/ppermute | solution.py:513
  48.6 1.1 %collective-permute-done.3 = f32[136,512]{1,0:T(8,128)S(1)} collective-permute-done((f32[136,512]{1,0:T(8,128)S(1)}, f32[136,512]{1,0:T(8,128)S(1)}, u32[]{:S(2)}, u32[]{:S(2)}) %collective-permute-start.3) | collective-permute-done | bytes 278560 | tf_op jit(solution)/shard_map/ppermute | solution.py:487
  49.7 0.2 multiply_add_fusion.3
  49.9 0.7 collective-permute-start.7
  50.6 1.5 %collective-permute-start.6 = (f32[128,512]{1,0:T(8,128)S(1)}, f32[128,512]{1,0:T(8,128)S(1)}, u32[]{:S(2)}, u32[]{:S(2)}) collective-permute-start(f32[128,512]{1,0:T(8,128)S(1)} %multiply_add_fusion.3), channel_id=1, source_target_pairs={{8,24},{12,28},{16,0},{20,4},{9,25},{13,29},{17,1},{21,5},{10,26},... | collective-permute-start | bytes 786440 | tf_op jit(solution)/shard_map/ppermute | solution.py:487
  52.1 11.0 %collective-permute-done.6 = f32[128,512]{1,0:T(8,128)S(1)} collective-permute-done((f32[128,512]{1,0:T(8,128)S(1)}, f32[128,512]{1,0:T(8,128)S(1)}, u32[]{:S(2)}, u32[]{:S(2)}) %collective-permute-start.6) | collective-permute-done | bytes 262176 | tf_op jit(solution)/shard_map/ppermute | solution.py:487
  63.1 0.2 add_select_fusion.2
  63.4 1.6 %collective-permute-start.8 = (f32[256,512]{1,0:T(8,128)S(1)}, f32[256,512]{1,0:T(8,128)S(1)}, u32[]{:S(2)}, u32[]{:S(2)}) collective-permute-start(f32[256,512]{1,0:T(8,128)S(1)} %pad_maximum_fusion.2), channel_id=1, source_target_pairs={{0,4},{4,0},{8,12},{12,8},{16,20},{20,16},{24,28},{28,24},{1,5},{5... | collective-permute-start | bytes 1572872 | tf_op jit(solution)/shard_map/ppermute | solution.py:513
  65.1 11.8 %local_grads.2 = (bf16[1024,2048]{1,0:T(8,128)(2,1)}, f32[1024,128]{1,0:T(8,128)S(1)}, f32[1024,128]{1,0:T(8,128)S(1)}, f32[4,8,1024]{2,1,0:T(8,128)}, f32[8,128]{1,0:T(8,128)S(1)}) custom-call(s32[1]{0:T(128)} %bitcast.refs_0_, bf16[1024,2048]{1,0:T(8,128)(2,1)S(1)} %copy-done, bf16[1024,2048]{1,0:T(8,128)(2,1)S(1)} %copy-done.1, ...), custom_call_target="tpu_custom_call" | custom-call | flops 4831838208 | bytes 6291456 | tf_op jit(solution)/shard_map/local_grads/pallas_call | solution.py:412
  76.9 12.1 %local_grads.3 = (bf16[1024,2048]{1,0:T(8,128)(2,1)}, f32[1024,128]{1,0:T(8,128)}, f32[1024,128]{1,0:T(8,128)}, f32[4,8,1024]{2,1,0:T(8,128)}, f32[8,128]{1,0:T(8,128)S(1)}) custom-call(s32[1]{0:T(128)} %bitcast.refs_0_, bf16[1024,2048]{1,0:T(8,128)(2,1)S(1)} %copy-done, ...), custom_call_target="tpu_custom_call", output_to_operand_aliasing={{0}: (17, {}), {3}: (18, {})} | custom-call | flops 4831838208 | bytes 6291456 | tf_op jit(solution)/shard_map/local_grads/pallas_call | solution.py:412
  89.0 0.1 collective-permute-start.12
  89.1 1.6 %collective-permute-start.11 = (f32[8,128]{1,0:T(8,128)S(1)}, f32[8,128]{1,0:T(8,128)S(1)}, u32[]{:S(2)}, u32[]{:S(2)}) collective-permute-start(f32[8,128]{1,0:T(8,128)S(1)} %get-tuple-element.71), channel_id=1, source_target_pairs={{0,2},{1,3},{2,0},{3,1},{4,6},{5,7},{6,4},{7,5},{8,10},{9,11},{10,... | collective-permute-start | bytes 12296 | tf_op jit(solution)/shard_map/ppermute | solution.py:440
  90.6 0.3 collective-permute-start.10
  90.9 1.2 %collective-permute-done.12 = f32[8,128]{1,0:T(8,128)S(1)} collective-permute-done((f32[8,128]{1,0:T(8,128)S(1)}, f32[8,128]{1,0:T(8,128)S(1)}, u32[]{:S(2)}, u32[]{:S(2)}) %collective-permute-start.12) | collective-permute-done | bytes 4128 | tf_op jit(solution)/shard_map/ppermute | solution.py:440
  92.1 0.7 collective-permute-done.11
  92.7 0.1 collective-permute-start.15
  92.8 2.0 %collective-permute-start.14 = (f32[8,128]{1,0:T(8,128)S(1)}, f32[8,128]{1,0:T(8,128)S(1)}, u32[]{:S(2)}, u32[]{:S(2)}) collective-permute-start(f32[8,128]{1,0:T(8,128)S(1)} %add_add_fusion.1), channel_id=1, source_target_pairs={{0,8},{4,12},{8,0},{12,4},{16,24},{20,28},{24,16},{28,20},{1,9},{5... | collective-permute-start | bytes 12296 | tf_op jit(solution)/shard_map/ppermute | solution.py:440
  94.8 1.5 %collective-permute-start.13 = (f32[8,128]{1,0:T(8,128)S(1)}, f32[8,128]{1,0:T(8,128)S(1)}, u32[]{:S(2)}, u32[]{:S(2)}) collective-permute-start(f32[8,128]{1,0:T(8,128)S(1)} %add_add_fusion.1), channel_id=1, source_target_pairs={{0,4},{4,0},{8,12},{12,8},{16,20},{20,16},{24,28},{28,24},{1,5},{5... | collective-permute-start | bytes 12296 | tf_op jit(solution)/shard_map/ppermute | solution.py:440
  96.3 1.0 collective-permute-done.15
  97.3 1.1 %collective-permute-done.13 = f32[8,128]{1,0:T(8,128)S(1)} collective-permute-done((f32[8,128]{1,0:T(8,128)S(1)}, f32[8,128]{1,0:T(8,128)S(1)}, u32[]{:S(2)}, u32[]{:S(2)}) %collective-permute-start.13) | collective-permute-done | bytes 4128 | tf_op jit(solution)/shard_map/ppermute | solution.py:440
  98.4 1.1 %collective-permute-start.16 = (f32[8,128]{1,0:T(8,128)S(1)}, f32[8,128]{1,0:T(8,128)S(1)}, u32[]{:S(2)}, u32[]{:S(2)}) collective-permute-start(f32[8,128]{1,0:T(8,128)S(1)} %add_add_fusion), channel_id=1, source_target_pairs={{0,16},{4,20},{8,24},{12,28},{16,0},{20,4},{24,8},{28,12},{1,17},{... | collective-permute-start | bytes 12296 | tf_op jit(solution)/shard_map/ppermute | solution.py:440
  99.6 3.4 %collective-permute-done.16 = f32[8,128]{1,0:T(8,128)S(1)} collective-permute-done((f32[8,128]{1,0:T(8,128)S(1)}, f32[8,128]{1,0:T(8,128)S(1)}, u32[]{:S(2)}, u32[]{:S(2)}) %collective-permute-start.16) | collective-permute-done | bytes 4128 | tf_op jit(solution)/shard_map/ppermute | solution.py:440
  102.9 0.5 slice_bitcast_fusion
  103.4 0.6 slice.154
  (38 shorter events, 0.3 us)
Async XLA Ops:
  5.2 15.5 %collective-permute-start.1 = (f32[264,512]{1,0:T(8,128)}, f32[264,512]{1,0:T(8,128)S(1)}, u32[]{:S(2)}, u32[]{:S(2)}) collective-permute-start(f32[264,512]{1,0:T(8,128)} %get-tuple-element.52), channel_id=1, source_target_pairs={{0,4},{4,0},{8,12},{12,8},{16,20},{20,16},{24,28},{28,24},{1,5},{5... | collective-permute-start | bytes 1622024 | tf_op jit(solution)/shard_map/ppermute | solution.py:473
  12.1 12.6 %copy-start.11 = (f32[264,512]{1,0:T(8,128)S(1)}, f32[264,512]{1,0:T(8,128)}, u32[]{:S(2)}) copy-start(f32[264,512]{1,0:T(8,128)} %get-tuple-element.50) | copy-start | bytes 1622020
  18.2 19.3 %copy-start.10 = (f32[264,512]{1,0:T(8,128)S(1)}, f32[264,512]{1,0:T(8,128)}, u32[]{:S(2)}) copy-start(f32[264,512]{1,0:T(8,128)} %get-tuple-element.56) | copy-start | bytes 1622020
  22.8 7.9 %collective-permute-start.2 = (f32[136,512]{1,0:T(8,128)S(1)}, f32[136,512]{1,0:T(8,128)S(1)}, u32[]{:S(2)}, u32[]{:S(2)}) collective-permute-start(f32[136,512]{1,0:T(8,128)S(1)} %pad_maximum_fusion.4), channel_id=1, source_target_pairs={{0,8},{4,12},{8,0},{12,4},{16,24},{20,28},{24,16},{28,20},{1,9},{5... | collective-permute-start | bytes 835592 | tf_op jit(solution)/shard_map/ppermute | solution.py:487
  24.6 12.9 %collective-permute-start = (f32[264,512]{1,0:T(8,128)S(1)}, f32[264,512]{1,0:T(8,128)S(1)}, u32[]{:S(2)}, u32[]{:S(2)}) collective-permute-start(f32[264,512]{1,0:T(8,128)S(1)} %copy-done.11), channel_id=1, source_target_pairs={{0,4},{4,0},{8,12},{12,8},{16,20},{20,16},{24,28},{28,24},{1,5},{5... | collective-permute-start | bytes 1622024 | tf_op jit(solution)/shard_map/ppermute | solution.py:473
  31.9 14.7 %collective-permute-start.5 = (f32[128,512]{1,0:T(8,128)S(1)}, f32[128,512]{1,0:T(8,128)S(1)}, u32[]{:S(2)}, u32[]{:S(2)}) collective-permute-start(f32[128,512]{1,0:T(8,128)S(1)} %multiply_add_fusion.5), channel_id=1, source_target_pairs={{8,16},{12,20},{16,8},{20,12},{9,17},{13,21},{17,9},{21,13},{10,18... | collective-permute-start | bytes 786440 | tf_op jit(solution)/shard_map/ppermute | solution.py:487
  32.6 14.1 %collective-permute-start.4 = (f32[128,512]{1,0:T(8,128)S(1)}, f32[128,512]{1,0:T(8,128)S(1)}, u32[]{:S(2)}, u32[]{:S(2)}) collective-permute-start(f32[128,512]{1,0:T(8,128)S(1)} %multiply_add_fusion.5), channel_id=1, source_target_pairs={{8,24},{12,28},{16,0},{20,4},{9,25},{13,29},{17,1},{21,5},{10,26},... | collective-permute-start | bytes 786440 | tf_op jit(solution)/shard_map/ppermute | solution.py:487
  37.7 12.0 %collective-permute-start.3 = (f32[136,512]{1,0:T(8,128)S(1)}, f32[136,512]{1,0:T(8,128)S(1)}, u32[]{:S(2)}, u32[]{:S(2)}) collective-permute-start(f32[136,512]{1,0:T(8,128)S(1)} %pad_maximum_fusion.5), channel_id=1, source_target_pairs={{0,8},{4,12},{8,0},{12,4},{16,24},{20,28},{24,16},{28,20},{1,9},{5... | collective-permute-start | bytes 835592 | tf_op jit(solution)/shard_map/ppermute | solution.py:487
  46.7 18.4 %copy-start.3 = (bf16[1,1024,128]{2,1,0:T(8,128)(2,1)S(1)}, bf16[1,1024,128]{2,1,0:T(8,128)(2,1)}, u32[]{:S(2)}) copy-start(bf16[1,1024,128]{2,1,0:T(8,128)(2,1)} %param.10) | copy-start | bytes 786436
  46.7 18.4 %copy-start.4 = (bf16[1024,128]{1,0:T(8,128)(2,1)S(1)}, bf16[1024,128]{1,0:T(8,128)(2,1)}, u32[]{:S(2)}) copy-start(bf16[1024,128]{1,0:T(8,128)(2,1)} %get-tuple-element.39.refs_5_.refs_7_) | copy-start | bytes 786436
  46.7 18.4 %copy-start.5 = (f32[16,2048]{1,0:T(8,128)S(1)}, f32[16,2048]{1,0:T(8,128)}, u32[]{:S(2)}) copy-start(f32[16,2048]{1,0:T(8,128)} %get-tuple-element.40.refs_6_.refs_8_) | copy-start | bytes 393220
  46.7 18.4 %copy-start.7 = (f32[1,32,1024]{2,1,0:T(8,128)S(1)}, f32[1,32,1024]{2,1,0:T(8,128)}, u32[]{:S(2)}) copy-start(f32[1,32,1024]{2,1,0:T(8,128)} %refs_5_.1) | copy-start | bytes 393220
  46.9 18.1 %copy-start = (bf16[1024,2048]{1,0:T(8,128)(2,1)S(1)}, bf16[1024,2048]{1,0:T(8,128)(2,1)}, u32[]{:S(2)}) copy-start(bf16[1024,2048]{1,0:T(8,128)(2,1)} %get-tuple-element.47.refs_1_) | copy-start | bytes 12582916
  46.9 18.1 %copy-start.1 = (bf16[1024,2048]{1,0:T(8,128)(2,1)S(1)}, bf16[1024,2048]{1,0:T(8,128)(2,1)}, u32[]{:S(2)}) copy-start(bf16[1024,2048]{1,0:T(8,128)(2,1)} %get-tuple-element.48.refs_2_) | copy-start | bytes 12582916
  46.9 18.1 %copy-start.2 = (bf16[1,1024,128]{2,1,0:T(8,128)(2,1)S(1)}, bf16[1,1024,128]{2,1,0:T(8,128)(2,1)}, u32[]{:S(2)}) copy-start(bf16[1,1024,128]{2,1,0:T(8,128)(2,1)} %param.9) | copy-start | bytes 786436
  47.0 18.1 %copy-start.6 = (f32[8,2048]{1,0:T(8,128)S(1)}, f32[8,2048]{1,0:T(8,128)}, u32[]{:S(2)}) copy-start(f32[8,2048]{1,0:T(8,128)} %get-tuple-element.49.refs_4_) | copy-start | bytes 196612
  47.0 18.1 %copy-start.8 = (f32[32]{0:T(128)S(1)}, f32[32]{0:T(128)}, u32[]{:S(2)}) copy-start(f32[32]{0:T(128)} %param.12) | copy-start | bytes 388
  47.0 18.1 %copy-start.9 = (f32[32]{0:T(128)S(1)}, f32[32]{0:T(128)}, u32[]{:S(2)}) copy-start(f32[32]{0:T(128)} %param.13) | copy-start | bytes 388
  47.0 18.0 %collective-permute-start.9 = (f32[256,512]{1,0:T(8,128)S(1)}, f32[256,512]{1,0:T(8,128)S(1)}, u32[]{:S(2)}, u32[]{:S(2)}) collective-permute-start(f32[256,512]{1,0:T(8,128)S(1)} %pad_maximum_fusion), channel_id=1, source_target_pairs={{0,4},{4,0},{8,12},{12,8},{16,20},{20,16},{24,28},{28,24},{1,5},{5... | collective-permute-start | bytes 1572872 | tf_op jit(solution)/shard_map/ppermute | solution.py:513
  49.9 13.2 %collective-permute-start.7 = (f32[128,512]{1,0:T(8,128)S(1)}, f32[128,512]{1,0:T(8,128)S(1)}, u32[]{:S(2)}, u32[]{:S(2)}) collective-permute-start(f32[128,512]{1,0:T(8,128)S(1)} %multiply_add_fusion.3), channel_id=1, source_target_pairs={{8,16},{12,20},{16,8},{20,12},{9,17},{13,21},{17,9},{21,13},{10,18... | collective-permute-start | bytes 786440 | tf_op jit(solution)/shard_map/ppermute | solution.py:487
  50.6 12.5 %collective-permute-start.6 = (f32[128,512]{1,0:T(8,128)S(1)}, f32[128,512]{1,0:T(8,128)S(1)}, u32[]{:S(2)}, u32[]{:S(2)}) collective-permute-start(f32[128,512]{1,0:T(8,128)S(1)} %multiply_add_fusion.3), channel_id=1, source_target_pairs={{8,24},{12,28},{16,0},{20,4},{9,25},{13,29},{17,1},{21,5},{10,26},... | collective-permute-start | bytes 786440 | tf_op jit(solution)/shard_map/ppermute | solution.py:487
  63.4 13.5 %collective-permute-start.8 = (f32[256,512]{1,0:T(8,128)S(1)}, f32[256,512]{1,0:T(8,128)S(1)}, u32[]{:S(2)}, u32[]{:S(2)}) collective-permute-start(f32[256,512]{1,0:T(8,128)S(1)} %pad_maximum_fusion.2), channel_id=1, source_target_pairs={{0,4},{4,0},{8,12},{12,8},{16,20},{20,16},{24,28},{28,24},{1,5},{5... | collective-permute-start | bytes 1572872 | tf_op jit(solution)/shard_map/ppermute | solution.py:513
  89.0 3.1 %collective-permute-start.12 = (f32[8,128]{1,0:T(8,128)S(1)}, f32[8,128]{1,0:T(8,128)S(1)}, u32[]{:S(2)}, u32[]{:S(2)}) collective-permute-start(f32[8,128]{1,0:T(8,128)S(1)} %get-tuple-element.71), channel_id=1, source_target_pairs={{0,3},{1,2},{2,1},{3,0},{4,7},{5,6},{6,5},{7,4},{8,11},{9,10},{10,... | collective-permute-start | bytes 12296 | tf_op jit(solution)/shard_map/ppermute | solution.py:440
  89.1 3.7 %collective-permute-start.11 = (f32[8,128]{1,0:T(8,128)S(1)}, f32[8,128]{1,0:T(8,128)S(1)}, u32[]{:S(2)}, u32[]{:S(2)}) collective-permute-start(f32[8,128]{1,0:T(8,128)S(1)} %get-tuple-element.71), channel_id=1, source_target_pairs={{0,2},{1,3},{2,0},{3,1},{4,6},{5,7},{6,4},{7,5},{8,10},{9,11},{10,... | collective-permute-start | bytes 12296 | tf_op jit(solution)/shard_map/ppermute | solution.py:440
  90.6 2.1 %collective-permute-start.10 = (f32[8,128]{1,0:T(8,128)S(1)}, f32[8,128]{1,0:T(8,128)S(1)}, u32[]{:S(2)}, u32[]{:S(2)}) collective-permute-start(f32[8,128]{1,0:T(8,128)S(1)} %get-tuple-element.71), channel_id=1, source_target_pairs={{0,1},{1,0},{2,3},{3,2},{4,5},{5,4},{6,7},{7,6},{8,9},{9,8},{10,11... | collective-permute-start | bytes 12296 | tf_op jit(solution)/shard_map/ppermute | solution.py:440
  92.7 4.6 %collective-permute-start.15 = (f32[8,128]{1,0:T(8,128)S(1)}, f32[8,128]{1,0:T(8,128)S(1)}, u32[]{:S(2)}, u32[]{:S(2)}) collective-permute-start(f32[8,128]{1,0:T(8,128)S(1)} %add_add_fusion.1), channel_id=1, source_target_pairs={{0,12},{4,8},{8,4},{12,0},{16,28},{20,24},{24,20},{28,16},{1,13},{... | collective-permute-start | bytes 12296 | tf_op jit(solution)/shard_map/ppermute | solution.py:440
  92.8 4.5 %collective-permute-start.14 = (f32[8,128]{1,0:T(8,128)S(1)}, f32[8,128]{1,0:T(8,128)S(1)}, u32[]{:S(2)}, u32[]{:S(2)}) collective-permute-start(f32[8,128]{1,0:T(8,128)S(1)} %add_add_fusion.1), channel_id=1, source_target_pairs={{0,8},{4,12},{8,0},{12,4},{16,24},{20,28},{24,16},{28,20},{1,9},{5... | collective-permute-start | bytes 12296 | tf_op jit(solution)/shard_map/ppermute | solution.py:440
  94.8 3.6 %collective-permute-start.13 = (f32[8,128]{1,0:T(8,128)S(1)}, f32[8,128]{1,0:T(8,128)S(1)}, u32[]{:S(2)}, u32[]{:S(2)}) collective-permute-start(f32[8,128]{1,0:T(8,128)S(1)} %add_add_fusion.1), channel_id=1, source_target_pairs={{0,4},{4,0},{8,12},{12,8},{16,20},{20,16},{24,28},{28,24},{1,5},{5... | collective-permute-start | bytes 12296 | tf_op jit(solution)/shard_map/ppermute | solution.py:440
  98.4 4.5 %collective-permute-start.16 = (f32[8,128]{1,0:T(8,128)S(1)}, f32[8,128]{1,0:T(8,128)S(1)}, u32[]{:S(2)}, u32[]{:S(2)}) collective-permute-start(f32[8,128]{1,0:T(8,128)S(1)} %add_add_fusion), channel_id=1, source_target_pairs={{0,16},{4,20},{8,24},{12,28},{16,0},{20,4},{24,8},{28,12},{1,17},{... | collective-permute-start | bytes 12296 | tf_op jit(solution)/shard_map/ppermute | solution.py:440

commit v5 on v3

--- a/solution.py
+++ b/solution.py
@@ -159,8 +159,8 @@
                 scores = dot(b_ref[rows, :], c_ref[rows, :], NT)
                 right[n] = jnp.where(triangle(GROUP, False), scores, 0.0).astype(BF16)
 
-    gain = picker(piece, heads, all_heads, width, True)
-    lift = picker(piece, heads, all_heads, width, False)
+    gain = dot(columns_ref[...], picker(piece, heads, all_heads, width, True), NN)
+    lift = dot(columns_ref[...], picker(piece, heads, all_heads, width, False), NN)
     table = table_ref[:, pl.ds(pl.multiple_of(piece * width, width), width)]
     state = jnp.zeros((states, width), F32)
     grad = jnp.zeros((states, width), F32)
@@ -170,8 +170,8 @@
         x = x_ref[rows, :].astype(F32)
         dy = dy_ref[rows, :].astype(F32)
         direct = direct + jnp.sum((dy * x).reshape(GROUP // 8, 8, width), axis=0)
-        scaled_x = (x * dot(columns_ref[rows, :], gain, NN)).astype(BF16)
-        scaled_dy = (dy * dot(columns_ref[rows, :], lift, NN)).astype(BF16)
+        scaled_x = (x * gain[rows]).astype(BF16)
+        scaled_dy = (dy * lift[rows]).astype(BF16)
         xs_ref[rows, :] = scaled_x
         ys_ref[rows, :] = scaled_dy
         later = table[blocks + n : blocks + n + 1]
@@ -259,6 +259,173 @@
     return out[:count], list(out[count:])
 
 
+def grads_kernel(first, scale, part, half, *refs):
+    y_ref, xs_ref, ys_ref, dy_ref, direct_ref, b_ref, c_ref, columns_ref, table_ref = refs[:9]
+    raw_ref, bias_ref, rate_ref, mine_ref, other_ref, bt, ct, left, right, adder = refs[9:19]
+    refs = refs[19:]
+    if not first:
+        dc_in, db_in, par_in = refs[:3]
+        refs = refs[5:]
+    dx_ref, dc_ref, db_ref, draw_ref, par_ref = refs[:5]
+    sums, dc_sum, db_sum, terms = refs[5:]
+    g = pl.program_id(0)
+    heads = raw_ref.shape[1]
+    length, width = xs_ref.shape
+    states = b_ref.shape[1]
+    blocks = length // GROUP
+    piece = g * half + part
+    all_heads = columns_ref.shape[1] // 4
+    member = head_matrix(heads, width).astype(BF16)
+    lower = triangle(GROUP, True)
+    rows = [slice(n * GROUP, (n + 1) * GROUP) for n in range(blocks)]
+
+    @pl.when(g == 0)
+    def _():
+        sums[...] = jnp.zeros_like(sums)
+        dc_sum[...] = jnp.zeros_like(dc_sum)
+        db_sum[...] = jnp.zeros_like(db_sum)
+        par_ref[...] = jnp.zeros_like(par_ref) if first else par_in[...]
+
+    own = g == y_ref[0]
+    state = jnp.where(own, mine_ref[:states], other_ref[:states])
+    grad = jnp.where(own, mine_ref[states:], other_ref[states:])
+    table = table_ref[...]
+    skip = table[3 * blocks + 1 : 3 * blocks + 2]
+    entering_low, ends = [], []
+    for n in range(blocks):
+        state = table[n : n + 1] * state
+        entering_low.append(state.astype(BF16))
+        state = state + dot(bt[:, rows[n]], xs_ref[rows[n], :], NN)
+        ends.append(state)
+    leaving_low, edges = [None] * blocks, [None] * blocks
+    for n in reversed(range(blocks)):
+        leaving_low[n] = grad.astype(BF16)
+        edges[n] = jnp.sum(ends[n] * grad, axis=0, keepdims=True)
+        grad = table[n : n + 1] * (grad + dot(ct[:, rows[n]], ys_ref[rows[n], :], NN))
+    gain = dot(columns_ref[...], picker(piece, heads, all_heads, width, True), NN)
+    for n in range(blocks):
+        scaled_x, scaled_dy = xs_ref[rows[n], :], ys_ref[rows[n], :]
+        forward = dot(left[n], scaled_x, NN) + dot(c_ref[rows[n], :], entering_low[n], NN)
+        backward = dot(right[n], scaled_dy, NN) + dot(b_ref[rows[n], :], leaving_low[n], NN)
+        weight = gain[rows[n]]
+        dx_ref[rows[n], :] = (weight * backward + skip * dy_ref[rows[n], :].astype(F32)).astype(
+            dx_ref.dtype
+        )
+        v = scaled_x.astype(F32) * backward
+        difference = scaled_dy.astype(F32) * forward - v
+        hi = difference.astype(BF16)
+        lo = (difference - hi.astype(F32)).astype(BF16)
+        terms[rows[n], :width] = hi
+        terms[rows[n], width : 2 * width] = lo
+        terms[rows[n], 2 * width :] = v.astype(BF16)
+        sums[n] += dot(scaled_dy, scaled_x, NT)
+        dc_sum[n] += dot(scaled_dy, entering_low[n], NT)
+        db_sum[n] += dot(scaled_x, leaving_low[n], NT)
+    added = dot(terms[...], adder[...], NN).T
+    added = [added[:, rows[n]] for n in range(blocks)]
+    edge = head_sums(jnp.concatenate(edges + [edges[0]] * (8 - blocks), axis=0), member)
+    slopes = running(
+        jnp.concatenate([a[:heads] for a in added], axis=0), lower.astype(BF16)
+    )
+    slope = jnp.concatenate(
+        [slopes[n * heads : (n + 1) * heads] + edge[:, n : n + 1] for n in range(blocks)], axis=1
+    )
+    v = jnp.concatenate([a[heads : 2 * heads] for a in added], axis=1)
+    raw = raw_ref[0] + column(bias_ref[...], piece, heads)
+    step = softplus(raw)
+    draw = (v / step - column(rate_ref[...], piece, heads) * slope) / (1.0 + jnp.exp(-raw))
+    draw_ref[0] = draw
+    values = (
+        jnp.sum(draw, axis=1, keepdims=True),
+        jnp.sum(head_sums(direct_ref[...], member), axis=1, keepdims=True),
+        -jnp.sum(step * slope, axis=1, keepdims=True),
+    )
+    for k, value in enumerate(values):
+        par_ref[k : k + 1] += lanes_of(value * scale, piece, (heads, par_ref.shape[1]))
+
+    @pl.when(g == pl.num_programs(0) - 1)
+    def _():
+        for n in range(blocks):
+            pair = jnp.where(lower, sums[n], 0.0).astype(BF16)
+            dc = dot(pair, b_ref[rows[n], :], NN) + dc_sum[n]
+            db = dot(pair, c_ref[rows[n], :], TN) + db_sum[n]
+            if not first:
+                dc = dc + dc_in[rows[n], :]
+                db = db + db_in[rows[n], :]
+            dc_ref[rows[n], :] = dc
+            db_ref[rows[n], :] = db
+
+
+def local_grads(part, scale, y, saved, dy, b, c, vectors, mine, other, before):
+    xs, ys, direct, factor_columns, table, left, right, bt, ct = saved
+    raw, bias, rate, _ = vectors
+    length, channels = xs.shape
+    pieces = 2 * PARTS
+    heads = raw.shape[1] // pieces
+    raw = raw.reshape(pieces, heads, length)
+    width = channels // pieces
+    states = b.shape[1]
+    blocks = length // GROUP
+    half = pieces // 2
+    first = before is None
+    whole = lambda g, y: (0, 0)
+    place = lambda g, y: (0, g * half + part)
+    columns = pl.BlockSpec((length, width), place)
+    maps = pl.BlockSpec((length, states), whole)
+    line = pl.BlockSpec(bias.shape, whole)
+    lines = pl.BlockSpec((1, heads, length), lambda g, y: (g * half + part, 0, 0))
+    held = pl.BlockSpec((2 * states, width), whole)
+    params = pl.BlockSpec((8, 128), whole)
+    anywhere = pl.BlockSpec(memory_space=pl.ANY)
+    in_specs = [columns, columns, columns, pl.BlockSpec((8, width), place), maps, maps]
+    in_specs += [
+        pl.BlockSpec(factor_columns.shape, whole),
+        pl.BlockSpec((table.shape[0], width), place),
+    ]
+    in_specs += [lines, line, line, held, held]
+    args = [xs, ys, dy, direct, b, c, factor_columns, table, raw, bias, rate, mine, other]
+    fixed = [bt, ct, left, right, adding(width, heads, (0, 0, 1))]
+    in_specs += [pl.BlockSpec(a.shape, lambda g, y, n=len(a.shape): (0,) * n) for a in fixed]
+    args += fixed
+    aliases = {}
+    if not first:
+        dx, dc, db, draw, par = before
+        args += [dc, db, par, dx, draw]
+        in_specs += [maps, maps, params, anywhere, anywhere]
+        aliases = {22: 0, 23: 3}
+    grid_spec = pltpu.PrefetchScalarGridSpec(
+        num_scalar_prefetch=1,
+        grid=(2,),
+        in_specs=in_specs,
+        out_specs=[columns, maps, maps, lines, params],
+        scratch_shapes=[
+            pltpu.VMEM((blocks, GROUP, GROUP), F32),
+            pltpu.VMEM((blocks, GROUP, states), F32),
+            pltpu.VMEM((blocks, GROUP, states), F32),
+            pltpu.VMEM((length, 3 * width), BF16),
+        ],
+    )
+    return pl.pallas_call(
+        functools.partial(grads_kernel, first, scale, part, half),
+        grid_spec=grid_spec,
+        out_shape=[
+            jax.ShapeDtypeStruct((length, channels), BF16),
+            jax.ShapeDtypeStruct((length, states), F32),
+            jax.ShapeDtypeStruct((length, states), F32),
+            jax.ShapeDtypeStruct((pieces, heads, length), F32),
+            jax.ShapeDtypeStruct((8, 128), F32),
+        ],
+        input_output_aliases=aliases,
+        compiler_params=pltpu.CompilerParams(vmem_limit_bytes=SMALL_LIMIT),
+        cost_estimate=pl.CostEstimate(
+            flops=24 * length * width * (GROUP + states),
+            bytes_accessed=12 * length * width,
+            transcendentals=0,
+        ),
+        name="local_grads",
+    )(y, *args)
+
+
 def adding(width, heads, places):
     out = np.zeros((len(places) * width, 128), np.float32)
     size = width // heads
@@ -281,7 +448,7 @@
     if not first:
         dc_in, db_in, par_in = refs[:3]
         refs = refs[5:]
-    dx_ref, dc_ref, db_ref, draw_ref, par_ref = refs
+    dx_ref, dc_ref, db_ref, draw_ref, par_ref, terms = refs
     heads = raw_ref.shape[1]
     length, width = xs_ref.shape
     states = b_ref.shape[1]
@@ -312,8 +479,7 @@
         if n:
             fresh = dot(ct[:, rows[n]], ys_ref[rows[n], :], NN)
             grad = table[n : n + 1] * (fresh if grad is None else grad + fresh)
-    gain = picker(piece, heads, all_heads, width, True)
-    added = []
+    gain = dot(columns_ref[...], picker(piece, heads, all_heads, width, True), NN)
     for n in range(blocks):
         scaled_x, scaled_dy = xs_ref[rows[n], :], ys_ref[rows[n], :]
         forward = dot(left[n], scaled_x, NN)
@@ -322,15 +488,16 @@
         backward = dot(right[n], scaled_dy, NN)
         if leaving_low[n] is not None:
             backward = backward + dot(b_ref[rows[n], :], leaving_low[n], NN)
-        weight = dot(columns_ref[rows[n], :], gain, NN)
-        dx_ref[rows[n], :] = (weight * backward + skip * dy_ref[rows[n], :].astype(F32)).astype(
+        dx_ref[rows[n], :] = (gain[rows[n]] * backward + skip * dy_ref[rows[n], :].astype(F32)).astype(
             dx_ref.dtype
         )
         v = scaled_x.astype(F32) * backward
         difference = scaled_dy.astype(F32) * forward - v
         hi = difference.astype(BF16)
         lo = (difference - hi.astype(F32)).astype(BF16)
-        added.append(dot(jnp.concatenate([hi, lo, v.astype(BF16)], axis=1), adder[...], NN))
+        terms[rows[n], :width] = hi
+        terms[rows[n], width : 2 * width] = lo
+        terms[rows[n], 2 * width :] = v.astype(BF16)
         pair = jnp.where(lower, dot(scaled_dy, scaled_x, NT), 0.0).astype(BF16)
         dc = dot(pair, b_ref[rows[n], :], NN)
         db = dot(pair, c_ref[rows[n], :], TN)
@@ -340,7 +507,8 @@
             db = db + dot(scaled_x, leaving_low[n], NT)
         dc_ref[rows[n], :] = dc if first else dc + dc_in[rows[n], :]
         db_ref[rows[n], :] = db if first else db + db_in[rows[n], :]
-    added = [a.T for a in added]
+    added = dot(terms[...], adder[...], NN).T
+    added = [added[:, rows[n]] for n in range(blocks)]
     edge = head_sums(jnp.concatenate(edges + [edges[0]] * (8 - blocks), axis=0), member)
     slopes = running(jnp.concatenate([a[:heads] for a in added], axis=0), lower.astype(BF16))
     slope = jnp.concatenate(
@@ -402,8 +570,9 @@
             jax.ShapeDtypeStruct((pieces, heads, length), F32),
             jax.ShapeDtypeStruct((8, 128), F32),
         ],
+        scratch_shapes=[pltpu.VMEM((length, 3 * width), BF16)],
         input_output_aliases=aliases,
-        compiler_params=pltpu.CompilerParams(vmem_limit_bytes=VMEM_LIMIT),
+        compiler_params=pltpu.CompilerParams(vmem_limit_bytes=VMEM_LIMIT if first else SMALL_LIMIT),
         cost_estimate=pl.CostEstimate(
             flops=24 * length * width * (GROUP + states),
             bytes_accessed=10 * length * width,
@@ -416,7 +585,7 @@
 def entering_kernel(scale, part, half, *refs):
     y_ref, xs_ref, ys_ref, b_ref, c_ref, adder, columns_ref, table_ref = refs[:8]
     raw_ref, bias_ref, rate_ref, mine_ref, other_ref, dx_in, draw_in, par_in = refs[8:16]
-    dx_ref, draw_ref, par_ref = refs[16:]
+    dx_ref, draw_ref, par_ref, terms = refs[16:]
     g = pl.program_id(0)
     heads = raw_ref.shape[1]
     length, width = xs_ref.shape
@@ -435,21 +604,19 @@
     state = jnp.where(own, mine_ref[:states], other_ref[:states])
     grad = jnp.where(own, mine_ref[states:], other_ref[states:])
     table = table_ref[...]
-    gain = picker(piece, heads, all_heads, width, True)
-    added = []
+    gain = dot(columns_ref[...], picker(piece, heads, all_heads, width, True), NN)
     for n in range(blocks):
         entered = (table[2 * blocks + n : 2 * blocks + n + 1] * state).astype(BF16)
         leaving = (table[blocks + n : blocks + n + 1] * grad).astype(BF16)
         forward = dot(c_ref[rows[n], :], entered, NN)
         backward = dot(b_ref[rows[n], :], leaving, NN)
-        weight = dot(columns_ref[rows[n], :], gain, NN)
-        dx_ref[rows[n], :] = (dx_in[rows[n], :].astype(F32) + weight * backward).astype(
+        dx_ref[rows[n], :] = (dx_in[rows[n], :].astype(F32) + gain[rows[n]] * backward).astype(
             dx_ref.dtype
         )
-        p = (xs_ref[rows[n], :].astype(F32) * backward).astype(BF16)
-        q = (ys_ref[rows[n], :].astype(F32) * forward).astype(BF16)
-        added.append(dot(jnp.concatenate([p, q], axis=1), adder[...], NN))
-    added = [a.T for a in added]
+        terms[rows[n], :width] = (xs_ref[rows[n], :].astype(F32) * backward).astype(BF16)
+        terms[rows[n], width:] = (ys_ref[rows[n], :].astype(F32) * forward).astype(BF16)
+    added = dot(terms[...], adder[...], NN).T
+    added = [added[:, rows[n]] for n in range(blocks)]
     cross = jnp.sum(state * grad, axis=0, keepdims=True) * table[3 * blocks : 3 * blocks + 1]
     cross = head_sums(jnp.broadcast_to(cross, (8, width)), member)[:, :1]
     ps, qs = [a[:heads] for a in added], [a[heads : 2 * heads] for a in added]
@@ -501,6 +668,7 @@
             grid=(2,),
             in_specs=in_specs,
             out_specs=[columns, lines, all_of(par)],
+            scratch_shapes=[pltpu.VMEM((length, 2 * width), BF16)],
         ),
         out_shape=[jax.ShapeDtypeStruct(a.shape, a.dtype) for a in (dx, draw, par)],
         input_output_aliases={13: 0, 14: 1},
@@ -512,9 +680,7 @@
     )(y, xs, ys, b, c, adder, factor_columns, table, raw, bias, rate, mine, other, dx, draw, par)
 
 
-def maps_kernel(*refs):
-    y_ref, xs_ref, ys_ref, table_ref, dc_in, db_in = refs[:6]
-    held, (dc_ref, db_ref) = refs[6:-2], refs[-2:]
+def maps_kernel(y_ref, xs_ref, ys_ref, table_ref, dc_in, db_in, mine, other, dc_ref, db_ref):
     g = pl.program_id(0)
     length = xs_ref.shape[0]
     states = dc_in.shape[1]
@@ -525,12 +691,7 @@
         dc_ref[...] = dc_in[...]
         db_ref[...] = db_in[...]
 
-    own = g // PARTS == y_ref[0]
-    both = None
-    for part in range(PARTS):
-        mine, other = held[2 * part], held[2 * part + 1]
-        one = jnp.where(own, mine[...], other[...])
-        both = one if both is None else jnp.where(g % PARTS == part, one, both)
+    both = jnp.where(g == y_ref[0], mine[...], other[...])
     state, grad = both[:states], both[states:]
     table = table_ref[...]
     for n in range(blocks):
@@ -541,32 +702,31 @@
         db_ref[rows, :] += dot(xs_ref[rows, :], leaving, NT)
 
 
-def maps_grads(y, saved, dc, db, held):
+def maps_grads(part, y, saved, dc, db, mine, other):
     xs, ys, _, _, table = saved[:5]
     length, channels = xs.shape
-    pieces = 2 * PARTS
-    width = channels // pieces
-    place = lambda g, y: (0, g)
+    width = channels // (2 * PARTS)
+    place = lambda g, y: (0, g * PARTS + part)
     all_of = lambda a: pl.BlockSpec(a.shape, lambda g, y: (0, 0))
     columns = pl.BlockSpec((length, width), place)
     return pl.pallas_call(
         maps_kernel,
         grid_spec=pltpu.PrefetchScalarGridSpec(
             num_scalar_prefetch=1,
-            grid=(pieces,),
+            grid=(2,),
             in_specs=[columns, columns, pl.BlockSpec((table.shape[0], width), place)]
-            + [all_of(a) for a in (dc, db, *held)],
+            + [all_of(a) for a in (dc, db, mine, other)],
             out_specs=[all_of(dc), all_of(db)],
         ),
         out_shape=[jax.ShapeDtypeStruct(a.shape, a.dtype) for a in (dc, db)],
         compiler_params=pltpu.CompilerParams(vmem_limit_bytes=SMALL_LIMIT),
         cost_estimate=pl.CostEstimate(
-            flops=16 * length * channels * dc.shape[1],
-            bytes_accessed=4 * length * channels,
+            flops=16 * length * width * dc.shape[1],
+            bytes_accessed=8 * length * width,
             transcendentals=0,
         ),
         name="maps_grads",
-    )(y, xs, ys, table, dc, db, *held)
+    )(y, xs, ys, table, dc, db, mine, other)
 
 
 def summed_over(value, axis):
@@ -575,16 +735,12 @@
         return lax.psum(value, axis)
     bit = 1
     while bit < size:
-        count = min(8, size // bit)
-        got = [
-            lax.ppermute(value, axis, [(i, i ^ (k * bit)) for i in range(size)])
-            for k in range(1, count)
-        ]
-        terms = [value] + got
-        while len(terms) > 1:
-            terms = [terms[k] + terms[k + 1] for k in range(0, len(terms), 2)]
-        value = terms[0]
-        bit *= count
+        steps = (bit, 2 * bit, 3 * bit) if 4 * bit <= size else (bit,)
+        got = [lax.ppermute(value, axis, [(i, i ^ s) for i in range(size)]) for s in steps]
+        value = value + got[0]
+        if len(got) == 3:
+            value = value + (got[1] + got[2])
+        bit *= 4 if len(got) == 3 else 2
     return value
 
 
@@ -598,38 +754,70 @@
     index = lax.axis_index("seq")
     place, second = index // 2, index % 2 == 1
     swap = [(i, i ^ 1) for i in range(size)]
-
-    def parts(a):
-        return a[:states], a[states : 2 * states], a[2 * states : 2 * states + 1]
-
-    message = sent if token is None else after(sent, token)
-    arrived = lax.ppermute(message, "seq", swap)
-    token = yield message, arrived
-    (own_l, own_k, own_d), (got_l, got_k, got_d) = parts(kept), parts(after(arrived, token))
-    l1, k1, d1 = [jnp.where(second, b, a) for a, b in ((own_l, got_l), (own_k, got_k), (own_d, got_d))]
-    l2, k2, d2 = [jnp.where(second, a, b) for a, b in ((own_l, got_l), (own_k, got_k), (own_d, got_d))]
-    whole_l = d2 * l1 + l2
-    whole_k = k1 + d1 * k2
-    whole_d = d1 * d2
-    start = jnp.zeros_like(whole_l)
-    end = jnp.zeros_like(whole_k)
-    for hop in range(1, pairs):
-        message = jnp.where(place == hop - 1, whole_d * start + whole_l, whole_d * end + whole_k)
-        route = []
-        for y in range(2):
-            route.append((2 * (hop - 1) + y, 2 * hop + y))
-            route.append((2 * (pairs - hop) + y, 2 * (pairs - hop - 1) + y))
-        arrived = lax.ppermute(message, "seq", route)
-        token = yield message, arrived
-        arrived = after(arrived, token)
-        start = jnp.where(place == hop, arrived, start)
-        end = jnp.where(place == pairs - 1 - hop, arrived, end)
-    for_first = jnp.concatenate([start, k2 + d2 * end], axis=0)
-    for_second = jnp.concatenate([d1 * start + l1, end], axis=0)
-    mine = jnp.where(second, for_second, for_first)
-    message = jnp.where(second, for_first, for_second)
+    both = lambda moves: [(2 * a + y, 2 * b + y) for a, b in moves for y in range(2)]
+    if pairs == 4:
+        steps = [([(0, 1), (1, 0), (2, 3), (3, 2)],), ([(1, 2), (2, 1)], [(1, 3), (2, 0)])]
+        up = [(place == 0) | (place == 2), place == 1]
+    else:
+        steps = [([(k - 1, k), (pairs - k, pairs - k - 1)],) for k in range(1, pairs)]
+        up = [place == k - 1 for k in range(1, pairs)]
+
+    def halves(got, copy):
+        spans = ((0, states), (states, 2 * states), (2 * states + copy, 2 * states + copy + 1))
+        for low, high in spans:
+            own, other = kept[low:high], got[low:high]
+            yield jnp.where(second, other, own), jnp.where(second, own, other)
+
+    message = sent if token is None else after(sent, *token)
+    got = lax.ppermute(message, "seq", swap)
+    token = yield message, got
+    arrived = []
+    for k, routes in enumerate(steps):
+        if arrived:
+            arrived[-1] = after(arrived[-1], token)
+        else:
+            got = after(got, token)
+        (l1, l2), (k1, k2), (d1, d2) = halves(got, min(k, 3))
+        message = jnp.where(up[k], d2 * l1 + l2, k1 + d1 * k2)
+        if arrived:
+            message = message + d1 * d2 * arrived[-1][:states]
+        if len(steps) == 2 and k == 0:
+            message = jnp.concatenate([message, jnp.broadcast_to(d1 * d2, (8, message.shape[1]))])
+        arrived += [lax.ppermute(message, "seq", both(route)) for route in routes]
+        token = yield message, arrived[-1]
+    arrived[-1] = after(arrived[-1], token)
+
+    def leaving(copy):
+        (l1, _), (_, k2), (d1, d2) = halves(got, copy)
+        zero = jnp.zeros_like(l1)
+        if pairs == 4:
+            near, middle, far = [a[:states] for a in arrived]
+            outer = arrived[0][states + copy : states + copy + 1] * far + near
+            starts, ends = [zero, near, middle, outer], [outer, middle, near, zero]
+        else:
+            starts, ends = [zero] + arrived, arrived[::-1] + [zero]
+        start, end = starts[0], ends[0]
+        for k in range(1, pairs):
+            start = jnp.where(place == k, starts[k], start)
+            end = jnp.where(place == k, ends[k], end)
+        return start, d1 * start + l1, k2 + d2 * end, end
+
+    first_start, second_start, first_end, second_end = leaving(4)
+    message = jnp.concatenate(
+        [
+            jnp.where(second, first_start, second_start),
+            jnp.where(second, first_end, second_end),
+        ]
+    )
     other = lax.ppermute(message, "seq", swap)
     yield message, other
+    first_start, second_start, first_end, second_end = leaving(5)
+    mine = jnp.concatenate(
+        [
+            jnp.where(second, second_start, first_start),
+            jnp.where(second, second_end, first_end),
+        ]
+    )
     yield mine, other
 
 
@@ -661,46 +849,47 @@
         sent += out
     kept, saved = local(y, 0, PARTS, saved)
 
-    transfers = size // 2 + 1
+    transfers = 4 if size == 8 else size // 2 + 1
     order = [(0, 0), (1, 0)] + [
         pick for k in range(1, transfers) for pick in ((0, k), (1, k - 1)) if pick != (1, 0)
     ]
     order.append((1, transfers - 1))
     flows, token = {}, None
     inner, piece = None, 0
+    last = PARTS - 1
+    windows = [(0, 2), (1, 2)] if transfers == 4 else []
 
     def inner_piece(token):
         bias = vectors[1] if token is None else after(vectors[1], token)
         moved = (vectors[0], bias, *vectors[2:])
-        return inner_grads(piece, scale, saved, dy, b, c, moved, inner)
+        return inner_grads(piece * PARTS + last, scale, saved, dy, b, c, moved, inner)
 
     for part, k in order:
         if k == 0:
             flows[part] = entering(sent[part], kept[part], states, token)
             message, arrived = next(flows[part])
-            token = arrived if part == 0 else message
+            token = None if part == 0 else message
         else:
             token = flows[part].send(token)[0]
-        if (part, k) == (0, 1) or (part == 1 and 0 < k < transfers - 1):
-            if piece < 2 * PARTS:
-                inner = inner_piece(token)
-                token = inner[-1]
-                piece += 1
-    while piece < 2 * PARTS:
+        if (part, k) in windows:
+            inner = inner_piece(token)
+            token = inner[-1]
+            piece += 1
+    while piece < 2:
         inner = inner_piece(token)
         token = inner[-1]
         piece += 1
     here = jnp.reshape(y, (1,)).astype(jnp.int32)
-    dx, dc, db, draw, params = inner
-    held = []
     for part in range(PARTS):
         mine, other = next(flows[part])
         other = after(other, token)
-        held += [mine, other]
-        dx, draw, params = entering_grads(
-            part, scale, here, saved, b, c, vectors, mine, other, dx, draw, params
-        )
-    dc, db = maps_grads(after(here, params), saved, dc, db, held)
+        if part < last:
+            inner = local_grads(part, scale, here, saved, dy, b, c, vectors, mine, other, inner)
+    dx, dc, db, draw, params = inner
+    dx, draw, params = entering_grads(
+        last, scale, here, saved, b, c, vectors, mine, other, dx, draw, params
+    )
+    dc, db = maps_grads(last, after(here, params), saved, dc, db, mine, other)
     summed = summed_over(summed_over(params, "batch"), "seq")
     return (
         dx[None],

time: 119 us -> 104 us (0.87)
  Pallas kernels: 68.2 us -> 50.9 us
  waiting for transfers between devices: 3.89 us -> 14.5 us
  starting transfers between devices: 32.3 us -> 26.6 us
  other arithmetic: 9.07 us -> 6.19 us
    pallas_call x4 -> x2, Pallas kernels: 32.5 us -> 14.1 us  [inner_grads(): pl.pallas_call(functools.partial(inner_kernel, first, scale, piece), grid...]
    ppermute x18 -> x15, waiting for transfers between devices: 1.85 us -> 14.5 us  [the longest x6 8.55 us: entering(): arrived += [lax.ppermute(message, 'seq', both(route)) for route in routes]]
    pallas_call x0 -> x1, Pallas kernels: none -> 11.5 us  [local_grads(): pl.pallas_call(functools.partial(grads_kernel, first, scale, part, half),...]
    ppermute x18 -> x15, starting transfers between devices: 30.1 us -> 23.4 us  [the longest x6 12.1 us: entering(): arrived += [lax.ppermute(message, 'seq', both(route)) for route in routes]]
    pallas_call x2 -> x1, Pallas kernels: 13 us -> 7.22 us  [entering_grads(): pl.pallas_call(functools.partial(entering_kernel, scale, part, half), gri...]
    pallas_call x3, Pallas kernels: 17.9 us -> 15.3 us  [local_states(): pl.pallas_call(functools.partial(local_kernel, first, last, count), grid_...]
    ppermute x2, waiting for transfers between devices: 2.04 us -> 0.01 us  [entering(): other = lax.ppermute(message, 'seq', swap)]
    select_n x8 -> x5, other arithmetic: 5.67 us -> 3.73 us  [the longest x1 1.34 us: entering(): jnp.where(second, second_end, first_end)]
  transfers between devices with their start and end apart: 20 -> 17, of which waited for: 3 -> 10; matrix products, arithmetic and copies ran while one was open for 8% -> 5% of each run, Pallas kernels for 48% -> 38%
where the time goes in v5:
time: 104 us; the launch traced here: 103 us
  Pallas kernels  50.9 us (49%)
  starting transfers between devices  26.6 us (26%)
  waiting for transfers between devices  14.5 us (14%)
  other arithmetic  6.19 us (6%)
  local copies, waits for them, and re-layouts  4.07 us (4%)
  between operations  1.12 us (1%)
    pallas_call x3, Pallas kernels, local_states(): pl.pallas_call(functools.partial(local_kernel, first, last, count), grid_...  15.3 us
    pallas_call x2, Pallas kernels, inner_grads(): pl.pallas_call(functools.partial(inner_kernel, first, scale, piece), grid...  14.1 us
    ppermute x6, starting transfers between devices, entering(): arrived += [lax.ppermute(message, 'seq', both(route)) for route in routes]  12.1 us
    pallas_call x1, Pallas kernels, local_grads(): pl.pallas_call(functools.partial(grads_kernel, first, scale, part, half),...  11.5 us
    ppermute x6, waiting for transfers between devices, entering(): arrived += [lax.ppermute(message, 'seq', both(route)) for route in routes]  8.55 us
    pallas_call x1, Pallas kernels, entering_grads(): pl.pallas_call(functools.partial(entering_kernel, scale, part, half), gri...  7.22 us
    ppermute x7, starting transfers between devices, summed_over(): lax.ppermute(value, axis, [(i, i ^ s) for i in range(size)])  6.88 us
    ppermute x2, starting transfers between devices, entering(): got = lax.ppermute(message, 'seq', swap)  4.46 us
  transfers between devices with their start and end apart: 17, of which 10 were waited for; matrix products, arithmetic and copies ran while one was open for 5% of the time, Pallas kernels for 38%

profile of v5, /device:TPU:0, one launch (start us, length us, event | category | flops | bytes accessed | tf_op | source)
XLA Modules:
  0.0 103.4 jit_solution(17993412825987489000)
XLA Ops:
  0.6 4.6 %local_states.3 = (f32[264,512]{1,0:T(8,128)}, bf16[1024,2048]{1,0:T(8,128)(2,1)}, bf16[1024,2048]{1,0:T(8,128)(2,1)}, f32[8,2048]{1,0:T(8,128)}, bf16[1024,128]{1,0:T(8,128)(2,1)}, /*index=5*/f32[16,2048]{1,0:T(8,128)}) custom-call(s32[1]{0:T(128)} %bitcast.6.refs_0_, bf16[1024,2048]{1,0:T(8,128)(2,1)} %bitcast.76, bf16[1024,2048]{1,0:T(8,128)(2,1)} %bitcast.70, ...), custom_call_target="tpu_custom_call" | custom-call | flops 536870912 | bytes 4194304 | tf_op jit(solution)/shard_map/local_states/pallas_call | solution.py:246
  5.2 3.0 %collective-permute-start.1 = (f32[264,512]{1,0:T(8,128)}, f32[264,512]{1,0:T(8,128)S(1)}, u32[]{:S(2)}, u32[]{:S(2)}) collective-permute-start(f32[264,512]{1,0:T(8,128)} %get-tuple-element.73), channel_id=1, source_target_pairs={{0,4},{4,0},{8,12},{12,8},{16,20},{20,16},{24,28},{28,24},{1,5},{5... | collective-permute-start | bytes 1622024 | tf_op jit(solution)/shard_map/ppermute | solution.py:772
  8.2 3.9 %local_states.4 = (f32[264,512]{1,0:T(8,128)}, bf16[1024,2048]{1,0:T(8,128)(2,1)}, bf16[1024,2048]{1,0:T(8,128)(2,1)}, f32[8,2048]{1,0:T(8,128)}) custom-call(s32[1]{0:T(128)} %bitcast.10.refs_0_, bf16[1024,2048]{1,0:T(8,128)(2,1)} %bitcast.77, bf16[1024,2048]{1,0:T(8,128)(2,1)} %bitcast.71, ...), custom_call_target="tpu_custom_call", output_to_operand_aliasing={{1}: (7, {}), {2}: (8, {}), {3}: (9, {})} | custom-call | flops 536870912 | bytes 4194304 | tf_op jit(solution)/shard_map/local_states/pallas_call | solution.py:246
  12.1 6.8 %local_states.5 = (f32[264,512]{1,0:T(8,128)}, f32[264,512]{1,0:T(8,128)}, bf16[1024,2048]{1,0:T(8,128)(2,1)}, bf16[1024,2048]{1,0:T(8,128)(2,1)}, f32[8,2048]{1...) custom-call(s32[1]{0:T(128)} %bitcast.1.refs_0_, ...), custom_call_target="tpu_custom_call", output_to_operand_aliasing={{2}: (7, {}), {3}: (8, {}), {4}: (9, {})} | custom-call | flops 1073741824 | bytes 8388608 | tf_op jit(solution)/shard_map/local_states/pallas_call | solution.py:246
  18.9 1.8 %collective-permute-done.1 = f32[264,512]{1,0:T(8,128)S(1)} collective-permute-done((f32[264,512]{1,0:T(8,128)}, f32[264,512]{1,0:T(8,128)S(1)}, u32[]{:S(2)}, u32[]{:S(2)}) %collective-permute-start.1) | collective-permute-done | bytes 540704 | tf_op jit(solution)/shard_map/ppermute | solution.py:772
  20.7 0.9 broadcast_select_fusion.1
  21.6 1.2 %add_select_fusion.9 = (f32[128,512]{1,0:T(8,128)S(1)}, f32[128,512]{1,0:T(8,128)S(1)}, f32[128,512]{1,0:T(8,128)S(1)}) fusion(f32[512]{0:T(512)S(1)} %bitcast.90, f32[512]{0:T(512)S(1)} %bitcast.89, pred[]{:T(512)S(6)} %or.4, f32[264,512]{1,0:T(8,128)S(1)} %collective-permute-done.1, f32[264,512]{1,0:T(8,128)} %get-tuple-element.72, pred[]{:T(512)S(6)} %eq.14), kind=kLoop, calls=%fused_computation.23 | loop fusion | flops 589824 | bytes 1839106 | tf_op jit(solution)/shard_map/jit(_where)/select_n | solution.py:781
  22.8 1.9 %collective-permute-start.2 = (f32[136,512]{1,0:T(8,128)S(1)}, f32[136,512]{1,0:T(8,128)S(1)}, u32[]{:S(2)}, u32[]{:S(2)}) collective-permute-start(f32[136,512]{1,0:T(8,128)S(1)} %pad_maximum_fusion.4), channel_id=1, source_target_pairs={{0,8},{4,12},{8,0},{12,4},{16,24},{20,28},{24,16},{28,20},{1,9},{5... | collective-permute-start | bytes 835592 | tf_op jit(solution)/shard_map/ppermute | solution.py:786
  24.6 1.5 %collective-permute-start = (f32[264,512]{1,0:T(8,128)}, f32[264,512]{1,0:T(8,128)S(1)}, u32[]{:S(2)}, u32[]{:S(2)}) collective-permute-start(f32[264,512]{1,0:T(8,128)} %get-tuple-element.66), channel_id=1, source_target_pairs={{0,4},{4,0},{8,12},{12,8},{16,20},{20,16},{24,28},{28,24},{1,5},{5... | collective-permute-start | bytes 1622024 | tf_op jit(solution)/shard_map/ppermute | solution.py:772
  26.2 4.5 %collective-permute-done.2 = f32[136,512]{1,0:T(8,128)S(1)} collective-permute-done((f32[136,512]{1,0:T(8,128)S(1)}, f32[136,512]{1,0:T(8,128)S(1)}, u32[]{:S(2)}, u32[]{:S(2)}) %collective-permute-start.2) | collective-permute-done | bytes 278560 | tf_op jit(solution)/shard_map/ppermute | solution.py:786
  30.7 2.0 %multiply_add_fusion.5 = f32[128,512]{1,0:T(8,128)} fusion(f32[128,512]{1,0:T(8,128)S(1)} %get-tuple-element.120, f32[128,512]{1,0:T(8,128)S(1)} %get-tuple-element.119, f32[136,512]{1,0:T(8,128)S(1)} %collective-permute-done.2, f32[512]{0:T(512)S(1)} %bitcast.84, f32[512]{0:T(512)S(1)} %bitcast.86, f32[512]{0:T(512)S(1)} %bitcast.85, pred[]{:T(512)S(6)} %eq.15, ...), kind=kLoop, calls=%fused_computation.22 | loop fusion | flops 589824 | bytes 2103298 | tf_op jit(solution)/shard_map/add | solution.py:783
  32.7 1.4 %collective-permute-start.5 = (f32[128,512]{1,0:T(8,128)}, f32[128,512]{1,0:T(8,128)}, u32[]{:S(2)}, u32[]{:S(2)}) collective-permute-start(f32[128,512]{1,0:T(8,128)} %multiply_add_fusion.5), channel_id=1, source_target_pairs={{8,16},{12,20},{16,8},{20,12},{9,17},{13,21},{17,9},{21,13},{10,18... | collective-permute-start | bytes 786440 | tf_op jit(solution)/shard_map/ppermute | solution.py:786
  34.1 1.3 %collective-permute-start.4 = (f32[128,512]{1,0:T(8,128)}, f32[128,512]{1,0:T(8,128)}, u32[]{:S(2)}, u32[]{:S(2)}) collective-permute-start(f32[128,512]{1,0:T(8,128)} %multiply_add_fusion.5), channel_id=1, source_target_pairs={{8,24},{12,28},{16,0},{20,4},{9,25},{13,29},{17,1},{21,5},{10,26},... | collective-permute-start | bytes 786440 | tf_op jit(solution)/shard_map/ppermute | solution.py:786
  35.4 0.0 copy-start.10
  35.5 7.7 %inner_grads.2 = (bf16[1024,2048]{1,0:T(8,128)(2,1)}, f32[1024,128]{1,0:T(8,128)}, f32[1024,128]{1,0:T(8,128)}, f32[4,8,1024]{2,1,0:T(8,128)}, f32[8,128]{1,0:T(8,128)}) custom-call(bf16[1024,2048]{1,0:T(8,128)(2,1)} %get-tuple-element.64.refs_0_.refs_1_.xs_ref, bf16[1024,2048]{1,0:T(8,128)(2,1)} %get-tuple-element.65.refs_1_.refs_2_.ys_ref, ...), custom_call_target="tpu_custom_call" | custom-call | flops 4831838208 | bytes 5242880 | tf_op jit(solution)/shard_map/inner_grads/pallas_call | solution.py:561
  43.3 0.1 add_select_fusion.8
  43.4 5.4 %collective-permute-start.3 = (f32[136,512]{1,0:T(8,128)S(1)}, f32[136,512]{1,0:T(8,128)S(1)}, u32[]{:S(2)}, u32[]{:S(2)}) collective-permute-start(f32[136,512]{1,0:T(8,128)S(1)} %pad_maximum_fusion.5), channel_id=1, source_target_pairs={{0,8},{4,12},{8,0},{12,4},{16,24},{20,28},{24,16},{28,20},{1,9},{5... | collective-permute-start | bytes 835592 | tf_op jit(solution)/shard_map/ppermute | solution.py:786
  48.9 0.8 fusion.4
  49.7 1.3 %add_select_fusion = (f32[128,512]{1,0:T(8,128)S(1)}, f32[128,512]{1,0:T(8,128)S(1)}, f32[128,512]{1,0:T(8,128)S(1)}, f32[128,512]{1,0:T(8,128)S(1)}) fusion(f32[128,512]{1,0:T(8,128)S(1)} %get-tuple-element.120, f32[128,512]{1,0:T(8,128)} %collective-permute-done.5, f32[128,512]{1,0:T(8,128)} %collective-permute-done.4, f32[136,512]{1,0:T(8,128)} %copy-done.21, ...), kind=kLoop, calls=%fused_computation.6 | loop fusion | flops 1703936 | bytes 2371588 | tf_op jit(solution)/shard_map/jit(_where)/select_n | solution.py:818
  51.1 1.6 %collective-permute-start.9 = (f32[256,512]{1,0:T(8,128)S(1)}, f32[256,512]{1,0:T(8,128)S(1)}, u32[]{:S(2)}, u32[]{:S(2)}) collective-permute-start(f32[256,512]{1,0:T(8,128)S(1)} %pad_maximum_fusion), channel_id=1, source_target_pairs={{0,4},{4,0},{8,12},{12,8},{16,20},{20,16},{24,28},{28,24},{1,5},{5... | collective-permute-start | bytes 1572872 | tf_op jit(solution)/shard_map/ppermute | solution.py:812
  52.7 0.9 collective-permute-done.3
  53.6 0.2 multiply_add_fusion.3
  53.8 0.7 collective-permute-start.7
  54.5 1.5 %collective-permute-start.6 = (f32[128,512]{1,0:T(8,128)S(1)}, f32[128,512]{1,0:T(8,128)S(1)}, u32[]{:S(2)}, u32[]{:S(2)}) collective-permute-start(f32[128,512]{1,0:T(8,128)S(1)} %multiply_add_fusion.3), channel_id=1, source_target_pairs={{8,24},{12,28},{16,0},{20,4},{9,25},{13,29},{17,1},{21,5},{10,26},... | collective-permute-start | bytes 786440 | tf_op jit(solution)/shard_map/ppermute | solution.py:786
  56.1 1.0 copy-done.14
  57.2 1.0 %copy-done.15 = f32[1024,128]{1,0:T(8,128)S(1)} copy-done((f32[1024,128]{1,0:T(8,128)S(1)}, f32[1024,128]{1,0:T(8,128)}, u32[]{:S(2)}) %copy-start.15) | copy-done | bytes 524312
  58.2 6.4 %inner_grads.3 = (bf16[1024,2048]{1,0:T(8,128)(2,1)}, f32[1024,128]{1,0:T(8,128)S(1)}, f32[1024,128]{1,0:T(8,128)S(1)}, f32[4,8,1024]{2,1,0:T(8,128)}, f32[8,128]{1,0:T(8,128)S(1)}) custom-call(bf16[1024,2048]{1,0:T(8,128)(2,1)S(1)} %copy-done, bf16[1024,2048]{1,0:T(8,128)(2,1)S(1)} %copy-done.1, ...), custom_call_target="tpu_custom_call", output_to_operand_aliasing={{0}: (19, {}), {3}: (20, {})} | custom-call | flops 4831838208 | bytes 5242880 | tf_op jit(solution)/shard_map/inner_grads/pallas_call | solution.py:561
  64.6 3.1 %collective-permute-done.6 = f32[128,512]{1,0:T(8,128)S(1)} collective-permute-done((f32[128,512]{1,0:T(8,128)S(1)}, f32[128,512]{1,0:T(8,128)S(1)}, u32[]{:S(2)}, u32[]{:S(2)}) %collective-permute-start.6) | collective-permute-done | bytes 262176 | tf_op jit(solution)/shard_map/ppermute | solution.py:786
  67.8 0.2 add_select_fusion.2
  68.1 1.6 %collective-permute-start.8 = (f32[256,512]{1,0:T(8,128)S(1)}, f32[256,512]{1,0:T(8,128)S(1)}, u32[]{:S(2)}, u32[]{:S(2)}) collective-permute-start(f32[256,512]{1,0:T(8,128)S(1)} %pad_maximum_fusion.2), channel_id=1, source_target_pairs={{0,4},{4,0},{8,12},{12,8},{16,20},{20,16},{24,28},{28,24},{1,5},{5... | collective-permute-start | bytes 1572872 | tf_op jit(solution)/shard_map/ppermute | solution.py:812
  69.7 0.0 copy-start.16
  69.7 11.5 %local_grads.1 = (bf16[1024,2048]{1,0:T(8,128)(2,1)}, f32[1024,128]{1,0:T(8,128)S(1)}, f32[1024,128]{1,0:T(8,128)S(1)}, f32[4,8,1024]{2,1,0:T(8,128)}, f32[8,128]{1,0:T(8,128)S(1)}) custom-call(s32[1]{0:T(128)} %bitcast.refs_0_.y_ref, bf16[1024,2048]{1,0:T(8,128)(2,1)S(1)} %copy-done, ...), custom_call_target="tpu_custom_call", output_to_operand_aliasing={{0}: (22, {}), {3}: (23, {})} | custom-call | flops 4831838208 | bytes 6291456 | tf_op jit(solution)/shard_map/local_grads/pallas_call | solution.py:408
  81.2 7.2 %entering_grads.1 = (bf16[1024,2048]{1,0:T(8,128)(2,1)}, f32[4,8,1024]{2,1,0:T(8,128)}, f32[8,128]{1,0:T(8,128)S(1)}) custom-call(s32[1]{0:T(128)} %bitcast.refs_0_.y_ref, bf16[1024,2048]{1,0:T(8,128)(2,1)S(1)} %copy-done, bf16[1024,2048]{1,0:T(8,128)(2,1)S(1)} %copy-done.2, ...), custom_call_target="tpu_custom_call", output_to_operand_aliasing={{0}: (13, {}), {1}: (14, {})} | custom-call | flops 3221225472 | bytes 8388608 | tf_op jit(solution)/shard_map/entering_grads/pallas_call | solution.py:664
  88.4 1.5 %collective-permute-start.11 = (f32[8,128]{1,0:T(8,128)S(1)}, f32[8,128]{1,0:T(8,128)S(1)}, u32[]{:S(2)}, u32[]{:S(2)}) collective-permute-start(f32[8,128]{1,0:T(8,128)S(1)} %get-tuple-element.99), channel_id=1, source_target_pairs={{0,2},{1,3},{2,0},{3,1},{4,6},{5,7},{6,4},{7,5},{8,10},{9,11},{10,... | collective-permute-start | bytes 12296 | tf_op jit(solution)/shard_map/ppermute | solution.py:739
  90.0 0.3 collective-permute-start.10
  90.3 1.2 %collective-permute-done.12 = f32[8,128]{1,0:T(8,128)S(1)} collective-permute-done((f32[8,128]{1,0:T(8,128)S(1)}, f32[8,128]{1,0:T(8,128)S(1)}, u32[]{:S(2)}, u32[]{:S(2)}) %collective-permute-start.12) | collective-permute-done | bytes 4128 | tf_op jit(solution)/shard_map/ppermute | solution.py:739
  91.5 0.6 collective-permute-done.11
  92.1 1.5 %collective-permute-start.15 = (f32[8,128]{1,0:T(8,128)S(1)}, f32[8,128]{1,0:T(8,128)S(1)}, u32[]{:S(2)}, u32[]{:S(2)}) collective-permute-start(f32[8,128]{1,0:T(8,128)S(1)} %add_add_fusion.1), channel_id=1, source_target_pairs={{0,12},{4,8},{8,4},{12,0},{16,28},{20,24},{24,20},{28,16},{1,13},{... | collective-permute-start | bytes 12296 | tf_op jit(solution)/shard_map/ppermute | solution.py:739
  93.6 0.6 collective-permute-start.14
  94.2 1.5 %collective-permute-start.13 = (f32[8,128]{1,0:T(8,128)S(1)}, f32[8,128]{1,0:T(8,128)S(1)}, u32[]{:S(2)}, u32[]{:S(2)}) collective-permute-start(f32[8,128]{1,0:T(8,128)S(1)} %add_add_fusion.1), channel_id=1, source_target_pairs={{0,4},{4,0},{8,12},{12,8},{16,20},{20,16},{24,28},{28,24},{1,5},{5... | collective-permute-start | bytes 12296 | tf_op jit(solution)/shard_map/ppermute | solution.py:739
  95.7 1.0 collective-permute-done.15
  96.7 0.5 collective-permute-done.14
  97.2 0.6 collective-permute-done.13
  97.8 1.4 %collective-permute-start.16 = (f32[8,128]{1,0:T(8,128)S(1)}, f32[8,128]{1,0:T(8,128)S(1)}, u32[]{:S(2)}, u32[]{:S(2)}) collective-permute-start(f32[8,128]{1,0:T(8,128)S(1)} %add_add_fusion), channel_id=1, source_target_pairs={{0,16},{4,20},{8,24},{12,28},{16,0},{20,4},{24,8},{28,12},{1,17},{... | collective-permute-start | bytes 12296 | tf_op jit(solution)/shard_map/ppermute | solution.py:739
  99.3 2.8 %maps_grads.1 = (f32[1024,128]{1,0:T(8,128)}, f32[1024,128]{1,0:T(8,128)}) custom-call(s32[1]{0:T(128)} %bitcast.refs_0_.y_ref, bf16[1024,2048]{1,0:T(8,128)(2,1)S(1)} %copy-done, bf16[1024,2048]{1,0:T(8,128)(2,1)S(1)} %copy-done.2, f32[16,2048]{1,0:T(8,128)S(1)} %copy-done.6, f32[1024,128]{1,0:T(8,128)S(1)} %get-tuple-element.101.dc_in, ...), custom_call_target="tpu_custom_call" | custom-call | flops 1073741824 | bytes 4194304 | tf_op jit(solution)/shard_map/maps_grads/pallas_call | solution.py:712
  102.1 0.3 collective-permute-done.16
  102.3 0.5 slice_bitcast_fusion
  102.8 0.6 slice.154
  (61 shorter events, 0.3 us)
Async XLA Ops:
  5.2 15.4 %collective-permute-start.1 = (f32[264,512]{1,0:T(8,128)}, f32[264,512]{1,0:T(8,128)S(1)}, u32[]{:S(2)}, u32[]{:S(2)}) collective-permute-start(f32[264,512]{1,0:T(8,128)} %get-tuple-element.73), channel_id=1, source_target_pairs={{0,4},{4,0},{8,12},{12,8},{16,20},{20,16},{24,28},{28,24},{1,5},{5... | collective-permute-start | bytes 1622024 | tf_op jit(solution)/shard_map/ppermute | solution.py:772
  22.8 7.9 %collective-permute-start.2 = (f32[136,512]{1,0:T(8,128)S(1)}, f32[136,512]{1,0:T(8,128)S(1)}, u32[]{:S(2)}, u32[]{:S(2)}) collective-permute-start(f32[136,512]{1,0:T(8,128)S(1)} %pad_maximum_fusion.4), channel_id=1, source_target_pairs={{0,8},{4,12},{8,0},{12,4},{16,24},{20,28},{24,16},{28,20},{1,9},{5... | collective-permute-start | bytes 835592 | tf_op jit(solution)/shard_map/ppermute | solution.py:786
  24.6 18.5 %collective-permute-start = (f32[264,512]{1,0:T(8,128)}, f32[264,512]{1,0:T(8,128)S(1)}, u32[]{:S(2)}, u32[]{:S(2)}) collective-permute-start(f32[264,512]{1,0:T(8,128)} %get-tuple-element.66), channel_id=1, source_target_pairs={{0,4},{4,0},{8,12},{12,8},{16,20},{20,16},{24,28},{28,24},{1,5},{5... | collective-permute-start | bytes 1622024 | tf_op jit(solution)/shard_map/ppermute | solution.py:772
  30.7 4.7 %copy-start.21 = (f32[136,512]{1,0:T(8,128)}, f32[136,512]{1,0:T(8,128)S(1)}, u32[]{:S(2)}) copy-start(f32[136,512]{1,0:T(8,128)S(1)} %collective-permute-done.2) | copy-start | bytes 835588
  32.7 17.0 %collective-permute-start.5 = (f32[128,512]{1,0:T(8,128)}, f32[128,512]{1,0:T(8,128)}, u32[]{:S(2)}, u32[]{:S(2)}) collective-permute-start(f32[128,512]{1,0:T(8,128)} %multiply_add_fusion.5), channel_id=1, source_target_pairs={{8,16},{12,20},{16,8},{20,12},{9,17},{13,21},{17,9},{21,13},{10,18... | collective-permute-start | bytes 786440 | tf_op jit(solution)/shard_map/ppermute | solution.py:786
  34.1 15.6 %collective-permute-start.4 = (f32[128,512]{1,0:T(8,128)}, f32[128,512]{1,0:T(8,128)}, u32[]{:S(2)}, u32[]{:S(2)}) collective-permute-start(f32[128,512]{1,0:T(8,128)} %multiply_add_fusion.5), channel_id=1, source_target_pairs={{8,24},{12,28},{16,0},{20,4},{9,25},{13,29},{17,1},{21,5},{10,26},... | collective-permute-start | bytes 786440 | tf_op jit(solution)/shard_map/ppermute | solution.py:786
  35.4 7.8 %copy-start.20 = (f32[264,512]{1,0:T(8,128)S(1)}, f32[264,512]{1,0:T(8,128)}, u32[]{:S(2)}) copy-start(f32[264,512]{1,0:T(8,128)} %get-tuple-element.79) | copy-start | bytes 1622020
  35.4 20.6 %copy-start.5 = (bf16[1024,128]{1,0:T(8,128)(2,1)S(1)}, bf16[1024,128]{1,0:T(8,128)(2,1)}, u32[]{:S(2)}) copy-start(bf16[1024,128]{1,0:T(8,128)(2,1)} %get-tuple-element.56.refs_5_.refs_11_.refs_7_.refs_6_) | copy-start | bytes 786436
  35.4 20.6 %copy-start.7 = (bf16[4,256,256]{2,1,0:T(8,128)(2,1)S(1)}, bf16[4,256,256]{2,1,0:T(8,128)(2,1)}, u32[]{:S(2)}) copy-start(bf16[4,256,256]{2,1,0:T(8,128)(2,1)} %get-tuple-element.70.refs_8_.refs_16_) | copy-start | bytes 1572868
  35.4 20.6 %copy-start.8 = (bf16[4,256,256]{2,1,0:T(8,128)(2,1)S(1)}, bf16[4,256,256]{2,1,0:T(8,128)(2,1)}, u32[]{:S(2)}) copy-start(bf16[4,256,256]{2,1,0:T(8,128)(2,1)} %get-tuple-element.71.refs_9_.refs_17_) | copy-start | bytes 1572868
  35.4 20.6 %copy-start.9 = (f32[1,32,1024]{2,1,0:T(8,128)S(1)}, f32[1,32,1024]{2,1,0:T(8,128)}, u32[]{:S(2)}) copy-start(f32[1,32,1024]{2,1,0:T(8,128)} %refs_5_.2) | copy-start | bytes 393220
  35.4 20.6 %copy-start.10 = (bf16[1536,128]{1,0:T(8,128)(2,1)S(1)}, bf16[1536,128]{1,0:T(8,128)(2,1)}, u32[]{:S(2)}) copy-start(bf16[1536,128]{1,0:T(8,128)(2,1)} %constant.46.clone.refs_10_.refs_18_) | copy-start | bytes 1179652
  35.4 20.6 %copy-start.11 = (bf16[128,1024]{1,0:T(8,128)(2,1)S(1)}, bf16[128,1024]{1,0:T(8,128)(2,1)}, u32[]{:S(2)}) copy-start(bf16[128,1024]{1,0:T(8,128)(2,1)} %get-tuple-element.68.refs_6_.refs_14_) | copy-start | bytes 786436
  35.5 20.6 %copy-start.12 = (bf16[128,1024]{1,0:T(8,128)(2,1)S(1)}, bf16[128,1024]{1,0:T(8,128)(2,1)}, u32[]{:S(2)}) copy-start(bf16[128,1024]{1,0:T(8,128)(2,1)} %get-tuple-element.69.refs_7_.refs_15_) | copy-start | bytes 786436
  35.5 20.6 %copy-start.13 = (f32[8,2048]{1,0:T(8,128)S(1)}, f32[8,2048]{1,0:T(8,128)}, u32[]{:S(2)}) copy-start(f32[8,2048]{1,0:T(8,128)} %get-tuple-element.67.refs_3_.refs_4_) | copy-start | bytes 196612
  43.2 12.9 %copy-start = (bf16[1024,2048]{1,0:T(8,128)(2,1)S(1)}, bf16[1024,2048]{1,0:T(8,128)(2,1)}, u32[]{:S(2)}) copy-start(bf16[1024,2048]{1,0:T(8,128)(2,1)} %get-tuple-element.64.refs_0_.refs_1_.xs_ref) | copy-start | bytes 12582916
  43.2 12.9 %copy-start.1 = (bf16[1024,2048]{1,0:T(8,128)(2,1)S(1)}, bf16[1024,2048]{1,0:T(8,128)(2,1)}, u32[]{:S(2)}) copy-start(bf16[1024,2048]{1,0:T(8,128)(2,1)} %get-tuple-element.65.refs_1_.refs_2_.ys_ref) | copy-start | bytes 12582916
  43.2 12.9 %copy-start.3 = (bf16[1,1024,128]{2,1,0:T(8,128)(2,1)S(1)}, bf16[1,1024,128]{2,1,0:T(8,128)(2,1)}, u32[]{:S(2)}) copy-start(bf16[1,1024,128]{2,1,0:T(8,128)(2,1)} %param.13) | copy-start | bytes 786436
  43.2 12.9 %copy-start.4 = (bf16[1,1024,128]{2,1,0:T(8,128)(2,1)S(1)}, bf16[1,1024,128]{2,1,0:T(8,128)(2,1)}, u32[]{:S(2)}) copy-start(bf16[1,1024,128]{2,1,0:T(8,128)(2,1)} %param.14) | copy-start | bytes 786436
  43.2 12.9 %copy-start.6 = (f32[16,2048]{1,0:T(8,128)S(1)}, f32[16,2048]{1,0:T(8,128)}, u32[]{:S(2)}) copy-start(f32[16,2048]{1,0:T(8,128)} %get-tuple-element.57.refs_6_.refs_12_.refs_8_.refs_7_.table_ref) | copy-start | bytes 393220
  43.2 12.9 %copy-start.17 = (f32[32]{0:T(128)S(1)}, f32[32]{0:T(128)}, u32[]{:S(2)}) copy-start(f32[32]{0:T(128)} %param.16) | copy-start | bytes 388
  43.2 12.9 %copy-start.18 = (f32[32]{0:T(128)S(1)}, f32[32]{0:T(128)}, u32[]{:S(2)}) copy-start(f32[32]{0:T(128)} %param.17) | copy-start | bytes 388
  43.3 12.9 %copy-start.19 = (f32[8,128]{1,0:T(8,128)S(1)}, f32[8,128]{1,0:T(8,128)}, u32[]{:S(2)}) copy-start(f32[8,128]{1,0:T(8,128)} %get-tuple-element.77.refs_18_) | copy-start | bytes 12292
  43.4 10.2 %collective-permute-start.3 = (f32[136,512]{1,0:T(8,128)S(1)}, f32[136,512]{1,0:T(8,128)S(1)}, u32[]{:S(2)}, u32[]{:S(2)}) collective-permute-start(f32[136,512]{1,0:T(8,128)S(1)} %pad_maximum_fusion.5), channel_id=1, source_target_pairs={{0,8},{4,12},{8,0},{12,4},{16,24},{20,28},{24,16},{28,20},{1,9},{5... | collective-permute-start | bytes 835592 | tf_op jit(solution)/shard_map/ppermute | solution.py:786
  51.1 18.6 %collective-permute-start.9 = (f32[256,512]{1,0:T(8,128)S(1)}, f32[256,512]{1,0:T(8,128)S(1)}, u32[]{:S(2)}, u32[]{:S(2)}) collective-permute-start(f32[256,512]{1,0:T(8,128)S(1)} %pad_maximum_fusion), channel_id=1, source_target_pairs={{0,4},{4,0},{8,12},{12,8},{16,20},{20,16},{24,28},{28,24},{1,5},{5... | collective-permute-start | bytes 1572872 | tf_op jit(solution)/shard_map/ppermute | solution.py:812
  53.8 14.0 %collective-permute-start.7 = (f32[128,512]{1,0:T(8,128)S(1)}, f32[128,512]{1,0:T(8,128)S(1)}, u32[]{:S(2)}, u32[]{:S(2)}) collective-permute-start(f32[128,512]{1,0:T(8,128)S(1)} %multiply_add_fusion.3), channel_id=1, source_target_pairs={{8,16},{12,20},{16,8},{20,12},{9,17},{13,21},{17,9},{21,13},{10,18... | collective-permute-start | bytes 786440 | tf_op jit(solution)/shard_map/ppermute | solution.py:786
  54.5 13.3 %collective-permute-start.6 = (f32[128,512]{1,0:T(8,128)S(1)}, f32[128,512]{1,0:T(8,128)S(1)}, u32[]{:S(2)}, u32[]{:S(2)}) collective-permute-start(f32[128,512]{1,0:T(8,128)S(1)} %multiply_add_fusion.3), channel_id=1, source_target_pairs={{8,24},{12,28},{16,0},{20,4},{9,25},{13,29},{17,1},{21,5},{10,26},... | collective-permute-start | bytes 786440 | tf_op jit(solution)/shard_map/ppermute | solution.py:786
  56.1 1.0 %copy-start.14 = (f32[1024,128]{1,0:T(8,128)S(1)}, f32[1024,128]{1,0:T(8,128)}, u32[]{:S(2)}) copy-start(f32[1024,128]{1,0:T(8,128)} %get-tuple-element.83.refs_16_) | copy-start | bytes 1572868
  57.2 1.0 %copy-start.15 = (f32[1024,128]{1,0:T(8,128)S(1)}, f32[1024,128]{1,0:T(8,128)}, u32[]{:S(2)}) copy-start(f32[1024,128]{1,0:T(8,128)} %get-tuple-element.84.refs_17_) | copy-start | bytes 1572868
  68.1 13.2 %collective-permute-start.8 = (f32[256,512]{1,0:T(8,128)S(1)}, f32[256,512]{1,0:T(8,128)S(1)}, u32[]{:S(2)}, u32[]{:S(2)}) collective-permute-start(f32[256,512]{1,0:T(8,128)S(1)} %pad_maximum_fusion.2), channel_id=1, source_target_pairs={{0,4},{4,0},{8,12},{12,8},{16,20},{20,16},{24,28},{28,24},{1,5},{5... | collective-permute-start | bytes 1572872 | tf_op jit(solution)/shard_map/ppermute | solution.py:812
  69.7 11.5 %copy-start.2 = (bf16[1024,2048]{1,0:T(8,128)(2,1)S(1)}, bf16[1024,2048]{1,0:T(8,128)(2,1)}, u32[]{:S(2)}) copy-start(bf16[1024,2048]{1,0:T(8,128)(2,1)} %get-tuple-element.65.refs_1_.refs_2_.ys_ref) | copy-start | bytes 12582916
  69.7 11.5 %copy-start.16 = (bf16[1024,128]{1,0:T(8,128)(2,1)S(1)}, bf16[1024,128]{1,0:T(8,128)(2,1)}, u32[]{:S(2)}) copy-start(bf16[1024,128]{1,0:T(8,128)(2,1)} %constant.47.clone.refs_5_) | copy-start | bytes 786436
  88.4 3.0 %collective-permute-start.12 = (f32[8,128]{1,0:T(8,128)S(1)}, f32[8,128]{1,0:T(8,128)S(1)}, u32[]{:S(2)}, u32[]{:S(2)}) collective-permute-start(f32[8,128]{1,0:T(8,128)S(1)} %get-tuple-element.99), channel_id=1, source_target_pairs={{0,3},{1,2},{2,1},{3,0},{4,7},{5,6},{6,5},{7,4},{8,11},{9,10},{10,... | collective-permute-start | bytes 12296 | tf_op jit(solution)/shard_map/ppermute | solution.py:739
  88.4 3.7 %collective-permute-start.11 = (f32[8,128]{1,0:T(8,128)S(1)}, f32[8,128]{1,0:T(8,128)S(1)}, u32[]{:S(2)}, u32[]{:S(2)}) collective-permute-start(f32[8,128]{1,0:T(8,128)S(1)} %get-tuple-element.99), channel_id=1, source_target_pairs={{0,2},{1,3},{2,0},{3,1},{4,6},{5,7},{6,4},{7,5},{8,10},{9,11},{10,... | collective-permute-start | bytes 12296 | tf_op jit(solution)/shard_map/ppermute | solution.py:739
  90.0 2.1 %collective-permute-start.10 = (f32[8,128]{1,0:T(8,128)S(1)}, f32[8,128]{1,0:T(8,128)S(1)}, u32[]{:S(2)}, u32[]{:S(2)}) collective-permute-start(f32[8,128]{1,0:T(8,128)S(1)} %get-tuple-element.99), channel_id=1, source_target_pairs={{0,1},{1,0},{2,3},{3,2},{4,5},{5,4},{6,7},{7,6},{8,9},{9,8},{10,11... | collective-permute-start | bytes 12296 | tf_op jit(solution)/shard_map/ppermute | solution.py:739
  92.1 4.6 %collective-permute-start.15 = (f32[8,128]{1,0:T(8,128)S(1)}, f32[8,128]{1,0:T(8,128)S(1)}, u32[]{:S(2)}, u32[]{:S(2)}) collective-permute-start(f32[8,128]{1,0:T(8,128)S(1)} %add_add_fusion.1), channel_id=1, source_target_pairs={{0,12},{4,8},{8,4},{12,0},{16,28},{20,24},{24,20},{28,16},{1,13},{... | collective-permute-start | bytes 12296 | tf_op jit(solution)/shard_map/ppermute | solution.py:739
  93.6 3.6 %collective-permute-start.14 = (f32[8,128]{1,0:T(8,128)S(1)}, f32[8,128]{1,0:T(8,128)S(1)}, u32[]{:S(2)}, u32[]{:S(2)}) collective-permute-start(f32[8,128]{1,0:T(8,128)S(1)} %add_add_fusion.1), channel_id=1, source_target_pairs={{0,8},{4,12},{8,0},{12,4},{16,24},{20,28},{24,16},{28,20},{1,9},{5... | collective-permute-start | bytes 12296 | tf_op jit(solution)/shard_map/ppermute | solution.py:739
  94.2 3.6 %collective-permute-start.13 = (f32[8,128]{1,0:T(8,128)S(1)}, f32[8,128]{1,0:T(8,128)S(1)}, u32[]{:S(2)}, u32[]{:S(2)}) collective-permute-start(f32[8,128]{1,0:T(8,128)S(1)} %add_add_fusion.1), channel_id=1, source_target_pairs={{0,4},{4,0},{8,12},{12,8},{16,20},{20,16},{24,28},{28,24},{1,5},{5... | collective-permute-start | bytes 12296 | tf_op jit(solution)/shard_map/ppermute | solution.py:739
  97.8 4.5 %collective-permute-start.16 = (f32[8,128]{1,0:T(8,128)S(1)}, f32[8,128]{1,0:T(8,128)S(1)}, u32[]{:S(2)}, u32[]{:S(2)}) collective-permute-start(f32[8,128]{1,0:T(8,128)S(1)} %add_add_fusion), channel_id=1, source_target_pairs={{0,16},{4,20},{8,24},{12,28},{16,0},{20,4},{24,8},{28,12},{1,17},{... | collective-permute-start | bytes 12296 | tf_op jit(solution)/shard_map/ppermute | solution.py:739

commit v6 on v4

--- a/solution.py
+++ b/solution.py
@@ -3,6 +3,7 @@
 
 import jax
 import jax.numpy as jnp
+import numpy as np
 from jax import lax
 from jax.experimental import pallas as pl
 from jax.experimental.pallas import tpu as pltpu
@@ -11,6 +12,7 @@
 GROUP = 256
 PARTS = 2
 VMEM_LIMIT = 60 * 1024 * 1024
+SMALL_LIMIT = 40 * 1024 * 1024
 F32 = jnp.float32
 BF16 = jnp.bfloat16
 
@@ -114,7 +116,7 @@
     return hit.astype(BF16)
 
 
-def local_kernel(first, *refs):
+def local_kernel(first, last, count, *refs):
     at_ref, x_ref, dy_ref, b_ref, c_ref = refs[:5]
     if first:
         raw_ref, bias_ref, rate_ref, skip_ref = refs[5:9]
@@ -122,8 +124,12 @@
         xs_ref, ys_ref, direct_ref, columns_ref, table_ref, bt, ct = refs[-7:]
     else:
         columns_ref, table_ref = refs[5:7]
-        outs = refs[10:-5]
-        xs_ref, ys_ref, direct_ref, bt, ct = refs[-5:]
+        outs = refs[10 : 10 + count]
+        xs_ref, ys_ref, direct_ref = refs[10 + count : 13 + count]
+        if last:
+            left, right, bt, ct = refs[13 + count :]
+        else:
+            bt, ct = refs[13 + count :]
     g = pl.program_id(0)
     length, width = x_ref.shape
     states = b_ref.shape[1]
@@ -145,6 +151,13 @@
                 columns_ref,
                 table_ref,
             )
+        if last:
+            for n in range(blocks):
+                rows = slice(n * GROUP, (n + 1) * GROUP)
+                scores = dot(c_ref[rows, :], b_ref[rows, :], NT)
+                left[n] = jnp.where(triangle(GROUP, True), scores, 0.0).astype(BF16)
+                scores = dot(b_ref[rows, :], c_ref[rows, :], NT)
+                right[n] = jnp.where(triangle(GROUP, False), scores, 0.0).astype(BF16)
 
     gain = dot(columns_ref[...], picker(piece, heads, all_heads, width, True), NN)
     lift = dot(columns_ref[...], picker(piece, heads, all_heads, width, False), NN)
@@ -176,7 +189,7 @@
             out_ref[2 * states :] = decay
 
 
-def local_states(at, count, x, dy, b, c, vectors, before):
+def local_states(at, count, last, x, dy, b, c, vectors, before):
     length, channels = x.shape
     states = b.shape[1]
     pieces = 2 * PARTS
@@ -215,18 +228,23 @@
         in_specs += [pl.BlockSpec(factor_columns.shape, whole), pl.BlockSpec(table.shape, whole)]
         in_specs += [anywhere] * 3
         aliases = {7: count, 8: count + 1, 9: count + 2}
+    scratch = [pltpu.VMEM((states, length), BF16)] * 2
+    if last:
+        blocks = length // GROUP
+        extra = [jax.ShapeDtypeStruct((blocks, GROUP, GROUP), BF16)] * 2
+        extra += [jax.ShapeDtypeStruct((states, length), BF16)] * 2
+        out_shape += extra
+        out_specs += [pl.BlockSpec(e.shape, lambda g, at, n=len(e.shape): (0,) * n) for e in extra]
+        scratch = []
     grid_spec = pltpu.PrefetchScalarGridSpec(
         num_scalar_prefetch=1,
         grid=(count,),
         in_specs=in_specs,
         out_specs=out_specs,
-        scratch_shapes=[
-            pltpu.VMEM((states, length), BF16),
-            pltpu.VMEM((states, length), BF16),
-        ],
+        scratch_shapes=scratch,
     )
     out = pl.pallas_call(
-        functools.partial(local_kernel, first),
+        functools.partial(local_kernel, first, last, count),
         grid_spec=grid_spec,
         out_shape=out_shape,
         input_output_aliases=aliases,
@@ -241,21 +259,25 @@
     return out[:count], list(out[count:])
 
 
-def grads_kernel(first, scale, part, half, *refs):
+def grads_kernel(first, scale, part, half, begin, *refs):
     y_ref, xs_ref, ys_ref, dy_ref, direct_ref, b_ref, c_ref, columns_ref, table_ref = refs[:9]
-    raw_ref, bias_ref, rate_ref, mine_ref, other_ref = refs[9:14]
-    refs = refs[14:]
+    raw_ref, bias_ref, rate_ref, bt, ct, left, right, adder = refs[9:17]
+    held = refs[17:21]
+    refs = refs[21:]
     if not first:
         dc_in, db_in, par_in = refs[:3]
         refs = refs[5:]
     dx_ref, dc_ref, db_ref, draw_ref, par_ref = refs[:5]
-    left, right, sums, dc_sum, db_sum, bt, ct, adder, terms = refs[5:]
+    sums, dc_sum, db_sum, terms = refs[5:9]
+    if not first:
+        dc_old, db_old, sems = refs[9:]
+        old = [(dc_in, dc_old, sems.at[0]), (db_in, db_old, sems.at[1])]
     g = pl.program_id(0)
     heads = raw_ref.shape[1]
     length, width = xs_ref.shape
     states = b_ref.shape[1]
     blocks = length // GROUP
-    piece = g * half + part
+    piece = (begin + g) * half + part
     all_heads = columns_ref.shape[1] // 4
     member = head_matrix(heads, width).astype(BF16)
     lower = triangle(GROUP, True)
@@ -263,30 +285,20 @@
 
     @pl.when(g == 0)
     def _():
-        bt[...] = b_ref[...].T
-        ct[...] = c_ref[...].T
-        upper = triangle(GROUP, False)
-        for n in range(blocks):
-            b, c = b_ref[rows[n], :], c_ref[rows[n], :]
-            left[n] = jnp.where(lower, dot(c, b, NT), 0.0).astype(BF16)
-            right[n] = jnp.where(upper, dot(b, c, NT), 0.0).astype(BF16)
+        if not first:
+            for source, target, sem in old:
+                pltpu.make_async_copy(source, target, sem).start()
         sums[...] = jnp.zeros_like(sums)
         dc_sum[...] = jnp.zeros_like(dc_sum)
         db_sum[...] = jnp.zeros_like(db_sum)
         par_ref[...] = jnp.zeros_like(par_ref) if first else par_in[...]
-        row = lax.broadcasted_iota(jnp.int32, (width, 128), 0)
-        col = lax.broadcasted_iota(jnp.int32, (width, 128), 1)
-        size = width // heads
-        one = ((row >= col * size) & (row < (col + 1) * size)).astype(BF16)
-        col = col - heads
-        two = ((row >= col * size) & (row < (col + 1) * size)).astype(BF16)
-        adder[:width] = one
-        adder[width : 2 * width] = one
-        adder[2 * width :] = two
-
-    own = g == y_ref[0]
-    state = jnp.where(own, mine_ref[:states], other_ref[:states])
-    grad = jnp.where(own, mine_ref[states:], other_ref[states:])
+
+    own = begin + g == y_ref[0]
+    early = jnp.where(own, held[0][...], held[2][...])
+    late = jnp.where(own, held[1][...], held[3][...])
+    state_early = y_ref[1] == 1
+    state = jnp.where(state_early, early, late)
+    grad = jnp.where(state_early, late, early)
     table = table_ref[...]
     skip = table[3 * blocks + 1 : 3 * blocks + 2]
     entering_low, ends = [], []
@@ -338,28 +350,27 @@
         jnp.sum(head_sums(direct_ref[...], member), axis=1, keepdims=True),
         -jnp.sum(step * slope, axis=1, keepdims=True),
     )
-    shape = (heads, par_ref.shape[1])
-    spot = lax.broadcasted_iota(jnp.int32, shape, 1) == (
-        lax.broadcasted_iota(jnp.int32, shape, 0) + piece * heads
-    )
     for k, value in enumerate(values):
-        par_ref[k : k + 1] += jnp.sum(jnp.where(spot, value * scale, 0.0), axis=0, keepdims=True)
+        par_ref[k : k + 1] += lanes_of(value * scale, piece, (heads, par_ref.shape[1]))
 
     @pl.when(g == pl.num_programs(0) - 1)
     def _():
+        if not first:
+            for source, target, sem in old:
+                pltpu.make_async_copy(source, target, sem).wait()
         for n in range(blocks):
             pair = jnp.where(lower, sums[n], 0.0).astype(BF16)
             dc = dot(pair, b_ref[rows[n], :], NN) + dc_sum[n]
             db = dot(pair, c_ref[rows[n], :], TN) + db_sum[n]
             if not first:
-                dc = dc + dc_in[rows[n], :]
-                db = db + db_in[rows[n], :]
+                dc = dc + dc_old[rows[n], :]
+                db = db + db_old[rows[n], :]
             dc_ref[rows[n], :] = dc
             db_ref[rows[n], :] = db
 
 
-def local_grads(part, scale, y, saved, dy, b, c, vectors, mine, other, before):
-    xs, ys, direct, factor_columns, table = saved
+def local_grads(part, begin, count, scale, y, saved, dy, b, c, vectors, held, before):
+    xs, ys, direct, factor_columns, table, left, right, bt, ct = saved
     raw, bias, rate, _ = vectors
     length, channels = xs.shape
     pieces = 2 * PARTS
@@ -371,12 +382,11 @@
     half = pieces // 2
     first = before is None
     whole = lambda g, y: (0, 0)
-    place = lambda g, y: (0, g * half + part)
+    place = lambda g, y: (0, (begin + g) * half + part)
     columns = pl.BlockSpec((length, width), place)
     maps = pl.BlockSpec((length, states), whole)
     line = pl.BlockSpec(bias.shape, whole)
-    lines = pl.BlockSpec((1, heads, length), lambda g, y: (g * half + part, 0, 0))
-    held = pl.BlockSpec((2 * states, width), whole)
+    lines = pl.BlockSpec((1, heads, length), lambda g, y: ((begin + g) * half + part, 0, 0))
     params = pl.BlockSpec((8, 128), whole)
     anywhere = pl.BlockSpec(memory_space=pl.ANY)
     in_specs = [columns, columns, columns, pl.BlockSpec((8, width), place), maps, maps]
@@ -384,33 +394,37 @@
         pl.BlockSpec(factor_columns.shape, whole),
         pl.BlockSpec((table.shape[0], width), place),
     ]
-    in_specs += [lines, line, line, held, held]
-    args = [xs, ys, dy, direct, b, c, factor_columns, table, raw, bias, rate, mine, other]
+    in_specs += [lines, line, line]
+    args = [xs, ys, dy, direct, b, c, factor_columns, table, raw, bias, rate]
+    fixed = [bt, ct, left, right, adding(width, heads, (0, 0, 1)), *held]
+    in_specs += [pl.BlockSpec(a.shape, lambda g, y, n=len(a.shape): (0,) * n) for a in fixed]
+    args += fixed
     aliases = {}
     if not first:
         dx, dc, db, draw, par = before
         args += [dc, db, par, dx, draw]
-        in_specs += [maps, maps, params, anywhere, anywhere]
-        aliases = {17: 0, 18: 3}
+        in_specs += [anywhere, anywhere, params, anywhere, anywhere]
+        aliases = {24: 0, 25: 3}
     grid_spec = pltpu.PrefetchScalarGridSpec(
         num_scalar_prefetch=1,
-        grid=(2,),
+        grid=(count,),
         in_specs=in_specs,
         out_specs=[columns, maps, maps, lines, params],
         scratch_shapes=[
-            pltpu.VMEM((blocks, GROUP, GROUP), BF16),
-            pltpu.VMEM((blocks, GROUP, GROUP), BF16),
             pltpu.VMEM((blocks, GROUP, GROUP), F32),
             pltpu.VMEM((blocks, GROUP, states), F32),
             pltpu.VMEM((blocks, GROUP, states), F32),
-            pltpu.VMEM((states, length), BF16),
-            pltpu.VMEM((states, length), BF16),
-            pltpu.VMEM((3 * width, 128), BF16),
             pltpu.VMEM((length, 3 * width), BF16),
-        ],
+        ]
+        + [
+            pltpu.VMEM((length, states), F32),
+            pltpu.VMEM((length, states), F32),
+            pltpu.SemaphoreType.DMA((2,)),
+        ]
+        * (not first),
     )
     return pl.pallas_call(
-        functools.partial(grads_kernel, first, scale, part, half),
+        functools.partial(grads_kernel, first, scale, part, half, begin),
         grid_spec=grid_spec,
         out_shape=[
             jax.ShapeDtypeStruct((length, channels), BF16),
@@ -420,14 +434,29 @@
             jax.ShapeDtypeStruct((8, 128), F32),
         ],
         input_output_aliases=aliases,
-        compiler_params=pltpu.CompilerParams(vmem_limit_bytes=40 * 1024 * 1024),
+        compiler_params=pltpu.CompilerParams(vmem_limit_bytes=SMALL_LIMIT),
         cost_estimate=pl.CostEstimate(
-            flops=24 * length * width * (GROUP + states),
-            bytes_accessed=12 * length * width,
+            flops=12 * count * length * width * (GROUP + states),
+            bytes_accessed=6 * count * length * width,
             transcendentals=0,
         ),
         name="local_grads",
     )(y, *args)
+
+
+def adding(width, heads, places):
+    out = np.zeros((len(places) * width, 128), np.float32)
+    size = width // heads
+    for k, place in enumerate(places):
+        for channel in range(width):
+            out[k * width + channel, place * heads + channel // size] = 1.0
+    return jnp.asarray(out, BF16)
+
+
+def lanes_of(values, piece, shape):
+    row = lax.broadcasted_iota(jnp.int32, shape, 0)
+    col = lax.broadcasted_iota(jnp.int32, shape, 1)
+    return jnp.sum(jnp.where(col == row + piece * shape[0], values, 0.0), axis=0, keepdims=True)
 
 
 def summed_over(value, axis):
@@ -456,12 +485,6 @@
     place, second = index // 2, index % 2 == 1
     swap = [(i, i ^ 1) for i in range(size)]
     both = lambda moves: [(2 * a + y, 2 * b + y) for a, b in moves for y in range(2)]
-    if pairs == 4:
-        steps = [([(0, 1), (1, 0), (2, 3), (3, 2)],), ([(1, 2), (2, 1)], [(1, 3), (2, 0)])]
-        up = [(place == 0) | (place == 2), place == 1]
-    else:
-        steps = [([(k - 1, k), (pairs - k, pairs - k - 1)],) for k in range(1, pairs)]
-        up = [place == k - 1 for k in range(1, pairs)]
 
     def halves(got, copy):
         spans = ((0, states), (states, 2 * states), (2 * states + copy, 2 * states + copy + 1))
@@ -469,57 +492,60 @@
             own, other = kept[low:high], got[low:high]
             yield jnp.where(second, other, own), jnp.where(second, own, other)
 
+    def message_of(up, got, arrived, copy):
+        (l1, l2), (k1, k2), (d1, d2) = halves(got, copy)
+        message = jnp.where(up, d2 * l1 + l2, k1 + d1 * k2)
+        return message if arrived is None else message + d1 * d2 * arrived[:states]
+
+    def shares(is_state, value, got, copy):
+        (l1, _), (_, k2), (d1, d2) = halves(got, copy)
+        for_first = jnp.where(is_state, value, k2 + d2 * value)
+        for_second = jnp.where(is_state, d1 * value + l1, value)
+        return jnp.where(second, for_second, for_first), jnp.where(second, for_first, for_second)
+
     message = sent if token is None else after(sent, *token)
     got = lax.ppermute(message, "seq", swap)
     token = yield message, got
-    arrived = []
-    for k, routes in enumerate(steps):
-        if arrived:
+    got = after(got, token)
+    lower = place < pairs // 2
+    if pairs == 4:
+        message = message_of((place == 0) | (place == 2), got, None, 0)
+        (_, _), (_, _), (d1, d2) = halves(got, 0)
+        message = jnp.concatenate([message, jnp.broadcast_to(d1 * d2, (8, message.shape[1]))])
+        near = lax.ppermute(message, "seq", both([(0, 1), (1, 0), (2, 3), (3, 2)]))
+        token = yield message, near
+        near = after(near, token)
+        message = message_of(place == 1, got, near, 1)
+        middle = lax.ppermute(message, "seq", both([(1, 2), (2, 1)]))
+        far = lax.ppermute(message, "seq", both([(1, 3), (2, 0)]))
+        inside = (place == 1) | (place == 2)
+        known = jnp.where(inside, near[:states], 0.0)
+        mine_early, early = shares(lower, known, got, 2)
+        other_early = lax.ppermute(early, "seq", swap)
+        token = yield early, far
+        far = after(far, token)
+        outer = near[states : states + 1] * far + near[:states]
+        mine_late, late = shares(~lower, jnp.where(inside, middle, outer), got, 3)
+        other_late = lax.ppermute(late, "seq", swap)
+        yield late, other_late
+    else:
+        arrived = []
+        for k in range(1, pairs):
+            message = message_of(place == k - 1, got, arrived[-1] if arrived else None, min(k, 4))
+            routes = both([(k - 1, k), (pairs - k, pairs - k - 1)])
+            arrived.append(lax.ppermute(message, "seq", routes))
+            token = yield message, arrived[-1]
             arrived[-1] = after(arrived[-1], token)
-        else:
-            got = after(got, token)
-        (l1, l2), (k1, k2), (d1, d2) = halves(got, min(k, 3))
-        message = jnp.where(up[k], d2 * l1 + l2, k1 + d1 * k2)
-        if arrived:
-            message = message + d1 * d2 * arrived[-1][:states]
-        if len(steps) == 2 and k == 0:
-            message = jnp.concatenate([message, jnp.broadcast_to(d1 * d2, (8, message.shape[1]))])
-        arrived += [lax.ppermute(message, "seq", both(route)) for route in routes]
-        token = yield message, arrived[-1]
-    arrived[-1] = after(arrived[-1], token)
-
-    def leaving(copy):
-        (l1, _), (_, k2), (d1, d2) = halves(got, copy)
-        zero = jnp.zeros_like(l1)
-        if pairs == 4:
-            near, middle, far = [a[:states] for a in arrived]
-            outer = arrived[0][states + copy : states + copy + 1] * far + near
-            starts, ends = [zero, near, middle, outer], [outer, middle, near, zero]
-        else:
-            starts, ends = [zero] + arrived, arrived[::-1] + [zero]
-        start, end = starts[0], ends[0]
+        start = end = jnp.zeros_like(arrived[0])
         for k in range(1, pairs):
-            start = jnp.where(place == k, starts[k], start)
-            end = jnp.where(place == k, ends[k], end)
-        return start, d1 * start + l1, k2 + d2 * end, end
-
-    first_start, second_start, first_end, second_end = leaving(4)
-    message = jnp.concatenate(
-        [
-            jnp.where(second, first_start, second_start),
-            jnp.where(second, first_end, second_end),
-        ]
-    )
-    other = lax.ppermute(message, "seq", swap)
-    yield message, other
-    first_start, second_start, first_end, second_end = leaving(5)
-    mine = jnp.concatenate(
-        [
-            jnp.where(second, second_start, first_start),
-            jnp.where(second, second_end, first_end),
-        ]
-    )
-    yield mine, other
+            start = jnp.where(place == k, arrived[k - 1], start)
+            end = jnp.where(place == pairs - 1 - k, arrived[k - 1], end)
+        mine_early, early = shares(lower, jnp.where(lower, start, end), got, 5)
+        mine_late, late = shares(~lower, jnp.where(lower, end, start), got, 6)
+        other_early = lax.ppermute(early, "seq", swap)
+        other_late = lax.ppermute(late, "seq", swap)
+        yield late, other_late
+    yield mine_early, mine_late, other_early, other_late
 
 
 def shards(inputs, input_map, output_map, step_raw, step_bias, decay_rate, skip_gain, cotangent):
@@ -539,8 +565,9 @@
 
     def local(half, part, count, before):
         at = jnp.reshape(half * PARTS + part, (1,)).astype(jnp.int32)
-        out, saved = local_states(at, count, x, dy, b, c, vectors, before)
-        return out, saved + list(before[3:] if before else [])
+        last = count == PARTS
+        out, saved = local_states(at, count, last, x, dy, b, c, vectors, before)
+        return out, saved[:3] + list(before[3:] if before else []) + saved[3:]
 
     sent, kept = [], []
     saved = None
@@ -555,20 +582,31 @@
     ]
     order.append((1, transfers - 1))
     flows, token = {}, None
+    lower = lax.axis_index("seq") < size // 2
+    here = jnp.stack([y, lower.astype(y.dtype)]).astype(jnp.int32)
+    found = None
+
+    def grads(part, begin, count, token, held):
+        *most, final = held
+        held = (*most, after(final, token))
+        return local_grads(
+            part, begin, count, scale, here, saved, dy, b, c, vectors, held, found
+        )
+
     for part, k in order:
+        if (part, k) == (1, transfers - 1):
+            held = next(flows[0])
+            found = grads(0, 0, 1, token, held)
+            token = found[-1]
         if k == 0:
             flows[part] = entering(sent[part], kept[part], states, token)
             message, arrived = next(flows[part])
             token = None if part == 0 else message
         else:
             token = flows[part].send(token)[0]
-    here = jnp.reshape(y, (1,)).astype(jnp.int32)
-    before = None
-    for part in range(PARTS):
-        mine, other = next(flows[part])
-        other = after(other, token)
-        before = local_grads(part, scale, here, saved, dy, b, c, vectors, mine, other, before)
-    dx, dc, db, draw, params = before
+    found = grads(0, 1, 1, token, held)
+    found = grads(1, 0, 2, found[-1], next(flows[1]))
+    dx, dc, db, draw, params = found
     summed = summed_over(summed_over(params, "batch"), "seq")
     return (
         dx[None],

time: 104 us -> 101 us (0.971)
  waiting for transfers between devices: 37.7 us -> 20.7 us
  starting transfers between devices: 21.4 us -> 30.3 us
  Pallas kernels: 38.4 us -> 42.8 us
    ppermute x8 -> x10, waiting for transfers between devices: 24.4 us -> 9.17 us  [the longest x2 7.77 us: entering(): near = lax.ppermute(message, 'seq', both([(0, 1), (1, 0), (2, 3), (3, 2)]))]
    ppermute x7, starting transfers between devices: 6.62 us -> 12.8 us  [summed_over(): lax.ppermute(value, axis, [(i, i ^ s) for i in range(size)])]
    pallas_call x5 -> x6, Pallas kernels: 38.4 us -> 42.8 us  [the longest x3 27.6 us: local_grads(): pl.pallas_call(functools.partial(grads_kernel, first, scale, part, half,...]
    ppermute x8 -> x10, starting transfers between devices: 10.3 us -> 13 us  [the longest x2 4.07 us: entering(): near = lax.ppermute(message, 'seq', both([(0, 1), (1, 0), (2, 3), (3, 2)]))]
    mul x1 -> x2, other arithmetic: 0.02 us -> 1.5 us  [message_of(): return message if arrived is None else message + d1 * d2 * arrived[:states]]
    add x2 -> x0, other arithmetic: 1.45 us -> none  [entering(): message = message + d1 * d2 * arrived[-1][:states]]
    ppermute x7, waiting for transfers between devices: 7.28 us -> 5.92 us  [summed_over(): lax.ppermute(value, axis, [(i, i ^ s) for i in range(size)])]
    select_n x5 -> x8, other arithmetic: 2.62 us -> 3.37 us  [the longest x3 1.6 us: shares(): jnp.where(second, for_second, for_first)]
  transfers between devices with their start and end apart: 17 -> 19, of which waited for: 11 -> 11; matrix products, arithmetic and copies ran while one was open for 2% -> 2% of each run, Pallas kernels for 21% -> 26%
where the time goes in v6:
time: 101 us
  Pallas kernels  42.8 us (42%)
  starting transfers between devices  30.3 us (30%)
  waiting for transfers between devices  20.7 us (20%)
  other arithmetic  5.01 us (5%)
  local copies, waits for them, and re-layouts  1.19 us (1%)
  between operations  1.06 us (1%)
    pallas_call x3, Pallas kernels, local_grads(): pl.pallas_call(functools.partial(grads_kernel, first, scale, part, half,...  27.6 us
    pallas_call x3, Pallas kernels, local_states(): pl.pallas_call(functools.partial(local_kernel, first, last, count), grid_...  15.2 us
    ppermute x7, starting transfers between devices, summed_over(): lax.ppermute(value, axis, [(i, i ^ s) for i in range(size)])  12.8 us
    ppermute x2, waiting for transfers between devices, entering(): near = lax.ppermute(message, 'seq', both([(0, 1), (1, 0), (2, 3), (3, 2)]))  7.77 us
    ppermute x7, waiting for transfers between devices, summed_over(): lax.ppermute(value, axis, [(i, i ^ s) for i in range(size)])  5.92 us
    ppermute x2, waiting for transfers between devices, entering(): got = lax.ppermute(message, 'seq', swap)  5.63 us
    ppermute x2, starting transfers between devices, entering(): got = lax.ppermute(message, 'seq', swap)  4.48 us
    ppermute x2, starting transfers between devices, entering(): near = lax.ppermute(message, 'seq', both([(0, 1), (1, 0), (2, 3), (3, 2)]))  4.07 us
  transfers between devices with their start and end apart: 19, of which 11 were waited for; matrix products, arithmetic and copies ran while one was open for 2% of the time, Pallas kernels for 26%

profile of v6, /device:TPU:0, one launch (start us, length us, event | category | flops | bytes accessed | tf_op | source)
XLA Modules:
  0.0 101.1 jit_solution(11073788852439690777)
XLA Ops:
  0.6 4.6 %local_states.3 = (f32[264,512]{1,0:T(8,128)}, bf16[1024,2048]{1,0:T(8,128)(2,1)}, bf16[1024,2048]{1,0:T(8,128)(2,1)}, f32[8,2048]{1,0:T(8,128)}, bf16[1024,128]{1,0:T(8,128)(2,1)}, /*index=5*/f32[16,2048]{1,0:T(8,128)}) custom-call(s32[1]{0:T(128)} %bitcast.7.refs_0_, bf16[1024,2048]{1,0:T(8,128)(2,1)} %bitcast.70, bf16[1024,2048]{1,0:T(8,128)(2,1)} %bitcast.64, ...), custom_call_target="tpu_custom_call" | custom-call | flops 536870912 | bytes 4194304 | tf_op jit(solution)/shard_map/local_states/pallas_call | solution.py:246
  5.2 3.0 %collective-permute-start.1 = (f32[264,512]{1,0:T(8,128)}, f32[264,512]{1,0:T(8,128)S(1)}, u32[]{:S(2)}, u32[]{:S(2)}) collective-permute-start(f32[264,512]{1,0:T(8,128)} %get-tuple-element.66), channel_id=1, source_target_pairs={{0,4},{4,0},{8,12},{12,8},{16,20},{20,16},{24,28},{28,24},{1,5},{5... | collective-permute-start | bytes 1622024 | tf_op jit(solution)/shard_map/ppermute | solution.py:507
  8.2 3.8 %local_states.4 = (f32[264,512]{1,0:T(8,128)}, bf16[1024,2048]{1,0:T(8,128)(2,1)}, bf16[1024,2048]{1,0:T(8,128)(2,1)}, f32[8,2048]{1,0:T(8,128)}) custom-call(s32[1]{0:T(128)} %bitcast.11.refs_0_, bf16[1024,2048]{1,0:T(8,128)(2,1)} %bitcast.71, bf16[1024,2048]{1,0:T(8,128)(2,1)} %bitcast.65, ...), custom_call_target="tpu_custom_call", output_to_operand_aliasing={{1}: (7, {}), {2}: (8, {}), {3}: (9, {})} | custom-call | flops 536870912 | bytes 4194304 | tf_op jit(solution)/shard_map/local_states/pallas_call | solution.py:246
  12.0 6.8 %local_states.5 = (f32[264,512]{1,0:T(8,128)}, f32[264,512]{1,0:T(8,128)}, bf16[1024,2048]{1,0:T(8,128)(2,1)}, bf16[1024,2048]{1,0:T(8,128)(2,1)}, f32[8,2048]{1...) custom-call(s32[1]{0:T(128)} %bitcast.2.refs_0_, ...), custom_call_target="tpu_custom_call", output_to_operand_aliasing={{2}: (7, {}), {3}: (8, {}), {4}: (9, {})} | custom-call | flops 1073741824 | bytes 8388608 | tf_op jit(solution)/shard_map/local_states/pallas_call | solution.py:246
  18.8 1.9 %collective-permute-done.1 = f32[264,512]{1,0:T(8,128)S(1)} collective-permute-done((f32[264,512]{1,0:T(8,128)}, f32[264,512]{1,0:T(8,128)S(1)}, u32[]{:S(2)}, u32[]{:S(2)}) %collective-permute-start.1) | collective-permute-done | bytes 540704 | tf_op jit(solution)/shard_map/ppermute | solution.py:507
  20.7 1.5 %fusion.1 = (f32[1,512]{1,0:T(1,128)}, f32[1,512]{1,0:T(1,128)}, f32[1,512]{1,0:T(1,128)}, f32[1,512]{1,0:T(1,128)}, f32[1,512]{1,0:T(1,128)}, /*index=5*/f32[1,...) fusion(f32[264,512]{1,0:T(8,128)S(1)} %collective-permute-done.1, ...), kind=kLoop, calls=%fused_computation.53 | loop fusion | flops 5120 | bytes 36865 | tf_op jit(solution)/shard_map/mul | solution.py:498
  22.2 1.2 %add_select_fusion.11 = (f32[128,512]{1,0:T(8,128)S(1)}, f32[128,512]{1,0:T(8,128)S(1)}, f32[128,512]{1,0:T(8,128)S(1)}) fusion(f32[512]{0:T(512)S(1)} %bitcast.96, f32[512]{0:T(512)S(1)} %bitcast.95, pred[]{:T(512)S(6)} %or.9, f32[264,512]{1,0:T(8,128)S(1)} %collective-permute-done.1, f32[264,512]{1,0:T(8,128)} %get-tuple-element.65, pred[]{:T(512)S(6)} %eq.12), kind=kLoop, calls=%fused_computation.15 | loop fusion | flops 589824 | bytes 1839106 | tf_op jit(solution)/shard_map/jit(_where)/select_n | solution.py:497
  23.4 1.9 %collective-permute-start.2 = (f32[136,512]{1,0:T(8,128)S(1)}, f32[136,512]{1,0:T(8,128)S(1)}, u32[]{:S(2)}, u32[]{:S(2)}) collective-permute-start(f32[136,512]{1,0:T(8,128)S(1)} %pad_maximum_fusion), channel_id=1, source_target_pairs={{0,8},{4,12},{8,0},{12,4},{16,24},{20,28},{24,16},{28,20},{1,9},{5... | collective-permute-start | bytes 835592 | tf_op jit(solution)/shard_map/ppermute | solution.py:515
  25.3 1.5 %collective-permute-start = (f32[264,512]{1,0:T(8,128)}, f32[264,512]{1,0:T(8,128)S(1)}, u32[]{:S(2)}, u32[]{:S(2)}) collective-permute-start(f32[264,512]{1,0:T(8,128)} %get-tuple-element.64), channel_id=1, source_target_pairs={{0,4},{4,0},{8,12},{12,8},{16,20},{20,16},{24,28},{28,24},{1,5},{5... | collective-permute-start | bytes 1622024 | tf_op jit(solution)/shard_map/ppermute | solution.py:507
  26.8 4.5 %collective-permute-done.2 = f32[136,512]{1,0:T(8,128)S(1)} collective-permute-done((f32[136,512]{1,0:T(8,128)S(1)}, f32[136,512]{1,0:T(8,128)S(1)}, u32[]{:S(2)}, u32[]{:S(2)}) %collective-permute-start.2) | collective-permute-done | bytes 278560 | tf_op jit(solution)/shard_map/ppermute | solution.py:515
  31.4 1.4 %broadcast_select_fusion.4 = (f32[128,512]{1,0:T(8,128)S(1)}, f32[128,512]{1,0:T(8,128)S(1)}, f32[128,512]{1,0:T(8,128)S(1)}) fusion(pred[]{:T(512)S(6)} %eq.12, f32[128,512]{1,0:T(8,128)S(1)} %get-tuple-element.110, f32[512]{0:T(512)} %bitcast.91, f32[136,512]{1,0:T(8,128)S(1)} %collective-permute-done.2, pred[]{:T(512)S(6)} %or.8, pred[]{:T(512)S(6)} %lt.19, ...), kind=kLoop, calls=%fused_computation.28 | loop fusion | flops 1179648 | bytes 2631684 | tf_op jit(solution)/shard_map/jit(_where)/select_n | solution.py:504
  32.8 0.0 copy-start.8
  32.8 1.6 %collective-permute-start.5 = (f32[128,512]{1,0:T(8,128)S(1)}, f32[128,512]{1,0:T(8,128)S(1)}, u32[]{:S(2)}, u32[]{:S(2)}) collective-permute-start(f32[128,512]{1,0:T(8,128)S(1)} %get-tuple-element.133), channel_id=1, source_target_pairs={{8,24},{12,28},{16,0},{20,4},{9,25},{13,29},{17,1},{21,5},{10,26},... | collective-permute-start | bytes 786440 | tf_op jit(solution)/shard_map/ppermute | solution.py:520
  34.4 0.8 collective-permute-start.4
  35.2 1.5 %collective-permute-start.8 = (f32[128,512]{1,0:T(8,128)S(1)}, f32[128,512]{1,0:T(8,128)S(1)}, u32[]{:S(2)}, u32[]{:S(2)}) collective-permute-start(f32[128,512]{1,0:T(8,128)S(1)} %get-tuple-element.131), channel_id=1, source_target_pairs={{0,4},{4,0},{8,12},{12,8},{16,20},{20,16},{24,28},{28,24},{1,5},{5... | collective-permute-start | bytes 786440 | tf_op jit(solution)/shard_map/ppermute | solution.py:524
  36.7 3.8 %collective-permute-done = f32[264,512]{1,0:T(8,128)S(1)} collective-permute-done((f32[264,512]{1,0:T(8,128)}, f32[264,512]{1,0:T(8,128)S(1)}, u32[]{:S(2)}, u32[]{:S(2)}) %collective-permute-start) | collective-permute-done | bytes 540704 | tf_op jit(solution)/shard_map/ppermute | solution.py:507
  40.5 0.1 add_select_fusion.8
  40.7 2.2 %collective-permute-start.3 = (f32[136,512]{1,0:T(8,128)S(1)}, f32[136,512]{1,0:T(8,128)S(1)}, u32[]{:S(2)}, u32[]{:S(2)}) collective-permute-start(f32[136,512]{1,0:T(8,128)S(1)} %pad_maximum_fusion.1), channel_id=1, source_target_pairs={{0,8},{4,12},{8,0},{12,4},{16,24},{20,28},{24,16},{28,20},{1,9},{5... | collective-permute-start | bytes 835592 | tf_op jit(solution)/shard_map/ppermute | solution.py:515
  42.9 1.2 %collective-permute-done.5 = f32[128,512]{1,0:T(8,128)S(1)} collective-permute-done((f32[128,512]{1,0:T(8,128)S(1)}, f32[128,512]{1,0:T(8,128)S(1)}, u32[]{:S(2)}, u32[]{:S(2)}) %collective-permute-start.5) | collective-permute-done | bytes 262176 | tf_op jit(solution)/shard_map/ppermute | solution.py:520
  44.1 0.1 broadcast_select_fusion.3
  44.3 0.1 broadcast_select_fusion.6
  44.4 1.0 collective-permute-start.9
  45.4 3.3 %collective-permute-done.3 = f32[136,512]{1,0:T(8,128)S(1)} collective-permute-done((f32[136,512]{1,0:T(8,128)S(1)}, f32[136,512]{1,0:T(8,128)S(1)}, u32[]{:S(2)}, u32[]{:S(2)}) %collective-permute-start.3) | collective-permute-done | bytes 278560 | tf_op jit(solution)/shard_map/ppermute | solution.py:515
  48.6 0.2 broadcast_select_fusion.2
  48.8 1.3 %collective-permute-start.7 = (f32[128,512]{1,0:T(8,128)S(1)}, f32[128,512]{1,0:T(8,128)S(1)}, u32[]{:S(2)}, u32[]{:S(2)}) collective-permute-start(f32[128,512]{1,0:T(8,128)S(1)} %get-tuple-element.132), channel_id=1, source_target_pairs={{8,24},{12,28},{16,0},{20,4},{9,25},{13,29},{17,1},{21,5},{10,26},... | collective-permute-start | bytes 786440 | tf_op jit(solution)/shard_map/ppermute | solution.py:520
  50.1 0.7 collective-permute-start.6
  50.8 0.1 pad_add_fusion.refs_0_
  50.9 1.1 %collective-permute-start.10 = (f32[128,512]{1,0:T(8,128)S(1)}, f32[128,512]{1,0:T(8,128)S(1)}, u32[]{:S(2)}, u32[]{:S(2)}) collective-permute-start(f32[128,512]{1,0:T(8,128)S(1)} %get-tuple-element.128), channel_id=1, source_target_pairs={{0,4},{4,0},{8,12},{12,8},{16,20},{20,16},{24,28},{28,24},{1,5},{5... | collective-permute-start | bytes 786440 | tf_op jit(solution)/shard_map/ppermute | solution.py:524
  52.1 7.1 %local_grads.3 = (bf16[1024,2048]{1,0:T(8,128)(2,1)}, f32[1024,128]{1,0:T(8,128)S(1)}, f32[1024,128]{1,0:T(8,128)S(1)}, f32[4,8,1024]{2,1,0:T(8,128)}, f32[8,128]{1,0:T(8,128)S(1)}) custom-call(s32[2]{0:T(128)S(1)} %pad_add_fusion.refs_0_, bf16[1024,2048]{1,0:T(8,128)(2,1)S(1)} %copy-done, bf16[1024,2048]{1,0:T(8,128)(2,1)S(1)} %copy-done.1, ...), custom_call_target="tpu_custom_call" | custom-call | flops 2415919104 | bytes 3145728 | tf_op jit(solution)/shard_map/local_grads/pallas_call | solution.py:426
  59.2 0.1 collective-permute-done.7
  59.3 0.1 broadcast_select_fusion
  59.5 1.1 %collective-permute-start.11 = (f32[128,512]{1,0:T(8,128)S(1)}, f32[128,512]{1,0:T(8,128)S(1)}, u32[]{:S(2)}, u32[]{:S(2)}) collective-permute-start(f32[128,512]{1,0:T(8,128)S(1)} %get-tuple-element.92), channel_id=1, source_target_pairs={{0,4},{4,0},{8,12},{12,8},{16,20},{20,16},{24,28},{28,24},{1,5},{5... | collective-permute-start | bytes 786440 | tf_op jit(solution)/shard_map/ppermute | solution.py:529
  60.5 8.3 %local_grads.4 = (bf16[1024,2048]{1,0:T(8,128)(2,1)}, f32[1024,128]{1,0:T(8,128)S(1)}, f32[1024,128]{1,0:T(8,128)S(1)}, f32[4,8,1024]{2,1,0:T(8,128)}, f32[8,128]{1,0:T(8,128)S(1)}) custom-call(s32[2]{0:T(128)S(1)} %pad_add_fusion.refs_0_, bf16[1024,2048]{1,0:T(8,128)(2,1)S(1)} %copy-done, ...), custom_call_target="tpu_custom_call", output_to_operand_aliasing={{0}: (24, {}), {3}: (25, {})} | custom-call | flops 2415919104 | bytes 3145728 | tf_op jit(solution)/shard_map/local_grads/pallas_call | solution.py:426
  68.8 0.1 broadcast_select_fusion.1.refs_18_
  68.9 12.3 %local_grads.5 = (bf16[1024,2048]{1,0:T(8,128)(2,1)}, f32[1024,128]{1,0:T(8,128)}, f32[1024,128]{1,0:T(8,128)}, f32[4,8,1024]{2,1,0:T(8,128)}, f32[8,128]{1,0:T(8,128)S(1)}) custom-call(s32[2]{0:T(128)S(1)} %pad_add_fusion.refs_0_, bf16[1024,2048]{1,0:T(8,128)(2,1)S(1)} %copy-done, ...), custom_call_target="tpu_custom_call", output_to_operand_aliasing={{0}: (24, {}), {3}: (25, {})} | custom-call | flops 4831838208 | bytes 6291456 | tf_op jit(solution)/shard_map/local_grads/pallas_call | solution.py:426
  81.2 0.1 collective-permute-start.14
  81.3 1.6 %collective-permute-start.13 = (f32[8,128]{1,0:T(8,128)S(1)}, f32[8,128]{1,0:T(8,128)S(1)}, u32[]{:S(2)}, u32[]{:S(2)}) collective-permute-start(f32[8,128]{1,0:T(8,128)S(1)} %get-tuple-element.91), channel_id=1, source_target_pairs={{0,2},{1,3},{2,0},{3,1},{4,6},{5,7},{6,4},{7,5},{8,10},{9,11},{10,... | collective-permute-start | bytes 12296 | tf_op jit(solution)/shard_map/ppermute | solution.py:469
  82.9 0.3 collective-permute-start.12
  83.2 1.2 %collective-permute-done.14 = f32[8,128]{1,0:T(8,128)S(1)} collective-permute-done((f32[8,128]{1,0:T(8,128)S(1)}, f32[8,128]{1,0:T(8,128)S(1)}, u32[]{:S(2)}, u32[]{:S(2)}) %collective-permute-start.14) | collective-permute-done | bytes 4128 | tf_op jit(solution)/shard_map/ppermute | solution.py:469
  84.3 0.7 collective-permute-done.13
  85.0 6.3 %collective-permute-start.17 = (f32[8,128]{1,0:T(8,128)S(1)}, f32[8,128]{1,0:T(8,128)S(1)}, u32[]{:S(2)}, u32[]{:S(2)}) collective-permute-start(f32[8,128]{1,0:T(8,128)S(1)} %add_add_fusion.1), channel_id=1, source_target_pairs={{0,12},{4,8},{8,4},{12,0},{16,28},{20,24},{24,20},{28,16},{1,13},{... | collective-permute-start | bytes 12296 | tf_op jit(solution)/shard_map/ppermute | solution.py:469
  91.3 1.1 %collective-permute-start.15 = (f32[8,128]{1,0:T(8,128)S(1)}, f32[8,128]{1,0:T(8,128)S(1)}, u32[]{:S(2)}, u32[]{:S(2)}) collective-permute-start(f32[8,128]{1,0:T(8,128)S(1)} %add_add_fusion.1), channel_id=1, source_target_pairs={{0,4},{4,0},{8,12},{12,8},{16,20},{20,16},{24,28},{28,24},{1,5},{5... | collective-permute-start | bytes 12296 | tf_op jit(solution)/shard_map/ppermute | solution.py:469
  92.4 0.5 collective-permute-done.17
  92.9 2.0 %collective-permute-done.16 = f32[8,128]{1,0:T(8,128)S(1)} collective-permute-done((f32[8,128]{1,0:T(8,128)S(1)}, f32[8,128]{1,0:T(8,128)S(1)}, u32[]{:S(2)}, u32[]{:S(2)}) %collective-permute-start.16) | collective-permute-done | bytes 4128 | tf_op jit(solution)/shard_map/ppermute | solution.py:469
  94.9 3.5 %collective-permute-start.18 = (f32[8,128]{1,0:T(8,128)S(1)}, f32[8,128]{1,0:T(8,128)S(1)}, u32[]{:S(2)}, u32[]{:S(2)}) collective-permute-start(f32[8,128]{1,0:T(8,128)S(1)} %add_add_fusion), channel_id=1, source_target_pairs={{0,16},{4,20},{8,24},{12,28},{16,0},{20,4},{24,8},{28,12},{1,17},{... | collective-permute-start | bytes 12296 | tf_op jit(solution)/shard_map/ppermute | solution.py:469
  98.4 1.6 %collective-permute-done.18 = f32[8,128]{1,0:T(8,128)S(1)} collective-permute-done((f32[8,128]{1,0:T(8,128)S(1)}, f32[8,128]{1,0:T(8,128)S(1)}, u32[]{:S(2)}, u32[]{:S(2)}) %collective-permute-start.18) | collective-permute-done | bytes 4128 | tf_op jit(solution)/shard_map/ppermute | solution.py:469
  100.0 0.5 slice_bitcast_fusion
  100.5 0.6 slice.150
  (56 shorter events, 0.2 us)
Async XLA Ops:
  5.2 15.5 %collective-permute-start.1 = (f32[264,512]{1,0:T(8,128)}, f32[264,512]{1,0:T(8,128)S(1)}, u32[]{:S(2)}, u32[]{:S(2)}) collective-permute-start(f32[264,512]{1,0:T(8,128)} %get-tuple-element.66), channel_id=1, source_target_pairs={{0,4},{4,0},{8,12},{12,8},{16,20},{20,16},{24,28},{28,24},{1,5},{5... | collective-permute-start | bytes 1622024 | tf_op jit(solution)/shard_map/ppermute | solution.py:507
  18.8 21.7 %copy-start.16 = (f32[264,512]{1,0:T(8,128)S(1)}, f32[264,512]{1,0:T(8,128)}, u32[]{:S(2)}) copy-start(f32[264,512]{1,0:T(8,128)} %get-tuple-element.70) | copy-start | bytes 1622020
  22.2 29.8 %copy-start.12 = (f32[1,32,1024]{2,1,0:T(8,128)S(1)}, f32[1,32,1024]{2,1,0:T(8,128)}, u32[]{:S(2)}) copy-start(f32[1,32,1024]{2,1,0:T(8,128)} %refs_5_.1) | copy-start | bytes 393220
  22.2 29.8 %copy-start.13 = (f32[8,2048]{1,0:T(8,128)S(1)}, f32[8,2048]{1,0:T(8,128)}, u32[]{:S(2)}) copy-start(f32[8,2048]{1,0:T(8,128)} %get-tuple-element.59.refs_4_) | copy-start | bytes 196612
  23.4 28.6 %copy-start.9 = (f32[16,2048]{1,0:T(8,128)S(1)}, f32[16,2048]{1,0:T(8,128)}, u32[]{:S(2)}) copy-start(f32[16,2048]{1,0:T(8,128)} %get-tuple-element.50.refs_6_.refs_8_) | copy-start | bytes 393220
  23.4 28.6 %copy-start.10 = (bf16[128,1024]{1,0:T(8,128)(2,1)S(1)}, bf16[128,1024]{1,0:T(8,128)(2,1)}, u32[]{:S(2)}) copy-start(bf16[128,1024]{1,0:T(8,128)(2,1)} %get-tuple-element.60.refs_12_) | copy-start | bytes 786436
  23.4 28.6 %copy-start.11 = (bf16[128,1024]{1,0:T(8,128)(2,1)S(1)}, bf16[128,1024]{1,0:T(8,128)(2,1)}, u32[]{:S(2)}) copy-start(bf16[128,1024]{1,0:T(8,128)(2,1)} %get-tuple-element.61.refs_13_) | copy-start | bytes 786436
  23.4 7.9 %collective-permute-start.2 = (f32[136,512]{1,0:T(8,128)S(1)}, f32[136,512]{1,0:T(8,128)S(1)}, u32[]{:S(2)}, u32[]{:S(2)}) collective-permute-start(f32[136,512]{1,0:T(8,128)S(1)} %pad_maximum_fusion), channel_id=1, source_target_pairs={{0,8},{4,12},{8,0},{12,4},{16,24},{20,28},{24,16},{28,20},{1,9},{5... | collective-permute-start | bytes 835592 | tf_op jit(solution)/shard_map/ppermute | solution.py:515
  25.3 15.2 %collective-permute-start = (f32[264,512]{1,0:T(8,128)}, f32[264,512]{1,0:T(8,128)S(1)}, u32[]{:S(2)}, u32[]{:S(2)}) collective-permute-start(f32[264,512]{1,0:T(8,128)} %get-tuple-element.64), channel_id=1, source_target_pairs={{0,4},{4,0},{8,12},{12,8},{16,20},{20,16},{24,28},{28,24},{1,5},{5... | collective-permute-start | bytes 1622024 | tf_op jit(solution)/shard_map/ppermute | solution.py:507
  26.8 17.3 %copy-start.17 = (f32[1,512]{1,0:T(1,128)S(1)}, f32[1,512]{1,0:T(1,128)}, u32[]{:S(2)}) copy-start(f32[1,512]{1,0:T(1,128)} %get-tuple-element.121) | copy-start | bytes 6148
  26.8 17.3 %copy-start.18 = (f32[1,512]{1,0:T(1,128)S(1)}, f32[1,512]{1,0:T(1,128)}, u32[]{:S(2)}) copy-start(f32[1,512]{1,0:T(1,128)} %get-tuple-element.122) | copy-start | bytes 6148
  31.4 20.7 %copy-start.1 = (bf16[1024,2048]{1,0:T(8,128)(2,1)S(1)}, bf16[1024,2048]{1,0:T(8,128)(2,1)}, u32[]{:S(2)}) copy-start(bf16[1024,2048]{1,0:T(8,128)(2,1)} %get-tuple-element.58.refs_2_) | copy-start | bytes 12582916
  32.7 19.3 %copy-start = (bf16[1024,2048]{1,0:T(8,128)(2,1)S(1)}, bf16[1024,2048]{1,0:T(8,128)(2,1)}, u32[]{:S(2)}) copy-start(bf16[1024,2048]{1,0:T(8,128)(2,1)} %get-tuple-element.57.refs_1_) | copy-start | bytes 12582916
  32.7 19.3 %copy-start.3 = (bf16[1,1024,128]{2,1,0:T(8,128)(2,1)S(1)}, bf16[1,1024,128]{2,1,0:T(8,128)(2,1)}, u32[]{:S(2)}) copy-start(bf16[1,1024,128]{2,1,0:T(8,128)(2,1)} %param.12) | copy-start | bytes 786436
  32.7 19.3 %copy-start.4 = (bf16[1,1024,128]{2,1,0:T(8,128)(2,1)S(1)}, bf16[1,1024,128]{2,1,0:T(8,128)(2,1)}, u32[]{:S(2)}) copy-start(bf16[1,1024,128]{2,1,0:T(8,128)(2,1)} %param.13) | copy-start | bytes 786436
  32.8 19.3 %copy-start.5 = (bf16[1024,128]{1,0:T(8,128)(2,1)S(1)}, bf16[1024,128]{1,0:T(8,128)(2,1)}, u32[]{:S(2)}) copy-start(bf16[1024,128]{1,0:T(8,128)(2,1)} %get-tuple-element.49.refs_5_.refs_7_) | copy-start | bytes 786436
  32.8 19.3 %copy-start.6 = (bf16[4,256,256]{2,1,0:T(8,128)(2,1)S(1)}, bf16[4,256,256]{2,1,0:T(8,128)(2,1)}, u32[]{:S(2)}) copy-start(bf16[4,256,256]{2,1,0:T(8,128)(2,1)} %get-tuple-element.62.refs_14_) | copy-start | bytes 1572868
  32.8 19.3 %copy-start.7 = (bf16[4,256,256]{2,1,0:T(8,128)(2,1)S(1)}, bf16[4,256,256]{2,1,0:T(8,128)(2,1)}, u32[]{:S(2)}) copy-start(bf16[4,256,256]{2,1,0:T(8,128)(2,1)} %get-tuple-element.63.refs_15_) | copy-start | bytes 1572868
  32.8 19.3 %copy-start.8 = (bf16[1536,128]{1,0:T(8,128)(2,1)S(1)}, bf16[1536,128]{1,0:T(8,128)(2,1)}, u32[]{:S(2)}) copy-start(bf16[1536,128]{1,0:T(8,128)(2,1)} %constant.44.clone.refs_16_) | copy-start | bytes 1179652
  32.8 19.3 %copy-start.14 = (f32[32]{0:T(128)S(1)}, f32[32]{0:T(128)}, u32[]{:S(2)}) copy-start(f32[32]{0:T(128)} %param.15) | copy-start | bytes 388
  32.8 19.3 %copy-start.15 = (f32[32]{0:T(128)S(1)}, f32[32]{0:T(128)}, u32[]{:S(2)}) copy-start(f32[32]{0:T(128)} %param.16) | copy-start | bytes 388
  32.8 11.3 %collective-permute-start.5 = (f32[128,512]{1,0:T(8,128)S(1)}, f32[128,512]{1,0:T(8,128)S(1)}, u32[]{:S(2)}, u32[]{:S(2)}) collective-permute-start(f32[128,512]{1,0:T(8,128)S(1)} %get-tuple-element.133), channel_id=1, source_target_pairs={{8,24},{12,28},{16,0},{20,4},{9,25},{13,29},{17,1},{21,5},{10,26},... | collective-permute-start | bytes 786440 | tf_op jit(solution)/shard_map/ppermute | solution.py:520
  34.4 9.7 %collective-permute-start.4 = (f32[128,512]{1,0:T(8,128)S(1)}, f32[128,512]{1,0:T(8,128)S(1)}, u32[]{:S(2)}, u32[]{:S(2)}) collective-permute-start(f32[128,512]{1,0:T(8,128)S(1)} %get-tuple-element.133), channel_id=1, source_target_pairs={{8,16},{12,20},{16,8},{20,12},{9,17},{13,21},{17,9},{21,13},{10,18... | collective-permute-start | bytes 786440 | tf_op jit(solution)/shard_map/ppermute | solution.py:519
  35.2 16.8 %collective-permute-start.8 = (f32[128,512]{1,0:T(8,128)S(1)}, f32[128,512]{1,0:T(8,128)S(1)}, u32[]{:S(2)}, u32[]{:S(2)}) collective-permute-start(f32[128,512]{1,0:T(8,128)S(1)} %get-tuple-element.131), channel_id=1, source_target_pairs={{0,4},{4,0},{8,12},{12,8},{16,20},{20,16},{24,28},{28,24},{1,5},{5... | collective-permute-start | bytes 786440 | tf_op jit(solution)/shard_map/ppermute | solution.py:524
  40.7 8.0 %collective-permute-start.3 = (f32[136,512]{1,0:T(8,128)S(1)}, f32[136,512]{1,0:T(8,128)S(1)}, u32[]{:S(2)}, u32[]{:S(2)}) collective-permute-start(f32[136,512]{1,0:T(8,128)S(1)} %pad_maximum_fusion.1), channel_id=1, source_target_pairs={{0,8},{4,12},{8,0},{12,4},{16,24},{20,28},{24,16},{28,20},{1,9},{5... | collective-permute-start | bytes 835592 | tf_op jit(solution)/shard_map/ppermute | solution.py:515
  44.4 7.6 %collective-permute-start.9 = (f32[128,512]{1,0:T(8,128)S(1)}, f32[128,512]{1,0:T(8,128)S(1)}, u32[]{:S(2)}, u32[]{:S(2)}) collective-permute-start(f32[128,512]{1,0:T(8,128)S(1)} %broadcast_select_fusion.6), channel_id=1, source_target_pairs={{0,4},{4,0},{8,12},{12,8},{16,20},{20,16},{24,28},{28,24},{1,5},{5... | collective-permute-start | bytes 786440 | tf_op jit(solution)/shard_map/ppermute | solution.py:529
  48.8 10.5 %collective-permute-start.7 = (f32[128,512]{1,0:T(8,128)S(1)}, f32[128,512]{1,0:T(8,128)S(1)}, u32[]{:S(2)}, u32[]{:S(2)}) collective-permute-start(f32[128,512]{1,0:T(8,128)S(1)} %get-tuple-element.132), channel_id=1, source_target_pairs={{8,24},{12,28},{16,0},{20,4},{9,25},{13,29},{17,1},{21,5},{10,26},... | collective-permute-start | bytes 786440 | tf_op jit(solution)/shard_map/ppermute | solution.py:520
  50.1 9.2 %collective-permute-start.6 = (f32[128,512]{1,0:T(8,128)S(1)}, f32[128,512]{1,0:T(8,128)S(1)}, u32[]{:S(2)}, u32[]{:S(2)}) collective-permute-start(f32[128,512]{1,0:T(8,128)S(1)} %get-tuple-element.132), channel_id=1, source_target_pairs={{8,16},{12,20},{16,8},{20,12},{9,17},{13,21},{17,9},{21,13},{10,18... | collective-permute-start | bytes 786440 | tf_op jit(solution)/shard_map/ppermute | solution.py:519
  50.9 18.0 %collective-permute-start.10 = (f32[128,512]{1,0:T(8,128)S(1)}, f32[128,512]{1,0:T(8,128)S(1)}, u32[]{:S(2)}, u32[]{:S(2)}) collective-permute-start(f32[128,512]{1,0:T(8,128)S(1)} %get-tuple-element.128), channel_id=1, source_target_pairs={{0,4},{4,0},{8,12},{12,8},{16,20},{20,16},{24,28},{28,24},{1,5},{5... | collective-permute-start | bytes 786440 | tf_op jit(solution)/shard_map/ppermute | solution.py:524
  59.5 9.4 %collective-permute-start.11 = (f32[128,512]{1,0:T(8,128)S(1)}, f32[128,512]{1,0:T(8,128)S(1)}, u32[]{:S(2)}, u32[]{:S(2)}) collective-permute-start(f32[128,512]{1,0:T(8,128)S(1)} %get-tuple-element.92), channel_id=1, source_target_pairs={{0,4},{4,0},{8,12},{12,8},{16,20},{20,16},{24,28},{28,24},{1,5},{5... | collective-permute-start | bytes 786440 | tf_op jit(solution)/shard_map/ppermute | solution.py:529
  60.5 8.4 %copy-start.2 = (bf16[1024,2048]{1,0:T(8,128)(2,1)S(1)}, bf16[1024,2048]{1,0:T(8,128)(2,1)}, u32[]{:S(2)}) copy-start(bf16[1024,2048]{1,0:T(8,128)(2,1)} %get-tuple-element.58.refs_2_) | copy-start | bytes 12582916
  81.2 3.1 %collective-permute-start.14 = (f32[8,128]{1,0:T(8,128)S(1)}, f32[8,128]{1,0:T(8,128)S(1)}, u32[]{:S(2)}, u32[]{:S(2)}) collective-permute-start(f32[8,128]{1,0:T(8,128)S(1)} %get-tuple-element.91), channel_id=1, source_target_pairs={{0,3},{1,2},{2,1},{3,0},{4,7},{5,6},{6,5},{7,4},{8,11},{9,10},{10,... | collective-permute-start | bytes 12296 | tf_op jit(solution)/shard_map/ppermute | solution.py:469
  81.3 3.7 %collective-permute-start.13 = (f32[8,128]{1,0:T(8,128)S(1)}, f32[8,128]{1,0:T(8,128)S(1)}, u32[]{:S(2)}, u32[]{:S(2)}) collective-permute-start(f32[8,128]{1,0:T(8,128)S(1)} %get-tuple-element.91), channel_id=1, source_target_pairs={{0,2},{1,3},{2,0},{3,1},{4,6},{5,7},{6,4},{7,5},{8,10},{9,11},{10,... | collective-permute-start | bytes 12296 | tf_op jit(solution)/shard_map/ppermute | solution.py:469
  82.9 2.1 %collective-permute-start.12 = (f32[8,128]{1,0:T(8,128)S(1)}, f32[8,128]{1,0:T(8,128)S(1)}, u32[]{:S(2)}, u32[]{:S(2)}) collective-permute-start(f32[8,128]{1,0:T(8,128)S(1)} %get-tuple-element.91), channel_id=1, source_target_pairs={{0,1},{1,0},{2,3},{3,2},{4,5},{5,4},{6,7},{7,6},{8,9},{9,8},{10,11... | collective-permute-start | bytes 12296 | tf_op jit(solution)/shard_map/ppermute | solution.py:469
  85.0 7.9 %collective-permute-start.17 = (f32[8,128]{1,0:T(8,128)S(1)}, f32[8,128]{1,0:T(8,128)S(1)}, u32[]{:S(2)}, u32[]{:S(2)}) collective-permute-start(f32[8,128]{1,0:T(8,128)S(1)} %add_add_fusion.1), channel_id=1, source_target_pairs={{0,12},{4,8},{8,4},{12,0},{16,28},{20,24},{24,20},{28,16},{1,13},{... | collective-permute-start | bytes 12296 | tf_op jit(solution)/shard_map/ppermute | solution.py:469
  91.3 3.6 %collective-permute-start.16 = (f32[8,128]{1,0:T(8,128)S(1)}, f32[8,128]{1,0:T(8,128)S(1)}, u32[]{:S(2)}, u32[]{:S(2)}) collective-permute-start(f32[8,128]{1,0:T(8,128)S(1)} %add_add_fusion.1), channel_id=1, source_target_pairs={{0,8},{4,12},{8,0},{12,4},{16,24},{20,28},{24,16},{28,20},{1,9},{5... | collective-permute-start | bytes 12296 | tf_op jit(solution)/shard_map/ppermute | solution.py:469
  91.3 3.6 %collective-permute-start.15 = (f32[8,128]{1,0:T(8,128)S(1)}, f32[8,128]{1,0:T(8,128)S(1)}, u32[]{:S(2)}, u32[]{:S(2)}) collective-permute-start(f32[8,128]{1,0:T(8,128)S(1)} %add_add_fusion.1), channel_id=1, source_target_pairs={{0,4},{4,0},{8,12},{12,8},{16,20},{20,16},{24,28},{28,24},{1,5},{5... | collective-permute-start | bytes 12296 | tf_op jit(solution)/shard_map/ppermute | solution.py:469
  94.9 5.1 %collective-permute-start.18 = (f32[8,128]{1,0:T(8,128)S(1)}, f32[8,128]{1,0:T(8,128)S(1)}, u32[]{:S(2)}, u32[]{:S(2)}) collective-permute-start(f32[8,128]{1,0:T(8,128)S(1)} %add_add_fusion), channel_id=1, source_target_pairs={{0,16},{4,20},{8,24},{12,28},{16,0},{20,4},{24,8},{28,12},{1,17},{... | collective-permute-start | bytes 12296 | tf_op jit(solution)/shard_map/ppermute | solution.py:469

commit v7 on v6

--- a/solution.py
+++ b/solution.py
@@ -120,8 +120,8 @@
     at_ref, x_ref, dy_ref, b_ref, c_ref = refs[:5]
     if first:
         raw_ref, bias_ref, rate_ref, skip_ref = refs[5:9]
-        outs = refs[9:-7]
-        xs_ref, ys_ref, direct_ref, columns_ref, table_ref, bt, ct = refs[-7:]
+        outs = refs[9 : 9 + count]
+        xs_ref, ys_ref, direct_ref, columns_ref, table_ref, bt, ct = refs[9 + count : 16 + count]
     else:
         columns_ref, table_ref = refs[5:7]
         outs = refs[10 : 10 + count]
@@ -129,12 +129,31 @@
         if last:
             left, right, bt, ct = refs[13 + count :]
         else:
-            bt, ct = refs[13 + count :]
+            bt, ct = refs[13 + count : 15 + count]
+    if not last:
+        near_x, near_dy, near_xs, near_ys, sems = refs[-5:]
     g = pl.program_id(0)
-    length, width = x_ref.shape
     states = b_ref.shape[1]
+    length, width = columns_ref.shape[0], outs[0].shape[1]
     blocks = length // GROUP
     piece = at_ref[0] + g
+    writes = []
+    if not last:
+        place = pl.ds(pl.multiple_of(piece * width, width), width)
+        reads = [
+            pltpu.make_async_copy(x_ref.at[:, place], near_x, sems.at[0]),
+            pltpu.make_async_copy(dy_ref.at[:, place], near_dy, sems.at[1]),
+        ]
+        for n in range(blocks):
+            rows = slice(n * GROUP, (n + 1) * GROUP)
+            for k, (near, far) in enumerate(((near_xs, xs_ref), (near_ys, ys_ref))):
+                target = far.at[rows, place]
+                writes.append(
+                    pltpu.make_async_copy(near.at[rows, :], target, sems.at[2 + 2 * n + k])
+                )
+        for copy in reads:
+            copy.start()
+        x_ref, dy_ref, xs_ref, ys_ref = near_x, near_dy, near_xs, near_ys
     all_heads = columns_ref.shape[1] // 4
     heads = all_heads * width // table_ref.shape[1]
 
@@ -161,6 +180,9 @@
 
     gain = dot(columns_ref[...], picker(piece, heads, all_heads, width, True), NN)
     lift = dot(columns_ref[...], picker(piece, heads, all_heads, width, False), NN)
+    if not last:
+        for copy in reads:
+            copy.wait()
     table = table_ref[:, pl.ds(pl.multiple_of(piece * width, width), width)]
     state = jnp.zeros((states, width), F32)
     grad = jnp.zeros((states, width), F32)
@@ -174,6 +196,8 @@
         scaled_dy = (dy * lift[rows]).astype(BF16)
         xs_ref[rows, :] = scaled_x
         ys_ref[rows, :] = scaled_dy
+        for copy in writes[2 * n : 2 * n + 2]:
+            copy.start()
         later = table[blocks + n : blocks + n + 1]
         earlier = table[2 * blocks + n : 2 * blocks + n + 1]
         state = state + later * dot(bt[:, rows], scaled_x, NN)
@@ -187,6 +211,9 @@
             out_ref[:states] = state
             out_ref[states : 2 * states] = grad
             out_ref[2 * states :] = decay
+
+    for copy in writes:
+        copy.wait()
 
 
 def local_states(at, count, last, x, dy, b, c, vectors, before):
@@ -202,8 +229,9 @@
     strip = pl.BlockSpec((8, width), lambda g, at: (0, at[0] + g))
     maps = pl.BlockSpec((length, states), whole)
     anywhere = pl.BlockSpec(memory_space=pl.ANY)
-    in_specs = [columns, columns, maps, maps]
-    out_specs = [pl.BlockSpec((2 * states + 8, width), whole)] * count + [columns, columns, strip]
+    wide = columns if last else anywhere
+    in_specs = [wide, wide, maps, maps]
+    out_specs = [pl.BlockSpec((2 * states + 8, width), whole)] * count + [wide, wide, strip]
     out_shape = [jax.ShapeDtypeStruct((2 * states + 8, width), F32)] * count + [
         jax.ShapeDtypeStruct((length, channels), BF16),
         jax.ShapeDtypeStruct((length, channels), BF16),
@@ -229,6 +257,8 @@
         in_specs += [anywhere] * 3
         aliases = {7: count, 8: count + 1, 9: count + 2}
     scratch = [pltpu.VMEM((states, length), BF16)] * 2
+    scratch += [pltpu.VMEM((length, width), BF16)] * 4
+    scratch += [pltpu.SemaphoreType.DMA((2 + 2 * (length // GROUP),))]
     if last:
         blocks = length // GROUP
         extra = [jax.ShapeDtypeStruct((blocks, GROUP, GROUP), BF16)] * 2
@@ -260,18 +290,24 @@
 
 
 def grads_kernel(first, scale, part, half, begin, *refs):
-    y_ref, xs_ref, ys_ref, dy_ref, direct_ref, b_ref, c_ref, columns_ref, table_ref = refs[:9]
-    raw_ref, bias_ref, rate_ref, bt, ct, left, right, adder = refs[9:17]
+    y_ref, xs_ref, ys_ref, dy_far, direct_ref, b_ref, c_ref, columns_far, table_ref = refs[:9]
+    raw_ref, bias_ref, rate_ref, bt, ct, left_far, right_far, adder_far = refs[9:17]
     held = refs[17:21]
     refs = refs[21:]
     if not first:
         dc_in, db_in, par_in = refs[:3]
         refs = refs[5:]
     dx_ref, dc_ref, db_ref, draw_ref, par_ref = refs[:5]
-    sums, dc_sum, db_sum, terms = refs[5:9]
+    sums, dc_sum, db_sum, terms, dy_ref, columns_ref, left, right, adder, sems = refs[5:15]
     if not first:
-        dc_old, db_old, sems = refs[9:]
+        dc_old, db_old = refs[15:]
         old = [(dc_in, dc_old, sems.at[0]), (db_in, db_old, sems.at[1])]
+    fixed = [
+        (left_far, left, sems.at[2]),
+        (right_far, right, sems.at[3]),
+        (adder_far, adder, sems.at[4]),
+        (columns_far, columns_ref, sems.at[5]),
+    ]
     g = pl.program_id(0)
     heads = raw_ref.shape[1]
     length, width = xs_ref.shape
@@ -283,8 +319,14 @@
     lower = triangle(GROUP, True)
     rows = [slice(n * GROUP, (n + 1) * GROUP) for n in range(blocks)]
 
+    own_columns = pl.ds(pl.multiple_of(piece * width, width), width)
+    dy_copy = pltpu.make_async_copy(dy_far.at[:, own_columns], dy_ref, sems.at[6])
+    dy_copy.start()
+
     @pl.when(g == 0)
     def _():
+        for source, target, sem in fixed:
+            pltpu.make_async_copy(source, target, sem).start()
         if not first:
             for source, target, sem in old:
                 pltpu.make_async_copy(source, target, sem).start()
@@ -312,6 +354,13 @@
         leaving_low[n] = grad.astype(BF16)
         edges[n] = jnp.sum(ends[n] * grad, axis=0, keepdims=True)
         grad = table[n : n + 1] * (grad + dot(ct[:, rows[n]], ys_ref[rows[n], :], NN))
+
+    @pl.when(g == 0)
+    def _():
+        for source, target, sem in fixed:
+            pltpu.make_async_copy(source, target, sem).wait()
+
+    dy_copy.wait()
     gain = dot(columns_ref[...], picker(piece, heads, all_heads, width, True), NN)
     for n in range(blocks):
         scaled_x, scaled_dy = xs_ref[rows[n], :], ys_ref[rows[n], :]
@@ -389,16 +438,16 @@
     lines = pl.BlockSpec((1, heads, length), lambda g, y: ((begin + g) * half + part, 0, 0))
     params = pl.BlockSpec((8, 128), whole)
     anywhere = pl.BlockSpec(memory_space=pl.ANY)
-    in_specs = [columns, columns, columns, pl.BlockSpec((8, width), place), maps, maps]
+    in_specs = [columns, columns, anywhere, pl.BlockSpec((8, width), place), maps, maps]
     in_specs += [
-        pl.BlockSpec(factor_columns.shape, whole),
+        anywhere,
         pl.BlockSpec((table.shape[0], width), place),
     ]
     in_specs += [lines, line, line]
     args = [xs, ys, dy, direct, b, c, factor_columns, table, raw, bias, rate]
-    fixed = [bt, ct, left, right, adding(width, heads, (0, 0, 1)), *held]
-    in_specs += [pl.BlockSpec(a.shape, lambda g, y, n=len(a.shape): (0,) * n) for a in fixed]
-    args += fixed
+    args += [bt, ct, left, right, adding(width, heads, (0, 0, 1)), *held]
+    in_specs += [pl.BlockSpec(bt.shape, whole)] * 2 + [anywhere] * 3
+    in_specs += [pl.BlockSpec(h.shape, whole) for h in held]
     aliases = {}
     if not first:
         dx, dc, db, draw, par = before
@@ -415,11 +464,16 @@
             pltpu.VMEM((blocks, GROUP, states), F32),
             pltpu.VMEM((blocks, GROUP, states), F32),
             pltpu.VMEM((length, 3 * width), BF16),
+            pltpu.VMEM((length, width), BF16),
+            pltpu.VMEM(factor_columns.shape, BF16),
+            pltpu.VMEM(left.shape, BF16),
+            pltpu.VMEM(right.shape, BF16),
+            pltpu.VMEM((3 * width, 128), BF16),
+            pltpu.SemaphoreType.DMA((7,)),
         ]
         + [
             pltpu.VMEM((length, states), F32),
             pltpu.VMEM((length, states), F32),
-            pltpu.SemaphoreType.DMA((2,)),
         ]
         * (not first),
     )
@@ -486,19 +540,19 @@
     swap = [(i, i ^ 1) for i in range(size)]
     both = lambda moves: [(2 * a + y, 2 * b + y) for a, b in moves for y in range(2)]
 
-    def halves(got, copy):
-        spans = ((0, states), (states, 2 * states), (2 * states + copy, 2 * states + copy + 1))
+    def halves(got):
+        spans = ((0, states), (states, 2 * states), (2 * states, 2 * states + 1))
         for low, high in spans:
             own, other = kept[low:high], got[low:high]
             yield jnp.where(second, other, own), jnp.where(second, own, other)
 
-    def message_of(up, got, arrived, copy):
-        (l1, l2), (k1, k2), (d1, d2) = halves(got, copy)
+    def message_of(up, got, arrived):
+        (l1, l2), (k1, k2), (d1, d2) = halves(got)
         message = jnp.where(up, d2 * l1 + l2, k1 + d1 * k2)
         return message if arrived is None else message + d1 * d2 * arrived[:states]
 
-    def shares(is_state, value, got, copy):
-        (l1, _), (_, k2), (d1, d2) = halves(got, copy)
+    def shares(is_state, value, got):
+        (l1, _), (_, k2), (d1, d2) = halves(got)
         for_first = jnp.where(is_state, value, k2 + d2 * value)
         for_second = jnp.where(is_state, d1 * value + l1, value)
         return jnp.where(second, for_second, for_first), jnp.where(second, for_first, for_second)
@@ -509,29 +563,29 @@
     got = after(got, token)
     lower = place < pairs // 2
     if pairs == 4:
-        message = message_of((place == 0) | (place == 2), got, None, 0)
-        (_, _), (_, _), (d1, d2) = halves(got, 0)
+        message = message_of((place == 0) | (place == 2), got, None)
+        (_, _), (_, _), (d1, d2) = halves(got)
         message = jnp.concatenate([message, jnp.broadcast_to(d1 * d2, (8, message.shape[1]))])
         near = lax.ppermute(message, "seq", both([(0, 1), (1, 0), (2, 3), (3, 2)]))
         token = yield message, near
         near = after(near, token)
-        message = message_of(place == 1, got, near, 1)
+        message = message_of(place == 1, got, near)
         middle = lax.ppermute(message, "seq", both([(1, 2), (2, 1)]))
         far = lax.ppermute(message, "seq", both([(1, 3), (2, 0)]))
         inside = (place == 1) | (place == 2)
         known = jnp.where(inside, near[:states], 0.0)
-        mine_early, early = shares(lower, known, got, 2)
+        mine_early, early = shares(lower, known, got)
         other_early = lax.ppermute(early, "seq", swap)
         token = yield early, far
         far = after(far, token)
         outer = near[states : states + 1] * far + near[:states]
-        mine_late, late = shares(~lower, jnp.where(inside, middle, outer), got, 3)
+        mine_late, late = shares(~lower, jnp.where(inside, middle, outer), got)
         other_late = lax.ppermute(late, "seq", swap)
         yield late, other_late
     else:
         arrived = []
         for k in range(1, pairs):
-            message = message_of(place == k - 1, got, arrived[-1] if arrived else None, min(k, 4))
+            message = message_of(place == k - 1, got, arrived[-1] if arrived else None)
             routes = both([(k - 1, k), (pairs - k, pairs - k - 1)])
             arrived.append(lax.ppermute(message, "seq", routes))
             token = yield message, arrived[-1]
@@ -540,8 +594,8 @@
         for k in range(1, pairs):
             start = jnp.where(place == k, arrived[k - 1], start)
             end = jnp.where(place == pairs - 1 - k, arrived[k - 1], end)
-        mine_early, early = shares(lower, jnp.where(lower, start, end), got, 5)
-        mine_late, late = shares(~lower, jnp.where(lower, end, start), got, 6)
+        mine_early, early = shares(lower, jnp.where(lower, start, end), got)
+        mine_late, late = shares(~lower, jnp.where(lower, end, start), got)
         other_early = lax.ppermute(early, "seq", swap)
         other_late = lax.ppermute(late, "seq", swap)
         yield late, other_late

time: 101 us -> 104 us (1.030)
  Pallas kernels: 42.8 us -> 46.8 us
  starting transfers between devices: 30.3 us -> 26.4 us
  waiting for transfers between devices: 20.7 us -> 22.7 us
    pallas_call x3, Pallas kernels: 15.2 us -> 18.4 us  [local_states(): pl.pallas_call(functools.partial(local_kernel, first, last, count), grid_...]
    ppermute x7, starting transfers between devices: 12.8 us -> 10.5 us  [summed_over(): lax.ppermute(value, axis, [(i, i ^ s) for i in range(size)])]
    ppermute x2, waiting for transfers between devices: 7.77 us -> 9.63 us  [entering(): near = lax.ppermute(message, 'seq', both([(0, 1), (1, 0), (2, 3), (3, 2)]))]
    ppermute x2, starting transfers between devices: 4.07 us -> 2.59 us  [entering(): near = lax.ppermute(message, 'seq', both([(0, 1), (1, 0), (2, 3), (3, 2)]))]
    select_n x3 -> x2, other arithmetic: 1.6 us -> 0.25 us  [shares(): jnp.where(second, for_second, for_first)]
    select_n x2, other arithmetic: 1.31 us -> 2.5 us  [message_of(): message = jnp.where(up, d2 * l1 + l2, k1 + d1 * k2)]
  transfers between devices with their start and end apart: 19 -> 19, of which waited for: 11 -> 10; matrix products, arithmetic and copies ran while one was open for 2% -> 3% of each run, Pallas kernels for 26% -> 26%
where the time goes in v7:
time: 104 us
  Pallas kernels  46.8 us (45%)
  starting transfers between devices  26.4 us (25%)
  waiting for transfers between devices  22.7 us (22%)
  other arithmetic  5.62 us (5%)
  local copies, waits for them, and re-layouts  1.18 us (1%)
  between operations  1.07 us (1%)
    pallas_call x3, Pallas kernels, local_grads(): pl.pallas_call(functools.partial(grads_kernel, first, scale, part, half,...  28.4 us
    pallas_call x3, Pallas kernels, local_states(): pl.pallas_call(functools.partial(local_kernel, first, last, count), grid_...  18.4 us
    ppermute x7, starting transfers between devices, summed_over(): lax.ppermute(value, axis, [(i, i ^ s) for i in range(size)])  10.5 us
    ppermute x2, waiting for transfers between devices, entering(): near = lax.ppermute(message, 'seq', both([(0, 1), (1, 0), (2, 3), (3, 2)]))  9.63 us
    ppermute x7, waiting for transfers between devices, summed_over(): lax.ppermute(value, axis, [(i, i ^ s) for i in range(size)])  6.38 us
    ppermute x2, waiting for transfers between devices, entering(): got = lax.ppermute(message, 'seq', swap)  5.33 us
    ppermute x2, starting transfers between devices, entering(): got = lax.ppermute(message, 'seq', swap)  4.49 us
    ppermute x2, starting transfers between devices, entering(): far = lax.ppermute(message, 'seq', both([(1, 3), (2, 0)]))  2.85 us
  transfers between devices with their start and end apart: 19, of which 10 were waited for; matrix products, arithmetic and copies ran while one was open for 3% of the time, Pallas kernels for 26%

profile of v7, /device:TPU:0, one launch (start us, length us, event | category | flops | bytes accessed | tf_op | source)
XLA Modules:
  0.0 103.9 jit_solution(12338248463111091942)
XLA Ops:
  0.6 6.1 %local_states.3 = (f32[264,512]{1,0:T(8,128)}, bf16[1024,2048]{1,0:T(8,128)(2,1)}, bf16[1024,2048]{1,0:T(8,128)(2,1)}, f32[8,2048]{1,0:T(8,128)}, bf16[1024,128]{1,0:T(8,128)(2,1)}, /*index=5*/f32[16,2048]{1,0:T(8,128)}) custom-call(s32[1]{0:T(128)} %bitcast.7.refs_0_, bf16[1024,2048]{1,0:T(8,128)(2,1)} %bitcast.56, bf16[1024,2048]{1,0:T(8,128)(2,1)} %bitcast.50, ...), custom_call_target="tpu_custom_call" | custom-call | flops 536870912 | bytes 4194304 | tf_op jit(solution)/shard_map/local_states/pallas_call | solution.py:276
  6.7 3.0 %collective-permute-start.1 = (f32[264,512]{1,0:T(8,128)}, f32[264,512]{1,0:T(8,128)S(1)}, u32[]{:S(2)}, u32[]{:S(2)}) collective-permute-start(f32[264,512]{1,0:T(8,128)} %get-tuple-element.66), channel_id=1, source_target_pairs={{0,4},{4,0},{8,12},{12,8},{16,20},{20,16},{24,28},{28,24},{1,5},{5... | collective-permute-start | bytes 1622024 | tf_op jit(solution)/shard_map/ppermute | solution.py:561
  9.7 5.5 %local_states.4 = (f32[264,512]{1,0:T(8,128)}, bf16[1024,2048]{1,0:T(8,128)(2,1)}, bf16[1024,2048]{1,0:T(8,128)(2,1)}, f32[8,2048]{1,0:T(8,128)}) custom-call(s32[1]{0:T(128)} %bitcast.11.refs_0_, bf16[1024,2048]{1,0:T(8,128)(2,1)} %bitcast.57, bf16[1024,2048]{1,0:T(8,128)(2,1)} %bitcast.51, ...), custom_call_target="tpu_custom_call", output_to_operand_aliasing={{1}: (7, {}), {2}: (8, {}), {3}: (9, {})} | custom-call | flops 536870912 | bytes 4194304 | tf_op jit(solution)/shard_map/local_states/pallas_call | solution.py:276
  15.3 6.8 %local_states.5 = (f32[264,512]{1,0:T(8,128)}, f32[264,512]{1,0:T(8,128)}, bf16[1024,2048]{1,0:T(8,128)(2,1)}, bf16[1024,2048]{1,0:T(8,128)(2,1)}, f32[8,2048]{1...) custom-call(s32[1]{0:T(128)} %bitcast.2.refs_0_, ...), custom_call_target="tpu_custom_call", output_to_operand_aliasing={{2}: (7, {}), {3}: (8, {}), {4}: (9, {})} | custom-call | flops 1073741824 | bytes 8388608 | tf_op jit(solution)/shard_map/local_states/pallas_call | solution.py:276
  22.1 0.1 collective-permute-done.1
  22.2 0.8 fusion.1
  23.0 1.3 %broadcast_select_fusion.1 = (f32[128,512]{1,0:T(8,128)S(1)}, f32[128,512]{1,0:T(8,128)S(1)}, f32[128,512]{1,0:T(8,128)S(1)}, f32[128,512]{1,0:T(8,128)S(1)}, f32[128,512]{1,0:T(8,128)S(1)}) fusion(pred[]{:T(512)S(6)} %or.9, f32[512]{0:T(512)S(1)} %bitcast.69, f32[264,512]{1,0:T(8,128)} %get-tuple-element.65, f32[264,512]{1,0:T(8,128)S(1)} %collective-permute-done.1, ...), kind=kLoop, calls=%fused_computation.23 | loop fusion | flops 589824 | bytes 2363394 | tf_op jit(solution)/shard_map/jit(_where)/select_n | solution.py:551
  24.4 0.7 pad_maximum_fusion
  25.1 1.8 %collective-permute-start.2 = (f32[136,512]{1,0:T(8,128)}, f32[136,512]{1,0:T(8,128)S(1)}, u32[]{:S(2)}, u32[]{:S(2)}) collective-permute-start(f32[136,512]{1,0:T(8,128)} %pad_maximum_fusion), channel_id=1, source_target_pairs={{0,8},{4,12},{8,0},{12,4},{16,24},{20,28},{24,16},{28,20},{1,9},{5... | collective-permute-start | bytes 835592 | tf_op jit(solution)/shard_map/ppermute | solution.py:569
  26.9 1.5 %collective-permute-start = (f32[264,512]{1,0:T(8,128)}, f32[264,512]{1,0:T(8,128)}, u32[]{:S(2)}, u32[]{:S(2)}) collective-permute-start(f32[264,512]{1,0:T(8,128)} %get-tuple-element.64), channel_id=1, source_target_pairs={{0,4},{4,0},{8,12},{12,8},{16,20},{20,16},{24,28},{28,24},{1,5},{5... | collective-permute-start | bytes 1622024 | tf_op jit(solution)/shard_map/ppermute | solution.py:561
  28.4 4.9 %collective-permute-done.2 = f32[136,512]{1,0:T(8,128)S(1)} collective-permute-done((f32[136,512]{1,0:T(8,128)}, f32[136,512]{1,0:T(8,128)S(1)}, u32[]{:S(2)}, u32[]{:S(2)}) %collective-permute-start.2) | collective-permute-done | bytes 278560 | tf_op jit(solution)/shard_map/ppermute | solution.py:569
  33.3 0.1 multiply_add_fusion.1
  33.6 1.6 %collective-permute-start.5 = (f32[128,512]{1,0:T(8,128)S(1)}, f32[128,512]{1,0:T(8,128)S(1)}, u32[]{:S(2)}, u32[]{:S(2)}) collective-permute-start(f32[128,512]{1,0:T(8,128)S(1)} %get-tuple-element.116), channel_id=1, source_target_pairs={{8,24},{12,28},{16,0},{20,4},{9,25},{13,29},{17,1},{21,5},{10,26},... | collective-permute-start | bytes 786440 | tf_op jit(solution)/shard_map/ppermute | solution.py:574
  35.1 0.8 collective-permute-start.4
  35.9 1.3 %collective-permute-start.8 = (f32[128,512]{1,0:T(8,128)S(1)}, f32[128,512]{1,0:T(8,128)S(1)}, u32[]{:S(2)}, u32[]{:S(2)}) collective-permute-start(f32[128,512]{1,0:T(8,128)S(1)} %get-tuple-element.117), channel_id=1, source_target_pairs={{0,4},{4,0},{8,12},{12,8},{16,20},{20,16},{24,28},{28,24},{1,5},{5... | collective-permute-start | bytes 786440 | tf_op jit(solution)/shard_map/ppermute | solution.py:578
  37.2 5.2 %collective-permute-done = f32[264,512]{1,0:T(8,128)} collective-permute-done((f32[264,512]{1,0:T(8,128)}, f32[264,512]{1,0:T(8,128)}, u32[]{:S(2)}, u32[]{:S(2)}) %collective-permute-start) | collective-permute-done | bytes 540704 | tf_op jit(solution)/shard_map/ppermute | solution.py:561
  42.4 0.7 fusion
  43.1 1.2 %broadcast_select_fusion = (f32[128,512]{1,0:T(8,128)S(1)}, f32[128,512]{1,0:T(8,128)S(1)}, f32[128,512]{1,0:T(8,128)S(1)}, f32[128,512]{1,0:T(8,128)S(1)}, f32[128,512]{1,0:T(8,128)S(1)}) fusion(pred[]{:T(512)S(6)} %or.9, f32[512]{0:T(512)S(1)} %bitcast.65, f32[264,512]{1,0:T(8,128)S(1)} %copy-done.16, f32[264,512]{1,0:T(8,128)} %collective-permute-done, ...), kind=kLoop, calls=%fused_computation.22 | loop fusion | flops 589824 | bytes 2363394 | tf_op jit(solution)/shard_map/jit(_where)/select_n | solution.py:551
  44.4 0.8 collective-permute-start.3
  45.2 0.2 broadcast_select_fusion.5
  45.4 0.1 broadcast_select_fusion.8
  45.4 0.9 collective-permute-start.9
  46.3 4.7 %collective-permute-done.3 = f32[136,512]{1,0:T(8,128)S(1)} collective-permute-done((f32[136,512]{1,0:T(8,128)S(1)}, f32[136,512]{1,0:T(8,128)S(1)}, u32[]{:S(2)}, u32[]{:S(2)}) %collective-permute-start.3) | collective-permute-done | bytes 278560 | tf_op jit(solution)/shard_map/ppermute | solution.py:569
  51.0 0.1 broadcast_select_fusion.4
  51.1 1.3 %collective-permute-start.7 = (f32[128,512]{1,0:T(8,128)S(1)}, f32[128,512]{1,0:T(8,128)S(1)}, u32[]{:S(2)}, u32[]{:S(2)}) collective-permute-start(f32[128,512]{1,0:T(8,128)S(1)} %get-tuple-element.115), channel_id=1, source_target_pairs={{8,24},{12,28},{16,0},{20,4},{9,25},{13,29},{17,1},{21,5},{10,26},... | collective-permute-start | bytes 786440 | tf_op jit(solution)/shard_map/ppermute | solution.py:574
  52.4 0.9 collective-permute-start.6
  53.3 0.1 pad_add_fusion.refs_0_
  53.4 1.5 %collective-permute-start.10 = (f32[128,512]{1,0:T(8,128)S(1)}, f32[128,512]{1,0:T(8,128)S(1)}, u32[]{:S(2)}, u32[]{:S(2)}) collective-permute-start(f32[128,512]{1,0:T(8,128)S(1)} %get-tuple-element.114), channel_id=1, source_target_pairs={{0,4},{4,0},{8,12},{12,8},{16,20},{20,16},{24,28},{28,24},{1,5},{5... | collective-permute-start | bytes 786440 | tf_op jit(solution)/shard_map/ppermute | solution.py:578
  55.1 6.7 %local_grads.3 = (bf16[1024,2048]{1,0:T(8,128)(2,1)}, f32[1024,128]{1,0:T(8,128)S(1)}, f32[1024,128]{1,0:T(8,128)S(1)}, f32[4,8,1024]{2,1,0:T(8,128)}, f32[8,128]{1,0:T(8,128)S(1)}) custom-call(s32[2]{0:T(128)S(1)} %pad_add_fusion.refs_0_, bf16[1024,2048]{1,0:T(8,128)(2,1)S(1)} %copy-done, bf16[1024,2048]{1,0:T(8,128)(2,1)S(1)} %copy-done.1, ...), custom_call_target="tpu_custom_call" | custom-call | flops 2415919104 | bytes 3145728 | tf_op jit(solution)/shard_map/local_grads/pallas_call | solution.py:480
  61.7 1.4 %collective-permute-done.7 = f32[128,512]{1,0:T(8,128)S(1)} collective-permute-done((f32[128,512]{1,0:T(8,128)S(1)}, f32[128,512]{1,0:T(8,128)S(1)}, u32[]{:S(2)}, u32[]{:S(2)}) %collective-permute-start.7) | collective-permute-done | bytes 262176 | tf_op jit(solution)/shard_map/ppermute | solution.py:574
  63.1 0.2 broadcast_select_fusion.2
  63.3 0.7 collective-permute-start.11
  63.9 8.5 %local_grads.4 = (bf16[1024,2048]{1,0:T(8,128)(2,1)}, f32[1024,128]{1,0:T(8,128)S(1)}, f32[1024,128]{1,0:T(8,128)S(1)}, f32[4,8,1024]{2,1,0:T(8,128)}, f32[8,128]{1,0:T(8,128)S(1)}) custom-call(s32[2]{0:T(128)S(1)} %pad_add_fusion.refs_0_, bf16[1024,2048]{1,0:T(8,128)(2,1)S(1)} %copy-done, ...), custom_call_target="tpu_custom_call", output_to_operand_aliasing={{0}: (24, {}), {3}: (25, {})} | custom-call | flops 2415919104 | bytes 3145728 | tf_op jit(solution)/shard_map/local_grads/pallas_call | solution.py:480
  72.4 0.1 broadcast_select_fusion.3.refs_18_
  72.6 13.3 %local_grads.5 = (bf16[1024,2048]{1,0:T(8,128)(2,1)}, f32[1024,128]{1,0:T(8,128)}, f32[1024,128]{1,0:T(8,128)}, f32[4,8,1024]{2,1,0:T(8,128)}, f32[8,128]{1,0:T(8,128)S(1)}) custom-call(s32[2]{0:T(128)S(1)} %pad_add_fusion.refs_0_, bf16[1024,2048]{1,0:T(8,128)(2,1)S(1)} %copy-done, ...), custom_call_target="tpu_custom_call", output_to_operand_aliasing={{0}: (24, {}), {3}: (25, {})} | custom-call | flops 4831838208 | bytes 6291456 | tf_op jit(solution)/shard_map/local_grads/pallas_call | solution.py:480
  85.8 0.1 collective-permute-start.14
  85.9 1.6 %collective-permute-start.13 = (f32[8,128]{1,0:T(8,128)S(1)}, f32[8,128]{1,0:T(8,128)S(1)}, u32[]{:S(2)}, u32[]{:S(2)}) collective-permute-start(f32[8,128]{1,0:T(8,128)S(1)} %get-tuple-element.91), channel_id=1, source_target_pairs={{0,2},{1,3},{2,0},{3,1},{4,6},{5,7},{6,4},{7,5},{8,10},{9,11},{10,... | collective-permute-start | bytes 12296 | tf_op jit(solution)/shard_map/ppermute | solution.py:523
  87.5 0.3 collective-permute-start.12
  87.8 1.2 %collective-permute-done.14 = f32[8,128]{1,0:T(8,128)S(1)} collective-permute-done((f32[8,128]{1,0:T(8,128)S(1)}, f32[8,128]{1,0:T(8,128)S(1)}, u32[]{:S(2)}, u32[]{:S(2)}) %collective-permute-start.14) | collective-permute-done | bytes 4128 | tf_op jit(solution)/shard_map/ppermute | solution.py:523
  88.9 0.7 collective-permute-done.13
  89.6 5.0 %collective-permute-start.17 = (f32[8,128]{1,0:T(8,128)S(1)}, f32[8,128]{1,0:T(8,128)S(1)}, u32[]{:S(2)}, u32[]{:S(2)}) collective-permute-start(f32[8,128]{1,0:T(8,128)S(1)} %add_add_fusion.1), channel_id=1, source_target_pairs={{0,12},{4,8},{8,4},{12,0},{16,28},{20,24},{24,20},{28,16},{1,13},{... | collective-permute-start | bytes 12296 | tf_op jit(solution)/shard_map/ppermute | solution.py:523
  94.5 0.6 collective-permute-start.15
  95.2 0.9 collective-permute-done.17
  96.1 2.0 %collective-permute-done.16 = f32[8,128]{1,0:T(8,128)S(1)} collective-permute-done((f32[8,128]{1,0:T(8,128)S(1)}, f32[8,128]{1,0:T(8,128)S(1)}, u32[]{:S(2)}, u32[]{:S(2)}) %collective-permute-start.16) | collective-permute-done | bytes 4128 | tf_op jit(solution)/shard_map/ppermute | solution.py:523
  98.2 3.0 %collective-permute-start.18 = (f32[8,128]{1,0:T(8,128)S(1)}, f32[8,128]{1,0:T(8,128)S(1)}, u32[]{:S(2)}, u32[]{:S(2)}) collective-permute-start(f32[8,128]{1,0:T(8,128)S(1)} %add_add_fusion), channel_id=1, source_target_pairs={{0,16},{4,20},{8,24},{12,28},{16,0},{20,4},{24,8},{28,12},{1,17},{... | collective-permute-start | bytes 12296 | tf_op jit(solution)/shard_map/ppermute | solution.py:523
  101.2 1.6 %collective-permute-done.18 = f32[8,128]{1,0:T(8,128)S(1)} collective-permute-done((f32[8,128]{1,0:T(8,128)S(1)}, f32[8,128]{1,0:T(8,128)S(1)}, u32[]{:S(2)}, u32[]{:S(2)}) %collective-permute-start.18) | collective-permute-done | bytes 4128 | tf_op jit(solution)/shard_map/ppermute | solution.py:523
  102.8 0.5 slice_bitcast_fusion
  103.3 0.6 slice.52
  (52 shorter events, 0.2 us)
Async XLA Ops:
  6.7 15.5 %collective-permute-start.1 = (f32[264,512]{1,0:T(8,128)}, f32[264,512]{1,0:T(8,128)S(1)}, u32[]{:S(2)}, u32[]{:S(2)}) collective-permute-start(f32[264,512]{1,0:T(8,128)} %get-tuple-element.66), channel_id=1, source_target_pairs={{0,4},{4,0},{8,12},{12,8},{16,20},{20,16},{24,28},{28,24},{1,5},{5... | collective-permute-start | bytes 1622024 | tf_op jit(solution)/shard_map/ppermute | solution.py:561
  22.1 20.4 %copy-start.16 = (f32[264,512]{1,0:T(8,128)S(1)}, f32[264,512]{1,0:T(8,128)}, u32[]{:S(2)}) copy-start(f32[264,512]{1,0:T(8,128)} %get-tuple-element.70) | copy-start | bytes 1622020
  23.0 31.9 %copy-start.8 = (bf16[1536,128]{1,0:T(8,128)(2,1)S(1)}, bf16[1536,128]{1,0:T(8,128)(2,1)}, u32[]{:S(2)}) copy-start(bf16[1536,128]{1,0:T(8,128)(2,1)} %constant.44.clone.refs_16_) | copy-start | bytes 1179652
  23.0 31.9 %copy-start.10 = (bf16[128,1024]{1,0:T(8,128)(2,1)S(1)}, bf16[128,1024]{1,0:T(8,128)(2,1)}, u32[]{:S(2)}) copy-start(bf16[128,1024]{1,0:T(8,128)(2,1)} %get-tuple-element.60.refs_12_) | copy-start | bytes 786436
  23.0 31.9 %copy-start.11 = (bf16[128,1024]{1,0:T(8,128)(2,1)S(1)}, bf16[128,1024]{1,0:T(8,128)(2,1)}, u32[]{:S(2)}) copy-start(bf16[128,1024]{1,0:T(8,128)(2,1)} %get-tuple-element.61.refs_13_) | copy-start | bytes 786436
  23.0 31.9 %copy-start.12 = (f32[1,32,1024]{2,1,0:T(8,128)S(1)}, f32[1,32,1024]{2,1,0:T(8,128)}, u32[]{:S(2)}) copy-start(f32[1,32,1024]{2,1,0:T(8,128)} %refs_5_.1) | copy-start | bytes 393220
  24.3 30.6 %copy-start.7 = (bf16[4,256,256]{2,1,0:T(8,128)(2,1)S(1)}, bf16[4,256,256]{2,1,0:T(8,128)(2,1)}, u32[]{:S(2)}) copy-start(bf16[4,256,256]{2,1,0:T(8,128)(2,1)} %get-tuple-element.63.refs_15_) | copy-start | bytes 1572868
  24.3 30.6 %copy-start.13 = (f32[8,2048]{1,0:T(8,128)S(1)}, f32[8,2048]{1,0:T(8,128)}, u32[]{:S(2)}) copy-start(f32[8,2048]{1,0:T(8,128)} %get-tuple-element.59.refs_4_) | copy-start | bytes 196612
  25.1 8.2 %collective-permute-start.2 = (f32[136,512]{1,0:T(8,128)}, f32[136,512]{1,0:T(8,128)S(1)}, u32[]{:S(2)}, u32[]{:S(2)}) collective-permute-start(f32[136,512]{1,0:T(8,128)} %pad_maximum_fusion), channel_id=1, source_target_pairs={{0,8},{4,12},{8,0},{12,4},{16,24},{20,28},{24,16},{28,20},{1,9},{5... | collective-permute-start | bytes 835592 | tf_op jit(solution)/shard_map/ppermute | solution.py:569
  26.9 15.5 %collective-permute-start = (f32[264,512]{1,0:T(8,128)}, f32[264,512]{1,0:T(8,128)}, u32[]{:S(2)}, u32[]{:S(2)}) collective-permute-start(f32[264,512]{1,0:T(8,128)} %get-tuple-element.64), channel_id=1, source_target_pairs={{0,4},{4,0},{8,12},{12,8},{16,20},{20,16},{24,28},{28,24},{1,5},{5... | collective-permute-start | bytes 1622024 | tf_op jit(solution)/shard_map/ppermute | solution.py:561
  33.3 21.6 %copy-start.1 = (bf16[1024,2048]{1,0:T(8,128)(2,1)S(1)}, bf16[1024,2048]{1,0:T(8,128)(2,1)}, u32[]{:S(2)}) copy-start(bf16[1024,2048]{1,0:T(8,128)(2,1)} %get-tuple-element.58.refs_2_) | copy-start | bytes 12582916
  33.5 21.5 %copy-start = (bf16[1024,2048]{1,0:T(8,128)(2,1)S(1)}, bf16[1024,2048]{1,0:T(8,128)(2,1)}, u32[]{:S(2)}) copy-start(bf16[1024,2048]{1,0:T(8,128)(2,1)} %get-tuple-element.57.refs_1_) | copy-start | bytes 12582916
  33.5 21.5 %copy-start.3 = (bf16[1,1024,128]{2,1,0:T(8,128)(2,1)S(1)}, bf16[1,1024,128]{2,1,0:T(8,128)(2,1)}, u32[]{:S(2)}) copy-start(bf16[1,1024,128]{2,1,0:T(8,128)(2,1)} %param.12) | copy-start | bytes 786436
  33.5 21.5 %copy-start.4 = (bf16[1,1024,128]{2,1,0:T(8,128)(2,1)S(1)}, bf16[1,1024,128]{2,1,0:T(8,128)(2,1)}, u32[]{:S(2)}) copy-start(bf16[1,1024,128]{2,1,0:T(8,128)(2,1)} %param.13) | copy-start | bytes 786436
  33.5 21.5 %copy-start.5 = (bf16[1024,128]{1,0:T(8,128)(2,1)S(1)}, bf16[1024,128]{1,0:T(8,128)(2,1)}, u32[]{:S(2)}) copy-start(bf16[1024,128]{1,0:T(8,128)(2,1)} %get-tuple-element.49.refs_5_.refs_7_) | copy-start | bytes 786436
  33.5 21.5 %copy-start.6 = (bf16[4,256,256]{2,1,0:T(8,128)(2,1)S(1)}, bf16[4,256,256]{2,1,0:T(8,128)(2,1)}, u32[]{:S(2)}) copy-start(bf16[4,256,256]{2,1,0:T(8,128)(2,1)} %get-tuple-element.62.refs_14_) | copy-start | bytes 1572868
  33.5 21.5 %copy-start.9 = (f32[16,2048]{1,0:T(8,128)S(1)}, f32[16,2048]{1,0:T(8,128)}, u32[]{:S(2)}) copy-start(f32[16,2048]{1,0:T(8,128)} %get-tuple-element.50.refs_6_.refs_8_) | copy-start | bytes 393220
  33.5 21.5 %copy-start.14 = (f32[32]{0:T(128)S(1)}, f32[32]{0:T(128)}, u32[]{:S(2)}) copy-start(f32[32]{0:T(128)} %param.15) | copy-start | bytes 388
  33.6 21.5 %copy-start.15 = (f32[32]{0:T(128)S(1)}, f32[32]{0:T(128)}, u32[]{:S(2)}) copy-start(f32[32]{0:T(128)} %param.16) | copy-start | bytes 388
  33.6 11.6 %collective-permute-start.5 = (f32[128,512]{1,0:T(8,128)S(1)}, f32[128,512]{1,0:T(8,128)S(1)}, u32[]{:S(2)}, u32[]{:S(2)}) collective-permute-start(f32[128,512]{1,0:T(8,128)S(1)} %get-tuple-element.116), channel_id=1, source_target_pairs={{8,24},{12,28},{16,0},{20,4},{9,25},{13,29},{17,1},{21,5},{10,26},... | collective-permute-start | bytes 786440 | tf_op jit(solution)/shard_map/ppermute | solution.py:574
  35.1 10.1 %collective-permute-start.4 = (f32[128,512]{1,0:T(8,128)S(1)}, f32[128,512]{1,0:T(8,128)S(1)}, u32[]{:S(2)}, u32[]{:S(2)}) collective-permute-start(f32[128,512]{1,0:T(8,128)S(1)} %get-tuple-element.116), channel_id=1, source_target_pairs={{8,16},{12,20},{16,8},{20,12},{9,17},{13,21},{17,9},{21,13},{10,18... | collective-permute-start | bytes 786440 | tf_op jit(solution)/shard_map/ppermute | solution.py:573
  35.9 19.0 %collective-permute-start.8 = (f32[128,512]{1,0:T(8,128)S(1)}, f32[128,512]{1,0:T(8,128)S(1)}, u32[]{:S(2)}, u32[]{:S(2)}) collective-permute-start(f32[128,512]{1,0:T(8,128)S(1)} %get-tuple-element.117), channel_id=1, source_target_pairs={{0,4},{4,0},{8,12},{12,8},{16,20},{20,16},{24,28},{28,24},{1,5},{5... | collective-permute-start | bytes 786440 | tf_op jit(solution)/shard_map/ppermute | solution.py:578
  44.4 6.6 %collective-permute-start.3 = (f32[136,512]{1,0:T(8,128)S(1)}, f32[136,512]{1,0:T(8,128)S(1)}, u32[]{:S(2)}, u32[]{:S(2)}) collective-permute-start(f32[136,512]{1,0:T(8,128)S(1)} %pad_maximum_fusion.1), channel_id=1, source_target_pairs={{0,8},{4,12},{8,0},{12,4},{16,24},{20,28},{24,16},{28,20},{1,9},{5... | collective-permute-start | bytes 835592 | tf_op jit(solution)/shard_map/ppermute | solution.py:569
  45.4 9.5 %collective-permute-start.9 = (f32[128,512]{1,0:T(8,128)S(1)}, f32[128,512]{1,0:T(8,128)S(1)}, u32[]{:S(2)}, u32[]{:S(2)}) collective-permute-start(f32[128,512]{1,0:T(8,128)S(1)} %broadcast_select_fusion.8), channel_id=1, source_target_pairs={{0,4},{4,0},{8,12},{12,8},{16,20},{20,16},{24,28},{28,24},{1,5},{5... | collective-permute-start | bytes 786440 | tf_op jit(solution)/shard_map/ppermute | solution.py:583
  51.1 12.0 %collective-permute-start.7 = (f32[128,512]{1,0:T(8,128)S(1)}, f32[128,512]{1,0:T(8,128)S(1)}, u32[]{:S(2)}, u32[]{:S(2)}) collective-permute-start(f32[128,512]{1,0:T(8,128)S(1)} %get-tuple-element.115), channel_id=1, source_target_pairs={{8,24},{12,28},{16,0},{20,4},{9,25},{13,29},{17,1},{21,5},{10,26},... | collective-permute-start | bytes 786440 | tf_op jit(solution)/shard_map/ppermute | solution.py:574
  52.4 10.7 %collective-permute-start.6 = (f32[128,512]{1,0:T(8,128)S(1)}, f32[128,512]{1,0:T(8,128)S(1)}, u32[]{:S(2)}, u32[]{:S(2)}) collective-permute-start(f32[128,512]{1,0:T(8,128)S(1)} %get-tuple-element.115), channel_id=1, source_target_pairs={{8,16},{12,20},{16,8},{20,12},{9,17},{13,21},{17,9},{21,13},{10,18... | collective-permute-start | bytes 786440 | tf_op jit(solution)/shard_map/ppermute | solution.py:573
  53.4 19.1 %collective-permute-start.10 = (f32[128,512]{1,0:T(8,128)S(1)}, f32[128,512]{1,0:T(8,128)S(1)}, u32[]{:S(2)}, u32[]{:S(2)}) collective-permute-start(f32[128,512]{1,0:T(8,128)S(1)} %get-tuple-element.114), channel_id=1, source_target_pairs={{0,4},{4,0},{8,12},{12,8},{16,20},{20,16},{24,28},{28,24},{1,5},{5... | collective-permute-start | bytes 786440 | tf_op jit(solution)/shard_map/ppermute | solution.py:578
  63.3 9.3 %collective-permute-start.11 = (f32[128,512]{1,0:T(8,128)S(1)}, f32[128,512]{1,0:T(8,128)S(1)}, u32[]{:S(2)}, u32[]{:S(2)}) collective-permute-start(f32[128,512]{1,0:T(8,128)S(1)} %get-tuple-element.92), channel_id=1, source_target_pairs={{0,4},{4,0},{8,12},{12,8},{16,20},{20,16},{24,28},{28,24},{1,5},{5... | collective-permute-start | bytes 786440 | tf_op jit(solution)/shard_map/ppermute | solution.py:583
  63.9 8.6 %copy-start.2 = (bf16[1024,2048]{1,0:T(8,128)(2,1)S(1)}, bf16[1024,2048]{1,0:T(8,128)(2,1)}, u32[]{:S(2)}) copy-start(bf16[1024,2048]{1,0:T(8,128)(2,1)} %get-tuple-element.58.refs_2_) | copy-start | bytes 12582916
  85.8 3.1 %collective-permute-start.14 = (f32[8,128]{1,0:T(8,128)S(1)}, f32[8,128]{1,0:T(8,128)S(1)}, u32[]{:S(2)}, u32[]{:S(2)}) collective-permute-start(f32[8,128]{1,0:T(8,128)S(1)} %get-tuple-element.91), channel_id=1, source_target_pairs={{0,3},{1,2},{2,1},{3,0},{4,7},{5,6},{6,5},{7,4},{8,11},{9,10},{10,... | collective-permute-start | bytes 12296 | tf_op jit(solution)/shard_map/ppermute | solution.py:523
  85.9 3.7 %collective-permute-start.13 = (f32[8,128]{1,0:T(8,128)S(1)}, f32[8,128]{1,0:T(8,128)S(1)}, u32[]{:S(2)}, u32[]{:S(2)}) collective-permute-start(f32[8,128]{1,0:T(8,128)S(1)} %get-tuple-element.91), channel_id=1, source_target_pairs={{0,2},{1,3},{2,0},{3,1},{4,6},{5,7},{6,4},{7,5},{8,10},{9,11},{10,... | collective-permute-start | bytes 12296 | tf_op jit(solution)/shard_map/ppermute | solution.py:523
  87.5 2.1 %collective-permute-start.12 = (f32[8,128]{1,0:T(8,128)S(1)}, f32[8,128]{1,0:T(8,128)S(1)}, u32[]{:S(2)}, u32[]{:S(2)}) collective-permute-start(f32[8,128]{1,0:T(8,128)S(1)} %get-tuple-element.91), channel_id=1, source_target_pairs={{0,1},{1,0},{2,3},{3,2},{4,5},{5,4},{6,7},{7,6},{8,9},{9,8},{10,11... | collective-permute-start | bytes 12296 | tf_op jit(solution)/shard_map/ppermute | solution.py:523
  89.6 6.5 %collective-permute-start.17 = (f32[8,128]{1,0:T(8,128)S(1)}, f32[8,128]{1,0:T(8,128)S(1)}, u32[]{:S(2)}, u32[]{:S(2)}) collective-permute-start(f32[8,128]{1,0:T(8,128)S(1)} %add_add_fusion.1), channel_id=1, source_target_pairs={{0,12},{4,8},{8,4},{12,0},{16,28},{20,24},{24,20},{28,16},{1,13},{... | collective-permute-start | bytes 12296 | tf_op jit(solution)/shard_map/ppermute | solution.py:523
  94.5 3.6 %collective-permute-start.16 = (f32[8,128]{1,0:T(8,128)S(1)}, f32[8,128]{1,0:T(8,128)S(1)}, u32[]{:S(2)}, u32[]{:S(2)}) collective-permute-start(f32[8,128]{1,0:T(8,128)S(1)} %add_add_fusion.1), channel_id=1, source_target_pairs={{0,8},{4,12},{8,0},{12,4},{16,24},{20,28},{24,16},{28,20},{1,9},{5... | collective-permute-start | bytes 12296 | tf_op jit(solution)/shard_map/ppermute | solution.py:523
  94.5 3.6 %collective-permute-start.15 = (f32[8,128]{1,0:T(8,128)S(1)}, f32[8,128]{1,0:T(8,128)S(1)}, u32[]{:S(2)}, u32[]{:S(2)}) collective-permute-start(f32[8,128]{1,0:T(8,128)S(1)} %add_add_fusion.1), channel_id=1, source_target_pairs={{0,4},{4,0},{8,12},{12,8},{16,20},{20,16},{24,28},{28,24},{1,5},{5... | collective-permute-start | bytes 12296 | tf_op jit(solution)/shard_map/ppermute | solution.py:523
  98.2 4.6 %collective-permute-start.18 = (f32[8,128]{1,0:T(8,128)S(1)}, f32[8,128]{1,0:T(8,128)S(1)}, u32[]{:S(2)}, u32[]{:S(2)}) collective-permute-start(f32[8,128]{1,0:T(8,128)S(1)} %add_add_fusion), channel_id=1, source_target_pairs={{0,16},{4,20},{8,24},{12,28},{16,0},{20,4},{24,8},{28,12},{1,17},{... | collective-permute-start | bytes 12296 | tf_op jit(solution)/shard_map/ppermute | solution.py:523

commit v8 on v6

--- a/solution.py
+++ b/solution.py
@@ -508,43 +508,27 @@
     token = yield message, got
     got = after(got, token)
     lower = place < pairs // 2
-    if pairs == 4:
-        message = message_of((place == 0) | (place == 2), got, None, 0)
-        (_, _), (_, _), (d1, d2) = halves(got, 0)
-        message = jnp.concatenate([message, jnp.broadcast_to(d1 * d2, (8, message.shape[1]))])
-        near = lax.ppermute(message, "seq", both([(0, 1), (1, 0), (2, 3), (3, 2)]))
-        token = yield message, near
-        near = after(near, token)
-        message = message_of(place == 1, got, near, 1)
-        middle = lax.ppermute(message, "seq", both([(1, 2), (2, 1)]))
-        far = lax.ppermute(message, "seq", both([(1, 3), (2, 0)]))
-        inside = (place == 1) | (place == 2)
-        known = jnp.where(inside, near[:states], 0.0)
-        mine_early, early = shares(lower, known, got, 2)
-        other_early = lax.ppermute(early, "seq", swap)
-        token = yield early, far
-        far = after(far, token)
-        outer = near[states : states + 1] * far + near[:states]
-        mine_late, late = shares(~lower, jnp.where(inside, middle, outer), got, 3)
-        other_late = lax.ppermute(late, "seq", swap)
-        yield late, other_late
-    else:
-        arrived = []
-        for k in range(1, pairs):
-            message = message_of(place == k - 1, got, arrived[-1] if arrived else None, min(k, 4))
-            routes = both([(k - 1, k), (pairs - k, pairs - k - 1)])
-            arrived.append(lax.ppermute(message, "seq", routes))
-            token = yield message, arrived[-1]
-            arrived[-1] = after(arrived[-1], token)
-        start = end = jnp.zeros_like(arrived[0])
-        for k in range(1, pairs):
-            start = jnp.where(place == k, arrived[k - 1], start)
-            end = jnp.where(place == pairs - 1 - k, arrived[k - 1], end)
-        mine_early, early = shares(lower, jnp.where(lower, start, end), got, 5)
-        mine_late, late = shares(~lower, jnp.where(lower, end, start), got, 6)
-        other_early = lax.ppermute(early, "seq", swap)
-        other_late = lax.ppermute(late, "seq", swap)
-        yield late, other_late
+    start = end = None
+    for k in range(1, pairs):
+        last = start if k == 1 else arrived
+        message = message_of(place == k - 1, got, last, 0)
+        routes = both([(k - 1, k), (pairs - k, pairs - k - 1)])
+        arriving = lax.ppermute(message, "seq", routes)
+        if k == pairs // 2:
+            known = jnp.where(lower, start, end)
+            mine_early, early = shares(lower, known, got, 0)
+            other_early = lax.ppermute(early, "seq", swap)
+        token = yield message, arriving
+        if k == pairs - 1:
+            arrived, other_early, _ = lax.optimization_barrier((arriving, other_early, token))
+        else:
+            arrived = after(arriving, token)
+        zero = jnp.zeros_like(arrived)
+        start = jnp.where(place == k, arrived, zero if start is None else start)
+        end = jnp.where(place == pairs - 1 - k, arrived, zero if end is None else end)
+    mine_late, late = shares(~lower, jnp.where(lower, end, start), got, 0)
+    other_late = lax.ppermute(late, "seq", swap)
+    yield late, other_late
     yield mine_early, mine_late, other_early, other_late
 
 
@@ -576,7 +560,7 @@
         sent += out
     kept, saved = local(y, 0, PARTS, saved)
 
-    transfers = 4 if size == 8 else size // 2 + 1
+    transfers = size // 2 + 1
     order = [(0, 0), (1, 0)] + [
         pick for k in range(1, transfers) for pick in ((0, k), (1, k - 1)) if pick != (1, 0)
     ]

time: 101 us -> 113 us (1.12)
  other arithmetic: 5.01 us -> 12.5 us
  local copies, waits for them, and re-layouts: 1.19 us -> 3.4 us
  waiting for transfers between devices: 20.7 us -> 22.2 us
    ppermute x6, starting transfers between devices: 8.4 us -> 16.1 us  [entering(): arriving = lax.ppermute(message, 'seq', routes)]
    ppermute x7, starting transfers between devices: 12.8 us -> 6.9 us  [summed_over(): lax.ppermute(value, axis, [(i, i ^ s) for i in range(size)])]
    ppermute x2, waiting for transfers between devices: 0.01 us -> 4.04 us  [entering(): other_late = lax.ppermute(late, 'seq', swap)]
    ppermute x6, waiting for transfers between devices: 9.16 us -> 5.74 us  [entering(): arriving = lax.ppermute(message, 'seq', routes)]
    select_n x3, other arithmetic: 0.46 us -> 3.62 us  [shares(): jnp.where(second, for_first, for_second)]
    ppermute x2, waiting for transfers between devices: 5.63 us -> 2.63 us  [entering(): got = lax.ppermute(message, 'seq', swap)]
    select_n x2, other arithmetic: 1.31 us -> 3.69 us  [message_of(): message = jnp.where(up, d2 * l1 + l2, k1 + d1 * k2)]
    unnamed x38 -> x52, local copies, waits for them, and re-layouts: 0.1 us -> 2.32 us
  transfers between devices with their start and end apart: 19 -> 19, of which waited for: 11 -> 11; matrix products, arithmetic and copies ran while one was open for 2% -> 10% of each run, Pallas kernels for 26% -> 23%
where the time goes in v8:
time: 113 us; the launch traced here: 112 us
  Pallas kernels  42.9 us (38%)
  starting transfers between devices  30.1 us (27%)
  waiting for transfers between devices  22.2 us (20%)
  other arithmetic  12.5 us (11%)
  local copies, waits for them, and re-layouts  3.4 us (3%)
    pallas_call x3, Pallas kernels, local_grads(): pl.pallas_call(functools.partial(grads_kernel, first, scale, part, half,...  27.7 us
    ppermute x6, starting transfers between devices, entering(): arriving = lax.ppermute(message, 'seq', routes)  16.1 us
    pallas_call x3, Pallas kernels, local_states(): pl.pallas_call(functools.partial(local_kernel, first, last, count), grid_...  15.2 us
    ppermute x7, waiting for transfers between devices, summed_over(): lax.ppermute(value, axis, [(i, i ^ s) for i in range(size)])  7.84 us
    ppermute x7, starting transfers between devices, summed_over(): lax.ppermute(value, axis, [(i, i ^ s) for i in range(size)])  6.9 us
    ppermute x6, waiting for transfers between devices, entering(): arriving = lax.ppermute(message, 'seq', routes)  5.74 us
    ppermute x2, waiting for transfers between devices, entering(): other_late = lax.ppermute(late, 'seq', swap)  4.04 us
    select_n x2, other arithmetic, message_of(): message = jnp.where(up, d2 * l1 + l2, k1 + d1 * k2)  3.69 us
  transfers between devices with their start and end apart: 19, of which 11 were waited for; matrix products, arithmetic and copies ran while one was open for 10% of the time, Pallas kernels for 23%

profile of v8, /device:TPU:0, one launch (start us, length us, event | category | flops | bytes accessed | tf_op | source)
XLA Modules:
  0.0 112.1 jit_solution(9117274242998476635)
XLA Ops:
  0.6 4.6 %local_states.3 = (f32[264,512]{1,0:T(8,128)}, bf16[1024,2048]{1,0:T(8,128)(2,1)}, bf16[1024,2048]{1,0:T(8,128)(2,1)}, f32[8,2048]{1,0:T(8,128)}, bf16[1024,128]{1,0:T(8,128)(2,1)}, /*index=5*/f32[16,2048]{1,0:T(8,128)}) custom-call(s32[1]{0:T(128)} %bitcast.7.refs_0_, bf16[1024,2048]{1,0:T(8,128)(2,1)} %bitcast.54, bf16[1024,2048]{1,0:T(8,128)(2,1)} %bitcast.48, ...), custom_call_target="tpu_custom_call" | custom-call | flops 536870912 | bytes 4194304 | tf_op jit(solution)/shard_map/local_states/pallas_call | solution.py:246
  5.2 3.0 %collective-permute-start.1 = (f32[264,512]{1,0:T(8,128)}, f32[264,512]{1,0:T(8,128)S(1)}, u32[]{:S(2)}, u32[]{:S(2)}) collective-permute-start(f32[264,512]{1,0:T(8,128)} %get-tuple-element.70), channel_id=1, source_target_pairs={{0,4},{4,0},{8,12},{12,8},{16,20},{20,16},{24,28},{28,24},{1,5},{5... | collective-permute-start | bytes 1622024 | tf_op jit(solution)/shard_map/ppermute | solution.py:507
  8.2 3.8 %local_states.4 = (f32[264,512]{1,0:T(8,128)}, bf16[1024,2048]{1,0:T(8,128)(2,1)}, bf16[1024,2048]{1,0:T(8,128)(2,1)}, f32[8,2048]{1,0:T(8,128)}) custom-call(s32[1]{0:T(128)} %bitcast.11.refs_0_, bf16[1024,2048]{1,0:T(8,128)(2,1)} %bitcast.55, bf16[1024,2048]{1,0:T(8,128)(2,1)} %bitcast.49, ...), custom_call_target="tpu_custom_call", output_to_operand_aliasing={{1}: (7, {}), {2}: (8, {}), {3}: (9, {})} | custom-call | flops 536870912 | bytes 4194304 | tf_op jit(solution)/shard_map/local_states/pallas_call | solution.py:246
  12.0 6.8 %local_states.5 = (f32[264,512]{1,0:T(8,128)}, f32[264,512]{1,0:T(8,128)}, bf16[1024,2048]{1,0:T(8,128)(2,1)}, bf16[1024,2048]{1,0:T(8,128)(2,1)}, f32[8,2048]{1...) custom-call(s32[1]{0:T(128)} %bitcast.2.refs_0_, ...), custom_call_target="tpu_custom_call", output_to_operand_aliasing={{2}: (7, {}), {3}: (8, {}), {4}: (9, {})} | custom-call | flops 1073741824 | bytes 8388608 | tf_op jit(solution)/shard_map/local_states/pallas_call | solution.py:246
  18.9 2.6 %collective-permute-done.1 = f32[264,512]{1,0:T(8,128)S(1)} collective-permute-done((f32[264,512]{1,0:T(8,128)}, f32[264,512]{1,0:T(8,128)S(1)}, u32[]{:S(2)}, u32[]{:S(2)}) %collective-permute-start.1) | collective-permute-done | bytes 540704 | tf_op jit(solution)/shard_map/ppermute | solution.py:507
  21.5 0.7 fusion.1
  22.2 1.2 %broadcast_select_fusion.1 = (f32[128,512]{1,0:T(8,128)S(1)}, f32[128,512]{1,0:T(8,128)S(1)}, f32[128,512]{1,0:T(8,128)S(1)}, f32[128,512]{1,0:T(8,128)S(1)}, f32[128,512]{1,0:T(8,128)S(1)}) fusion(pred[]{:T(512)S(6)} %eq.16, f32[512]{0:T(512)S(1)} %bitcast.67, f32[264,512]{1,0:T(8,128)} %get-tuple-element.69, f32[264,512]{1,0:T(8,128)S(1)} %collective-permute-done.1, ...), kind=kLoop, calls=%fused_computation.25 | loop fusion | flops 589824 | bytes 2363394 | tf_op jit(solution)/shard_map/jit(_where)/select_n | solution.py:497
  23.5 4.0 %collective-permute-start.2 = (f32[128,512]{1,0:T(8,128)S(1)}, f32[128,512]{1,0:T(8,128)S(1)}, u32[]{:S(2)}, u32[]{:S(2)}) collective-permute-start(f32[128,512]{1,0:T(8,128)S(1)} %get-tuple-element.115), channel_id=1, source_target_pairs={{0,8},{4,12},{24,16},{28,20},{1,9},{5,13},{25,17},{29,21},{2,10},{... | collective-permute-start | bytes 786440 | tf_op jit(solution)/shard_map/ppermute | solution.py:516
  27.6 3.8 %collective-permute-done.2 = f32[128,512]{1,0:T(8,128)S(1)} collective-permute-done((f32[128,512]{1,0:T(8,128)S(1)}, f32[128,512]{1,0:T(8,128)S(1)}, u32[]{:S(2)}, u32[]{:S(2)}) %collective-permute-start.2) | collective-permute-done | bytes 262176 | tf_op jit(solution)/shard_map/ppermute | solution.py:516
  31.4 1.0 broadcast_select_fusion.5
  32.4 1.4 %collective-permute-start.4 = (f32[128,512]{1,0:T(8,128)}, f32[128,512]{1,0:T(8,128)}, u32[]{:S(2)}, u32[]{:S(2)}) collective-permute-start(f32[128,512]{1,0:T(8,128)} %get-tuple-element.123), channel_id=1, source_target_pairs={{8,16},{12,20},{16,8},{20,12},{9,17},{13,21},{17,9},{21,13},{10,18... | collective-permute-start | bytes 786440 | tf_op jit(solution)/shard_map/ppermute | solution.py:516
  33.8 0.7 fusion
  34.7 2.5 %broadcast_select_fusion = (f32[128,512]{1,0:T(8,128)}, f32[128,512]{1,0:T(8,128)}, f32[128,512]{1,0:T(8,128)}, f32[128,512]{1,0:T(8,128)}, f32[128,512]{1,0:T(8,128)}) fusion(pred[]{:T(512)S(6)} %eq.16, f32[512]{0:T(512)S(1)} %bitcast.59, f32[264,512]{1,0:T(8,128)} %get-tuple-element.74, f32[264,512]{1,0:T(8,128)} %copy-done.25, pred[]{:T(512)S(6)} %eq.14, ...), kind=kLoop, calls=%fused_computation.24 | loop fusion | flops 589824 | bytes 2363394 | tf_op jit(solution)/shard_map/jit(_where)/select_n | solution.py:497
  37.2 7.2 %collective-permute-start.3 = (f32[128,512]{1,0:T(8,128)}, f32[128,512]{1,0:T(8,128)}, u32[]{:S(2)}, u32[]{:S(2)}) collective-permute-start(f32[128,512]{1,0:T(8,128)} %get-tuple-element.107), channel_id=1, source_target_pairs={{0,8},{4,12},{24,16},{28,20},{1,9},{5,13},{25,17},{29,21},{2,10},{... | collective-permute-start | bytes 786440 | tf_op jit(solution)/shard_map/ppermute | solution.py:516
  44.4 1.5 %collective-permute-start.7 = (f32[128,512]{1,0:T(8,128)}, f32[128,512]{1,0:T(8,128)S(1)}, u32[]{:S(2)}, u32[]{:S(2)}) collective-permute-start(f32[128,512]{1,0:T(8,128)} %get-tuple-element.122), channel_id=1, source_target_pairs={{0,4},{4,0},{8,12},{12,8},{16,20},{20,16},{24,28},{28,24},{1,5},{5... | collective-permute-start | bytes 786440 | tf_op jit(solution)/shard_map/ppermute | solution.py:520
  45.9 1.1 multiply_add_fusion.2
  47.0 1.3 %collective-permute-start.6 = (f32[128,512]{1,0:T(8,128)S(1)}, f32[128,512]{1,0:T(8,128)S(1)}, u32[]{:S(2)}, u32[]{:S(2)}) collective-permute-start(f32[128,512]{1,0:T(8,128)S(1)} %multiply_add_fusion.2), channel_id=1, source_target_pairs={{16,24},{20,28},{8,0},{12,4},{17,25},{21,29},{9,1},{13,5},{18,26},... | collective-permute-start | bytes 786440 | tf_op jit(solution)/shard_map/ppermute | solution.py:516
  48.3 1.3 %broadcast_select_fusion.6 = (f32[128,512]{1,0:T(8,128)S(1)}, f32[128,512]{1,0:T(8,128)S(1)}) fusion(pred[]{:T(512)S(6)} %eq.14, f32[128,512]{1,0:T(8,128)} %get-tuple-element.111, f32[128,512]{1,0:T(8,128)} %collective-permute-done.3, pred[]{:T(512)S(6)} %eq.17, pred[]{:T(512)S(6)} %eq.15, f32[512]{0:T(512)S(1)} %bitcast.60, pred[]{:T(512)S(6)} %lt.19, ...), kind=kLoop, calls=%fused_computation.30 | loop fusion | flops 851968 | bytes 1841156 | tf_op jit(solution)/shard_map/jit(_where)/select_n | solution.py:504
  49.7 1.1 %collective-permute-start.9 = (f32[128,512]{1,0:T(8,128)S(1)}, f32[128,512]{1,0:T(8,128)S(1)}, u32[]{:S(2)}, u32[]{:S(2)}) collective-permute-start(f32[128,512]{1,0:T(8,128)S(1)} %get-tuple-element.124), channel_id=1, source_target_pairs={{0,4},{4,0},{8,12},{12,8},{16,20},{20,16},{24,28},{28,24},{1,5},{5... | collective-permute-start | bytes 786440 | tf_op jit(solution)/shard_map/ppermute | solution.py:520
  50.8 0.7 collective-permute-start.5
  51.5 1.9 %collective-permute-done.7.refs_19_ = f32[128,512]{1,0:T(8,128)S(1)} collective-permute-done((f32[128,512]{1,0:T(8,128)}, f32[128,512]{1,0:T(8,128)S(1)}, u32[]{:S(2)}, u32[]{:S(2)}) %collective-permute-start.7) | collective-permute-done | bytes 262176 | tf_op jit(solution)/shard_map/ppermute | solution.py:520
  53.4 1.9 %collective-permute-done.6 = f32[128,512]{1,0:T(8,128)S(1)} collective-permute-done((f32[128,512]{1,0:T(8,128)S(1)}, f32[128,512]{1,0:T(8,128)S(1)}, u32[]{:S(2)}, u32[]{:S(2)}) %collective-permute-start.6) | collective-permute-done | bytes 262176 | tf_op jit(solution)/shard_map/ppermute | solution.py:516
  55.3 1.3 %broadcast_select_fusion.4 = (f32[128,512]{1,0:T(8,128)S(1)}, f32[128,512]{1,0:T(8,128)S(1)}) fusion(pred[]{:T(512)S(6)} %eq.14, f32[128,512]{1,0:T(8,128)} %copy-done.18, f32[512]{0:T(512)S(1)} %bitcast.73, pred[]{:T(512)S(6)} %not.4, f32[128,512]{1,0:T(8,128)} %copy-done.19, f32[512]{0:T(512)S(1)} %bitcast.69, f32[128,512]{1,0:T(8,128)S(1)} %collective-permute-done.6, ...), kind=kLoop, calls=%fused_computation.28 | loop fusion | flops 917504 | bytes 1839111 | tf_op jit(solution)/shard_map/jit(_where)/select_n | solution.py:504
  56.6 1.1 %broadcast_select_fusion.7 = f32[128,512]{1,0:T(8,128)S(1)} fusion(pred[]{:T(512)S(6)} %eq.14, f32[128,512]{1,0:T(8,128)S(1)} %get-tuple-element.103, f32[128,512]{1,0:T(8,128)} %copy-done.18, f32[512]{0:T(512)S(1)} %bitcast.74, pred[]{:T(512)S(6)} %not.4, f32[128,512]{1,0:T(8,128)} %copy-done.19, f32[512]{0:T(512)S(1)} %bitcast.70), kind=kLoop, calls=%fused_computation.31 | loop fusion | flops 458752 | bytes 1052674 | tf_op jit(solution)/shard_map/jit(_where)/select_n | solution.py:504
  57.8 0.7 collective-permute-start.10
  58.6 1.5 %collective-permute-start.8 = (f32[128,512]{1,0:T(8,128)S(1)}, f32[128,512]{1,0:T(8,128)S(1)}, u32[]{:S(2)}, u32[]{:S(2)}) collective-permute-start(f32[128,512]{1,0:T(8,128)S(1)} %multiply_add_fusion), channel_id=1, source_target_pairs={{16,24},{20,28},{8,0},{12,4},{17,25},{21,29},{9,1},{13,5},{18,26},... | collective-permute-start | bytes 786440 | tf_op jit(solution)/shard_map/ppermute | solution.py:516
  60.2 4.0 %collective-permute-done.10.refs_20_ = f32[128,512]{1,0:T(8,128)S(1)} collective-permute-done((f32[128,512]{1,0:T(8,128)S(1)}, f32[128,512]{1,0:T(8,128)S(1)}, u32[]{:S(2)}, u32[]{:S(2)}) %collective-permute-start.10) | collective-permute-done | bytes 262176 | tf_op jit(solution)/shard_map/ppermute | solution.py:530
  64.3 2.2 %copy-done.1 = bf16[1024,2048]{1,0:T(8,128)(2,1)S(1)} copy-done((bf16[1024,2048]{1,0:T(8,128)(2,1)S(1)}, bf16[1024,2048]{1,0:T(8,128)(2,1)}, u32[]{:S(2)}) %copy-start.1) | copy-done | bytes 4194328
  66.5 7.1 %local_grads.3 = (bf16[1024,2048]{1,0:T(8,128)(2,1)}, f32[1024,128]{1,0:T(8,128)S(1)}, f32[1024,128]{1,0:T(8,128)S(1)}, f32[4,8,1024]{2,1,0:T(8,128)}, f32[8,128]{1,0:T(8,128)S(1)}) custom-call(s32[2]{0:T(128)S(1)} %pad_add_fusion.refs_0_, bf16[1024,2048]{1,0:T(8,128)(2,1)S(1)} %copy-done, bf16[1024,2048]{1,0:T(8,128)(2,1)S(1)} %copy-done.1, ...), custom_call_target="tpu_custom_call" | custom-call | flops 2415919104 | bytes 3145728 | tf_op jit(solution)/shard_map/local_grads/pallas_call | solution.py:426
  73.6 1.1 %broadcast_select_fusion.2 = (f32[128,512]{1,0:T(8,128)S(1)}, f32[128,512]{1,0:T(8,128)S(1)}, f32[128,512]{1,0:T(8,128)S(1)}) fusion(pred[]{:T(512)S(6)} %eq.14, f32[128,512]{1,0:T(8,128)S(1)} %copy-done.17, f32[512]{0:T(512)S(1)} %bitcast.61, pred[]{:T(512)S(6)} %not.4, f32[128,512]{1,0:T(8,128)S(1)} %copy-done.16, f32[512]{0:T(512)S(1)} %bitcast.65, ...), kind=kLoop, calls=%fused_computation.26 | loop fusion | flops 1441792 | bytes 2101255 | tf_op jit(solution)/shard_map/jit(_where)/select_n | solution.py:504
  74.8 0.8 collective-permute-start.11
  75.5 8.3 %local_grads.4 = (bf16[1024,2048]{1,0:T(8,128)(2,1)}, f32[1024,128]{1,0:T(8,128)S(1)}, f32[1024,128]{1,0:T(8,128)S(1)}, f32[4,8,1024]{2,1,0:T(8,128)}, f32[8,128]{1,0:T(8,128)S(1)}) custom-call(s32[2]{0:T(128)S(1)} %pad_add_fusion.refs_0_, bf16[1024,2048]{1,0:T(8,128)(2,1)S(1)} %copy-done, ...), custom_call_target="tpu_custom_call", output_to_operand_aliasing={{0}: (24, {}), {3}: (25, {})} | custom-call | flops 2415919104 | bytes 3145728 | tf_op jit(solution)/shard_map/local_grads/pallas_call | solution.py:426
  83.9 0.1 broadcast_select_fusion.3.refs_18_
  84.0 12.3 %local_grads.5 = (bf16[1024,2048]{1,0:T(8,128)(2,1)}, f32[1024,128]{1,0:T(8,128)}, f32[1024,128]{1,0:T(8,128)}, f32[4,8,1024]{2,1,0:T(8,128)}, f32[8,128]{1,0:T(8,128)S(1)}) custom-call(s32[2]{0:T(128)S(1)} %pad_add_fusion.refs_0_, bf16[1024,2048]{1,0:T(8,128)(2,1)S(1)} %copy-done, ...), custom_call_target="tpu_custom_call", output_to_operand_aliasing={{0}: (24, {}), {3}: (25, {})} | custom-call | flops 4831838208 | bytes 6291456 | tf_op jit(solution)/shard_map/local_grads/pallas_call | solution.py:426
  96.3 1.6 %collective-permute-start.13 = (f32[8,128]{1,0:T(8,128)S(1)}, f32[8,128]{1,0:T(8,128)S(1)}, u32[]{:S(2)}, u32[]{:S(2)}) collective-permute-start(f32[8,128]{1,0:T(8,128)S(1)} %get-tuple-element.99), channel_id=1, source_target_pairs={{0,2},{1,3},{2,0},{3,1},{4,6},{5,7},{6,4},{7,5},{8,10},{9,11},{10,... | collective-permute-start | bytes 12296 | tf_op jit(solution)/shard_map/ppermute | solution.py:469
  97.9 0.3 collective-permute-start.12
  98.2 1.2 %collective-permute-done.14 = f32[8,128]{1,0:T(8,128)S(1)} collective-permute-done((f32[8,128]{1,0:T(8,128)S(1)}, f32[8,128]{1,0:T(8,128)S(1)}, u32[]{:S(2)}, u32[]{:S(2)}) %collective-permute-start.14) | collective-permute-done | bytes 4128 | tf_op jit(solution)/shard_map/ppermute | solution.py:469
  99.3 0.7 collective-permute-done.13
  100.0 1.2 %collective-permute-start.17 = (f32[8,128]{1,0:T(8,128)S(1)}, f32[8,128]{1,0:T(8,128)S(1)}, u32[]{:S(2)}, u32[]{:S(2)}) collective-permute-start(f32[8,128]{1,0:T(8,128)S(1)} %add_add_fusion.1), channel_id=1, source_target_pairs={{0,12},{4,8},{8,4},{12,0},{16,28},{20,24},{24,20},{28,16},{1,13},{... | collective-permute-start | bytes 12296 | tf_op jit(solution)/shard_map/ppermute | solution.py:469
  101.3 1.6 %collective-permute-start.16 = (f32[8,128]{1,0:T(8,128)S(1)}, f32[8,128]{1,0:T(8,128)S(1)}, u32[]{:S(2)}, u32[]{:S(2)}) collective-permute-start(f32[8,128]{1,0:T(8,128)S(1)} %add_add_fusion.1), channel_id=1, source_target_pairs={{0,8},{4,12},{8,0},{12,4},{16,24},{20,28},{24,16},{28,20},{1,9},{5... | collective-permute-start | bytes 12296 | tf_op jit(solution)/shard_map/ppermute | solution.py:469
  102.9 0.7 collective-permute-start.15
  103.6 1.0 collective-permute-done.17
  104.6 0.3 collective-permute-done.16
  104.9 1.6 %collective-permute-done.15 = f32[8,128]{1,0:T(8,128)S(1)} collective-permute-done((f32[8,128]{1,0:T(8,128)S(1)}, f32[8,128]{1,0:T(8,128)S(1)}, u32[]{:S(2)}, u32[]{:S(2)}) %collective-permute-start.15) | collective-permute-done | bytes 4128 | tf_op jit(solution)/shard_map/ppermute | solution.py:469
  106.5 1.4 %collective-permute-start.18 = (f32[8,128]{1,0:T(8,128)S(1)}, f32[8,128]{1,0:T(8,128)S(1)}, u32[]{:S(2)}, u32[]{:S(2)}) collective-permute-start(f32[8,128]{1,0:T(8,128)S(1)} %add_add_fusion), channel_id=1, source_target_pairs={{0,16},{4,20},{8,24},{12,28},{16,0},{20,4},{24,8},{28,12},{1,17},{... | collective-permute-start | bytes 12296 | tf_op jit(solution)/shard_map/ppermute | solution.py:469
  107.9 3.1 %collective-permute-done.18 = f32[8,128]{1,0:T(8,128)S(1)} collective-permute-done((f32[8,128]{1,0:T(8,128)S(1)}, f32[8,128]{1,0:T(8,128)S(1)}, u32[]{:S(2)}, u32[]{:S(2)}) %collective-permute-start.18) | collective-permute-done | bytes 4128 | tf_op jit(solution)/shard_map/ppermute | solution.py:469
  111.0 0.5 slice_bitcast_fusion
  111.5 0.6 slice.40
  (66 shorter events, 0.4 us)
Async XLA Ops:
  5.2 16.3 %collective-permute-start.1 = (f32[264,512]{1,0:T(8,128)}, f32[264,512]{1,0:T(8,128)S(1)}, u32[]{:S(2)}, u32[]{:S(2)}) collective-permute-start(f32[264,512]{1,0:T(8,128)} %get-tuple-element.70), channel_id=1, source_target_pairs={{0,4},{4,0},{8,12},{12,8},{16,20},{20,16},{24,28},{28,24},{1,5},{5... | collective-permute-start | bytes 1622024 | tf_op jit(solution)/shard_map/ppermute | solution.py:507
  12.0 21.7 %collective-permute-start = (f32[264,512]{1,0:T(8,128)}, f32[264,512]{1,0:T(8,128)S(1)}, u32[]{:S(2)}, u32[]{:S(2)}) collective-permute-start(f32[264,512]{1,0:T(8,128)} %get-tuple-element.68), channel_id=1, source_target_pairs={{0,4},{4,0},{8,12},{12,8},{16,20},{20,16},{24,28},{28,24},{1,5},{5... | collective-permute-start | bytes 1622024 | tf_op jit(solution)/shard_map/ppermute | solution.py:507
  23.5 11.0 %copy-start.18 = (f32[128,512]{1,0:T(8,128)}, f32[128,512]{1,0:T(8,128)S(1)}, u32[]{:S(2)}) copy-start(f32[128,512]{1,0:T(8,128)S(1)} %get-tuple-element.117) | copy-start | bytes 786436
  23.5 11.0 %copy-start.19 = (f32[128,512]{1,0:T(8,128)}, f32[128,512]{1,0:T(8,128)S(1)}, u32[]{:S(2)}) copy-start(f32[128,512]{1,0:T(8,128)S(1)} %get-tuple-element.119) | copy-start | bytes 786436
  23.5 11.0 %copy-start.22 = (f32[128,512]{1,0:T(8,128)}, f32[128,512]{1,0:T(8,128)S(1)}, u32[]{:S(2)}) copy-start(f32[128,512]{1,0:T(8,128)S(1)} %get-tuple-element.116) | copy-start | bytes 786436
  23.5 11.0 %copy-start.23 = (f32[128,512]{1,0:T(8,128)}, f32[128,512]{1,0:T(8,128)S(1)}, u32[]{:S(2)}) copy-start(f32[128,512]{1,0:T(8,128)S(1)} %get-tuple-element.118) | copy-start | bytes 786436
  23.5 7.9 %collective-permute-start.2 = (f32[128,512]{1,0:T(8,128)S(1)}, f32[128,512]{1,0:T(8,128)S(1)}, u32[]{:S(2)}, u32[]{:S(2)}) collective-permute-start(f32[128,512]{1,0:T(8,128)S(1)} %get-tuple-element.115), channel_id=1, source_target_pairs={{0,8},{4,12},{24,16},{28,20},{1,9},{5,13},{25,17},{29,21},{2,10},{... | collective-permute-start | bytes 786440 | tf_op jit(solution)/shard_map/ppermute | solution.py:516
  31.4 3.1 %copy-start.24 = (f32[128,512]{1,0:T(8,128)}, f32[128,512]{1,0:T(8,128)S(1)}, u32[]{:S(2)}) copy-start(f32[128,512]{1,0:T(8,128)S(1)} %collective-permute-done.2) | copy-start | bytes 786436
  32.4 13.5 %collective-permute-start.4 = (f32[128,512]{1,0:T(8,128)}, f32[128,512]{1,0:T(8,128)}, u32[]{:S(2)}, u32[]{:S(2)}) collective-permute-start(f32[128,512]{1,0:T(8,128)} %get-tuple-element.123), channel_id=1, source_target_pairs={{8,16},{12,20},{16,8},{20,12},{9,17},{13,21},{17,9},{21,13},{10,18... | collective-permute-start | bytes 786440 | tf_op jit(solution)/shard_map/ppermute | solution.py:516
  33.8 0.8 copy-start.25
  34.5 29.7 %copy-start.3 = (bf16[1,1024,128]{2,1,0:T(8,128)(2,1)S(1)}, bf16[1,1024,128]{2,1,0:T(8,128)(2,1)}, u32[]{:S(2)}) copy-start(bf16[1,1024,128]{2,1,0:T(8,128)(2,1)} %param.12) | copy-start | bytes 786436
  34.5 29.7 %copy-start.4 = (bf16[1,1024,128]{2,1,0:T(8,128)(2,1)S(1)}, bf16[1,1024,128]{2,1,0:T(8,128)(2,1)}, u32[]{:S(2)}) copy-start(bf16[1,1024,128]{2,1,0:T(8,128)(2,1)} %param.13) | copy-start | bytes 786436
  34.6 29.7 %copy-start.5 = (bf16[1024,128]{1,0:T(8,128)(2,1)S(1)}, bf16[1024,128]{1,0:T(8,128)(2,1)}, u32[]{:S(2)}) copy-start(bf16[1024,128]{1,0:T(8,128)(2,1)} %get-tuple-element.53.refs_5_.refs_7_) | copy-start | bytes 786436
  34.6 29.7 %copy-start.6 = (bf16[4,256,256]{2,1,0:T(8,128)(2,1)S(1)}, bf16[4,256,256]{2,1,0:T(8,128)(2,1)}, u32[]{:S(2)}) copy-start(bf16[4,256,256]{2,1,0:T(8,128)(2,1)} %get-tuple-element.66.refs_14_) | copy-start | bytes 1572868
  34.6 29.7 %copy-start.7 = (bf16[4,256,256]{2,1,0:T(8,128)(2,1)S(1)}, bf16[4,256,256]{2,1,0:T(8,128)(2,1)}, u32[]{:S(2)}) copy-start(bf16[4,256,256]{2,1,0:T(8,128)(2,1)} %get-tuple-element.67.refs_15_) | copy-start | bytes 1572868
  34.6 29.7 %copy-start.8 = (bf16[1536,128]{1,0:T(8,128)(2,1)S(1)}, bf16[1536,128]{1,0:T(8,128)(2,1)}, u32[]{:S(2)}) copy-start(bf16[1536,128]{1,0:T(8,128)(2,1)} %constant.46.clone.refs_16_) | copy-start | bytes 1179652
  34.6 29.7 %copy-start.9 = (f32[16,2048]{1,0:T(8,128)S(1)}, f32[16,2048]{1,0:T(8,128)}, u32[]{:S(2)}) copy-start(f32[16,2048]{1,0:T(8,128)} %get-tuple-element.54.refs_6_.refs_8_) | copy-start | bytes 393220
  34.6 29.7 %copy-start.10 = (bf16[128,1024]{1,0:T(8,128)(2,1)S(1)}, bf16[128,1024]{1,0:T(8,128)(2,1)}, u32[]{:S(2)}) copy-start(bf16[128,1024]{1,0:T(8,128)(2,1)} %get-tuple-element.64.refs_12_) | copy-start | bytes 786436
  34.6 29.7 %copy-start.11 = (bf16[128,1024]{1,0:T(8,128)(2,1)S(1)}, bf16[128,1024]{1,0:T(8,128)(2,1)}, u32[]{:S(2)}) copy-start(bf16[128,1024]{1,0:T(8,128)(2,1)} %get-tuple-element.65.refs_13_) | copy-start | bytes 786436
  34.6 29.7 %copy-start.12 = (f32[1,32,1024]{2,1,0:T(8,128)S(1)}, f32[1,32,1024]{2,1,0:T(8,128)}, u32[]{:S(2)}) copy-start(f32[1,32,1024]{2,1,0:T(8,128)} %refs_5_.1) | copy-start | bytes 393220
  34.6 29.7 %copy-start.13 = (f32[8,2048]{1,0:T(8,128)S(1)}, f32[8,2048]{1,0:T(8,128)}, u32[]{:S(2)}) copy-start(f32[8,2048]{1,0:T(8,128)} %get-tuple-element.63.refs_4_) | copy-start | bytes 196612
  34.7 29.7 %copy-start.14 = (f32[32]{0:T(128)S(1)}, f32[32]{0:T(128)}, u32[]{:S(2)}) copy-start(f32[32]{0:T(128)} %param.15) | copy-start | bytes 388
  34.7 29.6 %copy-start.15 = (f32[32]{0:T(128)S(1)}, f32[32]{0:T(128)}, u32[]{:S(2)}) copy-start(f32[32]{0:T(128)} %param.16) | copy-start | bytes 388
  37.2 11.2 %collective-permute-start.3 = (f32[128,512]{1,0:T(8,128)}, f32[128,512]{1,0:T(8,128)}, u32[]{:S(2)}, u32[]{:S(2)}) collective-permute-start(f32[128,512]{1,0:T(8,128)} %get-tuple-element.107), channel_id=1, source_target_pairs={{0,8},{4,12},{24,16},{28,20},{1,9},{5,13},{25,17},{29,21},{2,10},{... | collective-permute-start | bytes 786440 | tf_op jit(solution)/shard_map/ppermute | solution.py:516
  44.4 14.1 %copy-start.20 = (f32[128,512]{1,0:T(8,128)S(1)}, f32[128,512]{1,0:T(8,128)}, u32[]{:S(2)}) copy-start(f32[128,512]{1,0:T(8,128)} %get-tuple-element.108) | copy-start | bytes 786436
  44.4 14.1 %copy-start.21 = (f32[128,512]{1,0:T(8,128)S(1)}, f32[128,512]{1,0:T(8,128)}, u32[]{:S(2)}) copy-start(f32[128,512]{1,0:T(8,128)} %get-tuple-element.110) | copy-start | bytes 786436
  44.4 19.9 %copy-start = (bf16[1024,2048]{1,0:T(8,128)(2,1)S(1)}, bf16[1024,2048]{1,0:T(8,128)(2,1)}, u32[]{:S(2)}) copy-start(bf16[1024,2048]{1,0:T(8,128)(2,1)} %get-tuple-element.61.refs_1_) | copy-start | bytes 12582916
  44.4 9.0 %collective-permute-start.7 = (f32[128,512]{1,0:T(8,128)}, f32[128,512]{1,0:T(8,128)S(1)}, u32[]{:S(2)}, u32[]{:S(2)}) collective-permute-start(f32[128,512]{1,0:T(8,128)} %get-tuple-element.122), channel_id=1, source_target_pairs={{0,4},{4,0},{8,12},{12,8},{16,20},{20,16},{24,28},{28,24},{1,5},{5... | collective-permute-start | bytes 786440 | tf_op jit(solution)/shard_map/ppermute | solution.py:520
  47.0 8.3 %collective-permute-start.6 = (f32[128,512]{1,0:T(8,128)S(1)}, f32[128,512]{1,0:T(8,128)S(1)}, u32[]{:S(2)}, u32[]{:S(2)}) collective-permute-start(f32[128,512]{1,0:T(8,128)S(1)} %multiply_add_fusion.2), channel_id=1, source_target_pairs={{16,24},{20,28},{8,0},{12,4},{17,25},{21,29},{9,1},{13,5},{18,26},... | collective-permute-start | bytes 786440 | tf_op jit(solution)/shard_map/ppermute | solution.py:516
  49.7 23.9 %collective-permute-start.9 = (f32[128,512]{1,0:T(8,128)S(1)}, f32[128,512]{1,0:T(8,128)S(1)}, u32[]{:S(2)}, u32[]{:S(2)}) collective-permute-start(f32[128,512]{1,0:T(8,128)S(1)} %get-tuple-element.124), channel_id=1, source_target_pairs={{0,4},{4,0},{8,12},{12,8},{16,20},{20,16},{24,28},{28,24},{1,5},{5... | collective-permute-start | bytes 786440 | tf_op jit(solution)/shard_map/ppermute | solution.py:520
  50.8 7.7 %collective-permute-start.5 = (f32[128,512]{1,0:T(8,128)S(1)}, f32[128,512]{1,0:T(8,128)S(1)}, u32[]{:S(2)}, u32[]{:S(2)}) collective-permute-start(f32[128,512]{1,0:T(8,128)S(1)} %get-tuple-element.125), channel_id=1, source_target_pairs={{8,16},{12,20},{16,8},{20,12},{9,17},{13,21},{17,9},{21,13},{10,18... | collective-permute-start | bytes 786440 | tf_op jit(solution)/shard_map/ppermute | solution.py:516
  57.8 6.4 %collective-permute-start.10 = (f32[128,512]{1,0:T(8,128)S(1)}, f32[128,512]{1,0:T(8,128)S(1)}, u32[]{:S(2)}, u32[]{:S(2)}) collective-permute-start(f32[128,512]{1,0:T(8,128)S(1)} %broadcast_select_fusion.7), channel_id=1, source_target_pairs={{0,4},{4,0},{8,12},{12,8},{16,20},{20,16},{24,28},{28,24},{1,5},{5... | collective-permute-start | bytes 786440 | tf_op jit(solution)/shard_map/ppermute | solution.py:530
  58.6 15.0 %collective-permute-start.8 = (f32[128,512]{1,0:T(8,128)S(1)}, f32[128,512]{1,0:T(8,128)S(1)}, u32[]{:S(2)}, u32[]{:S(2)}) collective-permute-start(f32[128,512]{1,0:T(8,128)S(1)} %multiply_add_fusion), channel_id=1, source_target_pairs={{16,24},{20,28},{8,0},{12,4},{17,25},{21,29},{9,1},{13,5},{18,26},... | collective-permute-start | bytes 786440 | tf_op jit(solution)/shard_map/ppermute | solution.py:516
  64.3 2.2 %copy-start.1 = (bf16[1024,2048]{1,0:T(8,128)(2,1)S(1)}, bf16[1024,2048]{1,0:T(8,128)(2,1)}, u32[]{:S(2)}) copy-start(bf16[1024,2048]{1,0:T(8,128)(2,1)} %get-tuple-element.62.refs_2_) | copy-start | bytes 12582916
  66.5 7.1 %copy-start.16 = (f32[128,512]{1,0:T(8,128)S(1)}, f32[128,512]{1,0:T(8,128)}, u32[]{:S(2)}) copy-start(f32[128,512]{1,0:T(8,128)} %get-tuple-element.109) | copy-start | bytes 786436
  66.5 7.1 %copy-start.17 = (f32[128,512]{1,0:T(8,128)S(1)}, f32[128,512]{1,0:T(8,128)}, u32[]{:S(2)}) copy-start(f32[128,512]{1,0:T(8,128)} %get-tuple-element.111) | copy-start | bytes 786436
  74.8 9.2 %collective-permute-start.11 = (f32[128,512]{1,0:T(8,128)S(1)}, f32[128,512]{1,0:T(8,128)S(1)}, u32[]{:S(2)}, u32[]{:S(2)}) collective-permute-start(f32[128,512]{1,0:T(8,128)S(1)} %get-tuple-element.100), channel_id=1, source_target_pairs={{0,4},{4,0},{8,12},{12,8},{16,20},{20,16},{24,28},{28,24},{1,5},{5... | collective-permute-start | bytes 786440 | tf_op jit(solution)/shard_map/ppermute | solution.py:530
  75.5 8.5 %copy-start.2 = (bf16[1024,2048]{1,0:T(8,128)(2,1)S(1)}, bf16[1024,2048]{1,0:T(8,128)(2,1)}, u32[]{:S(2)}) copy-start(bf16[1024,2048]{1,0:T(8,128)(2,1)} %get-tuple-element.62.refs_2_) | copy-start | bytes 12582916
  96.2 3.1 %collective-permute-start.14 = (f32[8,128]{1,0:T(8,128)S(1)}, f32[8,128]{1,0:T(8,128)S(1)}, u32[]{:S(2)}, u32[]{:S(2)}) collective-permute-start(f32[8,128]{1,0:T(8,128)S(1)} %get-tuple-element.99), channel_id=1, source_target_pairs={{0,3},{1,2},{2,1},{3,0},{4,7},{5,6},{6,5},{7,4},{8,11},{9,10},{10,... | collective-permute-start | bytes 12296 | tf_op jit(solution)/shard_map/ppermute | solution.py:469
  96.3 3.7 %collective-permute-start.13 = (f32[8,128]{1,0:T(8,128)S(1)}, f32[8,128]{1,0:T(8,128)S(1)}, u32[]{:S(2)}, u32[]{:S(2)}) collective-permute-start(f32[8,128]{1,0:T(8,128)S(1)} %get-tuple-element.99), channel_id=1, source_target_pairs={{0,2},{1,3},{2,0},{3,1},{4,6},{5,7},{6,4},{7,5},{8,10},{9,11},{10,... | collective-permute-start | bytes 12296 | tf_op jit(solution)/shard_map/ppermute | solution.py:469
  97.9 2.1 %collective-permute-start.12 = (f32[8,128]{1,0:T(8,128)S(1)}, f32[8,128]{1,0:T(8,128)S(1)}, u32[]{:S(2)}, u32[]{:S(2)}) collective-permute-start(f32[8,128]{1,0:T(8,128)S(1)} %get-tuple-element.99), channel_id=1, source_target_pairs={{0,1},{1,0},{2,3},{3,2},{4,5},{5,4},{6,7},{7,6},{8,9},{9,8},{10,11... | collective-permute-start | bytes 12296 | tf_op jit(solution)/shard_map/ppermute | solution.py:469
  100.0 4.6 %collective-permute-start.17 = (f32[8,128]{1,0:T(8,128)S(1)}, f32[8,128]{1,0:T(8,128)S(1)}, u32[]{:S(2)}, u32[]{:S(2)}) collective-permute-start(f32[8,128]{1,0:T(8,128)S(1)} %add_add_fusion.1), channel_id=1, source_target_pairs={{0,12},{4,8},{8,4},{12,0},{16,28},{20,24},{24,20},{28,16},{1,13},{... | collective-permute-start | bytes 12296 | tf_op jit(solution)/shard_map/ppermute | solution.py:469
  101.3 3.6 %collective-permute-start.16 = (f32[8,128]{1,0:T(8,128)S(1)}, f32[8,128]{1,0:T(8,128)S(1)}, u32[]{:S(2)}, u32[]{:S(2)}) collective-permute-start(f32[8,128]{1,0:T(8,128)S(1)} %add_add_fusion.1), channel_id=1, source_target_pairs={{0,8},{4,12},{8,0},{12,4},{16,24},{20,28},{24,16},{28,20},{1,9},{5... | collective-permute-start | bytes 12296 | tf_op jit(solution)/shard_map/ppermute | solution.py:469
  102.9 3.6 %collective-permute-start.15 = (f32[8,128]{1,0:T(8,128)S(1)}, f32[8,128]{1,0:T(8,128)S(1)}, u32[]{:S(2)}, u32[]{:S(2)}) collective-permute-start(f32[8,128]{1,0:T(8,128)S(1)} %add_add_fusion.1), channel_id=1, source_target_pairs={{0,4},{4,0},{8,12},{12,8},{16,20},{20,16},{24,28},{28,24},{1,5},{5... | collective-permute-start | bytes 12296 | tf_op jit(solution)/shard_map/ppermute | solution.py:469
  106.5 4.5 %collective-permute-start.18 = (f32[8,128]{1,0:T(8,128)S(1)}, f32[8,128]{1,0:T(8,128)S(1)}, u32[]{:S(2)}, u32[]{:S(2)}) collective-permute-start(f32[8,128]{1,0:T(8,128)S(1)} %add_add_fusion), channel_id=1, source_target_pairs={{0,16},{4,20},{8,24},{12,28},{16,0},{20,4},{24,8},{28,12},{1,17},{... | collective-permute-start | bytes 12296 | tf_op jit(solution)/shard_map/ppermute | solution.py:469

commit v9 on v6

--- a/solution.py
+++ b/solution.py
@@ -259,19 +259,47 @@
     return out[:count], list(out[count:])
 
 
+def pairs_kernel(xs_ref, ys_ref, b_ref, c_ref, dc_ref, db_ref):
+    pair = jnp.where(triangle(GROUP, True), dot(ys_ref[...], xs_ref[...], NT), 0.0).astype(BF16)
+    dc_ref[...] = dot(pair, b_ref[...], NN)
+    db_ref[...] = dot(pair, c_ref[...], TN)
+
+
+def pairs_grads(saved, b, c):
+    xs, ys = saved[:2]
+    length, channels = xs.shape
+    states = b.shape[1]
+    columns = pl.BlockSpec((GROUP, channels), lambda n: (n, 0))
+    maps = pl.BlockSpec((GROUP, states), lambda n: (n, 0))
+    return pl.pallas_call(
+        pairs_kernel,
+        grid=(length // GROUP,),
+        in_specs=[columns, columns, maps, maps],
+        out_specs=[maps, maps],
+        out_shape=[jax.ShapeDtypeStruct((length, states), F32)] * 2,
+        compiler_params=pltpu.CompilerParams(vmem_limit_bytes=VMEM_LIMIT),
+        cost_estimate=pl.CostEstimate(
+            flops=2 * length * GROUP * channels,
+            bytes_accessed=4 * length * channels,
+            transcendentals=0,
+        ),
+        name="pairs_grads",
+    )(xs, ys, b, c)
+
+
 def grads_kernel(first, scale, part, half, begin, *refs):
     y_ref, xs_ref, ys_ref, dy_ref, direct_ref, b_ref, c_ref, columns_ref, table_ref = refs[:9]
     raw_ref, bias_ref, rate_ref, bt, ct, left, right, adder = refs[9:17]
     held = refs[17:21]
     refs = refs[21:]
+    dc_in, db_in = refs[:2]
+    refs = refs[2:]
     if not first:
-        dc_in, db_in, par_in = refs[:3]
-        refs = refs[5:]
+        par_in = refs[0]
+        refs = refs[3:]
     dx_ref, dc_ref, db_ref, draw_ref, par_ref = refs[:5]
-    sums, dc_sum, db_sum, terms = refs[5:9]
-    if not first:
-        dc_old, db_old, sems = refs[9:]
-        old = [(dc_in, dc_old, sems.at[0]), (db_in, db_old, sems.at[1])]
+    dc_sum, db_sum, terms, dc_old, db_old, sems = refs[5:]
+    old = [(dc_in, dc_old, sems.at[0]), (db_in, db_old, sems.at[1])]
     g = pl.program_id(0)
     heads = raw_ref.shape[1]
     length, width = xs_ref.shape
@@ -285,10 +313,8 @@
 
     @pl.when(g == 0)
     def _():
-        if not first:
-            for source, target, sem in old:
-                pltpu.make_async_copy(source, target, sem).start()
-        sums[...] = jnp.zeros_like(sums)
+        for source, target, sem in old:
+            pltpu.make_async_copy(source, target, sem).start()
         dc_sum[...] = jnp.zeros_like(dc_sum)
         db_sum[...] = jnp.zeros_like(db_sum)
         par_ref[...] = jnp.zeros_like(par_ref) if first else par_in[...]
@@ -328,7 +354,6 @@
         terms[rows[n], :width] = hi
         terms[rows[n], width : 2 * width] = lo
         terms[rows[n], 2 * width :] = v.astype(BF16)
-        sums[n] += dot(scaled_dy, scaled_x, NT)
         dc_sum[n] += dot(scaled_dy, entering_low[n], NT)
         db_sum[n] += dot(scaled_x, leaving_low[n], NT)
     added = dot(terms[...], adder[...], NN).T
@@ -355,18 +380,11 @@
 
     @pl.when(g == pl.num_programs(0) - 1)
     def _():
-        if not first:
-            for source, target, sem in old:
-                pltpu.make_async_copy(source, target, sem).wait()
+        for source, target, sem in old:
+            pltpu.make_async_copy(source, target, sem).wait()
         for n in range(blocks):
-            pair = jnp.where(lower, sums[n], 0.0).astype(BF16)
-            dc = dot(pair, b_ref[rows[n], :], NN) + dc_sum[n]
-            db = dot(pair, c_ref[rows[n], :], TN) + db_sum[n]
-            if not first:
-                dc = dc + dc_old[rows[n], :]
-                db = db + db_old[rows[n], :]
-            dc_ref[rows[n], :] = dc
-            db_ref[rows[n], :] = db
+            dc_ref[rows[n], :] = dc_old[rows[n], :] + dc_sum[n]
+            db_ref[rows[n], :] = db_old[rows[n], :] + db_sum[n]
 
 
 def local_grads(part, begin, count, scale, y, saved, dy, b, c, vectors, held, before):
@@ -380,7 +398,7 @@
     states = b.shape[1]
     blocks = length // GROUP
     half = pieces // 2
-    first = before is None
+    first = before[0] is None
     whole = lambda g, y: (0, 0)
     place = lambda g, y: (0, (begin + g) * half + part)
     columns = pl.BlockSpec((length, width), place)
@@ -400,10 +418,12 @@
     in_specs += [pl.BlockSpec(a.shape, lambda g, y, n=len(a.shape): (0,) * n) for a in fixed]
     args += fixed
     aliases = {}
+    dx, dc, db, draw, par = before
+    args += [dc, db]
+    in_specs += [anywhere, anywhere]
     if not first:
-        dx, dc, db, draw, par = before
-        args += [dc, db, par, dx, draw]
-        in_specs += [anywhere, anywhere, params, anywhere, anywhere]
+        args += [par, dx, draw]
+        in_specs += [params, anywhere, anywhere]
         aliases = {24: 0, 25: 3}
     grid_spec = pltpu.PrefetchScalarGridSpec(
         num_scalar_prefetch=1,
@@ -411,17 +431,13 @@
         in_specs=in_specs,
         out_specs=[columns, maps, maps, lines, params],
         scratch_shapes=[
-            pltpu.VMEM((blocks, GROUP, GROUP), F32),
             pltpu.VMEM((blocks, GROUP, states), F32),
             pltpu.VMEM((blocks, GROUP, states), F32),
             pltpu.VMEM((length, 3 * width), BF16),
-        ]
-        + [
             pltpu.VMEM((length, states), F32),
             pltpu.VMEM((length, states), F32),
             pltpu.SemaphoreType.DMA((2,)),
-        ]
-        * (not first),
+        ],
     )
     return pl.pallas_call(
         functools.partial(grads_kernel, first, scale, part, half, begin),
@@ -604,6 +620,10 @@
             token = None if part == 0 else message
         else:
             token = flows[part].send(token)[0]
+        if (part, k) == (0, 1):
+            dc, db = pairs_grads(saved, after(b, token), c)
+            token = dc
+            found = (None, dc, db, None, None)
     found = grads(0, 1, 1, token, held)
     found = grads(1, 0, 2, found[-1], next(flows[1]))
     dx, dc, db, draw, params = found

time: 101 us -> 99.4 us (0.984)
  Pallas kernels: 42.8 us -> 48 us
  starting transfers between devices: 30.3 us -> 27.3 us
  waiting for transfers between devices: 20.7 us -> 18.1 us
  other arithmetic: 5.01 us -> 3.21 us
    pallas_call x0 -> x1, Pallas kernels: none -> 6.39 us  [pairs_grads(): pl.pallas_call(pairs_kernel, grid=(length // GROUP,), in_specs=[columns,...]
    ppermute x2, waiting for transfers between devices: 7.77 us -> 2.62 us  [entering(): near = lax.ppermute(message, 'seq', both([(0, 1), (1, 0), (2, 3), (3, 2)]))]
    ppermute x2, waiting for transfers between devices: 1.38 us -> 5.25 us  [entering(): far = lax.ppermute(message, 'seq', both([(1, 3), (2, 0)]))]
    ppermute x7, starting transfers between devices: 12.8 us -> 10.9 us  [summed_over(): lax.ppermute(value, axis, [(i, i ^ s) for i in range(size)])]
    pallas_call x3, Pallas kernels: 27.6 us -> 26.4 us  [local_grads(): pl.pallas_call(functools.partial(grads_kernel, first, scale, part, half,...]
    ppermute x2, waiting for transfers between devices: 5.63 us -> 4.41 us  [entering(): got = lax.ppermute(message, 'seq', swap)]
    select_n x3, other arithmetic: 1.6 us -> 0.46 us  [shares(): jnp.where(second, for_second, for_first)]
    ppermute x2, starting transfers between devices: 2.55 us -> 1.45 us  [entering(): other_early = lax.ppermute(early, 'seq', swap)]
  transfers between devices with their start and end apart: 19 -> 19, of which waited for: 11 -> 10; matrix products, arithmetic and copies ran while one was open for 2% -> 1% of each run, Pallas kernels for 26% -> 32%
where the time goes in v9:
time: 99.4 us; the launch traced here: 99 us
  Pallas kernels  48 us (48%)
  starting transfers between devices  27.3 us (27%)
  waiting for transfers between devices  18.1 us (18%)
  other arithmetic  3.21 us (3%)
  local copies, waits for them, and re-layouts  1.19 us (1%)
  between operations  1.11 us (1%)
    pallas_call x3, Pallas kernels, local_grads(): pl.pallas_call(functools.partial(grads_kernel, first, scale, part, half,...  26.4 us
    pallas_call x3, Pallas kernels, local_states(): pl.pallas_call(functools.partial(local_kernel, first, last, count), grid_...  15.2 us
    ppermute x7, starting transfers between devices, summed_over(): lax.ppermute(value, axis, [(i, i ^ s) for i in range(size)])  10.9 us
    pallas_call x1, Pallas kernels, pairs_grads(): pl.pallas_call(pairs_kernel, grid=(length // GROUP,), in_specs=[columns,...  6.39 us
    ppermute x7, waiting for transfers between devices, summed_over(): lax.ppermute(value, axis, [(i, i ^ s) for i in range(size)])  5.86 us
    ppermute x2, waiting for transfers between devices, entering(): far = lax.ppermute(message, 'seq', both([(1, 3), (2, 0)]))  5.25 us
    ppermute x2, starting transfers between devices, entering(): near = lax.ppermute(message, 'seq', both([(0, 1), (1, 0), (2, 3), (3, 2)]))  4.68 us
    ppermute x2, starting transfers between devices, entering(): got = lax.ppermute(message, 'seq', swap)  4.48 us
  transfers between devices with their start and end apart: 19, of which 10 were waited for; matrix products, arithmetic and copies ran while one was open for 1% of the time, Pallas kernels for 32%

profile of v9, /device:TPU:0, one launch (start us, length us, event | category | flops | bytes accessed | tf_op | source)
XLA Modules:
  0.0 99.0 jit_solution(13700645389789614289)
XLA Ops:
  0.6 4.6 %local_states.3 = (f32[264,512]{1,0:T(8,128)}, bf16[1024,2048]{1,0:T(8,128)(2,1)}, bf16[1024,2048]{1,0:T(8,128)(2,1)}, f32[8,2048]{1,0:T(8,128)}, bf16[1024,128]{1,0:T(8,128)(2,1)}, /*index=5*/f32[16,2048]{1,0:T(8,128)}) custom-call(s32[1]{0:T(128)} %bitcast.7.refs_0_, bf16[1024,2048]{1,0:T(8,128)(2,1)} %bitcast.72, bf16[1024,2048]{1,0:T(8,128)(2,1)} %bitcast.66, ...), custom_call_target="tpu_custom_call" | custom-call | flops 536870912 | bytes 4194304 | tf_op jit(solution)/shard_map/local_states/pallas_call | solution.py:246
  5.2 3.0 %collective-permute-start.1 = (f32[264,512]{1,0:T(8,128)}, f32[264,512]{1,0:T(8,128)S(1)}, u32[]{:S(2)}, u32[]{:S(2)}) collective-permute-start(f32[264,512]{1,0:T(8,128)} %get-tuple-element.69), channel_id=1, source_target_pairs={{0,4},{4,0},{8,12},{12,8},{16,20},{20,16},{24,28},{28,24},{1,5},{5... | collective-permute-start | bytes 1622024 | tf_op jit(solution)/shard_map/ppermute | solution.py:523
  8.2 3.8 %local_states.4 = (f32[264,512]{1,0:T(8,128)}, bf16[1024,2048]{1,0:T(8,128)(2,1)}, bf16[1024,2048]{1,0:T(8,128)(2,1)}, f32[8,2048]{1,0:T(8,128)}) custom-call(s32[1]{0:T(128)} %bitcast.11.refs_0_, bf16[1024,2048]{1,0:T(8,128)(2,1)} %bitcast.73, bf16[1024,2048]{1,0:T(8,128)(2,1)} %bitcast.67, ...), custom_call_target="tpu_custom_call", output_to_operand_aliasing={{1}: (7, {}), {2}: (8, {}), {3}: (9, {})} | custom-call | flops 536870912 | bytes 4194304 | tf_op jit(solution)/shard_map/local_states/pallas_call | solution.py:246
  12.0 6.8 %local_states.5 = (f32[264,512]{1,0:T(8,128)}, f32[264,512]{1,0:T(8,128)}, bf16[1024,2048]{1,0:T(8,128)(2,1)}, bf16[1024,2048]{1,0:T(8,128)(2,1)}, f32[8,2048]{1...) custom-call(s32[1]{0:T(128)} %bitcast.2.refs_0_, ...), custom_call_target="tpu_custom_call", output_to_operand_aliasing={{2}: (7, {}), {3}: (8, {}), {4}: (9, {})} | custom-call | flops 1073741824 | bytes 8388608 | tf_op jit(solution)/shard_map/local_states/pallas_call | solution.py:246
  18.9 1.8 %collective-permute-done.1 = f32[264,512]{1,0:T(8,128)S(1)} collective-permute-done((f32[264,512]{1,0:T(8,128)}, f32[264,512]{1,0:T(8,128)S(1)}, u32[]{:S(2)}, u32[]{:S(2)}) %collective-permute-start.1) | collective-permute-done | bytes 540704 | tf_op jit(solution)/shard_map/ppermute | solution.py:523
  20.7 0.9 fusion.1
  21.6 1.2 %add_select_fusion.11 = (f32[128,512]{1,0:T(8,128)S(1)}, f32[128,512]{1,0:T(8,128)S(1)}, f32[128,512]{1,0:T(8,128)S(1)}) fusion(f32[512]{0:T(512)S(1)} %bitcast.98, f32[512]{0:T(512)S(1)} %bitcast.97, pred[]{:T(512)S(6)} %or.9, f32[264,512]{1,0:T(8,128)S(1)} %collective-permute-done.1, f32[264,512]{1,0:T(8,128)} %get-tuple-element.68, pred[]{:T(512)S(6)} %eq.12), kind=kLoop, calls=%fused_computation.15 | loop fusion | flops 589824 | bytes 1839106 | tf_op jit(solution)/shard_map/jit(_where)/select_n | solution.py:513
  22.8 1.9 %collective-permute-start.2 = (f32[136,512]{1,0:T(8,128)S(1)}, f32[136,512]{1,0:T(8,128)S(1)}, u32[]{:S(2)}, u32[]{:S(2)}) collective-permute-start(f32[136,512]{1,0:T(8,128)S(1)} %pad_maximum_fusion), channel_id=1, source_target_pairs={{0,8},{4,12},{8,0},{12,4},{16,24},{20,28},{24,16},{28,20},{1,9},{5... | collective-permute-start | bytes 835592 | tf_op jit(solution)/shard_map/ppermute | solution.py:531
  24.6 1.5 %collective-permute-start = (f32[264,512]{1,0:T(8,128)S(1)}, f32[264,512]{1,0:T(8,128)S(1)}, u32[]{:S(2)}, u32[]{:S(2)}) collective-permute-start(f32[264,512]{1,0:T(8,128)S(1)} %copy-done.19), channel_id=1, source_target_pairs={{0,4},{4,0},{8,12},{12,8},{16,20},{20,16},{24,28},{28,24},{1,5},{5... | collective-permute-start | bytes 1622024 | tf_op jit(solution)/shard_map/ppermute | solution.py:523
  26.1 6.4 %pairs_grads.1 = (f32[1024,128]{1,0:T(8,128)}, f32[1024,128]{1,0:T(8,128)}) custom-call(bf16[1024,2048]{1,0:T(8,128)(2,1)} %get-tuple-element.60.xs_ref.refs_1_, bf16[1024,2048]{1,0:T(8,128)(2,1)} %get-tuple-element.61.ys_ref.refs_2_, bf16[1024,128]{1,0:T(8,128)(2,1)} %bitcast.44, bf16[1024,128]{1,0:T(8,128)(2,1)} %bitcast.51), custom_call_target="tpu_custom_call" | custom-call | flops 1073741824 | bytes 8388608 | tf_op jit(solution)/shard_map/pairs_grads/pallas_call | solution.py:274
  32.6 0.2 broadcast_select_fusion.4
  32.9 0.0 copy-start.7
  33.0 1.6 %collective-permute-start.5 = (f32[128,512]{1,0:T(8,128)S(1)}, f32[128,512]{1,0:T(8,128)S(1)}, u32[]{:S(2)}, u32[]{:S(2)}) collective-permute-start(f32[128,512]{1,0:T(8,128)S(1)} %get-tuple-element.139), channel_id=1, source_target_pairs={{8,24},{12,28},{16,0},{20,4},{9,25},{13,29},{17,1},{21,5},{10,26},... | collective-permute-start | bytes 786440 | tf_op jit(solution)/shard_map/ppermute | solution.py:536
  34.5 0.8 collective-permute-start.4
  35.4 0.6 collective-permute-start.8
  35.9 2.6 %collective-permute-done = f32[264,512]{1,0:T(8,128)S(1)} collective-permute-done((f32[264,512]{1,0:T(8,128)S(1)}, f32[264,512]{1,0:T(8,128)S(1)}, u32[]{:S(2)}, u32[]{:S(2)}) %collective-permute-start) | collective-permute-done | bytes 540704 | tf_op jit(solution)/shard_map/ppermute | solution.py:523
  38.6 0.1 add_select_fusion.8
  38.7 2.8 %collective-permute-start.3 = (f32[136,512]{1,0:T(8,128)S(1)}, f32[136,512]{1,0:T(8,128)S(1)}, u32[]{:S(2)}, u32[]{:S(2)}) collective-permute-start(f32[136,512]{1,0:T(8,128)S(1)} %pad_maximum_fusion.1), channel_id=1, source_target_pairs={{0,8},{4,12},{8,0},{12,4},{16,24},{20,28},{24,16},{28,20},{1,9},{5... | collective-permute-start | bytes 835592 | tf_op jit(solution)/shard_map/ppermute | solution.py:531
  41.5 3.8 %collective-permute-done.5 = f32[128,512]{1,0:T(8,128)S(1)} collective-permute-done((f32[128,512]{1,0:T(8,128)S(1)}, f32[128,512]{1,0:T(8,128)S(1)}, u32[]{:S(2)}, u32[]{:S(2)}) %collective-permute-start.5) | collective-permute-done | bytes 262176 | tf_op jit(solution)/shard_map/ppermute | solution.py:536
  45.3 0.1 broadcast_select_fusion.3
  45.4 0.1 broadcast_select_fusion.6
  45.5 0.6 collective-permute-start.9
  46.1 2.6 %collective-permute-done.3 = f32[136,512]{1,0:T(8,128)S(1)} collective-permute-done((f32[136,512]{1,0:T(8,128)S(1)}, f32[136,512]{1,0:T(8,128)S(1)}, u32[]{:S(2)}, u32[]{:S(2)}) %collective-permute-start.3) | collective-permute-done | bytes 278560 | tf_op jit(solution)/shard_map/ppermute | solution.py:531
  48.7 0.2 broadcast_select_fusion.2
  49.0 1.3 %collective-permute-start.7 = (f32[128,512]{1,0:T(8,128)S(1)}, f32[128,512]{1,0:T(8,128)S(1)}, u32[]{:S(2)}, u32[]{:S(2)}) collective-permute-start(f32[128,512]{1,0:T(8,128)S(1)} %get-tuple-element.138), channel_id=1, source_target_pairs={{8,24},{12,28},{16,0},{20,4},{9,25},{13,29},{17,1},{21,5},{10,26},... | collective-permute-start | bytes 786440 | tf_op jit(solution)/shard_map/ppermute | solution.py:536
  50.3 0.9 collective-permute-start.6
  51.1 0.1 pad_add_fusion.refs_0_
  51.2 0.9 collective-permute-start.10
  52.3 7.3 %local_grads.3 = (bf16[1024,2048]{1,0:T(8,128)(2,1)}, f32[1024,128]{1,0:T(8,128)S(1)}, f32[1024,128]{1,0:T(8,128)S(1)}, f32[4,8,1024]{2,1,0:T(8,128)}, f32[8,128]{1,0:T(8,128)S(1)}) custom-call(s32[2]{0:T(128)S(1)} %pad_add_fusion.refs_0_, bf16[1024,2048]{1,0:T(8,128)(2,1)S(1)} %copy-done, bf16[1024,2048]{1,0:T(8,128)(2,1)} %get-tuple-element.61.ys_ref.refs_2_, ...), custom_call_target="tpu_custom_call" | custom-call | flops 2415919104 | bytes 3145728 | tf_op jit(solution)/shard_map/local_grads/pallas_call | solution.py:442
  59.5 1.5 %collective-permute-done.7 = f32[128,512]{1,0:T(8,128)S(1)} collective-permute-done((f32[128,512]{1,0:T(8,128)S(1)}, f32[128,512]{1,0:T(8,128)S(1)}, u32[]{:S(2)}, u32[]{:S(2)}) %collective-permute-start.7) | collective-permute-done | bytes 262176 | tf_op jit(solution)/shard_map/ppermute | solution.py:536
  61.0 0.1 broadcast_select_fusion
  61.2 0.7 collective-permute-start.11
  61.9 7.5 %local_grads.4 = (bf16[1024,2048]{1,0:T(8,128)(2,1)}, f32[1024,128]{1,0:T(8,128)S(1)}, f32[1024,128]{1,0:T(8,128)S(1)}, f32[4,8,1024]{2,1,0:T(8,128)}, f32[8,128]{1,0:T(8,128)S(1)}) custom-call(s32[2]{0:T(128)S(1)} %pad_add_fusion.refs_0_, bf16[1024,2048]{1,0:T(8,128)(2,1)S(1)} %copy-done, ...), custom_call_target="tpu_custom_call", output_to_operand_aliasing={{0}: (24, {}), {3}: (25, {})} | custom-call | flops 2415919104 | bytes 3145728 | tf_op jit(solution)/shard_map/local_grads/pallas_call | solution.py:442
  69.4 0.1 broadcast_select_fusion.1.refs_18_
  69.5 11.6 %local_grads.5 = (bf16[1024,2048]{1,0:T(8,128)(2,1)}, f32[1024,128]{1,0:T(8,128)}, f32[1024,128]{1,0:T(8,128)}, f32[4,8,1024]{2,1,0:T(8,128)}, f32[8,128]{1,0:T(8,128)S(1)}) custom-call(s32[2]{0:T(128)S(1)} %pad_add_fusion.refs_0_, bf16[1024,2048]{1,0:T(8,128)(2,1)S(1)} %copy-done, ...), custom_call_target="tpu_custom_call", output_to_operand_aliasing={{0}: (24, {}), {3}: (25, {})} | custom-call | flops 4831838208 | bytes 6291456 | tf_op jit(solution)/shard_map/local_grads/pallas_call | solution.py:442
  81.1 0.1 collective-permute-start.14
  81.2 1.6 %collective-permute-start.13 = (f32[8,128]{1,0:T(8,128)S(1)}, f32[8,128]{1,0:T(8,128)S(1)}, u32[]{:S(2)}, u32[]{:S(2)}) collective-permute-start(f32[8,128]{1,0:T(8,128)S(1)} %get-tuple-element.97), channel_id=1, source_target_pairs={{0,2},{1,3},{2,0},{3,1},{4,6},{5,7},{6,4},{7,5},{8,10},{9,11},{10,... | collective-permute-start | bytes 12296 | tf_op jit(solution)/shard_map/ppermute | solution.py:485
  82.8 0.3 collective-permute-start.12
  83.1 1.2 %collective-permute-done.14 = f32[8,128]{1,0:T(8,128)S(1)} collective-permute-done((f32[8,128]{1,0:T(8,128)S(1)}, f32[8,128]{1,0:T(8,128)S(1)}, u32[]{:S(2)}, u32[]{:S(2)}) %collective-permute-start.14) | collective-permute-done | bytes 4128 | tf_op jit(solution)/shard_map/ppermute | solution.py:485
  84.2 0.7 collective-permute-done.13
  84.9 4.8 %collective-permute-start.17 = (f32[8,128]{1,0:T(8,128)S(1)}, f32[8,128]{1,0:T(8,128)S(1)}, u32[]{:S(2)}, u32[]{:S(2)}) collective-permute-start(f32[8,128]{1,0:T(8,128)S(1)} %add_add_fusion.1), channel_id=1, source_target_pairs={{0,12},{4,8},{8,4},{12,0},{16,28},{20,24},{24,20},{28,16},{1,13},{... | collective-permute-start | bytes 12296 | tf_op jit(solution)/shard_map/ppermute | solution.py:485
  89.7 1.2 %collective-permute-start.15 = (f32[8,128]{1,0:T(8,128)S(1)}, f32[8,128]{1,0:T(8,128)S(1)}, u32[]{:S(2)}, u32[]{:S(2)}) collective-permute-start(f32[8,128]{1,0:T(8,128)S(1)} %add_add_fusion.1), channel_id=1, source_target_pairs={{0,4},{4,0},{8,12},{12,8},{16,20},{20,16},{24,28},{28,24},{1,5},{5... | collective-permute-start | bytes 12296 | tf_op jit(solution)/shard_map/ppermute | solution.py:485
  90.8 0.4 collective-permute-done.17
  91.2 2.0 %collective-permute-done.16 = f32[8,128]{1,0:T(8,128)S(1)} collective-permute-done((f32[8,128]{1,0:T(8,128)S(1)}, f32[8,128]{1,0:T(8,128)S(1)}, u32[]{:S(2)}, u32[]{:S(2)}) %collective-permute-start.16) | collective-permute-done | bytes 4128 | tf_op jit(solution)/shard_map/ppermute | solution.py:485
  93.3 3.0 %collective-permute-start.18 = (f32[8,128]{1,0:T(8,128)S(1)}, f32[8,128]{1,0:T(8,128)S(1)}, u32[]{:S(2)}, u32[]{:S(2)}) collective-permute-start(f32[8,128]{1,0:T(8,128)S(1)} %add_add_fusion), channel_id=1, source_target_pairs={{0,16},{4,20},{8,24},{12,28},{16,0},{20,4},{24,8},{28,12},{1,17},{... | collective-permute-start | bytes 12296 | tf_op jit(solution)/shard_map/ppermute | solution.py:485
  96.3 1.6 %collective-permute-done.18 = f32[8,128]{1,0:T(8,128)S(1)} collective-permute-done((f32[8,128]{1,0:T(8,128)S(1)}, f32[8,128]{1,0:T(8,128)S(1)}, u32[]{:S(2)}, u32[]{:S(2)}) %collective-permute-start.18) | collective-permute-done | bytes 4128 | tf_op jit(solution)/shard_map/ppermute | solution.py:485
  97.9 0.5 slice_bitcast_fusion
  98.4 0.6 slice.150
  (59 shorter events, 0.2 us)
Async XLA Ops:
  5.2 15.5 %collective-permute-start.1 = (f32[264,512]{1,0:T(8,128)}, f32[264,512]{1,0:T(8,128)S(1)}, u32[]{:S(2)}, u32[]{:S(2)}) collective-permute-start(f32[264,512]{1,0:T(8,128)} %get-tuple-element.69), channel_id=1, source_target_pairs={{0,4},{4,0},{8,12},{12,8},{16,20},{20,16},{24,28},{28,24},{1,5},{5... | collective-permute-start | bytes 1622024 | tf_op jit(solution)/shard_map/ppermute | solution.py:523
  12.0 12.6 %copy-start.19 = (f32[264,512]{1,0:T(8,128)S(1)}, f32[264,512]{1,0:T(8,128)}, u32[]{:S(2)}) copy-start(f32[264,512]{1,0:T(8,128)} %get-tuple-element.67) | copy-start | bytes 1622020
  22.8 9.8 %collective-permute-start.2 = (f32[136,512]{1,0:T(8,128)S(1)}, f32[136,512]{1,0:T(8,128)S(1)}, u32[]{:S(2)}, u32[]{:S(2)}) collective-permute-start(f32[136,512]{1,0:T(8,128)S(1)} %pad_maximum_fusion), channel_id=1, source_target_pairs={{0,8},{4,12},{8,0},{12,4},{16,24},{20,28},{24,16},{28,20},{1,9},{5... | collective-permute-start | bytes 835592 | tf_op jit(solution)/shard_map/ppermute | solution.py:531
  24.6 13.9 %collective-permute-start = (f32[264,512]{1,0:T(8,128)S(1)}, f32[264,512]{1,0:T(8,128)S(1)}, u32[]{:S(2)}, u32[]{:S(2)}) collective-permute-start(f32[264,512]{1,0:T(8,128)S(1)} %copy-done.19), channel_id=1, source_target_pairs={{0,4},{4,0},{8,12},{12,8},{16,20},{20,16},{24,28},{28,24},{1,5},{5... | collective-permute-start | bytes 1622024 | tf_op jit(solution)/shard_map/ppermute | solution.py:523
  26.1 6.4 %copy-start.18 = (f32[264,512]{1,0:T(8,128)S(1)}, f32[264,512]{1,0:T(8,128)}, u32[]{:S(2)}) copy-start(f32[264,512]{1,0:T(8,128)} %get-tuple-element.68) | copy-start | bytes 1622020
  26.1 12.4 %copy-start.17 = (f32[264,512]{1,0:T(8,128)S(1)}, f32[264,512]{1,0:T(8,128)}, u32[]{:S(2)}) copy-start(f32[264,512]{1,0:T(8,128)} %get-tuple-element.75) | copy-start | bytes 1622020
  32.6 19.5 %copy-start.14 = (f32[1024,128]{1,0:T(8,128)S(1)}, f32[1024,128]{1,0:T(8,128)}, u32[]{:S(2)}) copy-start(f32[1024,128]{1,0:T(8,128)} %get-tuple-element.79.refs_22_) | copy-start | bytes 1572868
  32.8 19.3 %copy-start = (bf16[1024,2048]{1,0:T(8,128)(2,1)S(1)}, bf16[1024,2048]{1,0:T(8,128)(2,1)}, u32[]{:S(2)}) copy-start(bf16[1024,2048]{1,0:T(8,128)(2,1)} %get-tuple-element.60.xs_ref.refs_1_) | copy-start | bytes 12582916
  32.8 19.3 %copy-start.2 = (bf16[1,1024,128]{2,1,0:T(8,128)(2,1)S(1)}, bf16[1,1024,128]{2,1,0:T(8,128)(2,1)}, u32[]{:S(2)}) copy-start(bf16[1,1024,128]{2,1,0:T(8,128)(2,1)} %param.12) | copy-start | bytes 786436
  32.8 19.3 %copy-start.3 = (bf16[1,1024,128]{2,1,0:T(8,128)(2,1)S(1)}, bf16[1,1024,128]{2,1,0:T(8,128)(2,1)}, u32[]{:S(2)}) copy-start(bf16[1,1024,128]{2,1,0:T(8,128)(2,1)} %param.13) | copy-start | bytes 786436
  32.8 19.3 %copy-start.4 = (bf16[1024,128]{1,0:T(8,128)(2,1)S(1)}, bf16[1024,128]{1,0:T(8,128)(2,1)}, u32[]{:S(2)}) copy-start(bf16[1024,128]{1,0:T(8,128)(2,1)} %get-tuple-element.52.refs_5_.refs_7_) | copy-start | bytes 786436
  32.9 19.3 %copy-start.5 = (bf16[4,256,256]{2,1,0:T(8,128)(2,1)S(1)}, bf16[4,256,256]{2,1,0:T(8,128)(2,1)}, u32[]{:S(2)}) copy-start(bf16[4,256,256]{2,1,0:T(8,128)(2,1)} %get-tuple-element.65.refs_14_) | copy-start | bytes 1572868
  32.9 19.3 %copy-start.6 = (bf16[4,256,256]{2,1,0:T(8,128)(2,1)S(1)}, bf16[4,256,256]{2,1,0:T(8,128)(2,1)}, u32[]{:S(2)}) copy-start(bf16[4,256,256]{2,1,0:T(8,128)(2,1)} %get-tuple-element.66.refs_15_) | copy-start | bytes 1572868
  32.9 19.3 %copy-start.7 = (bf16[1536,128]{1,0:T(8,128)(2,1)S(1)}, bf16[1536,128]{1,0:T(8,128)(2,1)}, u32[]{:S(2)}) copy-start(bf16[1536,128]{1,0:T(8,128)(2,1)} %constant.44.clone.refs_16_) | copy-start | bytes 1179652
  32.9 19.3 %copy-start.8 = (f32[16,2048]{1,0:T(8,128)S(1)}, f32[16,2048]{1,0:T(8,128)}, u32[]{:S(2)}) copy-start(f32[16,2048]{1,0:T(8,128)} %get-tuple-element.53.refs_6_.refs_8_) | copy-start | bytes 393220
  32.9 19.3 %copy-start.9 = (bf16[128,1024]{1,0:T(8,128)(2,1)S(1)}, bf16[128,1024]{1,0:T(8,128)(2,1)}, u32[]{:S(2)}) copy-start(bf16[128,1024]{1,0:T(8,128)(2,1)} %get-tuple-element.63.refs_12_) | copy-start | bytes 786436
  32.9 19.3 %copy-start.10 = (bf16[128,1024]{1,0:T(8,128)(2,1)S(1)}, bf16[128,1024]{1,0:T(8,128)(2,1)}, u32[]{:S(2)}) copy-start(bf16[128,1024]{1,0:T(8,128)(2,1)} %get-tuple-element.64.refs_13_) | copy-start | bytes 786436
  32.9 19.3 %copy-start.11 = (f32[1,32,1024]{2,1,0:T(8,128)S(1)}, f32[1,32,1024]{2,1,0:T(8,128)}, u32[]{:S(2)}) copy-start(f32[1,32,1024]{2,1,0:T(8,128)} %refs_5_.1) | copy-start | bytes 393220
  32.9 19.3 %copy-start.12 = (f32[8,2048]{1,0:T(8,128)S(1)}, f32[8,2048]{1,0:T(8,128)}, u32[]{:S(2)}) copy-start(f32[8,2048]{1,0:T(8,128)} %get-tuple-element.62.refs_4_) | copy-start | bytes 196612
  32.9 19.3 %copy-start.13 = (f32[1024,128]{1,0:T(8,128)S(1)}, f32[1024,128]{1,0:T(8,128)}, u32[]{:S(2)}) copy-start(f32[1024,128]{1,0:T(8,128)} %get-tuple-element.72.refs_21_) | copy-start | bytes 1572868
  33.0 19.3 %copy-start.15 = (f32[32]{0:T(128)S(1)}, f32[32]{0:T(128)}, u32[]{:S(2)}) copy-start(f32[32]{0:T(128)} %param.15) | copy-start | bytes 388
  33.0 19.3 %copy-start.16 = (f32[32]{0:T(128)S(1)}, f32[32]{0:T(128)}, u32[]{:S(2)}) copy-start(f32[32]{0:T(128)} %param.16) | copy-start | bytes 388
  33.0 12.3 %collective-permute-start.5 = (f32[128,512]{1,0:T(8,128)S(1)}, f32[128,512]{1,0:T(8,128)S(1)}, u32[]{:S(2)}, u32[]{:S(2)}) collective-permute-start(f32[128,512]{1,0:T(8,128)S(1)} %get-tuple-element.139), channel_id=1, source_target_pairs={{8,24},{12,28},{16,0},{20,4},{9,25},{13,29},{17,1},{21,5},{10,26},... | collective-permute-start | bytes 786440 | tf_op jit(solution)/shard_map/ppermute | solution.py:536
  34.5 10.8 %collective-permute-start.4 = (f32[128,512]{1,0:T(8,128)S(1)}, f32[128,512]{1,0:T(8,128)S(1)}, u32[]{:S(2)}, u32[]{:S(2)}) collective-permute-start(f32[128,512]{1,0:T(8,128)S(1)} %get-tuple-element.139), channel_id=1, source_target_pairs={{8,16},{12,20},{16,8},{20,12},{9,17},{13,21},{17,9},{21,13},{10,18... | collective-permute-start | bytes 786440 | tf_op jit(solution)/shard_map/ppermute | solution.py:535
  35.4 16.7 %collective-permute-start.8 = (f32[128,512]{1,0:T(8,128)S(1)}, f32[128,512]{1,0:T(8,128)S(1)}, u32[]{:S(2)}, u32[]{:S(2)}) collective-permute-start(f32[128,512]{1,0:T(8,128)S(1)} %get-tuple-element.137), channel_id=1, source_target_pairs={{0,4},{4,0},{8,12},{12,8},{16,20},{20,16},{24,28},{28,24},{1,5},{5... | collective-permute-start | bytes 786440 | tf_op jit(solution)/shard_map/ppermute | solution.py:540
  38.7 10.0 %collective-permute-start.3 = (f32[136,512]{1,0:T(8,128)S(1)}, f32[136,512]{1,0:T(8,128)S(1)}, u32[]{:S(2)}, u32[]{:S(2)}) collective-permute-start(f32[136,512]{1,0:T(8,128)S(1)} %pad_maximum_fusion.1), channel_id=1, source_target_pairs={{0,8},{4,12},{8,0},{12,4},{16,24},{20,28},{24,16},{28,20},{1,9},{5... | collective-permute-start | bytes 835592 | tf_op jit(solution)/shard_map/ppermute | solution.py:531
  45.5 6.6 %collective-permute-start.9 = (f32[128,512]{1,0:T(8,128)S(1)}, f32[128,512]{1,0:T(8,128)S(1)}, u32[]{:S(2)}, u32[]{:S(2)}) collective-permute-start(f32[128,512]{1,0:T(8,128)S(1)} %broadcast_select_fusion.6), channel_id=1, source_target_pairs={{0,4},{4,0},{8,12},{12,8},{16,20},{20,16},{24,28},{28,24},{1,5},{5... | collective-permute-start | bytes 786440 | tf_op jit(solution)/shard_map/ppermute | solution.py:545
  49.0 12.0 %collective-permute-start.7 = (f32[128,512]{1,0:T(8,128)S(1)}, f32[128,512]{1,0:T(8,128)S(1)}, u32[]{:S(2)}, u32[]{:S(2)}) collective-permute-start(f32[128,512]{1,0:T(8,128)S(1)} %get-tuple-element.138), channel_id=1, source_target_pairs={{8,24},{12,28},{16,0},{20,4},{9,25},{13,29},{17,1},{21,5},{10,26},... | collective-permute-start | bytes 786440 | tf_op jit(solution)/shard_map/ppermute | solution.py:536
  50.3 10.7 %collective-permute-start.6 = (f32[128,512]{1,0:T(8,128)S(1)}, f32[128,512]{1,0:T(8,128)S(1)}, u32[]{:S(2)}, u32[]{:S(2)}) collective-permute-start(f32[128,512]{1,0:T(8,128)S(1)} %get-tuple-element.138), channel_id=1, source_target_pairs={{8,16},{12,20},{16,8},{20,12},{9,17},{13,21},{17,9},{21,13},{10,18... | collective-permute-start | bytes 786440 | tf_op jit(solution)/shard_map/ppermute | solution.py:535
  51.2 18.3 %collective-permute-start.10 = (f32[128,512]{1,0:T(8,128)S(1)}, f32[128,512]{1,0:T(8,128)S(1)}, u32[]{:S(2)}, u32[]{:S(2)}) collective-permute-start(f32[128,512]{1,0:T(8,128)S(1)} %get-tuple-element.134), channel_id=1, source_target_pairs={{0,4},{4,0},{8,12},{12,8},{16,20},{20,16},{24,28},{28,24},{1,5},{5... | collective-permute-start | bytes 786440 | tf_op jit(solution)/shard_map/ppermute | solution.py:540
  61.2 8.4 %collective-permute-start.11 = (f32[128,512]{1,0:T(8,128)S(1)}, f32[128,512]{1,0:T(8,128)S(1)}, u32[]{:S(2)}, u32[]{:S(2)}) collective-permute-start(f32[128,512]{1,0:T(8,128)S(1)} %get-tuple-element.98), channel_id=1, source_target_pairs={{0,4},{4,0},{8,12},{12,8},{16,20},{20,16},{24,28},{28,24},{1,5},{5... | collective-permute-start | bytes 786440 | tf_op jit(solution)/shard_map/ppermute | solution.py:545
  61.9 7.6 %copy-start.1 = (bf16[1024,2048]{1,0:T(8,128)(2,1)S(1)}, bf16[1024,2048]{1,0:T(8,128)(2,1)}, u32[]{:S(2)}) copy-start(bf16[1024,2048]{1,0:T(8,128)(2,1)} %get-tuple-element.61.ys_ref.refs_2_) | copy-start | bytes 12582916
  81.1 3.1 %collective-permute-start.14 = (f32[8,128]{1,0:T(8,128)S(1)}, f32[8,128]{1,0:T(8,128)S(1)}, u32[]{:S(2)}, u32[]{:S(2)}) collective-permute-start(f32[8,128]{1,0:T(8,128)S(1)} %get-tuple-element.97), channel_id=1, source_target_pairs={{0,3},{1,2},{2,1},{3,0},{4,7},{5,6},{6,5},{7,4},{8,11},{9,10},{10,... | collective-permute-start | bytes 12296 | tf_op jit(solution)/shard_map/ppermute | solution.py:485
  81.2 3.7 %collective-permute-start.13 = (f32[8,128]{1,0:T(8,128)S(1)}, f32[8,128]{1,0:T(8,128)S(1)}, u32[]{:S(2)}, u32[]{:S(2)}) collective-permute-start(f32[8,128]{1,0:T(8,128)S(1)} %get-tuple-element.97), channel_id=1, source_target_pairs={{0,2},{1,3},{2,0},{3,1},{4,6},{5,7},{6,4},{7,5},{8,10},{9,11},{10,... | collective-permute-start | bytes 12296 | tf_op jit(solution)/shard_map/ppermute | solution.py:485
  82.8 2.1 %collective-permute-start.12 = (f32[8,128]{1,0:T(8,128)S(1)}, f32[8,128]{1,0:T(8,128)S(1)}, u32[]{:S(2)}, u32[]{:S(2)}) collective-permute-start(f32[8,128]{1,0:T(8,128)S(1)} %get-tuple-element.97), channel_id=1, source_target_pairs={{0,1},{1,0},{2,3},{3,2},{4,5},{5,4},{6,7},{7,6},{8,9},{9,8},{10,11... | collective-permute-start | bytes 12296 | tf_op jit(solution)/shard_map/ppermute | solution.py:485
  84.9 6.3 %collective-permute-start.17 = (f32[8,128]{1,0:T(8,128)S(1)}, f32[8,128]{1,0:T(8,128)S(1)}, u32[]{:S(2)}, u32[]{:S(2)}) collective-permute-start(f32[8,128]{1,0:T(8,128)S(1)} %add_add_fusion.1), channel_id=1, source_target_pairs={{0,12},{4,8},{8,4},{12,0},{16,28},{20,24},{24,20},{28,16},{1,13},{... | collective-permute-start | bytes 12296 | tf_op jit(solution)/shard_map/ppermute | solution.py:485
  89.7 3.6 %collective-permute-start.16 = (f32[8,128]{1,0:T(8,128)S(1)}, f32[8,128]{1,0:T(8,128)S(1)}, u32[]{:S(2)}, u32[]{:S(2)}) collective-permute-start(f32[8,128]{1,0:T(8,128)S(1)} %add_add_fusion.1), channel_id=1, source_target_pairs={{0,8},{4,12},{8,0},{12,4},{16,24},{20,28},{24,16},{28,20},{1,9},{5... | collective-permute-start | bytes 12296 | tf_op jit(solution)/shard_map/ppermute | solution.py:485
  89.7 3.6 %collective-permute-start.15 = (f32[8,128]{1,0:T(8,128)S(1)}, f32[8,128]{1,0:T(8,128)S(1)}, u32[]{:S(2)}, u32[]{:S(2)}) collective-permute-start(f32[8,128]{1,0:T(8,128)S(1)} %add_add_fusion.1), channel_id=1, source_target_pairs={{0,4},{4,0},{8,12},{12,8},{16,20},{20,16},{24,28},{28,24},{1,5},{5... | collective-permute-start | bytes 12296 | tf_op jit(solution)/shard_map/ppermute | solution.py:485
  93.3 4.6 %collective-permute-start.18 = (f32[8,128]{1,0:T(8,128)S(1)}, f32[8,128]{1,0:T(8,128)S(1)}, u32[]{:S(2)}, u32[]{:S(2)}) collective-permute-start(f32[8,128]{1,0:T(8,128)S(1)} %add_add_fusion), channel_id=1, source_target_pairs={{0,16},{4,20},{8,24},{12,28},{16,0},{20,4},{24,8},{28,12},{1,17},{... | collective-permute-start | bytes 12296 | tf_op jit(solution)/shard_map/ppermute | solution.py:485

commit v10 on v9

--- a/solution.py
+++ b/solution.py
@@ -287,21 +287,16 @@
     )(xs, ys, b, c)
 
 
-def grads_kernel(first, scale, part, half, begin, *refs):
-    y_ref, xs_ref, ys_ref, dy_ref, direct_ref, b_ref, c_ref, columns_ref, table_ref = refs[:9]
-    raw_ref, bias_ref, rate_ref, bt, ct, left, right, adder = refs[9:17]
-    held = refs[17:21]
-    refs = refs[21:]
-    dc_in, db_in = refs[:2]
-    refs = refs[2:]
-    if not first:
-        par_in = refs[0]
-        refs = refs[3:]
-    dx_ref, dc_ref, db_ref, draw_ref, par_ref = refs[:5]
-    dc_sum, db_sum, terms, dc_old, db_old, sems = refs[5:]
+def grads_kernel(first, part, half, begin, heads, *refs):
+    y_ref, xs_ref, ys_ref, dy_ref, b_ref, c_ref, columns_ref, table_ref = refs[:8]
+    bt, ct, left, right, adder = refs[8:13]
+    held = refs[13:17]
+    dc_in, db_in = refs[17:19]
+    refs = refs[19:] if first else refs[21:]
+    dx_ref, dc_ref, db_ref, sums_ref = refs[:4]
+    dc_sum, db_sum, terms, dc_old, db_old, sems = refs[4:]
     old = [(dc_in, dc_old, sems.at[0]), (db_in, db_old, sems.at[1])]
     g = pl.program_id(0)
-    heads = raw_ref.shape[1]
     length, width = xs_ref.shape
     states = b_ref.shape[1]
     blocks = length // GROUP
@@ -317,7 +312,6 @@
             pltpu.make_async_copy(source, target, sem).start()
         dc_sum[...] = jnp.zeros_like(dc_sum)
         db_sum[...] = jnp.zeros_like(db_sum)
-        par_ref[...] = jnp.zeros_like(par_ref) if first else par_in[...]
 
     own = begin + g == y_ref[0]
     early = jnp.where(own, held[0][...], held[2][...])
@@ -357,26 +351,9 @@
         dc_sum[n] += dot(scaled_dy, entering_low[n], NT)
         db_sum[n] += dot(scaled_x, leaving_low[n], NT)
     added = dot(terms[...], adder[...], NN).T
-    added = [added[:, rows[n]] for n in range(blocks)]
+    sums_ref[0, : 2 * heads] = added[: 2 * heads]
     edge = head_sums(jnp.concatenate(edges + [edges[0]] * (8 - blocks), axis=0), member)
-    slopes = running(
-        jnp.concatenate([a[:heads] for a in added], axis=0), lower.astype(BF16)
-    )
-    slope = jnp.concatenate(
-        [slopes[n * heads : (n + 1) * heads] + edge[:, n : n + 1] for n in range(blocks)], axis=1
-    )
-    v = jnp.concatenate([a[heads : 2 * heads] for a in added], axis=1)
-    raw = raw_ref[0] + column(bias_ref[...], piece, heads)
-    step = softplus(raw)
-    draw = (v / step - column(rate_ref[...], piece, heads) * slope) / (1.0 + jnp.exp(-raw))
-    draw_ref[0] = draw
-    values = (
-        jnp.sum(draw, axis=1, keepdims=True),
-        jnp.sum(head_sums(direct_ref[...], member), axis=1, keepdims=True),
-        -jnp.sum(step * slope, axis=1, keepdims=True),
-    )
-    for k, value in enumerate(values):
-        par_ref[k : k + 1] += lanes_of(value * scale, piece, (heads, par_ref.shape[1]))
+    sums_ref[0, 2 * heads :, :8] = edge
 
     @pl.when(g == pl.num_programs(0) - 1)
     def _():
@@ -387,13 +364,10 @@
             db_ref[rows[n], :] = db_old[rows[n], :] + db_sum[n]
 
 
-def local_grads(part, begin, count, scale, y, saved, dy, b, c, vectors, held, before):
+def local_grads(part, begin, count, heads, y, saved, dy, b, c, held, before):
     xs, ys, direct, factor_columns, table, left, right, bt, ct = saved
-    raw, bias, rate, _ = vectors
     length, channels = xs.shape
     pieces = 2 * PARTS
-    heads = raw.shape[1] // pieces
-    raw = raw.reshape(pieces, heads, length)
     width = channels // pieces
     states = b.shape[1]
     blocks = length // GROUP
@@ -403,33 +377,30 @@
     place = lambda g, y: (0, (begin + g) * half + part)
     columns = pl.BlockSpec((length, width), place)
     maps = pl.BlockSpec((length, states), whole)
-    line = pl.BlockSpec(bias.shape, whole)
-    lines = pl.BlockSpec((1, heads, length), lambda g, y: ((begin + g) * half + part, 0, 0))
-    params = pl.BlockSpec((8, 128), whole)
+    lines = pl.BlockSpec((1, 3 * heads, length), lambda g, y: ((begin + g) * half + part, 0, 0))
     anywhere = pl.BlockSpec(memory_space=pl.ANY)
-    in_specs = [columns, columns, columns, pl.BlockSpec((8, width), place), maps, maps]
+    in_specs = [columns, columns, columns, maps, maps]
     in_specs += [
         pl.BlockSpec(factor_columns.shape, whole),
         pl.BlockSpec((table.shape[0], width), place),
     ]
-    in_specs += [lines, line, line]
-    args = [xs, ys, dy, direct, b, c, factor_columns, table, raw, bias, rate]
+    args = [xs, ys, dy, b, c, factor_columns, table]
     fixed = [bt, ct, left, right, adding(width, heads, (0, 0, 1)), *held]
     in_specs += [pl.BlockSpec(a.shape, lambda g, y, n=len(a.shape): (0,) * n) for a in fixed]
     args += fixed
     aliases = {}
-    dx, dc, db, draw, par = before
+    dx, dc, db, sums = before
     args += [dc, db]
     in_specs += [anywhere, anywhere]
     if not first:
-        args += [par, dx, draw]
-        in_specs += [params, anywhere, anywhere]
-        aliases = {24: 0, 25: 3}
+        args += [dx, sums]
+        in_specs += [anywhere, anywhere]
+        aliases = {19: 0, 20: 3}
     grid_spec = pltpu.PrefetchScalarGridSpec(
         num_scalar_prefetch=1,
         grid=(count,),
         in_specs=in_specs,
-        out_specs=[columns, maps, maps, lines, params],
+        out_specs=[columns, maps, maps, lines],
         scratch_shapes=[
             pltpu.VMEM((blocks, GROUP, states), F32),
             pltpu.VMEM((blocks, GROUP, states), F32),
@@ -440,14 +411,13 @@
         ],
     )
     return pl.pallas_call(
-        functools.partial(grads_kernel, first, scale, part, half, begin),
+        functools.partial(grads_kernel, first, part, half, begin, heads),
         grid_spec=grid_spec,
         out_shape=[
             jax.ShapeDtypeStruct((length, channels), BF16),
             jax.ShapeDtypeStruct((length, states), F32),
             jax.ShapeDtypeStruct((length, states), F32),
-            jax.ShapeDtypeStruct((pieces, heads, length), F32),
-            jax.ShapeDtypeStruct((8, 128), F32),
+            jax.ShapeDtypeStruct((pieces, 3 * heads, length), F32),
         ],
         input_output_aliases=aliases,
         compiler_params=pltpu.CompilerParams(vmem_limit_bytes=SMALL_LIMIT),
@@ -458,6 +428,54 @@
         ),
         name="local_grads",
     )(y, *args)
+
+
+def steps_kernel(scale, sums_ref, raw_ref, bias_ref, rate_ref, direct_ref, draw_ref, par_ref):
+    pieces, heads, length = draw_ref.shape
+    all_heads = pieces * heads
+    blocks = length // GROUP
+    rows = [slice(n * GROUP, (n + 1) * GROUP) for n in range(blocks)]
+    stacked = [sums_ref[p, :heads, rows[n]] for p in range(pieces) for n in range(blocks)]
+    slopes = running(jnp.concatenate(stacked, axis=0), triangle(GROUP, True).astype(BF16))
+    lines = []
+    for p in range(pieces):
+        edge = sums_ref[p, 2 * heads :, :8]
+        at = [(p * blocks + n) * heads for n in range(blocks)]
+        parts = [slopes[at[n] : at[n] + heads] + edge[:, n : n + 1] for n in range(blocks)]
+        lines.append(jnp.concatenate(parts, axis=1))
+    slope = jnp.concatenate(lines, axis=0)
+    v = jnp.concatenate([sums_ref[p, heads : 2 * heads] for p in range(pieces)], axis=0)
+    raw = raw_ref[0] + column(bias_ref[...], 0, all_heads)
+    step = softplus(raw)
+    draw = (v / step - column(rate_ref[...], 0, all_heads) * slope) / (1.0 + jnp.exp(-raw))
+    for p in range(pieces):
+        draw_ref[p] = draw[p * heads : (p + 1) * heads]
+    member = head_matrix(all_heads, direct_ref.shape[1]).astype(BF16)
+    values = (
+        jnp.sum(draw, axis=1, keepdims=True),
+        jnp.sum(head_sums(direct_ref[...], member), axis=1, keepdims=True),
+        -jnp.sum(step * slope, axis=1, keepdims=True),
+    )
+    par_ref[...] = jnp.zeros_like(par_ref)
+    for k, value in enumerate(values):
+        par_ref[k : k + 1] = lanes_of(value * scale, 0, (all_heads, par_ref.shape[1]))
+
+
+def steps_grads(scale, sums, vectors, direct):
+    raw, bias, rate, _ = vectors
+    pieces, rows, length = sums.shape
+    return pl.pallas_call(
+        functools.partial(steps_kernel, scale),
+        out_shape=[
+            jax.ShapeDtypeStruct((pieces, rows // 3, length), F32),
+            jax.ShapeDtypeStruct((8, 128), F32),
+        ],
+        compiler_params=pltpu.CompilerParams(vmem_limit_bytes=SMALL_LIMIT),
+        cost_estimate=pl.CostEstimate(
+            flops=1000 * length * pieces, bytes_accessed=8 * sums.size, transcendentals=0
+        ),
+        name="steps_grads",
+    )(sums, raw, bias, rate, direct)
 
 
 def adding(width, heads, places):
@@ -606,7 +624,7 @@
         *most, final = held
         held = (*most, after(final, token))
         return local_grads(
-            part, begin, count, scale, here, saved, dy, b, c, vectors, held, found
+            part, begin, count, heads // (2 * PARTS), here, saved, dy, b, c, held, found
         )
 
     for part, k in order:
@@ -623,10 +641,11 @@
         if (part, k) == (0, 1):
             dc, db = pairs_grads(saved, after(b, token), c)
             token = dc
-            found = (None, dc, db, None, None)
+            found = (None, dc, db, None)
     found = grads(0, 1, 1, token, held)
     found = grads(1, 0, 2, found[-1], next(flows[1]))
-    dx, dc, db, draw, params = found
+    dx, dc, db, sums = found
+    draw, params = steps_grads(scale, sums, vectors, saved[2])
     summed = summed_over(summed_over(params, "batch"), "seq")
     return (
         dx[None],

time: 99.4 us -> 100 us (level)
    pallas_call x3 -> x4, Pallas kernels: 26.4 us -> 27.2 us  [the longest x3 26.1 us: local_grads(): pl.pallas_call(functools.partial(grads_kernel, first, part, half, begin,...]
where the time goes in v10:
time: 100 us; the launch traced here: 99.7 us
  Pallas kernels  48.8 us (49%)
  starting transfers between devices  26.9 us (27%)
  waiting for transfers between devices  18.4 us (18%)
  other arithmetic  3.23 us (3%)
  local copies, waits for them, and re-layouts  1.19 us (1%)
  between operations  1.1 us (1%)
    pallas_call x3, Pallas kernels, local_grads(): pl.pallas_call(functools.partial(grads_kernel, first, part, half, begin,...  26.1 us
    pallas_call x3, Pallas kernels, local_states(): pl.pallas_call(functools.partial(local_kernel, first, last, count), grid_...  15.3 us
    ppermute x7, starting transfers between devices, summed_over(): lax.ppermute(value, axis, [(i, i ^ s) for i in range(size)])  10.5 us
    pallas_call x1, Pallas kernels, pairs_grads(): pl.pallas_call(pairs_kernel, grid=(length // GROUP,), in_specs=[columns,...  6.41 us
    ppermute x7, waiting for transfers between devices, summed_over(): lax.ppermute(value, axis, [(i, i ^ s) for i in range(size)])  5.94 us
    ppermute x2, waiting for transfers between devices, entering(): far = lax.ppermute(message, 'seq', both([(1, 3), (2, 0)]))  5.42 us
    ppermute x2, starting transfers between devices, entering(): near = lax.ppermute(message, 'seq', both([(0, 1), (1, 0), (2, 3), (3, 2)]))  4.62 us
    ppermute x2, starting transfers between devices, entering(): got = lax.ppermute(message, 'seq', swap)  4.48 us
  transfers between devices with their start and end apart: 19, of which 10 were waited for; matrix products, arithmetic and copies ran while one was open for 1% of the time, Pallas kernels for 32%

profile of v10, /device:TPU:0, one launch (start us, length us, event | category | flops | bytes accessed | tf_op | source)
XLA Modules:
  0.0 99.7 jit_solution(11182241793237654266)
XLA Ops:
  0.6 4.6 %local_states.3 = (f32[264,512]{1,0:T(8,128)}, bf16[1024,2048]{1,0:T(8,128)(2,1)}, bf16[1024,2048]{1,0:T(8,128)(2,1)}, f32[8,2048]{1,0:T(8,128)}, bf16[1024,128]{1,0:T(8,128)(2,1)}, /*index=5*/f32[16,2048]{1,0:T(8,128)}) custom-call(s32[1]{0:T(128)} %bitcast.7.refs_0_, bf16[1024,2048]{1,0:T(8,128)(2,1)} %bitcast.64, bf16[1024,2048]{1,0:T(8,128)(2,1)} %bitcast.58, ...), custom_call_target="tpu_custom_call" | custom-call | flops 536870912 | bytes 4194304 | tf_op jit(solution)/shard_map/local_states/pallas_call | solution.py:246
  5.2 3.0 %collective-permute-start.1 = (f32[264,512]{1,0:T(8,128)}, f32[264,512]{1,0:T(8,128)S(1)}, u32[]{:S(2)}, u32[]{:S(2)}) collective-permute-start(f32[264,512]{1,0:T(8,128)} %get-tuple-element.67), channel_id=1, source_target_pairs={{0,4},{4,0},{8,12},{12,8},{16,20},{20,16},{24,28},{28,24},{1,5},{5... | collective-permute-start | bytes 1622024 | tf_op jit(solution)/shard_map/ppermute | solution.py:541
  8.2 3.8 %local_states.4 = (f32[264,512]{1,0:T(8,128)}, bf16[1024,2048]{1,0:T(8,128)(2,1)}, bf16[1024,2048]{1,0:T(8,128)(2,1)}, f32[8,2048]{1,0:T(8,128)}) custom-call(s32[1]{0:T(128)} %bitcast.11.refs_0_, bf16[1024,2048]{1,0:T(8,128)(2,1)} %bitcast.65, bf16[1024,2048]{1,0:T(8,128)(2,1)} %bitcast.59, ...), custom_call_target="tpu_custom_call", output_to_operand_aliasing={{1}: (7, {}), {2}: (8, {}), {3}: (9, {})} | custom-call | flops 536870912 | bytes 4194304 | tf_op jit(solution)/shard_map/local_states/pallas_call | solution.py:246
  12.0 6.9 %local_states.5 = (f32[264,512]{1,0:T(8,128)}, f32[264,512]{1,0:T(8,128)}, bf16[1024,2048]{1,0:T(8,128)(2,1)}, bf16[1024,2048]{1,0:T(8,128)(2,1)}, f32[8,2048]{1...) custom-call(s32[1]{0:T(128)} %bitcast.2.refs_0_, ...), custom_call_target="tpu_custom_call", output_to_operand_aliasing={{2}: (7, {}), {3}: (8, {}), {4}: (9, {})} | custom-call | flops 1073741824 | bytes 8388608 | tf_op jit(solution)/shard_map/local_states/pallas_call | solution.py:246
  18.9 1.8 %collective-permute-done.1 = f32[264,512]{1,0:T(8,128)S(1)} collective-permute-done((f32[264,512]{1,0:T(8,128)}, f32[264,512]{1,0:T(8,128)S(1)}, u32[]{:S(2)}, u32[]{:S(2)}) %collective-permute-start.1) | collective-permute-done | bytes 540704 | tf_op jit(solution)/shard_map/ppermute | solution.py:541
  20.7 0.9 fusion.1
  21.6 1.2 %add_select_fusion.11 = (f32[128,512]{1,0:T(8,128)S(1)}, f32[128,512]{1,0:T(8,128)S(1)}, f32[128,512]{1,0:T(8,128)S(1)}) fusion(f32[512]{0:T(512)S(1)} %bitcast.89, f32[512]{0:T(512)S(1)} %bitcast.88, pred[]{:T(512)S(6)} %or.9, f32[264,512]{1,0:T(8,128)S(1)} %collective-permute-done.1, f32[264,512]{1,0:T(8,128)} %get-tuple-element.66, pred[]{:T(512)S(6)} %eq.12), kind=kLoop, calls=%fused_computation.15 | loop fusion | flops 589824 | bytes 1839106 | tf_op jit(solution)/shard_map/jit(_where)/select_n | solution.py:531
  22.8 1.9 %collective-permute-start.2 = (f32[136,512]{1,0:T(8,128)S(1)}, f32[136,512]{1,0:T(8,128)S(1)}, u32[]{:S(2)}, u32[]{:S(2)}) collective-permute-start(f32[136,512]{1,0:T(8,128)S(1)} %pad_maximum_fusion), channel_id=1, source_target_pairs={{0,8},{4,12},{8,0},{12,4},{16,24},{20,28},{24,16},{28,20},{1,9},{5... | collective-permute-start | bytes 835592 | tf_op jit(solution)/shard_map/ppermute | solution.py:549
  24.6 1.5 %collective-permute-start = (f32[264,512]{1,0:T(8,128)S(1)}, f32[264,512]{1,0:T(8,128)S(1)}, u32[]{:S(2)}, u32[]{:S(2)}) collective-permute-start(f32[264,512]{1,0:T(8,128)S(1)} %copy-done.19), channel_id=1, source_target_pairs={{0,4},{4,0},{8,12},{12,8},{16,20},{20,16},{24,28},{28,24},{1,5},{5... | collective-permute-start | bytes 1622024 | tf_op jit(solution)/shard_map/ppermute | solution.py:541
  26.1 6.4 %pairs_grads.1 = (f32[1024,128]{1,0:T(8,128)}, f32[1024,128]{1,0:T(8,128)}) custom-call(bf16[1024,2048]{1,0:T(8,128)(2,1)} %get-tuple-element.59.xs_ref.refs_1_, bf16[1024,2048]{1,0:T(8,128)(2,1)} %get-tuple-element.60.ys_ref.refs_2_, bf16[1024,128]{1,0:T(8,128)(2,1)} %bitcast.43, bf16[1024,128]{1,0:T(8,128)(2,1)} %bitcast.50), custom_call_target="tpu_custom_call" | custom-call | flops 1073741824 | bytes 8388608 | tf_op jit(solution)/shard_map/pairs_grads/pallas_call | solution.py:274
  32.6 0.2 broadcast_select_fusion.4
  32.9 0.0 copy-start.7
  32.9 1.6 %collective-permute-start.5 = (f32[128,512]{1,0:T(8,128)S(1)}, f32[128,512]{1,0:T(8,128)S(1)}, u32[]{:S(2)}, u32[]{:S(2)}) collective-permute-start(f32[128,512]{1,0:T(8,128)S(1)} %get-tuple-element.137), channel_id=1, source_target_pairs={{8,24},{12,28},{16,0},{20,4},{9,25},{13,29},{17,1},{21,5},{10,26},... | collective-permute-start | bytes 786440 | tf_op jit(solution)/shard_map/ppermute | solution.py:554
  34.5 0.8 collective-permute-start.4
  35.3 0.6 collective-permute-start.8
  35.9 2.7 %collective-permute-done = f32[264,512]{1,0:T(8,128)S(1)} collective-permute-done((f32[264,512]{1,0:T(8,128)S(1)}, f32[264,512]{1,0:T(8,128)S(1)}, u32[]{:S(2)}, u32[]{:S(2)}) %collective-permute-start) | collective-permute-done | bytes 540704 | tf_op jit(solution)/shard_map/ppermute | solution.py:541
  38.6 0.1 add_select_fusion.8
  38.7 2.8 %collective-permute-start.3 = (f32[136,512]{1,0:T(8,128)S(1)}, f32[136,512]{1,0:T(8,128)S(1)}, u32[]{:S(2)}, u32[]{:S(2)}) collective-permute-start(f32[136,512]{1,0:T(8,128)S(1)} %pad_maximum_fusion.1), channel_id=1, source_target_pairs={{0,8},{4,12},{8,0},{12,4},{16,24},{20,28},{24,16},{28,20},{1,9},{5... | collective-permute-start | bytes 835592 | tf_op jit(solution)/shard_map/ppermute | solution.py:549
  41.5 3.8 %collective-permute-done.5 = f32[128,512]{1,0:T(8,128)S(1)} collective-permute-done((f32[128,512]{1,0:T(8,128)S(1)}, f32[128,512]{1,0:T(8,128)S(1)}, u32[]{:S(2)}, u32[]{:S(2)}) %collective-permute-start.5) | collective-permute-done | bytes 262176 | tf_op jit(solution)/shard_map/ppermute | solution.py:554
  45.3 0.1 broadcast_select_fusion.3
  45.4 0.1 broadcast_select_fusion.6
  45.5 0.6 collective-permute-start.9
  46.1 2.6 %collective-permute-done.3 = f32[136,512]{1,0:T(8,128)S(1)} collective-permute-done((f32[136,512]{1,0:T(8,128)S(1)}, f32[136,512]{1,0:T(8,128)S(1)}, u32[]{:S(2)}, u32[]{:S(2)}) %collective-permute-start.3) | collective-permute-done | bytes 278560 | tf_op jit(solution)/shard_map/ppermute | solution.py:549
  48.7 0.2 broadcast_select_fusion.2
  48.9 1.3 %collective-permute-start.7 = (f32[128,512]{1,0:T(8,128)S(1)}, f32[128,512]{1,0:T(8,128)S(1)}, u32[]{:S(2)}, u32[]{:S(2)}) collective-permute-start(f32[128,512]{1,0:T(8,128)S(1)} %get-tuple-element.136), channel_id=1, source_target_pairs={{8,24},{12,28},{16,0},{20,4},{9,25},{13,29},{17,1},{21,5},{10,26},... | collective-permute-start | bytes 786440 | tf_op jit(solution)/shard_map/ppermute | solution.py:554
  50.2 0.9 collective-permute-start.6
  51.1 0.1 pad_add_fusion.refs_0_
  51.2 0.9 collective-permute-start.10
  52.2 7.1 %local_grads.3 = (bf16[1024,2048]{1,0:T(8,128)(2,1)}, f32[1024,128]{1,0:T(8,128)S(1)}, f32[1024,128]{1,0:T(8,128)S(1)}, f32[4,24,1024]{2,1,0:T(8,128)S(1)}) custom-call(s32[2]{0:T(128)S(1)} %pad_add_fusion.refs_0_, bf16[1024,2048]{1,0:T(8,128)(2,1)S(1)} %copy-done, bf16[1024,2048]{1,0:T(8,128)(2,1)} %get-tuple-element.60.ys_ref.refs_2_, ...), custom_call_target="tpu_custom_call" | custom-call | flops 2415919104 | bytes 3145728 | tf_op jit(solution)/shard_map/local_grads/pallas_call | solution.py:413
  59.3 1.7 %collective-permute-done.7 = f32[128,512]{1,0:T(8,128)S(1)} collective-permute-done((f32[128,512]{1,0:T(8,128)S(1)}, f32[128,512]{1,0:T(8,128)S(1)}, u32[]{:S(2)}, u32[]{:S(2)}) %collective-permute-start.7) | collective-permute-done | bytes 262176 | tf_op jit(solution)/shard_map/ppermute | solution.py:554
  61.0 0.2 broadcast_select_fusion
  61.1 0.7 collective-permute-start.11
  61.9 7.4 %local_grads.4 = (bf16[1024,2048]{1,0:T(8,128)(2,1)}, f32[1024,128]{1,0:T(8,128)S(1)}, f32[1024,128]{1,0:T(8,128)S(1)}, f32[4,24,1024]{2,1,0:T(8,128)S(1)}) custom-call(s32[2]{0:T(128)S(1)} %pad_add_fusion.refs_0_, bf16[1024,2048]{1,0:T(8,128)(2,1)S(1)} %copy-done, ...), custom_call_target="tpu_custom_call", output_to_operand_aliasing={{0}: (19, {}), {3}: (20, {})} | custom-call | flops 2415919104 | bytes 3145728 | tf_op jit(solution)/shard_map/local_grads/pallas_call | solution.py:413
  69.3 0.1 broadcast_select_fusion.1.refs_14_
  69.5 11.6 %local_grads.5 = (bf16[1024,2048]{1,0:T(8,128)(2,1)}, f32[1024,128]{1,0:T(8,128)}, f32[1024,128]{1,0:T(8,128)}, f32[4,24,1024]{2,1,0:T(8,128)S(1)}) custom-call(s32[2]{0:T(128)S(1)} %pad_add_fusion.refs_0_, bf16[1024,2048]{1,0:T(8,128)(2,1)S(1)} %copy-done, bf16[1024,2048]{1,0:T(8,128)(2,1)S(1)} %copy-done.1, ...), custom_call_target="tpu_custom_call", output_to_operand_aliasing={{0}: (19, {}), {3}: (20, {})} | custom-call | flops 4831838208 | bytes 6291456 | tf_op jit(solution)/shard_map/local_grads/pallas_call | solution.py:413
  81.1 1.0 %steps_grads.1 = (f32[4,8,1024]{2,1,0:T(8,128)}, f32[8,128]{1,0:T(8,128)S(1)}) custom-call(f32[4,24,1024]{2,1,0:T(8,128)S(1)} %get-tuple-element.92.sums_ref, f32[1,32,1024]{2,1,0:T(8,128)S(1)} %copy-done.12, f32[1,32]{1,0:T(1,128)S(1)} %bitcast.55, f32[1,32]{1,0:T(1,128)S(1)} %bitcast.57, f32[8,2048]{1,0:T(8,128)S(1)} %copy-done.11), custom_call_target="tpu_custom_call" | custom-call | flops 4096000 | bytes 786432 | tf_op jit(solution)/shard_map/steps_grads/pallas_call | solution.py:467
  82.1 1.5 %collective-permute-start.13 = (f32[8,128]{1,0:T(8,128)S(1)}, f32[8,128]{1,0:T(8,128)S(1)}, u32[]{:S(2)}, u32[]{:S(2)}) collective-permute-start(f32[8,128]{1,0:T(8,128)S(1)} %get-tuple-element.95), channel_id=1, source_target_pairs={{0,2},{1,3},{2,0},{3,1},{4,6},{5,7},{6,4},{7,5},{8,10},{9,11},{10,... | collective-permute-start | bytes 12296 | tf_op jit(solution)/shard_map/ppermute | solution.py:503
  83.7 0.3 collective-permute-start.12
  84.0 1.2 %collective-permute-done.14 = f32[8,128]{1,0:T(8,128)S(1)} collective-permute-done((f32[8,128]{1,0:T(8,128)S(1)}, f32[8,128]{1,0:T(8,128)S(1)}, u32[]{:S(2)}, u32[]{:S(2)}) %collective-permute-start.14) | collective-permute-done | bytes 4128 | tf_op jit(solution)/shard_map/ppermute | solution.py:503
  85.2 0.6 collective-permute-done.13
  85.8 4.7 %collective-permute-start.17 = (f32[8,128]{1,0:T(8,128)S(1)}, f32[8,128]{1,0:T(8,128)S(1)}, u32[]{:S(2)}, u32[]{:S(2)}) collective-permute-start(f32[8,128]{1,0:T(8,128)S(1)} %add_add_fusion.1), channel_id=1, source_target_pairs={{0,12},{4,8},{8,4},{12,0},{16,28},{20,24},{24,20},{28,16},{1,13},{... | collective-permute-start | bytes 12296 | tf_op jit(solution)/shard_map/ppermute | solution.py:503
  90.5 1.1 %collective-permute-start.15 = (f32[8,128]{1,0:T(8,128)S(1)}, f32[8,128]{1,0:T(8,128)S(1)}, u32[]{:S(2)}, u32[]{:S(2)}) collective-permute-start(f32[8,128]{1,0:T(8,128)S(1)} %add_add_fusion.1), channel_id=1, source_target_pairs={{0,4},{4,0},{8,12},{12,8},{16,20},{20,16},{24,28},{28,24},{1,5},{5... | collective-permute-start | bytes 12296 | tf_op jit(solution)/shard_map/ppermute | solution.py:503
  91.5 0.5 collective-permute-done.17
  92.0 2.0 %collective-permute-done.16 = f32[8,128]{1,0:T(8,128)S(1)} collective-permute-done((f32[8,128]{1,0:T(8,128)S(1)}, f32[8,128]{1,0:T(8,128)S(1)}, u32[]{:S(2)}, u32[]{:S(2)}) %collective-permute-start.16) | collective-permute-done | bytes 4128 | tf_op jit(solution)/shard_map/ppermute | solution.py:503
  94.1 2.9 %collective-permute-start.18 = (f32[8,128]{1,0:T(8,128)S(1)}, f32[8,128]{1,0:T(8,128)S(1)}, u32[]{:S(2)}, u32[]{:S(2)}) collective-permute-start(f32[8,128]{1,0:T(8,128)S(1)} %add_add_fusion), channel_id=1, source_target_pairs={{0,16},{4,20},{8,24},{12,28},{16,0},{20,4},{24,8},{28,12},{1,17},{... | collective-permute-start | bytes 12296 | tf_op jit(solution)/shard_map/ppermute | solution.py:503
  97.0 1.6 %collective-permute-done.18 = f32[8,128]{1,0:T(8,128)S(1)} collective-permute-done((f32[8,128]{1,0:T(8,128)S(1)}, f32[8,128]{1,0:T(8,128)S(1)}, u32[]{:S(2)}, u32[]{:S(2)}) %collective-permute-start.18) | collective-permute-done | bytes 4128 | tf_op jit(solution)/shard_map/ppermute | solution.py:503
  98.6 0.5 slice_bitcast_fusion
  99.2 0.6 slice.150
  (60 shorter events, 0.2 us)
Async XLA Ops:
  5.2 15.5 %collective-permute-start.1 = (f32[264,512]{1,0:T(8,128)}, f32[264,512]{1,0:T(8,128)S(1)}, u32[]{:S(2)}, u32[]{:S(2)}) collective-permute-start(f32[264,512]{1,0:T(8,128)} %get-tuple-element.67), channel_id=1, source_target_pairs={{0,4},{4,0},{8,12},{12,8},{16,20},{20,16},{24,28},{28,24},{1,5},{5... | collective-permute-start | bytes 1622024 | tf_op jit(solution)/shard_map/ppermute | solution.py:541
  12.0 12.6 %copy-start.19 = (f32[264,512]{1,0:T(8,128)S(1)}, f32[264,512]{1,0:T(8,128)}, u32[]{:S(2)}) copy-start(f32[264,512]{1,0:T(8,128)} %get-tuple-element.65) | copy-start | bytes 1622020
  22.8 9.8 %collective-permute-start.2 = (f32[136,512]{1,0:T(8,128)S(1)}, f32[136,512]{1,0:T(8,128)S(1)}, u32[]{:S(2)}, u32[]{:S(2)}) collective-permute-start(f32[136,512]{1,0:T(8,128)S(1)} %pad_maximum_fusion), channel_id=1, source_target_pairs={{0,8},{4,12},{8,0},{12,4},{16,24},{20,28},{24,16},{28,20},{1,9},{5... | collective-permute-start | bytes 835592 | tf_op jit(solution)/shard_map/ppermute | solution.py:549
  24.6 13.9 %collective-permute-start = (f32[264,512]{1,0:T(8,128)S(1)}, f32[264,512]{1,0:T(8,128)S(1)}, u32[]{:S(2)}, u32[]{:S(2)}) collective-permute-start(f32[264,512]{1,0:T(8,128)S(1)} %copy-done.19), channel_id=1, source_target_pairs={{0,4},{4,0},{8,12},{12,8},{16,20},{20,16},{24,28},{28,24},{1,5},{5... | collective-permute-start | bytes 1622024 | tf_op jit(solution)/shard_map/ppermute | solution.py:541
  26.1 6.4 %copy-start.18 = (f32[264,512]{1,0:T(8,128)S(1)}, f32[264,512]{1,0:T(8,128)}, u32[]{:S(2)}) copy-start(f32[264,512]{1,0:T(8,128)} %get-tuple-element.66) | copy-start | bytes 1622020
  26.1 12.4 %copy-start.17 = (f32[264,512]{1,0:T(8,128)S(1)}, f32[264,512]{1,0:T(8,128)}, u32[]{:S(2)}) copy-start(f32[264,512]{1,0:T(8,128)} %get-tuple-element.73) | copy-start | bytes 1622020
  32.6 19.5 %copy-start.14 = (f32[1024,128]{1,0:T(8,128)S(1)}, f32[1024,128]{1,0:T(8,128)}, u32[]{:S(2)}) copy-start(f32[1024,128]{1,0:T(8,128)} %get-tuple-element.77.refs_18_) | copy-start | bytes 1572868
  32.8 19.3 %copy-start = (bf16[1024,2048]{1,0:T(8,128)(2,1)S(1)}, bf16[1024,2048]{1,0:T(8,128)(2,1)}, u32[]{:S(2)}) copy-start(bf16[1024,2048]{1,0:T(8,128)(2,1)} %get-tuple-element.59.xs_ref.refs_1_) | copy-start | bytes 12582916
  32.8 19.3 %copy-start.2 = (bf16[1,1024,128]{2,1,0:T(8,128)(2,1)S(1)}, bf16[1,1024,128]{2,1,0:T(8,128)(2,1)}, u32[]{:S(2)}) copy-start(bf16[1,1024,128]{2,1,0:T(8,128)(2,1)} %param.12) | copy-start | bytes 786436
  32.8 19.3 %copy-start.3 = (bf16[1,1024,128]{2,1,0:T(8,128)(2,1)S(1)}, bf16[1,1024,128]{2,1,0:T(8,128)(2,1)}, u32[]{:S(2)}) copy-start(bf16[1,1024,128]{2,1,0:T(8,128)(2,1)} %param.13) | copy-start | bytes 786436
  32.9 19.3 %copy-start.4 = (bf16[1024,128]{1,0:T(8,128)(2,1)S(1)}, bf16[1024,128]{1,0:T(8,128)(2,1)}, u32[]{:S(2)}) copy-start(bf16[1024,128]{1,0:T(8,128)(2,1)} %get-tuple-element.51.refs_5_.refs_6_) | copy-start | bytes 786436
  32.9 19.3 %copy-start.5 = (bf16[4,256,256]{2,1,0:T(8,128)(2,1)S(1)}, bf16[4,256,256]{2,1,0:T(8,128)(2,1)}, u32[]{:S(2)}) copy-start(bf16[4,256,256]{2,1,0:T(8,128)(2,1)} %get-tuple-element.63.refs_10_) | copy-start | bytes 1572868
  32.9 19.3 %copy-start.6 = (bf16[4,256,256]{2,1,0:T(8,128)(2,1)S(1)}, bf16[4,256,256]{2,1,0:T(8,128)(2,1)}, u32[]{:S(2)}) copy-start(bf16[4,256,256]{2,1,0:T(8,128)(2,1)} %get-tuple-element.64.refs_11_) | copy-start | bytes 1572868
  32.9 19.3 %copy-start.7 = (bf16[1536,128]{1,0:T(8,128)(2,1)S(1)}, bf16[1536,128]{1,0:T(8,128)(2,1)}, u32[]{:S(2)}) copy-start(bf16[1536,128]{1,0:T(8,128)(2,1)} %constant.44.clone.refs_12_) | copy-start | bytes 1179652
  32.9 19.2 %copy-start.8 = (f32[16,2048]{1,0:T(8,128)S(1)}, f32[16,2048]{1,0:T(8,128)}, u32[]{:S(2)}) copy-start(f32[16,2048]{1,0:T(8,128)} %get-tuple-element.52.refs_6_.refs_7_) | copy-start | bytes 393220
  32.9 19.2 %copy-start.9 = (bf16[128,1024]{1,0:T(8,128)(2,1)S(1)}, bf16[128,1024]{1,0:T(8,128)(2,1)}, u32[]{:S(2)}) copy-start(bf16[128,1024]{1,0:T(8,128)(2,1)} %get-tuple-element.61.refs_8_) | copy-start | bytes 786436
  32.9 19.2 %copy-start.10 = (bf16[128,1024]{1,0:T(8,128)(2,1)S(1)}, bf16[128,1024]{1,0:T(8,128)(2,1)}, u32[]{:S(2)}) copy-start(bf16[128,1024]{1,0:T(8,128)(2,1)} %get-tuple-element.62.refs_9_) | copy-start | bytes 786436
  32.9 19.2 %copy-start.13 = (f32[1024,128]{1,0:T(8,128)S(1)}, f32[1024,128]{1,0:T(8,128)}, u32[]{:S(2)}) copy-start(f32[1024,128]{1,0:T(8,128)} %get-tuple-element.70.refs_17_) | copy-start | bytes 1572868
  32.9 12.3 %collective-permute-start.5 = (f32[128,512]{1,0:T(8,128)S(1)}, f32[128,512]{1,0:T(8,128)S(1)}, u32[]{:S(2)}, u32[]{:S(2)}) collective-permute-start(f32[128,512]{1,0:T(8,128)S(1)} %get-tuple-element.137), channel_id=1, source_target_pairs={{8,24},{12,28},{16,0},{20,4},{9,25},{13,29},{17,1},{21,5},{10,26},... | collective-permute-start | bytes 786440 | tf_op jit(solution)/shard_map/ppermute | solution.py:554
  34.5 10.7 %collective-permute-start.4 = (f32[128,512]{1,0:T(8,128)S(1)}, f32[128,512]{1,0:T(8,128)S(1)}, u32[]{:S(2)}, u32[]{:S(2)}) collective-permute-start(f32[128,512]{1,0:T(8,128)S(1)} %get-tuple-element.137), channel_id=1, source_target_pairs={{8,16},{12,20},{16,8},{20,12},{9,17},{13,21},{17,9},{21,13},{10,18... | collective-permute-start | bytes 786440 | tf_op jit(solution)/shard_map/ppermute | solution.py:553
  35.3 16.7 %collective-permute-start.8 = (f32[128,512]{1,0:T(8,128)S(1)}, f32[128,512]{1,0:T(8,128)S(1)}, u32[]{:S(2)}, u32[]{:S(2)}) collective-permute-start(f32[128,512]{1,0:T(8,128)S(1)} %get-tuple-element.135), channel_id=1, source_target_pairs={{0,4},{4,0},{8,12},{12,8},{16,20},{20,16},{24,28},{28,24},{1,5},{5... | collective-permute-start | bytes 786440 | tf_op jit(solution)/shard_map/ppermute | solution.py:558
  38.7 10.0 %collective-permute-start.3 = (f32[136,512]{1,0:T(8,128)S(1)}, f32[136,512]{1,0:T(8,128)S(1)}, u32[]{:S(2)}, u32[]{:S(2)}) collective-permute-start(f32[136,512]{1,0:T(8,128)S(1)} %pad_maximum_fusion.1), channel_id=1, source_target_pairs={{0,8},{4,12},{8,0},{12,4},{16,24},{20,28},{24,16},{28,20},{1,9},{5... | collective-permute-start | bytes 835592 | tf_op jit(solution)/shard_map/ppermute | solution.py:549
  45.5 6.6 %collective-permute-start.9 = (f32[128,512]{1,0:T(8,128)S(1)}, f32[128,512]{1,0:T(8,128)S(1)}, u32[]{:S(2)}, u32[]{:S(2)}) collective-permute-start(f32[128,512]{1,0:T(8,128)S(1)} %broadcast_select_fusion.6), channel_id=1, source_target_pairs={{0,4},{4,0},{8,12},{12,8},{16,20},{20,16},{24,28},{28,24},{1,5},{5... | collective-permute-start | bytes 786440 | tf_op jit(solution)/shard_map/ppermute | solution.py:563
  48.9 12.0 %collective-permute-start.7 = (f32[128,512]{1,0:T(8,128)S(1)}, f32[128,512]{1,0:T(8,128)S(1)}, u32[]{:S(2)}, u32[]{:S(2)}) collective-permute-start(f32[128,512]{1,0:T(8,128)S(1)} %get-tuple-element.136), channel_id=1, source_target_pairs={{8,24},{12,28},{16,0},{20,4},{9,25},{13,29},{17,1},{21,5},{10,26},... | collective-permute-start | bytes 786440 | tf_op jit(solution)/shard_map/ppermute | solution.py:554
  50.2 10.7 %collective-permute-start.6 = (f32[128,512]{1,0:T(8,128)S(1)}, f32[128,512]{1,0:T(8,128)S(1)}, u32[]{:S(2)}, u32[]{:S(2)}) collective-permute-start(f32[128,512]{1,0:T(8,128)S(1)} %get-tuple-element.136), channel_id=1, source_target_pairs={{8,16},{12,20},{16,8},{20,12},{9,17},{13,21},{17,9},{21,13},{10,18... | collective-permute-start | bytes 786440 | tf_op jit(solution)/shard_map/ppermute | solution.py:553
  51.2 18.2 %collective-permute-start.10 = (f32[128,512]{1,0:T(8,128)S(1)}, f32[128,512]{1,0:T(8,128)S(1)}, u32[]{:S(2)}, u32[]{:S(2)}) collective-permute-start(f32[128,512]{1,0:T(8,128)S(1)} %get-tuple-element.132), channel_id=1, source_target_pairs={{0,4},{4,0},{8,12},{12,8},{16,20},{20,16},{24,28},{28,24},{1,5},{5... | collective-permute-start | bytes 786440 | tf_op jit(solution)/shard_map/ppermute | solution.py:558
  61.1 8.3 %collective-permute-start.11 = (f32[128,512]{1,0:T(8,128)S(1)}, f32[128,512]{1,0:T(8,128)S(1)}, u32[]{:S(2)}, u32[]{:S(2)}) collective-permute-start(f32[128,512]{1,0:T(8,128)S(1)} %get-tuple-element.96), channel_id=1, source_target_pairs={{0,4},{4,0},{8,12},{12,8},{16,20},{20,16},{24,28},{28,24},{1,5},{5... | collective-permute-start | bytes 786440 | tf_op jit(solution)/shard_map/ppermute | solution.py:563
  61.9 7.6 %copy-start.1 = (bf16[1024,2048]{1,0:T(8,128)(2,1)S(1)}, bf16[1024,2048]{1,0:T(8,128)(2,1)}, u32[]{:S(2)}) copy-start(bf16[1024,2048]{1,0:T(8,128)(2,1)} %get-tuple-element.60.ys_ref.refs_2_) | copy-start | bytes 12582916
  69.4 11.7 %copy-start.11 = (f32[8,2048]{1,0:T(8,128)S(1)}, f32[8,2048]{1,0:T(8,128)}, u32[]{:S(2)}) copy-start(f32[8,2048]{1,0:T(8,128)} %get-tuple-element.93.direct_ref) | copy-start | bytes 196612
  69.4 11.7 %copy-start.12 = (f32[1,32,1024]{2,1,0:T(8,128)S(1)}, f32[1,32,1024]{2,1,0:T(8,128)}, u32[]{:S(2)}) copy-start(f32[1,32,1024]{2,1,0:T(8,128)} %raw_ref.1) | copy-start | bytes 393220
  69.4 11.7 %copy-start.15 = (f32[32]{0:T(128)S(1)}, f32[32]{0:T(128)}, u32[]{:S(2)}) copy-start(f32[32]{0:T(128)} %param.15) | copy-start | bytes 388
  69.5 11.7 %copy-start.16 = (f32[32]{0:T(128)S(1)}, f32[32]{0:T(128)}, u32[]{:S(2)}) copy-start(f32[32]{0:T(128)} %param.16) | copy-start | bytes 388
  82.1 3.0 %collective-permute-start.14 = (f32[8,128]{1,0:T(8,128)S(1)}, f32[8,128]{1,0:T(8,128)S(1)}, u32[]{:S(2)}, u32[]{:S(2)}) collective-permute-start(f32[8,128]{1,0:T(8,128)S(1)} %get-tuple-element.95), channel_id=1, source_target_pairs={{0,3},{1,2},{2,1},{3,0},{4,7},{5,6},{6,5},{7,4},{8,11},{9,10},{10,... | collective-permute-start | bytes 12296 | tf_op jit(solution)/shard_map/ppermute | solution.py:503
  82.1 3.6 %collective-permute-start.13 = (f32[8,128]{1,0:T(8,128)S(1)}, f32[8,128]{1,0:T(8,128)S(1)}, u32[]{:S(2)}, u32[]{:S(2)}) collective-permute-start(f32[8,128]{1,0:T(8,128)S(1)} %get-tuple-element.95), channel_id=1, source_target_pairs={{0,2},{1,3},{2,0},{3,1},{4,6},{5,7},{6,4},{7,5},{8,10},{9,11},{10,... | collective-permute-start | bytes 12296 | tf_op jit(solution)/shard_map/ppermute | solution.py:503
  83.7 2.1 %collective-permute-start.12 = (f32[8,128]{1,0:T(8,128)S(1)}, f32[8,128]{1,0:T(8,128)S(1)}, u32[]{:S(2)}, u32[]{:S(2)}) collective-permute-start(f32[8,128]{1,0:T(8,128)S(1)} %get-tuple-element.95), channel_id=1, source_target_pairs={{0,1},{1,0},{2,3},{3,2},{4,5},{5,4},{6,7},{7,6},{8,9},{9,8},{10,11... | collective-permute-start | bytes 12296 | tf_op jit(solution)/shard_map/ppermute | solution.py:503
  85.8 6.2 %collective-permute-start.17 = (f32[8,128]{1,0:T(8,128)S(1)}, f32[8,128]{1,0:T(8,128)S(1)}, u32[]{:S(2)}, u32[]{:S(2)}) collective-permute-start(f32[8,128]{1,0:T(8,128)S(1)} %add_add_fusion.1), channel_id=1, source_target_pairs={{0,12},{4,8},{8,4},{12,0},{16,28},{20,24},{24,20},{28,16},{1,13},{... | collective-permute-start | bytes 12296 | tf_op jit(solution)/shard_map/ppermute | solution.py:503
  90.5 3.6 %collective-permute-start.16 = (f32[8,128]{1,0:T(8,128)S(1)}, f32[8,128]{1,0:T(8,128)S(1)}, u32[]{:S(2)}, u32[]{:S(2)}) collective-permute-start(f32[8,128]{1,0:T(8,128)S(1)} %add_add_fusion.1), channel_id=1, source_target_pairs={{0,8},{4,12},{8,0},{12,4},{16,24},{20,28},{24,16},{28,20},{1,9},{5... | collective-permute-start | bytes 12296 | tf_op jit(solution)/shard_map/ppermute | solution.py:503
  90.5 3.6 %collective-permute-start.15 = (f32[8,128]{1,0:T(8,128)S(1)}, f32[8,128]{1,0:T(8,128)S(1)}, u32[]{:S(2)}, u32[]{:S(2)}) collective-permute-start(f32[8,128]{1,0:T(8,128)S(1)} %add_add_fusion.1), channel_id=1, source_target_pairs={{0,4},{4,0},{8,12},{12,8},{16,20},{20,16},{24,28},{28,24},{1,5},{5... | collective-permute-start | bytes 12296 | tf_op jit(solution)/shard_map/ppermute | solution.py:503
  94.1 4.6 %collective-permute-start.18 = (f32[8,128]{1,0:T(8,128)S(1)}, f32[8,128]{1,0:T(8,128)S(1)}, u32[]{:S(2)}, u32[]{:S(2)}) collective-permute-start(f32[8,128]{1,0:T(8,128)S(1)} %add_add_fusion), channel_id=1, source_target_pairs={{0,16},{4,20},{8,24},{12,28},{16,0},{20,4},{24,8},{28,12},{1,17},{... | collective-permute-start | bytes 12296 | tf_op jit(solution)/shard_map/ppermute | solution.py:503

commit v11 on v9

--- a/solution.py
+++ b/solution.py
@@ -618,11 +618,12 @@
             flows[part] = entering(sent[part], kept[part], states, token)
             message, arrived = next(flows[part])
             token = None if part == 0 else message
+            second_got = arrived
         else:
             token = flows[part].send(token)[0]
         if (part, k) == (0, 1):
             dc, db = pairs_grads(saved, after(b, token), c)
-            token = dc
+            token = (dc, second_got)
             found = (None, dc, db, None, None)
     found = grads(0, 1, 1, token, held)
     found = grads(1, 0, 2, found[-1], next(flows[1]))

time: 99.4 us -> 102 us (1.026)
  starting transfers between devices: 27.3 us -> 33.3 us
  waiting for transfers between devices: 18.1 us -> 14.3 us
    ppermute x2, starting transfers between devices: 4.68 us -> 8.15 us  [entering(): near = lax.ppermute(message, 'seq', both([(0, 1), (1, 0), (2, 3), (3, 2)]))]
    ppermute x2, waiting for transfers between devices: 5.25 us -> 2.35 us  [entering(): far = lax.ppermute(message, 'seq', both([(1, 3), (2, 0)]))]
    ppermute x2, waiting for transfers between devices: 4.41 us -> 2.62 us  [entering(): got = lax.ppermute(message, 'seq', swap)]
    ppermute x2, starting transfers between devices: 1.45 us -> 3.07 us  [entering(): other_early = lax.ppermute(early, 'seq', swap)]
    ppermute x2, starting transfers between devices: 1.31 us -> 2.85 us  [entering(): other_late = lax.ppermute(late, 'seq', swap)]
    ppermute x2, starting transfers between devices: 4.48 us -> 3.04 us  [entering(): got = lax.ppermute(message, 'seq', swap)]
  transfers between devices with their start and end apart: 19 -> 19, of which waited for: 10 -> 10; matrix products, arithmetic and copies ran while one was open for 1% -> 3% of each run, Pallas kernels for 32% -> 32%
where the time goes in v11:
time: 102 us; the launch traced here: 101 us
  Pallas kernels  48.1 us (47%)
  starting transfers between devices  33.3 us (33%)
  waiting for transfers between devices  14.3 us (14%)
  other arithmetic  3.22 us (3%)
  local copies, waits for them, and re-layouts  1.19 us (1%)
  between operations  1.1 us (1%)
    pallas_call x3, Pallas kernels, local_grads(): pl.pallas_call(functools.partial(grads_kernel, first, scale, part, half,...  26.4 us
    pallas_call x3, Pallas kernels, local_states(): pl.pallas_call(functools.partial(local_kernel, first, last, count), grid_...  15.3 us
    ppermute x7, starting transfers between devices, summed_over(): lax.ppermute(value, axis, [(i, i ^ s) for i in range(size)])  11.7 us
    ppermute x2, starting transfers between devices, entering(): near = lax.ppermute(message, 'seq', both([(0, 1), (1, 0), (2, 3), (3, 2)]))  8.15 us
    pallas_call x1, Pallas kernels, pairs_grads(): pl.pallas_call(pairs_kernel, grid=(length // GROUP,), in_specs=[columns,...  6.4 us
    ppermute x7, waiting for transfers between devices, summed_over(): lax.ppermute(value, axis, [(i, i ^ s) for i in range(size)])  6.21 us
    ppermute x2, waiting for transfers between devices, entering(): near = lax.ppermute(message, 'seq', both([(0, 1), (1, 0), (2, 3), (3, 2)]))  3.08 us
    ppermute x2, starting transfers between devices, entering(): other_early = lax.ppermute(early, 'seq', swap)  3.07 us
  transfers between devices with their start and end apart: 19, of which 10 were waited for; matrix products, arithmetic and copies ran while one was open for 3% of the time, Pallas kernels for 32%

profile of v11, /device:TPU:0, one launch (start us, length us, event | category | flops | bytes accessed | tf_op | source)
XLA Modules:
  0.0 101.1 jit_solution(4946998341343659268)
XLA Ops:
  0.6 4.6 %local_states.3 = (f32[264,512]{1,0:T(8,128)}, bf16[1024,2048]{1,0:T(8,128)(2,1)}, bf16[1024,2048]{1,0:T(8,128)(2,1)}, f32[8,2048]{1,0:T(8,128)}, bf16[1024,128]{1,0:T(8,128)(2,1)}, /*index=5*/f32[16,2048]{1,0:T(8,128)}) custom-call(s32[1]{0:T(128)} %bitcast.7.refs_0_, bf16[1024,2048]{1,0:T(8,128)(2,1)} %bitcast.72, bf16[1024,2048]{1,0:T(8,128)(2,1)} %bitcast.66, ...), custom_call_target="tpu_custom_call" | custom-call | flops 536870912 | bytes 4194304 | tf_op jit(solution)/shard_map/local_states/pallas_call | solution.py:246
  5.2 3.0 %collective-permute-start.1 = (f32[264,512]{1,0:T(8,128)}, f32[264,512]{1,0:T(8,128)S(1)}, u32[]{:S(2)}, u32[]{:S(2)}) collective-permute-start(f32[264,512]{1,0:T(8,128)} %get-tuple-element.69), channel_id=1, source_target_pairs={{0,4},{4,0},{8,12},{12,8},{16,20},{20,16},{24,28},{28,24},{1,5},{5... | collective-permute-start | bytes 1622024 | tf_op jit(solution)/shard_map/ppermute | solution.py:523
  8.2 3.8 %local_states.4 = (f32[264,512]{1,0:T(8,128)}, bf16[1024,2048]{1,0:T(8,128)(2,1)}, bf16[1024,2048]{1,0:T(8,128)(2,1)}, f32[8,2048]{1,0:T(8,128)}) custom-call(s32[1]{0:T(128)} %bitcast.11.refs_0_, bf16[1024,2048]{1,0:T(8,128)(2,1)} %bitcast.73, bf16[1024,2048]{1,0:T(8,128)(2,1)} %bitcast.67, ...), custom_call_target="tpu_custom_call", output_to_operand_aliasing={{1}: (7, {}), {2}: (8, {}), {3}: (9, {})} | custom-call | flops 536870912 | bytes 4194304 | tf_op jit(solution)/shard_map/local_states/pallas_call | solution.py:246
  12.0 0.1 collective-permute-start
  12.1 6.9 %local_states.5 = (f32[264,512]{1,0:T(8,128)}, f32[264,512]{1,0:T(8,128)}, bf16[1024,2048]{1,0:T(8,128)(2,1)}, bf16[1024,2048]{1,0:T(8,128)(2,1)}, f32[8,2048]{1...) custom-call(s32[1]{0:T(128)} %bitcast.2.refs_0_, ...), custom_call_target="tpu_custom_call", output_to_operand_aliasing={{2}: (7, {}), {3}: (8, {}), {4}: (9, {})} | custom-call | flops 1073741824 | bytes 8388608 | tf_op jit(solution)/shard_map/local_states/pallas_call | solution.py:246
  19.0 2.5 %collective-permute-done.1 = f32[264,512]{1,0:T(8,128)S(1)} collective-permute-done((f32[264,512]{1,0:T(8,128)}, f32[264,512]{1,0:T(8,128)S(1)}, u32[]{:S(2)}, u32[]{:S(2)}) %collective-permute-start.1) | collective-permute-done | bytes 540704 | tf_op jit(solution)/shard_map/ppermute | solution.py:523
  21.5 0.9 fusion.1
  22.4 1.2 %add_select_fusion.11 = (f32[128,512]{1,0:T(8,128)S(1)}, f32[128,512]{1,0:T(8,128)S(1)}, f32[128,512]{1,0:T(8,128)S(1)}) fusion(f32[512]{0:T(512)S(1)} %bitcast.98, f32[512]{0:T(512)S(1)} %bitcast.97, pred[]{:T(512)S(6)} %or.9, f32[264,512]{1,0:T(8,128)S(1)} %collective-permute-done.1, f32[264,512]{1,0:T(8,128)} %get-tuple-element.68, pred[]{:T(512)S(6)} %eq.12), kind=kLoop, calls=%fused_computation.15 | loop fusion | flops 589824 | bytes 1839106 | tf_op jit(solution)/shard_map/jit(_where)/select_n | solution.py:513
  23.6 2.2 %collective-permute-start.2 = (f32[136,512]{1,0:T(8,128)S(1)}, f32[136,512]{1,0:T(8,128)S(1)}, u32[]{:S(2)}, u32[]{:S(2)}) collective-permute-start(f32[136,512]{1,0:T(8,128)S(1)} %pad_maximum_fusion), channel_id=1, source_target_pairs={{0,8},{4,12},{8,0},{12,4},{16,24},{20,28},{24,16},{28,20},{1,9},{5... | collective-permute-start | bytes 835592 | tf_op jit(solution)/shard_map/ppermute | solution.py:531
  25.8 6.4 %pairs_grads.1 = (f32[1024,128]{1,0:T(8,128)}, f32[1024,128]{1,0:T(8,128)}) custom-call(bf16[1024,2048]{1,0:T(8,128)(2,1)} %get-tuple-element.60.xs_ref.refs_1_, bf16[1024,2048]{1,0:T(8,128)(2,1)} %get-tuple-element.61.ys_ref.refs_2_, bf16[1024,128]{1,0:T(8,128)(2,1)} %bitcast.44, bf16[1024,128]{1,0:T(8,128)(2,1)} %bitcast.51), custom_call_target="tpu_custom_call" | custom-call | flops 1073741824 | bytes 8388608 | tf_op jit(solution)/shard_map/pairs_grads/pallas_call | solution.py:274
  32.2 0.1 collective-permute-done
  32.3 0.2 broadcast_select_fusion.4
  32.6 0.0 copy-start.7
  32.7 1.6 %collective-permute-start.5 = (f32[128,512]{1,0:T(8,128)S(1)}, f32[128,512]{1,0:T(8,128)S(1)}, u32[]{:S(2)}, u32[]{:S(2)}) collective-permute-start(f32[128,512]{1,0:T(8,128)S(1)} %get-tuple-element.139), channel_id=1, source_target_pairs={{8,24},{12,28},{16,0},{20,4},{9,25},{13,29},{17,1},{21,5},{10,26},... | collective-permute-start | bytes 786440 | tf_op jit(solution)/shard_map/ppermute | solution.py:536
  34.3 0.8 collective-permute-start.4
  35.1 1.8 %collective-permute-start.8 = (f32[128,512]{1,0:T(8,128)S(1)}, f32[128,512]{1,0:T(8,128)S(1)}, u32[]{:S(2)}, u32[]{:S(2)}) collective-permute-start(f32[128,512]{1,0:T(8,128)S(1)} %get-tuple-element.137), channel_id=1, source_target_pairs={{0,4},{4,0},{8,12},{12,8},{16,20},{20,16},{24,28},{28,24},{1,5},{5... | collective-permute-start | bytes 786440 | tf_op jit(solution)/shard_map/ppermute | solution.py:540
  36.9 0.1 add_select_fusion.8
  37.1 6.0 %collective-permute-start.3 = (f32[136,512]{1,0:T(8,128)S(1)}, f32[136,512]{1,0:T(8,128)S(1)}, u32[]{:S(2)}, u32[]{:S(2)}) collective-permute-start(f32[136,512]{1,0:T(8,128)S(1)} %pad_maximum_fusion.1), channel_id=1, source_target_pairs={{0,8},{4,12},{8,0},{12,4},{16,24},{20,28},{24,16},{28,20},{1,9},{5... | collective-permute-start | bytes 835592 | tf_op jit(solution)/shard_map/ppermute | solution.py:531
  43.0 1.8 %collective-permute-done.5 = f32[128,512]{1,0:T(8,128)S(1)} collective-permute-done((f32[128,512]{1,0:T(8,128)S(1)}, f32[128,512]{1,0:T(8,128)S(1)}, u32[]{:S(2)}, u32[]{:S(2)}) %collective-permute-start.5) | collective-permute-done | bytes 262176 | tf_op jit(solution)/shard_map/ppermute | solution.py:536
  44.8 0.1 broadcast_select_fusion.3
  45.0 0.1 broadcast_select_fusion.6
  45.1 1.4 %collective-permute-start.9 = (f32[128,512]{1,0:T(8,128)S(1)}, f32[128,512]{1,0:T(8,128)S(1)}, u32[]{:S(2)}, u32[]{:S(2)}) collective-permute-start(f32[128,512]{1,0:T(8,128)S(1)} %broadcast_select_fusion.6), channel_id=1, source_target_pairs={{0,4},{4,0},{8,12},{12,8},{16,20},{20,16},{24,28},{28,24},{1,5},{5... | collective-permute-start | bytes 786440 | tf_op jit(solution)/shard_map/ppermute | solution.py:545
  46.4 3.1 %collective-permute-done.3 = f32[136,512]{1,0:T(8,128)S(1)} collective-permute-done((f32[136,512]{1,0:T(8,128)S(1)}, f32[136,512]{1,0:T(8,128)S(1)}, u32[]{:S(2)}, u32[]{:S(2)}) %collective-permute-start.3) | collective-permute-done | bytes 278560 | tf_op jit(solution)/shard_map/ppermute | solution.py:531
  49.5 0.2 broadcast_select_fusion.2
  49.7 1.3 %collective-permute-start.7 = (f32[128,512]{1,0:T(8,128)S(1)}, f32[128,512]{1,0:T(8,128)S(1)}, u32[]{:S(2)}, u32[]{:S(2)}) collective-permute-start(f32[128,512]{1,0:T(8,128)S(1)} %get-tuple-element.138), channel_id=1, source_target_pairs={{8,24},{12,28},{16,0},{20,4},{9,25},{13,29},{17,1},{21,5},{10,26},... | collective-permute-start | bytes 786440 | tf_op jit(solution)/shard_map/ppermute | solution.py:536
  51.0 0.9 collective-permute-start.6
  51.9 0.1 pad_add_fusion.refs_0_
  52.0 1.3 %collective-permute-start.10 = (f32[128,512]{1,0:T(8,128)S(1)}, f32[128,512]{1,0:T(8,128)S(1)}, u32[]{:S(2)}, u32[]{:S(2)}) collective-permute-start(f32[128,512]{1,0:T(8,128)S(1)} %get-tuple-element.134), channel_id=1, source_target_pairs={{0,4},{4,0},{8,12},{12,8},{16,20},{20,16},{24,28},{28,24},{1,5},{5... | collective-permute-start | bytes 786440 | tf_op jit(solution)/shard_map/ppermute | solution.py:540
  53.4 7.3 %local_grads.3 = (bf16[1024,2048]{1,0:T(8,128)(2,1)}, f32[1024,128]{1,0:T(8,128)S(1)}, f32[1024,128]{1,0:T(8,128)S(1)}, f32[4,8,1024]{2,1,0:T(8,128)}, f32[8,128]{1,0:T(8,128)S(1)}) custom-call(s32[2]{0:T(128)S(1)} %pad_add_fusion.refs_0_, bf16[1024,2048]{1,0:T(8,128)(2,1)S(1)} %copy-done, bf16[1024,2048]{1,0:T(8,128)(2,1)} %get-tuple-element.61.ys_ref.refs_2_, ...), custom_call_target="tpu_custom_call" | custom-call | flops 2415919104 | bytes 3145728 | tf_op jit(solution)/shard_map/local_grads/pallas_call | solution.py:442
  60.7 0.6 collective-permute-done.7
  61.3 0.1 broadcast_select_fusion
  61.4 1.5 %collective-permute-start.11 = (f32[128,512]{1,0:T(8,128)S(1)}, f32[128,512]{1,0:T(8,128)S(1)}, u32[]{:S(2)}, u32[]{:S(2)}) collective-permute-start(f32[128,512]{1,0:T(8,128)S(1)} %get-tuple-element.98), channel_id=1, source_target_pairs={{0,4},{4,0},{8,12},{12,8},{16,20},{20,16},{24,28},{28,24},{1,5},{5... | collective-permute-start | bytes 786440 | tf_op jit(solution)/shard_map/ppermute | solution.py:545
  62.9 7.5 %local_grads.4 = (bf16[1024,2048]{1,0:T(8,128)(2,1)}, f32[1024,128]{1,0:T(8,128)S(1)}, f32[1024,128]{1,0:T(8,128)S(1)}, f32[4,8,1024]{2,1,0:T(8,128)}, f32[8,128]{1,0:T(8,128)S(1)}) custom-call(s32[2]{0:T(128)S(1)} %pad_add_fusion.refs_0_, bf16[1024,2048]{1,0:T(8,128)(2,1)S(1)} %copy-done, ...), custom_call_target="tpu_custom_call", output_to_operand_aliasing={{0}: (24, {}), {3}: (25, {})} | custom-call | flops 2415919104 | bytes 3145728 | tf_op jit(solution)/shard_map/local_grads/pallas_call | solution.py:442
  70.4 0.1 broadcast_select_fusion.1.refs_18_
  70.5 11.6 %local_grads.5 = (bf16[1024,2048]{1,0:T(8,128)(2,1)}, f32[1024,128]{1,0:T(8,128)}, f32[1024,128]{1,0:T(8,128)}, f32[4,8,1024]{2,1,0:T(8,128)}, f32[8,128]{1,0:T(8,128)S(1)}) custom-call(s32[2]{0:T(128)S(1)} %pad_add_fusion.refs_0_, bf16[1024,2048]{1,0:T(8,128)(2,1)S(1)} %copy-done, ...), custom_call_target="tpu_custom_call", output_to_operand_aliasing={{0}: (24, {}), {3}: (25, {})} | custom-call | flops 4831838208 | bytes 6291456 | tf_op jit(solution)/shard_map/local_grads/pallas_call | solution.py:442
  82.1 0.1 collective-permute-start.14
  82.2 1.6 %collective-permute-start.13 = (f32[8,128]{1,0:T(8,128)S(1)}, f32[8,128]{1,0:T(8,128)S(1)}, u32[]{:S(2)}, u32[]{:S(2)}) collective-permute-start(f32[8,128]{1,0:T(8,128)S(1)} %get-tuple-element.97), channel_id=1, source_target_pairs={{0,2},{1,3},{2,0},{3,1},{4,6},{5,7},{6,4},{7,5},{8,10},{9,11},{10,... | collective-permute-start | bytes 12296 | tf_op jit(solution)/shard_map/ppermute | solution.py:485
  83.8 0.3 collective-permute-start.12
  84.1 1.2 %collective-permute-done.14 = f32[8,128]{1,0:T(8,128)S(1)} collective-permute-done((f32[8,128]{1,0:T(8,128)S(1)}, f32[8,128]{1,0:T(8,128)S(1)}, u32[]{:S(2)}, u32[]{:S(2)}) %collective-permute-start.14) | collective-permute-done | bytes 4128 | tf_op jit(solution)/shard_map/ppermute | solution.py:485
  85.2 0.7 collective-permute-done.13
  85.9 5.5 %collective-permute-start.17 = (f32[8,128]{1,0:T(8,128)S(1)}, f32[8,128]{1,0:T(8,128)S(1)}, u32[]{:S(2)}, u32[]{:S(2)}) collective-permute-start(f32[8,128]{1,0:T(8,128)S(1)} %add_add_fusion.1), channel_id=1, source_target_pairs={{0,12},{4,8},{8,4},{12,0},{16,28},{20,24},{24,20},{28,16},{1,13},{... | collective-permute-start | bytes 12296 | tf_op jit(solution)/shard_map/ppermute | solution.py:485
  91.4 0.8 collective-permute-start.15
  92.2 0.8 collective-permute-done.17
  93.0 2.0 %collective-permute-done.16 = f32[8,128]{1,0:T(8,128)S(1)} collective-permute-done((f32[8,128]{1,0:T(8,128)S(1)}, f32[8,128]{1,0:T(8,128)S(1)}, u32[]{:S(2)}, u32[]{:S(2)}) %collective-permute-start.16) | collective-permute-done | bytes 4128 | tf_op jit(solution)/shard_map/ppermute | solution.py:485
  95.0 3.5 %collective-permute-start.18 = (f32[8,128]{1,0:T(8,128)S(1)}, f32[8,128]{1,0:T(8,128)S(1)}, u32[]{:S(2)}, u32[]{:S(2)}) collective-permute-start(f32[8,128]{1,0:T(8,128)S(1)} %add_add_fusion), channel_id=1, source_target_pairs={{0,16},{4,20},{8,24},{12,28},{16,0},{20,4},{24,8},{28,12},{1,17},{... | collective-permute-start | bytes 12296 | tf_op jit(solution)/shard_map/ppermute | solution.py:485
  98.5 1.6 %collective-permute-done.18 = f32[8,128]{1,0:T(8,128)S(1)} collective-permute-done((f32[8,128]{1,0:T(8,128)S(1)}, f32[8,128]{1,0:T(8,128)S(1)}, u32[]{:S(2)}, u32[]{:S(2)}) %collective-permute-start.18) | collective-permute-done | bytes 4128 | tf_op jit(solution)/shard_map/ppermute | solution.py:485
  100.1 0.5 slice_bitcast_fusion
  100.6 0.6 slice.150
  (57 shorter events, 0.2 us)
Async XLA Ops:
  5.2 16.3 %collective-permute-start.1 = (f32[264,512]{1,0:T(8,128)}, f32[264,512]{1,0:T(8,128)S(1)}, u32[]{:S(2)}, u32[]{:S(2)}) collective-permute-start(f32[264,512]{1,0:T(8,128)} %get-tuple-element.69), channel_id=1, source_target_pairs={{0,4},{4,0},{8,12},{12,8},{16,20},{20,16},{24,28},{28,24},{1,5},{5... | collective-permute-start | bytes 1622024 | tf_op jit(solution)/shard_map/ppermute | solution.py:523
  12.0 20.2 %collective-permute-start = (f32[264,512]{1,0:T(8,128)}, f32[264,512]{1,0:T(8,128)S(1)}, u32[]{:S(2)}, u32[]{:S(2)}) collective-permute-start(f32[264,512]{1,0:T(8,128)} %get-tuple-element.67), channel_id=1, source_target_pairs={{0,4},{4,0},{8,12},{12,8},{16,20},{20,16},{24,28},{28,24},{1,5},{5... | collective-permute-start | bytes 1622024 | tf_op jit(solution)/shard_map/ppermute | solution.py:523
  23.6 8.7 %collective-permute-start.2 = (f32[136,512]{1,0:T(8,128)S(1)}, f32[136,512]{1,0:T(8,128)S(1)}, u32[]{:S(2)}, u32[]{:S(2)}) collective-permute-start(f32[136,512]{1,0:T(8,128)S(1)} %pad_maximum_fusion), channel_id=1, source_target_pairs={{0,8},{4,12},{8,0},{12,4},{16,24},{20,28},{24,16},{28,20},{1,9},{5... | collective-permute-start | bytes 835592 | tf_op jit(solution)/shard_map/ppermute | solution.py:531
  25.8 6.5 %copy-start.18 = (f32[264,512]{1,0:T(8,128)S(1)}, f32[264,512]{1,0:T(8,128)}, u32[]{:S(2)}) copy-start(f32[264,512]{1,0:T(8,128)} %get-tuple-element.68) | copy-start | bytes 1622020
  25.8 11.1 %copy-start.17 = (f32[264,512]{1,0:T(8,128)S(1)}, f32[264,512]{1,0:T(8,128)}, u32[]{:S(2)}) copy-start(f32[264,512]{1,0:T(8,128)} %get-tuple-element.75) | copy-start | bytes 1622020
  32.3 21.0 %copy-start.14 = (f32[1024,128]{1,0:T(8,128)S(1)}, f32[1024,128]{1,0:T(8,128)}, u32[]{:S(2)}) copy-start(f32[1024,128]{1,0:T(8,128)} %get-tuple-element.79.refs_22_) | copy-start | bytes 1572868
  32.5 20.8 %copy-start = (bf16[1024,2048]{1,0:T(8,128)(2,1)S(1)}, bf16[1024,2048]{1,0:T(8,128)(2,1)}, u32[]{:S(2)}) copy-start(bf16[1024,2048]{1,0:T(8,128)(2,1)} %get-tuple-element.60.xs_ref.refs_1_) | copy-start | bytes 12582916
  32.5 20.7 %copy-start.2 = (bf16[1,1024,128]{2,1,0:T(8,128)(2,1)S(1)}, bf16[1,1024,128]{2,1,0:T(8,128)(2,1)}, u32[]{:S(2)}) copy-start(bf16[1,1024,128]{2,1,0:T(8,128)(2,1)} %param.12) | copy-start | bytes 786436
  32.5 20.7 %copy-start.3 = (bf16[1,1024,128]{2,1,0:T(8,128)(2,1)S(1)}, bf16[1,1024,128]{2,1,0:T(8,128)(2,1)}, u32[]{:S(2)}) copy-start(bf16[1,1024,128]{2,1,0:T(8,128)(2,1)} %param.13) | copy-start | bytes 786436
  32.6 20.7 %copy-start.4 = (bf16[1024,128]{1,0:T(8,128)(2,1)S(1)}, bf16[1024,128]{1,0:T(8,128)(2,1)}, u32[]{:S(2)}) copy-start(bf16[1024,128]{1,0:T(8,128)(2,1)} %get-tuple-element.52.refs_5_.refs_7_) | copy-start | bytes 786436
  32.6 20.7 %copy-start.5 = (bf16[4,256,256]{2,1,0:T(8,128)(2,1)S(1)}, bf16[4,256,256]{2,1,0:T(8,128)(2,1)}, u32[]{:S(2)}) copy-start(bf16[4,256,256]{2,1,0:T(8,128)(2,1)} %get-tuple-element.65.refs_14_) | copy-start | bytes 1572868
  32.6 20.7 %copy-start.6 = (bf16[4,256,256]{2,1,0:T(8,128)(2,1)S(1)}, bf16[4,256,256]{2,1,0:T(8,128)(2,1)}, u32[]{:S(2)}) copy-start(bf16[4,256,256]{2,1,0:T(8,128)(2,1)} %get-tuple-element.66.refs_15_) | copy-start | bytes 1572868
  32.6 20.7 %copy-start.7 = (bf16[1536,128]{1,0:T(8,128)(2,1)S(1)}, bf16[1536,128]{1,0:T(8,128)(2,1)}, u32[]{:S(2)}) copy-start(bf16[1536,128]{1,0:T(8,128)(2,1)} %constant.44.clone.refs_16_) | copy-start | bytes 1179652
  32.6 20.7 %copy-start.8 = (f32[16,2048]{1,0:T(8,128)S(1)}, f32[16,2048]{1,0:T(8,128)}, u32[]{:S(2)}) copy-start(f32[16,2048]{1,0:T(8,128)} %get-tuple-element.53.refs_6_.refs_8_) | copy-start | bytes 393220
  32.6 20.7 %copy-start.9 = (bf16[128,1024]{1,0:T(8,128)(2,1)S(1)}, bf16[128,1024]{1,0:T(8,128)(2,1)}, u32[]{:S(2)}) copy-start(bf16[128,1024]{1,0:T(8,128)(2,1)} %get-tuple-element.63.refs_12_) | copy-start | bytes 786436
  32.6 20.7 %copy-start.10 = (bf16[128,1024]{1,0:T(8,128)(2,1)S(1)}, bf16[128,1024]{1,0:T(8,128)(2,1)}, u32[]{:S(2)}) copy-start(bf16[128,1024]{1,0:T(8,128)(2,1)} %get-tuple-element.64.refs_13_) | copy-start | bytes 786436
  32.6 20.7 %copy-start.11 = (f32[1,32,1024]{2,1,0:T(8,128)S(1)}, f32[1,32,1024]{2,1,0:T(8,128)}, u32[]{:S(2)}) copy-start(f32[1,32,1024]{2,1,0:T(8,128)} %refs_5_.1) | copy-start | bytes 393220
  32.7 20.7 %copy-start.12 = (f32[8,2048]{1,0:T(8,128)S(1)}, f32[8,2048]{1,0:T(8,128)}, u32[]{:S(2)}) copy-start(f32[8,2048]{1,0:T(8,128)} %get-tuple-element.62.refs_4_) | copy-start | bytes 196612
  32.7 20.7 %copy-start.13 = (f32[1024,128]{1,0:T(8,128)S(1)}, f32[1024,128]{1,0:T(8,128)}, u32[]{:S(2)}) copy-start(f32[1024,128]{1,0:T(8,128)} %get-tuple-element.72.refs_21_) | copy-start | bytes 1572868
  32.7 20.7 %copy-start.15 = (f32[32]{0:T(128)S(1)}, f32[32]{0:T(128)}, u32[]{:S(2)}) copy-start(f32[32]{0:T(128)} %param.15) | copy-start | bytes 388
  32.7 20.7 %copy-start.16 = (f32[32]{0:T(128)S(1)}, f32[32]{0:T(128)}, u32[]{:S(2)}) copy-start(f32[32]{0:T(128)} %param.16) | copy-start | bytes 388
  32.7 12.1 %collective-permute-start.5 = (f32[128,512]{1,0:T(8,128)S(1)}, f32[128,512]{1,0:T(8,128)S(1)}, u32[]{:S(2)}, u32[]{:S(2)}) collective-permute-start(f32[128,512]{1,0:T(8,128)S(1)} %get-tuple-element.139), channel_id=1, source_target_pairs={{8,24},{12,28},{16,0},{20,4},{9,25},{13,29},{17,1},{21,5},{10,26},... | collective-permute-start | bytes 786440 | tf_op jit(solution)/shard_map/ppermute | solution.py:536
  34.3 10.5 %collective-permute-start.4 = (f32[128,512]{1,0:T(8,128)S(1)}, f32[128,512]{1,0:T(8,128)S(1)}, u32[]{:S(2)}, u32[]{:S(2)}) collective-permute-start(f32[128,512]{1,0:T(8,128)S(1)} %get-tuple-element.139), channel_id=1, source_target_pairs={{8,16},{12,20},{16,8},{20,12},{9,17},{13,21},{17,9},{21,13},{10,18... | collective-permute-start | bytes 786440 | tf_op jit(solution)/shard_map/ppermute | solution.py:535
  35.1 18.2 %collective-permute-start.8 = (f32[128,512]{1,0:T(8,128)S(1)}, f32[128,512]{1,0:T(8,128)S(1)}, u32[]{:S(2)}, u32[]{:S(2)}) collective-permute-start(f32[128,512]{1,0:T(8,128)S(1)} %get-tuple-element.137), channel_id=1, source_target_pairs={{0,4},{4,0},{8,12},{12,8},{16,20},{20,16},{24,28},{28,24},{1,5},{5... | collective-permute-start | bytes 786440 | tf_op jit(solution)/shard_map/ppermute | solution.py:540
  37.1 12.5 %collective-permute-start.3 = (f32[136,512]{1,0:T(8,128)S(1)}, f32[136,512]{1,0:T(8,128)S(1)}, u32[]{:S(2)}, u32[]{:S(2)}) collective-permute-start(f32[136,512]{1,0:T(8,128)S(1)} %pad_maximum_fusion.1), channel_id=1, source_target_pairs={{0,8},{4,12},{8,0},{12,4},{16,24},{20,28},{24,16},{28,20},{1,9},{5... | collective-permute-start | bytes 835592 | tf_op jit(solution)/shard_map/ppermute | solution.py:531
  45.1 8.2 %collective-permute-start.9 = (f32[128,512]{1,0:T(8,128)S(1)}, f32[128,512]{1,0:T(8,128)S(1)}, u32[]{:S(2)}, u32[]{:S(2)}) collective-permute-start(f32[128,512]{1,0:T(8,128)S(1)} %broadcast_select_fusion.6), channel_id=1, source_target_pairs={{0,4},{4,0},{8,12},{12,8},{16,20},{20,16},{24,28},{28,24},{1,5},{5... | collective-permute-start | bytes 786440 | tf_op jit(solution)/shard_map/ppermute | solution.py:545
  49.7 11.5 %collective-permute-start.7 = (f32[128,512]{1,0:T(8,128)S(1)}, f32[128,512]{1,0:T(8,128)S(1)}, u32[]{:S(2)}, u32[]{:S(2)}) collective-permute-start(f32[128,512]{1,0:T(8,128)S(1)} %get-tuple-element.138), channel_id=1, source_target_pairs={{8,24},{12,28},{16,0},{20,4},{9,25},{13,29},{17,1},{21,5},{10,26},... | collective-permute-start | bytes 786440 | tf_op jit(solution)/shard_map/ppermute | solution.py:536
  51.0 10.2 %collective-permute-start.6 = (f32[128,512]{1,0:T(8,128)S(1)}, f32[128,512]{1,0:T(8,128)S(1)}, u32[]{:S(2)}, u32[]{:S(2)}) collective-permute-start(f32[128,512]{1,0:T(8,128)S(1)} %get-tuple-element.138), channel_id=1, source_target_pairs={{8,16},{12,20},{16,8},{20,12},{9,17},{13,21},{17,9},{21,13},{10,18... | collective-permute-start | bytes 786440 | tf_op jit(solution)/shard_map/ppermute | solution.py:535
  52.0 18.5 %collective-permute-start.10 = (f32[128,512]{1,0:T(8,128)S(1)}, f32[128,512]{1,0:T(8,128)S(1)}, u32[]{:S(2)}, u32[]{:S(2)}) collective-permute-start(f32[128,512]{1,0:T(8,128)S(1)} %get-tuple-element.134), channel_id=1, source_target_pairs={{0,4},{4,0},{8,12},{12,8},{16,20},{20,16},{24,28},{28,24},{1,5},{5... | collective-permute-start | bytes 786440 | tf_op jit(solution)/shard_map/ppermute | solution.py:540
  61.4 9.1 %collective-permute-start.11 = (f32[128,512]{1,0:T(8,128)S(1)}, f32[128,512]{1,0:T(8,128)S(1)}, u32[]{:S(2)}, u32[]{:S(2)}) collective-permute-start(f32[128,512]{1,0:T(8,128)S(1)} %get-tuple-element.98), channel_id=1, source_target_pairs={{0,4},{4,0},{8,12},{12,8},{16,20},{20,16},{24,28},{28,24},{1,5},{5... | collective-permute-start | bytes 786440 | tf_op jit(solution)/shard_map/ppermute | solution.py:545
  62.9 7.6 %copy-start.1 = (bf16[1024,2048]{1,0:T(8,128)(2,1)S(1)}, bf16[1024,2048]{1,0:T(8,128)(2,1)}, u32[]{:S(2)}) copy-start(bf16[1024,2048]{1,0:T(8,128)(2,1)} %get-tuple-element.61.ys_ref.refs_2_) | copy-start | bytes 12582916
  82.1 3.1 %collective-permute-start.14 = (f32[8,128]{1,0:T(8,128)S(1)}, f32[8,128]{1,0:T(8,128)S(1)}, u32[]{:S(2)}, u32[]{:S(2)}) collective-permute-start(f32[8,128]{1,0:T(8,128)S(1)} %get-tuple-element.97), channel_id=1, source_target_pairs={{0,3},{1,2},{2,1},{3,0},{4,7},{5,6},{6,5},{7,4},{8,11},{9,10},{10,... | collective-permute-start | bytes 12296 | tf_op jit(solution)/shard_map/ppermute | solution.py:485
  82.2 3.7 %collective-permute-start.13 = (f32[8,128]{1,0:T(8,128)S(1)}, f32[8,128]{1,0:T(8,128)S(1)}, u32[]{:S(2)}, u32[]{:S(2)}) collective-permute-start(f32[8,128]{1,0:T(8,128)S(1)} %get-tuple-element.97), channel_id=1, source_target_pairs={{0,2},{1,3},{2,0},{3,1},{4,6},{5,7},{6,4},{7,5},{8,10},{9,11},{10,... | collective-permute-start | bytes 12296 | tf_op jit(solution)/shard_map/ppermute | solution.py:485
  83.8 2.1 %collective-permute-start.12 = (f32[8,128]{1,0:T(8,128)S(1)}, f32[8,128]{1,0:T(8,128)S(1)}, u32[]{:S(2)}, u32[]{:S(2)}) collective-permute-start(f32[8,128]{1,0:T(8,128)S(1)} %get-tuple-element.97), channel_id=1, source_target_pairs={{0,1},{1,0},{2,3},{3,2},{4,5},{5,4},{6,7},{7,6},{8,9},{9,8},{10,11... | collective-permute-start | bytes 12296 | tf_op jit(solution)/shard_map/ppermute | solution.py:485
  85.9 7.1 %collective-permute-start.17 = (f32[8,128]{1,0:T(8,128)S(1)}, f32[8,128]{1,0:T(8,128)S(1)}, u32[]{:S(2)}, u32[]{:S(2)}) collective-permute-start(f32[8,128]{1,0:T(8,128)S(1)} %add_add_fusion.1), channel_id=1, source_target_pairs={{0,12},{4,8},{8,4},{12,0},{16,28},{20,24},{24,20},{28,16},{1,13},{... | collective-permute-start | bytes 12296 | tf_op jit(solution)/shard_map/ppermute | solution.py:485
  91.4 3.6 %collective-permute-start.16 = (f32[8,128]{1,0:T(8,128)S(1)}, f32[8,128]{1,0:T(8,128)S(1)}, u32[]{:S(2)}, u32[]{:S(2)}) collective-permute-start(f32[8,128]{1,0:T(8,128)S(1)} %add_add_fusion.1), channel_id=1, source_target_pairs={{0,8},{4,12},{8,0},{12,4},{16,24},{20,28},{24,16},{28,20},{1,9},{5... | collective-permute-start | bytes 12296 | tf_op jit(solution)/shard_map/ppermute | solution.py:485
  91.4 3.6 %collective-permute-start.15 = (f32[8,128]{1,0:T(8,128)S(1)}, f32[8,128]{1,0:T(8,128)S(1)}, u32[]{:S(2)}, u32[]{:S(2)}) collective-permute-start(f32[8,128]{1,0:T(8,128)S(1)} %add_add_fusion.1), channel_id=1, source_target_pairs={{0,4},{4,0},{8,12},{12,8},{16,20},{20,16},{24,28},{28,24},{1,5},{5... | collective-permute-start | bytes 12296 | tf_op jit(solution)/shard_map/ppermute | solution.py:485
  95.0 5.1 %collective-permute-start.18 = (f32[8,128]{1,0:T(8,128)S(1)}, f32[8,128]{1,0:T(8,128)S(1)}, u32[]{:S(2)}, u32[]{:S(2)}) collective-permute-start(f32[8,128]{1,0:T(8,128)S(1)} %add_add_fusion), channel_id=1, source_target_pairs={{0,16},{4,20},{8,24},{12,28},{16,0},{20,4},{24,8},{28,12},{1,17},{... | collective-permute-start | bytes 12296 | tf_op jit(solution)/shard_map/ppermute | solution.py:485

commit v12 on v9

--- a/solution.py
+++ b/solution.py
@@ -120,16 +120,16 @@
     at_ref, x_ref, dy_ref, b_ref, c_ref = refs[:5]
     if first:
         raw_ref, bias_ref, rate_ref, skip_ref = refs[5:9]
-        outs = refs[9:-7]
-        xs_ref, ys_ref, direct_ref, columns_ref, table_ref, bt, ct = refs[-7:]
+        outs = refs[9:-8]
+        xs_ref, ys_ref, direct_ref, fresh_ref, columns_ref, table_ref, bt, ct = refs[-8:]
     else:
         columns_ref, table_ref = refs[5:7]
-        outs = refs[10 : 10 + count]
-        xs_ref, ys_ref, direct_ref = refs[10 + count : 13 + count]
+        outs = refs[11 : 11 + count]
+        xs_ref, ys_ref, direct_ref, fresh_ref = refs[11 + count : 15 + count]
         if last:
-            left, right, bt, ct = refs[13 + count :]
+            left, right, bt, ct = refs[15 + count :]
         else:
-            bt, ct = refs[13 + count :]
+            bt, ct = refs[15 + count :]
     g = pl.program_id(0)
     length, width = x_ref.shape
     states = b_ref.shape[1]
@@ -176,8 +176,12 @@
         ys_ref[rows, :] = scaled_dy
         later = table[blocks + n : blocks + n + 1]
         earlier = table[2 * blocks + n : 2 * blocks + n + 1]
-        state = state + later * dot(bt[:, rows], scaled_x, NN)
-        grad = grad + earlier * dot(ct[:, rows], scaled_dy, NN)
+        fresh_x = dot(bt[:, rows], scaled_x, NN)
+        fresh_dy = dot(ct[:, rows], scaled_dy, NN)
+        fresh_ref[n] = fresh_x.astype(BF16)
+        fresh_ref[blocks + n] = fresh_dy.astype(BF16)
+        state = state + later * fresh_x
+        grad = grad + earlier * fresh_dy
     direct_ref[...] = direct
     decay = jnp.broadcast_to(table[3 * blocks : 3 * blocks + 1], (8, width))
     for k, out_ref in enumerate(outs):
@@ -200,14 +204,17 @@
     whole = lambda g, at: (0, 0)
     columns = pl.BlockSpec((length, width), lambda g, at: (0, at[0] + g))
     strip = pl.BlockSpec((8, width), lambda g, at: (0, at[0] + g))
+    steps = 2 * (length // GROUP)
+    made = pl.BlockSpec((steps, states, width), lambda g, at: (0, 0, at[0] + g))
     maps = pl.BlockSpec((length, states), whole)
     anywhere = pl.BlockSpec(memory_space=pl.ANY)
     in_specs = [columns, columns, maps, maps]
-    out_specs = [pl.BlockSpec((2 * states + 8, width), whole)] * count + [columns, columns, strip]
+    out_specs = [pl.BlockSpec((2 * states + 8, width), whole)] * count + [columns, columns, strip, made]
     out_shape = [jax.ShapeDtypeStruct((2 * states + 8, width), F32)] * count + [
         jax.ShapeDtypeStruct((length, channels), BF16),
         jax.ShapeDtypeStruct((length, channels), BF16),
         jax.ShapeDtypeStruct((8, channels), F32),
+        jax.ShapeDtypeStruct((steps, states, channels), BF16),
     ]
     aliases = {}
     if first:
@@ -223,11 +230,11 @@
         out_shape += tables
         out_specs += [pl.BlockSpec(t.shape, whole) for t in tables]
     else:
-        xs, ys, direct, factor_columns, table = before
-        args = [factor_columns, table, xs, ys, direct]
+        xs, ys, direct, fresh, factor_columns, table = before
+        args = [factor_columns, table, xs, ys, direct, fresh]
         in_specs += [pl.BlockSpec(factor_columns.shape, whole), pl.BlockSpec(table.shape, whole)]
-        in_specs += [anywhere] * 3
-        aliases = {7: count, 8: count + 1, 9: count + 2}
+        in_specs += [anywhere] * 4
+        aliases = {7: count, 8: count + 1, 9: count + 2, 10: count + 3}
     scratch = [pltpu.VMEM((states, length), BF16)] * 2
     if last:
         blocks = length // GROUP
@@ -289,9 +296,9 @@
 
 def grads_kernel(first, scale, part, half, begin, *refs):
     y_ref, xs_ref, ys_ref, dy_ref, direct_ref, b_ref, c_ref, columns_ref, table_ref = refs[:9]
-    raw_ref, bias_ref, rate_ref, bt, ct, left, right, adder = refs[9:17]
-    held = refs[17:21]
-    refs = refs[21:]
+    raw_ref, bias_ref, rate_ref, fresh_ref, left, right, adder = refs[9:16]
+    held = refs[16:20]
+    refs = refs[20:]
     dc_in, db_in = refs[:2]
     refs = refs[2:]
     if not first:
@@ -331,13 +338,13 @@
     for n in range(blocks):
         state = table[n : n + 1] * state
         entering_low.append(state.astype(BF16))
-        state = state + dot(bt[:, rows[n]], xs_ref[rows[n], :], NN)
+        state = state + fresh_ref[n].astype(F32)
         ends.append(state)
     leaving_low, edges = [None] * blocks, [None] * blocks
     for n in reversed(range(blocks)):
         leaving_low[n] = grad.astype(BF16)
         edges[n] = jnp.sum(ends[n] * grad, axis=0, keepdims=True)
-        grad = table[n : n + 1] * (grad + dot(ct[:, rows[n]], ys_ref[rows[n], :], NN))
+        grad = table[n : n + 1] * (grad + fresh_ref[blocks + n].astype(F32))
     gain = dot(columns_ref[...], picker(piece, heads, all_heads, width, True), NN)
     for n in range(blocks):
         scaled_x, scaled_dy = xs_ref[rows[n], :], ys_ref[rows[n], :]
@@ -388,7 +395,7 @@
 
 
 def local_grads(part, begin, count, scale, y, saved, dy, b, c, vectors, held, before):
-    xs, ys, direct, factor_columns, table, left, right, bt, ct = saved
+    xs, ys, direct, fresh, factor_columns, table, left, right, _, _ = saved
     raw, bias, rate, _ = vectors
     length, channels = xs.shape
     pieces = 2 * PARTS
@@ -414,8 +421,11 @@
     ]
     in_specs += [lines, line, line]
     args = [xs, ys, dy, direct, b, c, factor_columns, table, raw, bias, rate]
-    fixed = [bt, ct, left, right, adding(width, heads, (0, 0, 1)), *held]
+    fixed = [left, right, adding(width, heads, (0, 0, 1)), *held]
+    made = pl.BlockSpec((2 * blocks, states, width), lambda g, y: (0, *place(g, y)))
+    in_specs += [made]
     in_specs += [pl.BlockSpec(a.shape, lambda g, y, n=len(a.shape): (0,) * n) for a in fixed]
+    args += [fresh]
     args += fixed
     aliases = {}
     dx, dc, db, draw, par = before
@@ -424,7 +434,7 @@
     if not first:
         args += [par, dx, draw]
         in_specs += [params, anywhere, anywhere]
-        aliases = {24: 0, 25: 3}
+        aliases = {23: 0, 24: 3}
     grid_spec = pltpu.PrefetchScalarGridSpec(
         num_scalar_prefetch=1,
         grid=(count,),
@@ -583,7 +593,7 @@
         at = jnp.reshape(half * PARTS + part, (1,)).astype(jnp.int32)
         last = count == PARTS
         out, saved = local_states(at, count, last, x, dy, b, c, vectors, before)
-        return out, saved[:3] + list(before[3:] if before else []) + saved[3:]
+        return out, saved[:4] + list(before[4:] if before else []) + saved[4:]
 
     sent, kept = [], []
     saved = None

time: 99.4 us -> 103 us (1.036)
  waiting for transfers between devices: 18.1 us -> 20.9 us
  local copies, waits for them, and re-layouts: 1.19 us -> 3.24 us
  starting transfers between devices: 27.3 us -> 26 us
    ppermute x7, waiting for transfers between devices: 5.86 us -> 10.3 us  [summed_over(): lax.ppermute(value, axis, [(i, i ^ s) for i in range(size)])]
    unnamed x40 -> x34, local copies, waits for them, and re-layouts: 0.1 us -> 2.15 us
    ppermute x2, waiting for transfers between devices: 5.25 us -> 3.63 us  [entering(): far = lax.ppermute(message, 'seq', both([(1, 3), (2, 0)]))]
    ppermute x7, starting transfers between devices: 10.9 us -> 9.67 us  [summed_over(): lax.ppermute(value, axis, [(i, i ^ s) for i in range(size)])]
  transfers between devices with their start and end apart: 19 -> 19, of which waited for: 10 -> 9; matrix products, arithmetic and copies ran while one was open for 1% -> 1% of each run, Pallas kernels for 32% -> 31%
where the time goes in v12:
time: 103 us
  Pallas kernels  48.3 us (47%)
  starting transfers between devices  26 us (25%)
  waiting for transfers between devices  20.9 us (20%)
  local copies, waits for them, and re-layouts  3.24 us (3%)
  other arithmetic  3.22 us (3%)
  between operations  1.06 us (1%)
    pallas_call x3, Pallas kernels, local_grads(): pl.pallas_call(functools.partial(grads_kernel, first, scale, part, half,...  25.7 us
    pallas_call x3, Pallas kernels, local_states(): pl.pallas_call(functools.partial(local_kernel, first, last, count), grid_...  16.1 us
    ppermute x7, waiting for transfers between devices, summed_over(): lax.ppermute(value, axis, [(i, i ^ s) for i in range(size)])  10.3 us
    ppermute x7, starting transfers between devices, summed_over(): lax.ppermute(value, axis, [(i, i ^ s) for i in range(size)])  9.67 us
    pallas_call x1, Pallas kernels, pairs_grads(): pl.pallas_call(pairs_kernel, grid=(length // GROUP,), in_specs=[columns,...  6.42 us
    ppermute x2, starting transfers between devices, entering(): got = lax.ppermute(message, 'seq', swap)  4.49 us
    ppermute x2, waiting for transfers between devices, entering(): got = lax.ppermute(message, 'seq', swap)  4.34 us
    ppermute x2, starting transfers between devices, entering(): near = lax.ppermute(message, 'seq', both([(0, 1), (1, 0), (2, 3), (3, 2)]))  4.23 us
  transfers between devices with their start and end apart: 19, of which 9 were waited for; matrix products, arithmetic and copies ran while one was open for 1% of the time, Pallas kernels for 31%

profile of v12, /device:TPU:0, one launch (start us, length us, event | category | flops | bytes accessed | tf_op | source)
XLA Modules:
  0.0 102.7 jit_solution(18179791741863029470)
XLA Ops:
  0.6 4.8 %local_states.3 = (f32[264,512]{1,0:T(8,128)}, bf16[1024,2048]{1,0:T(8,128)(2,1)}, bf16[1024,2048]{1,0:T(8,128)(2,1)}, f32[8,2048]{1,0:T(8,128)}, bf16[8,128,204...) custom-call(s32[1]{0:T(128)} %bitcast.7.refs_0_, bf16[1024,2048]{1,0:T(8,128)(2,1)} %bitcast.72, ...), custom_call_target="tpu_custom_call" | custom-call | flops 536870912 | bytes 4194304 | tf_op jit(solution)/shard_map/local_states/pallas_call | solution.py:253
  5.5 3.0 %collective-permute-start.1 = (f32[264,512]{1,0:T(8,128)}, f32[264,512]{1,0:T(8,128)S(1)}, u32[]{:S(2)}, u32[]{:S(2)}) collective-permute-start(f32[264,512]{1,0:T(8,128)} %get-tuple-element.71), channel_id=1, source_target_pairs={{0,4},{4,0},{8,12},{12,8},{16,20},{20,16},{24,28},{28,24},{1,5},{5... | collective-permute-start | bytes 1622024 | tf_op jit(solution)/shard_map/ppermute | solution.py:533
  8.4 4.2 %local_states.4 = (f32[264,512]{1,0:T(8,128)}, bf16[1024,2048]{1,0:T(8,128)(2,1)}, bf16[1024,2048]{1,0:T(8,128)(2,1)}, f32[8,2048]{1,0:T(8,128)}, bf16[8,128,2048]{2,1,0:T(8,128)(2,1)}) custom-call(s32[1]{0:T(128)} %bitcast.11.refs_0_, bf16[1024,2048]{1,0:T(8,128)(2,1)} %bitcast.73, ...), custom_call_target="tpu_custom_call", output_to_operand_aliasing={{1}: (7, {}), {2}: (8, {}), {3}: (9, {}), {4}: (10, {})} | custom-call | flops 536870912 | bytes 4194304 | tf_op jit(solution)/shard_map/local_states/pallas_call | solution.py:253
  12.6 7.2 %local_states.5 = (f32[264,512]{1,0:T(8,128)}, f32[264,512]{1,0:T(8,128)}, bf16[1024,2048]{1,0:T(8,128)(2,1)}, bf16[1024,2048]{1,0:T(8,128)(2,1)}, f32[8,2048]{1...) custom-call(s32[1]{0:T(128)} %bitcast.2.refs_0_, ...), custom_call_target="tpu_custom_call", output_to_operand_aliasing={{2}: (7, {}), {3}: (8, {}), {4}: (9, {}), {5}: (10, {})} | custom-call | flops 1073741824 | bytes 8388608 | tf_op jit(solution)/shard_map/local_states/pallas_call | solution.py:253
  19.8 1.2 %collective-permute-done.1 = f32[264,512]{1,0:T(8,128)S(1)} collective-permute-done((f32[264,512]{1,0:T(8,128)}, f32[264,512]{1,0:T(8,128)S(1)}, u32[]{:S(2)}, u32[]{:S(2)}) %collective-permute-start.1) | collective-permute-done | bytes 540704 | tf_op jit(solution)/shard_map/ppermute | solution.py:533
  20.9 0.9 fusion.1
  21.8 1.2 %add_select_fusion.11 = (f32[128,512]{1,0:T(8,128)S(1)}, f32[128,512]{1,0:T(8,128)S(1)}, f32[128,512]{1,0:T(8,128)S(1)}) fusion(f32[512]{0:T(512)S(1)} %bitcast.98, f32[512]{0:T(512)S(1)} %bitcast.97, pred[]{:T(512)S(6)} %or.9, f32[264,512]{1,0:T(8,128)S(1)} %collective-permute-done.1, f32[264,512]{1,0:T(8,128)} %get-tuple-element.70, pred[]{:T(512)S(6)} %eq.12), kind=kLoop, calls=%fused_computation.15 | loop fusion | flops 589824 | bytes 1839106 | tf_op jit(solution)/shard_map/jit(_where)/select_n | solution.py:523
  23.0 1.9 %collective-permute-start.2 = (f32[136,512]{1,0:T(8,128)S(1)}, f32[136,512]{1,0:T(8,128)S(1)}, u32[]{:S(2)}, u32[]{:S(2)}) collective-permute-start(f32[136,512]{1,0:T(8,128)S(1)} %pad_maximum_fusion), channel_id=1, source_target_pairs={{0,8},{4,12},{8,0},{12,4},{16,24},{20,28},{24,16},{28,20},{1,9},{5... | collective-permute-start | bytes 835592 | tf_op jit(solution)/shard_map/ppermute | solution.py:541
  24.9 1.5 %collective-permute-start = (f32[264,512]{1,0:T(8,128)}, f32[264,512]{1,0:T(8,128)S(1)}, u32[]{:S(2)}, u32[]{:S(2)}) collective-permute-start(f32[264,512]{1,0:T(8,128)} %get-tuple-element.69), channel_id=1, source_target_pairs={{0,4},{4,0},{8,12},{12,8},{16,20},{20,16},{24,28},{28,24},{1,5},{5... | collective-permute-start | bytes 1622024 | tf_op jit(solution)/shard_map/ppermute | solution.py:533
  26.4 6.4 %pairs_grads.1 = (f32[1024,128]{1,0:T(8,128)}, f32[1024,128]{1,0:T(8,128)}) custom-call(bf16[1024,2048]{1,0:T(8,128)(2,1)} %get-tuple-element.63.xs_ref.refs_1_, bf16[1024,2048]{1,0:T(8,128)(2,1)} %get-tuple-element.64.ys_ref.refs_2_, bf16[1024,128]{1,0:T(8,128)(2,1)} %bitcast.44, bf16[1024,128]{1,0:T(8,128)(2,1)} %bitcast.51), custom_call_target="tpu_custom_call" | custom-call | flops 1073741824 | bytes 8388608 | tf_op jit(solution)/shard_map/pairs_grads/pallas_call | solution.py:281
  32.8 0.2 broadcast_select_fusion.4
  33.2 1.6 %collective-permute-start.5 = (f32[128,512]{1,0:T(8,128)S(1)}, f32[128,512]{1,0:T(8,128)S(1)}, u32[]{:S(2)}, u32[]{:S(2)}) collective-permute-start(f32[128,512]{1,0:T(8,128)S(1)} %get-tuple-element.141), channel_id=1, source_target_pairs={{8,24},{12,28},{16,0},{20,4},{9,25},{13,29},{17,1},{21,5},{10,26},... | collective-permute-start | bytes 786440 | tf_op jit(solution)/shard_map/ppermute | solution.py:546
  34.8 0.8 collective-permute-start.4
  35.6 0.6 collective-permute-start.8
  36.2 3.2 %collective-permute-done = f32[264,512]{1,0:T(8,128)S(1)} collective-permute-done((f32[264,512]{1,0:T(8,128)}, f32[264,512]{1,0:T(8,128)S(1)}, u32[]{:S(2)}, u32[]{:S(2)}) %collective-permute-start) | collective-permute-done | bytes 540704 | tf_op jit(solution)/shard_map/ppermute | solution.py:533
  39.4 0.1 add_select_fusion.8
  39.5 2.4 %collective-permute-start.3 = (f32[136,512]{1,0:T(8,128)S(1)}, f32[136,512]{1,0:T(8,128)S(1)}, u32[]{:S(2)}, u32[]{:S(2)}) collective-permute-start(f32[136,512]{1,0:T(8,128)S(1)} %pad_maximum_fusion.1), channel_id=1, source_target_pairs={{0,8},{4,12},{8,0},{12,4},{16,24},{20,28},{24,16},{28,20},{1,9},{5... | collective-permute-start | bytes 835592 | tf_op jit(solution)/shard_map/ppermute | solution.py:541
  41.9 3.6 %collective-permute-done.5 = f32[128,512]{1,0:T(8,128)S(1)} collective-permute-done((f32[128,512]{1,0:T(8,128)S(1)}, f32[128,512]{1,0:T(8,128)S(1)}, u32[]{:S(2)}, u32[]{:S(2)}) %collective-permute-start.5) | collective-permute-done | bytes 262176 | tf_op jit(solution)/shard_map/ppermute | solution.py:546
  45.5 0.1 broadcast_select_fusion.3
  45.7 0.1 broadcast_select_fusion.6
  45.8 0.5 collective-permute-start.9
  46.3 2.6 %collective-permute-done.3 = f32[136,512]{1,0:T(8,128)S(1)} collective-permute-done((f32[136,512]{1,0:T(8,128)S(1)}, f32[136,512]{1,0:T(8,128)S(1)}, u32[]{:S(2)}, u32[]{:S(2)}) %collective-permute-start.3) | collective-permute-done | bytes 278560 | tf_op jit(solution)/shard_map/ppermute | solution.py:541
  49.0 0.2 broadcast_select_fusion.2
  49.2 1.3 %collective-permute-start.7 = (f32[128,512]{1,0:T(8,128)S(1)}, f32[128,512]{1,0:T(8,128)S(1)}, u32[]{:S(2)}, u32[]{:S(2)}) collective-permute-start(f32[128,512]{1,0:T(8,128)S(1)} %get-tuple-element.140), channel_id=1, source_target_pairs={{8,24},{12,28},{16,0},{20,4},{9,25},{13,29},{17,1},{21,5},{10,26},... | collective-permute-start | bytes 786440 | tf_op jit(solution)/shard_map/ppermute | solution.py:546
  50.5 0.7 collective-permute-start.6
  51.2 0.1 pad_add_fusion.refs_0_
  51.3 0.9 collective-permute-start.10
  52.3 1.0 %copy-done.11 = f32[1024,128]{1,0:T(8,128)S(1)} copy-done((f32[1024,128]{1,0:T(8,128)S(1)}, f32[1024,128]{1,0:T(8,128)}, u32[]{:S(2)}) %copy-start.11) | copy-done | bytes 524312
  53.4 1.0 %copy-done.12 = f32[1024,128]{1,0:T(8,128)S(1)} copy-done((f32[1024,128]{1,0:T(8,128)S(1)}, f32[1024,128]{1,0:T(8,128)}, u32[]{:S(2)}) %copy-start.12) | copy-done | bytes 524312
  54.4 7.2 %local_grads.3 = (bf16[1024,2048]{1,0:T(8,128)(2,1)}, f32[1024,128]{1,0:T(8,128)S(1)}, f32[1024,128]{1,0:T(8,128)S(1)}, f32[4,8,1024]{2,1,0:T(8,128)}, f32[8,128]{1,0:T(8,128)S(1)}) custom-call(s32[2]{0:T(128)S(1)} %pad_add_fusion.refs_0_, bf16[1024,2048]{1,0:T(8,128)(2,1)S(1)} %copy-done, bf16[1024,2048]{1,0:T(8,128)(2,1)S(1)} %copy-done.1, ...), custom_call_target="tpu_custom_call" | custom-call | flops 2415919104 | bytes 3145728 | tf_op jit(solution)/shard_map/local_grads/pallas_call | solution.py:452
  61.6 0.2 broadcast_select_fusion
  61.8 1.2 %collective-permute-start.11 = (f32[128,512]{1,0:T(8,128)S(1)}, f32[128,512]{1,0:T(8,128)S(1)}, u32[]{:S(2)}, u32[]{:S(2)}) collective-permute-start(f32[128,512]{1,0:T(8,128)S(1)} %get-tuple-element.100), channel_id=1, source_target_pairs={{0,4},{4,0},{8,12},{12,8},{16,20},{20,16},{24,28},{28,24},{1,5},{5... | collective-permute-start | bytes 786440 | tf_op jit(solution)/shard_map/ppermute | solution.py:555
  63.0 7.0 %local_grads.4 = (bf16[1024,2048]{1,0:T(8,128)(2,1)}, f32[1024,128]{1,0:T(8,128)S(1)}, f32[1024,128]{1,0:T(8,128)S(1)}, f32[4,8,1024]{2,1,0:T(8,128)}, f32[8,128]{1,0:T(8,128)S(1)}) custom-call(s32[2]{0:T(128)S(1)} %pad_add_fusion.refs_0_, bf16[1024,2048]{1,0:T(8,128)(2,1)S(1)} %copy-done, ...), custom_call_target="tpu_custom_call", output_to_operand_aliasing={{0}: (23, {}), {3}: (24, {})} | custom-call | flops 2415919104 | bytes 3145728 | tf_op jit(solution)/shard_map/local_grads/pallas_call | solution.py:452
  70.0 0.1 broadcast_select_fusion.1.refs_17_
  70.1 11.5 %local_grads.5 = (bf16[1024,2048]{1,0:T(8,128)(2,1)}, f32[1024,128]{1,0:T(8,128)}, f32[1024,128]{1,0:T(8,128)}, f32[4,8,1024]{2,1,0:T(8,128)}, f32[8,128]{1,0:T(8,128)S(1)}) custom-call(s32[2]{0:T(128)S(1)} %pad_add_fusion.refs_0_, bf16[1024,2048]{1,0:T(8,128)(2,1)S(1)} %copy-done, ...), custom_call_target="tpu_custom_call", output_to_operand_aliasing={{0}: (23, {}), {3}: (24, {})} | custom-call | flops 4831838208 | bytes 6291456 | tf_op jit(solution)/shard_map/local_grads/pallas_call | solution.py:452
  81.7 1.6 %collective-permute-start.13 = (f32[8,128]{1,0:T(8,128)S(1)}, f32[8,128]{1,0:T(8,128)S(1)}, u32[]{:S(2)}, u32[]{:S(2)}) collective-permute-start(f32[8,128]{1,0:T(8,128)S(1)} %get-tuple-element.99), channel_id=1, source_target_pairs={{0,2},{1,3},{2,0},{3,1},{4,6},{5,7},{6,4},{7,5},{8,10},{9,11},{10,... | collective-permute-start | bytes 12296 | tf_op jit(solution)/shard_map/ppermute | solution.py:495
  83.3 0.3 collective-permute-start.14
  83.6 1.8 %collective-permute-done.13 = f32[8,128]{1,0:T(8,128)S(1)} collective-permute-done((f32[8,128]{1,0:T(8,128)S(1)}, f32[8,128]{1,0:T(8,128)S(1)}, u32[]{:S(2)}, u32[]{:S(2)}) %collective-permute-start.13) | collective-permute-done | bytes 4128 | tf_op jit(solution)/shard_map/ppermute | solution.py:495
  85.4 0.9 collective-permute-done.14
  86.3 0.9 collective-permute-start.15
  87.2 5.3 %collective-permute-start.16 = (f32[8,128]{1,0:T(8,128)S(1)}, f32[8,128]{1,0:T(8,128)S(1)}, u32[]{:S(2)}, u32[]{:S(2)}) collective-permute-start(f32[8,128]{1,0:T(8,128)S(1)} %add_add_fusion.1), channel_id=1, source_target_pairs={{0,8},{4,12},{8,0},{12,4},{16,24},{20,28},{24,16},{28,20},{1,9},{5... | collective-permute-start | bytes 12296 | tf_op jit(solution)/shard_map/ppermute | solution.py:495
  92.6 0.5 collective-permute-start.17
  93.1 1.0 %collective-permute-done.16 = f32[8,128]{1,0:T(8,128)S(1)} collective-permute-done((f32[8,128]{1,0:T(8,128)S(1)}, f32[8,128]{1,0:T(8,128)S(1)}, u32[]{:S(2)}, u32[]{:S(2)}) %collective-permute-start.16) | collective-permute-done | bytes 4128 | tf_op jit(solution)/shard_map/ppermute | solution.py:495
  94.2 2.9 %collective-permute-done.17 = f32[8,128]{1,0:T(8,128)S(1)} collective-permute-done((f32[8,128]{1,0:T(8,128)S(1)}, f32[8,128]{1,0:T(8,128)S(1)}, u32[]{:S(2)}, u32[]{:S(2)}) %collective-permute-start.17) | collective-permute-done | bytes 4128 | tf_op jit(solution)/shard_map/ppermute | solution.py:495
  97.1 0.9 collective-permute-start.18
  98.0 3.6 %collective-permute-done.18 = f32[8,128]{1,0:T(8,128)S(1)} collective-permute-done((f32[8,128]{1,0:T(8,128)S(1)}, f32[8,128]{1,0:T(8,128)S(1)}, u32[]{:S(2)}, u32[]{:S(2)}) %collective-permute-start.18) | collective-permute-done | bytes 4128 | tf_op jit(solution)/shard_map/ppermute | solution.py:495
  101.6 0.6 slice.150
  102.2 0.5 slice_bitcast_fusion
  (53 shorter events, 0.3 us)
Async XLA Ops:
  5.5 15.4 %collective-permute-start.1 = (f32[264,512]{1,0:T(8,128)}, f32[264,512]{1,0:T(8,128)S(1)}, u32[]{:S(2)}, u32[]{:S(2)}) collective-permute-start(f32[264,512]{1,0:T(8,128)} %get-tuple-element.71), channel_id=1, source_target_pairs={{0,4},{4,0},{8,12},{12,8},{16,20},{20,16},{24,28},{28,24},{1,5},{5... | collective-permute-start | bytes 1622024 | tf_op jit(solution)/shard_map/ppermute | solution.py:533
  23.0 9.8 %collective-permute-start.2 = (f32[136,512]{1,0:T(8,128)S(1)}, f32[136,512]{1,0:T(8,128)S(1)}, u32[]{:S(2)}, u32[]{:S(2)}) collective-permute-start(f32[136,512]{1,0:T(8,128)S(1)} %pad_maximum_fusion), channel_id=1, source_target_pairs={{0,8},{4,12},{8,0},{12,4},{16,24},{20,28},{24,16},{28,20},{1,9},{5... | collective-permute-start | bytes 835592 | tf_op jit(solution)/shard_map/ppermute | solution.py:541
  24.9 14.5 %collective-permute-start = (f32[264,512]{1,0:T(8,128)}, f32[264,512]{1,0:T(8,128)S(1)}, u32[]{:S(2)}, u32[]{:S(2)}) collective-permute-start(f32[264,512]{1,0:T(8,128)} %get-tuple-element.69), channel_id=1, source_target_pairs={{0,4},{4,0},{8,12},{12,8},{16,20},{20,16},{24,28},{28,24},{1,5},{5... | collective-permute-start | bytes 1622024 | tf_op jit(solution)/shard_map/ppermute | solution.py:533
  26.4 6.4 %copy-start.16 = (f32[264,512]{1,0:T(8,128)S(1)}, f32[264,512]{1,0:T(8,128)}, u32[]{:S(2)}) copy-start(f32[264,512]{1,0:T(8,128)} %get-tuple-element.70) | copy-start | bytes 1622020
  26.4 13.0 %copy-start.15 = (f32[264,512]{1,0:T(8,128)S(1)}, f32[264,512]{1,0:T(8,128)}, u32[]{:S(2)}) copy-start(f32[264,512]{1,0:T(8,128)} %get-tuple-element.77) | copy-start | bytes 1622020
  26.4 25.8 %copy-start.8 = (f32[16,2048]{1,0:T(8,128)S(1)}, f32[16,2048]{1,0:T(8,128)}, u32[]{:S(2)}) copy-start(f32[16,2048]{1,0:T(8,128)} %get-tuple-element.54.refs_6_.refs_8_) | copy-start | bytes 393220
  26.4 25.8 %copy-start.9 = (f32[1,32,1024]{2,1,0:T(8,128)S(1)}, f32[1,32,1024]{2,1,0:T(8,128)}, u32[]{:S(2)}) copy-start(f32[1,32,1024]{2,1,0:T(8,128)} %refs_5_.1) | copy-start | bytes 393220
  32.8 19.4 %copy-start.1 = (bf16[1024,2048]{1,0:T(8,128)(2,1)S(1)}, bf16[1024,2048]{1,0:T(8,128)(2,1)}, u32[]{:S(2)}) copy-start(bf16[1024,2048]{1,0:T(8,128)(2,1)} %get-tuple-element.64.ys_ref.refs_2_) | copy-start | bytes 12582916
  33.1 19.2 %copy-start = (bf16[1024,2048]{1,0:T(8,128)(2,1)S(1)}, bf16[1024,2048]{1,0:T(8,128)(2,1)}, u32[]{:S(2)}) copy-start(bf16[1024,2048]{1,0:T(8,128)(2,1)} %get-tuple-element.63.xs_ref.refs_1_) | copy-start | bytes 12582916
  33.1 19.1 %copy-start.2 = (bf16[1,1024,128]{2,1,0:T(8,128)(2,1)S(1)}, bf16[1,1024,128]{2,1,0:T(8,128)(2,1)}, u32[]{:S(2)}) copy-start(bf16[1,1024,128]{2,1,0:T(8,128)(2,1)} %param.12) | copy-start | bytes 786436
  33.1 19.1 %copy-start.3 = (bf16[1,1024,128]{2,1,0:T(8,128)(2,1)S(1)}, bf16[1,1024,128]{2,1,0:T(8,128)(2,1)}, u32[]{:S(2)}) copy-start(bf16[1,1024,128]{2,1,0:T(8,128)(2,1)} %param.13) | copy-start | bytes 786436
  33.1 19.1 %copy-start.4 = (bf16[1024,128]{1,0:T(8,128)(2,1)S(1)}, bf16[1024,128]{1,0:T(8,128)(2,1)}, u32[]{:S(2)}) copy-start(bf16[1024,128]{1,0:T(8,128)(2,1)} %get-tuple-element.53.refs_5_.refs_7_) | copy-start | bytes 786436
  33.1 19.1 %copy-start.5 = (bf16[4,256,256]{2,1,0:T(8,128)(2,1)S(1)}, bf16[4,256,256]{2,1,0:T(8,128)(2,1)}, u32[]{:S(2)}) copy-start(bf16[4,256,256]{2,1,0:T(8,128)(2,1)} %get-tuple-element.67.refs_13_) | copy-start | bytes 1572868
  33.1 19.1 %copy-start.6 = (bf16[4,256,256]{2,1,0:T(8,128)(2,1)S(1)}, bf16[4,256,256]{2,1,0:T(8,128)(2,1)}, u32[]{:S(2)}) copy-start(bf16[4,256,256]{2,1,0:T(8,128)(2,1)} %get-tuple-element.68.refs_14_) | copy-start | bytes 1572868
  33.1 19.1 %copy-start.7 = (bf16[1536,128]{1,0:T(8,128)(2,1)S(1)}, bf16[1536,128]{1,0:T(8,128)(2,1)}, u32[]{:S(2)}) copy-start(bf16[1536,128]{1,0:T(8,128)(2,1)} %constant.44.clone.refs_15_) | copy-start | bytes 1179652
  33.2 19.1 %copy-start.10 = (f32[8,2048]{1,0:T(8,128)S(1)}, f32[8,2048]{1,0:T(8,128)}, u32[]{:S(2)}) copy-start(f32[8,2048]{1,0:T(8,128)} %get-tuple-element.65.refs_4_) | copy-start | bytes 196612
  33.2 19.1 %copy-start.13 = (f32[32]{0:T(128)S(1)}, f32[32]{0:T(128)}, u32[]{:S(2)}) copy-start(f32[32]{0:T(128)} %param.15) | copy-start | bytes 388
  33.2 19.1 %copy-start.14 = (f32[32]{0:T(128)S(1)}, f32[32]{0:T(128)}, u32[]{:S(2)}) copy-start(f32[32]{0:T(128)} %param.16) | copy-start | bytes 388
  33.2 12.3 %collective-permute-start.5 = (f32[128,512]{1,0:T(8,128)S(1)}, f32[128,512]{1,0:T(8,128)S(1)}, u32[]{:S(2)}, u32[]{:S(2)}) collective-permute-start(f32[128,512]{1,0:T(8,128)S(1)} %get-tuple-element.141), channel_id=1, source_target_pairs={{8,24},{12,28},{16,0},{20,4},{9,25},{13,29},{17,1},{21,5},{10,26},... | collective-permute-start | bytes 786440 | tf_op jit(solution)/shard_map/ppermute | solution.py:546
  34.8 10.8 %collective-permute-start.4 = (f32[128,512]{1,0:T(8,128)S(1)}, f32[128,512]{1,0:T(8,128)S(1)}, u32[]{:S(2)}, u32[]{:S(2)}) collective-permute-start(f32[128,512]{1,0:T(8,128)S(1)} %get-tuple-element.141), channel_id=1, source_target_pairs={{8,16},{12,20},{16,8},{20,12},{9,17},{13,21},{17,9},{21,13},{10,18... | collective-permute-start | bytes 786440 | tf_op jit(solution)/shard_map/ppermute | solution.py:545
  35.6 16.6 %collective-permute-start.8 = (f32[128,512]{1,0:T(8,128)S(1)}, f32[128,512]{1,0:T(8,128)S(1)}, u32[]{:S(2)}, u32[]{:S(2)}) collective-permute-start(f32[128,512]{1,0:T(8,128)S(1)} %get-tuple-element.139), channel_id=1, source_target_pairs={{0,4},{4,0},{8,12},{12,8},{16,20},{20,16},{24,28},{28,24},{1,5},{5... | collective-permute-start | bytes 786440 | tf_op jit(solution)/shard_map/ppermute | solution.py:550
  39.5 9.4 %collective-permute-start.3 = (f32[136,512]{1,0:T(8,128)S(1)}, f32[136,512]{1,0:T(8,128)S(1)}, u32[]{:S(2)}, u32[]{:S(2)}) collective-permute-start(f32[136,512]{1,0:T(8,128)S(1)} %pad_maximum_fusion.1), channel_id=1, source_target_pairs={{0,8},{4,12},{8,0},{12,4},{16,24},{20,28},{24,16},{28,20},{1,9},{5... | collective-permute-start | bytes 835592 | tf_op jit(solution)/shard_map/ppermute | solution.py:541
  45.8 6.4 %collective-permute-start.9 = (f32[128,512]{1,0:T(8,128)S(1)}, f32[128,512]{1,0:T(8,128)S(1)}, u32[]{:S(2)}, u32[]{:S(2)}) collective-permute-start(f32[128,512]{1,0:T(8,128)S(1)} %broadcast_select_fusion.6), channel_id=1, source_target_pairs={{0,4},{4,0},{8,12},{12,8},{16,20},{20,16},{24,28},{28,24},{1,5},{5... | collective-permute-start | bytes 786440 | tf_op jit(solution)/shard_map/ppermute | solution.py:555
  49.2 12.4 %collective-permute-start.7 = (f32[128,512]{1,0:T(8,128)S(1)}, f32[128,512]{1,0:T(8,128)S(1)}, u32[]{:S(2)}, u32[]{:S(2)}) collective-permute-start(f32[128,512]{1,0:T(8,128)S(1)} %get-tuple-element.140), channel_id=1, source_target_pairs={{8,24},{12,28},{16,0},{20,4},{9,25},{13,29},{17,1},{21,5},{10,26},... | collective-permute-start | bytes 786440 | tf_op jit(solution)/shard_map/ppermute | solution.py:546
  50.5 11.1 %collective-permute-start.6 = (f32[128,512]{1,0:T(8,128)S(1)}, f32[128,512]{1,0:T(8,128)S(1)}, u32[]{:S(2)}, u32[]{:S(2)}) collective-permute-start(f32[128,512]{1,0:T(8,128)S(1)} %get-tuple-element.140), channel_id=1, source_target_pairs={{8,16},{12,20},{16,8},{20,12},{9,17},{13,21},{17,9},{21,13},{10,18... | collective-permute-start | bytes 786440 | tf_op jit(solution)/shard_map/ppermute | solution.py:545
  51.3 18.8 %collective-permute-start.10 = (f32[128,512]{1,0:T(8,128)S(1)}, f32[128,512]{1,0:T(8,128)S(1)}, u32[]{:S(2)}, u32[]{:S(2)}) collective-permute-start(f32[128,512]{1,0:T(8,128)S(1)} %get-tuple-element.136), channel_id=1, source_target_pairs={{0,4},{4,0},{8,12},{12,8},{16,20},{20,16},{24,28},{28,24},{1,5},{5... | collective-permute-start | bytes 786440 | tf_op jit(solution)/shard_map/ppermute | solution.py:550
  52.3 1.0 %copy-start.11 = (f32[1024,128]{1,0:T(8,128)S(1)}, f32[1024,128]{1,0:T(8,128)}, u32[]{:S(2)}) copy-start(f32[1024,128]{1,0:T(8,128)} %get-tuple-element.74.refs_20_) | copy-start | bytes 1572868
  53.4 1.0 %copy-start.12 = (f32[1024,128]{1,0:T(8,128)S(1)}, f32[1024,128]{1,0:T(8,128)}, u32[]{:S(2)}) copy-start(f32[1024,128]{1,0:T(8,128)} %get-tuple-element.81.refs_21_) | copy-start | bytes 1572868
  61.8 8.3 %collective-permute-start.11 = (f32[128,512]{1,0:T(8,128)S(1)}, f32[128,512]{1,0:T(8,128)S(1)}, u32[]{:S(2)}, u32[]{:S(2)}) collective-permute-start(f32[128,512]{1,0:T(8,128)S(1)} %get-tuple-element.100), channel_id=1, source_target_pairs={{0,4},{4,0},{8,12},{12,8},{16,20},{20,16},{24,28},{28,24},{1,5},{5... | collective-permute-start | bytes 786440 | tf_op jit(solution)/shard_map/ppermute | solution.py:555
  81.6 1.9 %collective-permute-start.12 = (f32[8,128]{1,0:T(8,128)S(1)}, f32[8,128]{1,0:T(8,128)S(1)}, u32[]{:S(2)}, u32[]{:S(2)}) collective-permute-start(f32[8,128]{1,0:T(8,128)S(1)} %get-tuple-element.99), channel_id=1, source_target_pairs={{0,1},{1,0},{2,3},{3,2},{4,5},{5,4},{6,7},{7,6},{8,9},{9,8},{10,11... | collective-permute-start | bytes 12296 | tf_op jit(solution)/shard_map/ppermute | solution.py:495
  81.7 3.7 %collective-permute-start.13 = (f32[8,128]{1,0:T(8,128)S(1)}, f32[8,128]{1,0:T(8,128)S(1)}, u32[]{:S(2)}, u32[]{:S(2)}) collective-permute-start(f32[8,128]{1,0:T(8,128)S(1)} %get-tuple-element.99), channel_id=1, source_target_pairs={{0,2},{1,3},{2,0},{3,1},{4,6},{5,7},{6,4},{7,5},{8,10},{9,11},{10,... | collective-permute-start | bytes 12296 | tf_op jit(solution)/shard_map/ppermute | solution.py:495
  83.3 3.0 %collective-permute-start.14 = (f32[8,128]{1,0:T(8,128)S(1)}, f32[8,128]{1,0:T(8,128)S(1)}, u32[]{:S(2)}, u32[]{:S(2)}) collective-permute-start(f32[8,128]{1,0:T(8,128)S(1)} %get-tuple-element.99), channel_id=1, source_target_pairs={{0,3},{1,2},{2,1},{3,0},{4,7},{5,6},{6,5},{7,4},{8,11},{9,10},{10,... | collective-permute-start | bytes 12296 | tf_op jit(solution)/shard_map/ppermute | solution.py:495
  86.3 6.8 %collective-permute-start.15 = (f32[8,128]{1,0:T(8,128)S(1)}, f32[8,128]{1,0:T(8,128)S(1)}, u32[]{:S(2)}, u32[]{:S(2)}) collective-permute-start(f32[8,128]{1,0:T(8,128)S(1)} %add_add_fusion.1), channel_id=1, source_target_pairs={{0,4},{4,0},{8,12},{12,8},{16,20},{20,16},{24,28},{28,24},{1,5},{5... | collective-permute-start | bytes 12296 | tf_op jit(solution)/shard_map/ppermute | solution.py:495
  87.2 6.9 %collective-permute-start.16 = (f32[8,128]{1,0:T(8,128)S(1)}, f32[8,128]{1,0:T(8,128)S(1)}, u32[]{:S(2)}, u32[]{:S(2)}) collective-permute-start(f32[8,128]{1,0:T(8,128)S(1)} %add_add_fusion.1), channel_id=1, source_target_pairs={{0,8},{4,12},{8,0},{12,4},{16,24},{20,28},{24,16},{28,20},{1,9},{5... | collective-permute-start | bytes 12296 | tf_op jit(solution)/shard_map/ppermute | solution.py:495
  92.6 4.5 %collective-permute-start.17 = (f32[8,128]{1,0:T(8,128)S(1)}, f32[8,128]{1,0:T(8,128)S(1)}, u32[]{:S(2)}, u32[]{:S(2)}) collective-permute-start(f32[8,128]{1,0:T(8,128)S(1)} %add_add_fusion.1), channel_id=1, source_target_pairs={{0,12},{4,8},{8,4},{12,0},{16,28},{20,24},{24,20},{28,16},{1,13},{... | collective-permute-start | bytes 12296 | tf_op jit(solution)/shard_map/ppermute | solution.py:495
  97.1 4.5 %collective-permute-start.18 = (f32[8,128]{1,0:T(8,128)S(1)}, f32[8,128]{1,0:T(8,128)S(1)}, u32[]{:S(2)}, u32[]{:S(2)}) collective-permute-start(f32[8,128]{1,0:T(8,128)S(1)} %add_add_fusion), channel_id=1, source_target_pairs={{0,16},{4,20},{8,24},{12,28},{16,0},{20,4},{24,8},{28,12},{1,17},{... | collective-permute-start | bytes 12296 | tf_op jit(solution)/shard_map/ppermute | solution.py:495

commit v13 on v9

--- a/solution.py
+++ b/solution.py
@@ -537,7 +537,7 @@
         inside = (place == 1) | (place == 2)
         known = jnp.where(inside, near[:states], 0.0)
         mine_early, early = shares(lower, known, got, 2)
-        other_early = lax.ppermute(early, "seq", swap)
+        other_early = lax.ppermute(early, "seq", [m for m in swap if m not in ((1, 0), (size - 2, size - 1))])
         token = yield early, far
         far = after(far, token)
         outer = near[states : states + 1] * far + near[:states]

time: 99.4 us -> 102 us (1.026)
  starting transfers between devices: 27.3 us -> 35 us
  waiting for transfers between devices: 18.1 us -> 13.1 us
    ppermute x2, starting transfers between devices: 1.45 us -> 5.53 us  [entering(): lax.ppermute(early, 'seq', [m for m in swap if m not in ((1, 0), (size -...]
    ppermute x2, waiting for transfers between devices: 5.25 us -> 1.89 us  [entering(): far = lax.ppermute(message, 'seq', both([(1, 3), (2, 0)]))]
    ppermute x2, waiting for transfers between devices: 4.41 us -> 1.81 us  [entering(): got = lax.ppermute(message, 'seq', swap)]
    ppermute x2, starting transfers between devices: 4.68 us -> 7.27 us  [entering(): near = lax.ppermute(message, 'seq', both([(0, 1), (1, 0), (2, 3), (3, 2)]))]
    ppermute x7, starting transfers between devices: 10.9 us -> 12.8 us  [summed_over(): lax.ppermute(value, axis, [(i, i ^ s) for i in range(size)])]
  transfers between devices with their start and end apart: 19 -> 19, of which waited for: 10 -> 8; matrix products, arithmetic and copies ran while one was open for 1% -> 1% of each run, Pallas kernels for 32% -> 31%
where the time goes in v13:
time: 102 us
  Pallas kernels  48.1 us (47%)
  starting transfers between devices  35 us (34%)
  waiting for transfers between devices  13.1 us (13%)
  other arithmetic  3.22 us (3%)
  between operations  1.2 us (1%)
  local copies, waits for them, and re-layouts  1.19 us (1%)
    pallas_call x3, Pallas kernels, local_grads(): pl.pallas_call(functools.partial(grads_kernel, first, scale, part, half,...  26.4 us
    pallas_call x3, Pallas kernels, local_states(): pl.pallas_call(functools.partial(local_kernel, first, last, count), grid_...  15.2 us
    ppermute x7, starting transfers between devices, summed_over(): lax.ppermute(value, axis, [(i, i ^ s) for i in range(size)])  12.8 us
    ppermute x2, starting transfers between devices, entering(): near = lax.ppermute(message, 'seq', both([(0, 1), (1, 0), (2, 3), (3, 2)]))  7.27 us
    pallas_call x1, Pallas kernels, pairs_grads(): pl.pallas_call(pairs_kernel, grid=(length // GROUP,), in_specs=[columns,...  6.39 us
    ppermute x7, waiting for transfers between devices, summed_over(): lax.ppermute(value, axis, [(i, i ^ s) for i in range(size)])  6.01 us
    ppermute x2, starting transfers between devices, entering(): lax.ppermute(early, 'seq', [m for m in swap if m not in ((1, 0), (size -...  5.53 us
    ppermute x2, starting transfers between devices, entering(): got = lax.ppermute(message, 'seq', swap)  4.48 us
  transfers between devices with their start and end apart: 19, of which 8 were waited for; matrix products, arithmetic and copies ran while one was open for 1% of the time, Pallas kernels for 31%

profile of v13, /device:TPU:0, one launch (start us, length us, event | category | flops | bytes accessed | tf_op | source)
XLA Modules:
  0.0 101.8 jit_solution(16298589905801516850)
XLA Ops:
  0.6 4.6 %local_states.3 = (f32[264,512]{1,0:T(8,128)}, bf16[1024,2048]{1,0:T(8,128)(2,1)}, bf16[1024,2048]{1,0:T(8,128)(2,1)}, f32[8,2048]{1,0:T(8,128)}, bf16[1024,128]{1,0:T(8,128)(2,1)}, /*index=5*/f32[16,2048]{1,0:T(8,128)}) custom-call(s32[1]{0:T(128)} %bitcast.7.refs_0_, bf16[1024,2048]{1,0:T(8,128)(2,1)} %bitcast.72, bf16[1024,2048]{1,0:T(8,128)(2,1)} %bitcast.66, ...), custom_call_target="tpu_custom_call" | custom-call | flops 536870912 | bytes 4194304 | tf_op jit(solution)/shard_map/local_states/pallas_call | solution.py:246
  5.2 3.0 %collective-permute-start.1 = (f32[264,512]{1,0:T(8,128)}, f32[264,512]{1,0:T(8,128)S(1)}, u32[]{:S(2)}, u32[]{:S(2)}) collective-permute-start(f32[264,512]{1,0:T(8,128)} %get-tuple-element.69), channel_id=1, source_target_pairs={{0,4},{4,0},{8,12},{12,8},{16,20},{20,16},{24,28},{28,24},{1,5},{5... | collective-permute-start | bytes 1622024 | tf_op jit(solution)/shard_map/ppermute | solution.py:523
  8.2 3.8 %local_states.4 = (f32[264,512]{1,0:T(8,128)}, bf16[1024,2048]{1,0:T(8,128)(2,1)}, bf16[1024,2048]{1,0:T(8,128)(2,1)}, f32[8,2048]{1,0:T(8,128)}) custom-call(s32[1]{0:T(128)} %bitcast.11.refs_0_, bf16[1024,2048]{1,0:T(8,128)(2,1)} %bitcast.73, bf16[1024,2048]{1,0:T(8,128)(2,1)} %bitcast.67, ...), custom_call_target="tpu_custom_call", output_to_operand_aliasing={{1}: (7, {}), {2}: (8, {}), {3}: (9, {})} | custom-call | flops 536870912 | bytes 4194304 | tf_op jit(solution)/shard_map/local_states/pallas_call | solution.py:246
  12.0 6.8 %local_states.5 = (f32[264,512]{1,0:T(8,128)}, f32[264,512]{1,0:T(8,128)}, bf16[1024,2048]{1,0:T(8,128)(2,1)}, bf16[1024,2048]{1,0:T(8,128)(2,1)}, f32[8,2048]{1...) custom-call(s32[1]{0:T(128)} %bitcast.2.refs_0_, ...), custom_call_target="tpu_custom_call", output_to_operand_aliasing={{2}: (7, {}), {3}: (8, {}), {4}: (9, {})} | custom-call | flops 1073741824 | bytes 8388608 | tf_op jit(solution)/shard_map/local_states/pallas_call | solution.py:246
  18.9 1.8 %collective-permute-done.1 = f32[264,512]{1,0:T(8,128)S(1)} collective-permute-done((f32[264,512]{1,0:T(8,128)}, f32[264,512]{1,0:T(8,128)S(1)}, u32[]{:S(2)}, u32[]{:S(2)}) %collective-permute-start.1) | collective-permute-done | bytes 540704 | tf_op jit(solution)/shard_map/ppermute | solution.py:523
  20.7 0.9 fusion.1
  21.6 1.2 %add_select_fusion.11 = (f32[128,512]{1,0:T(8,128)S(1)}, f32[128,512]{1,0:T(8,128)S(1)}, f32[128,512]{1,0:T(8,128)S(1)}) fusion(f32[512]{0:T(512)S(1)} %bitcast.98, f32[512]{0:T(512)S(1)} %bitcast.97, pred[]{:T(512)S(6)} %or.9, f32[264,512]{1,0:T(8,128)S(1)} %collective-permute-done.1, f32[264,512]{1,0:T(8,128)} %get-tuple-element.68, pred[]{:T(512)S(6)} %eq.12), kind=kLoop, calls=%fused_computation.15 | loop fusion | flops 589824 | bytes 1839106 | tf_op jit(solution)/shard_map/jit(_where)/select_n | solution.py:513
  22.8 1.9 %collective-permute-start.2 = (f32[136,512]{1,0:T(8,128)S(1)}, f32[136,512]{1,0:T(8,128)S(1)}, u32[]{:S(2)}, u32[]{:S(2)}) collective-permute-start(f32[136,512]{1,0:T(8,128)S(1)} %pad_maximum_fusion), channel_id=1, source_target_pairs={{0,8},{4,12},{8,0},{12,4},{16,24},{20,28},{24,16},{28,20},{1,9},{5... | collective-permute-start | bytes 835592 | tf_op jit(solution)/shard_map/ppermute | solution.py:531
  24.6 1.5 %collective-permute-start = (f32[264,512]{1,0:T(8,128)S(1)}, f32[264,512]{1,0:T(8,128)S(1)}, u32[]{:S(2)}, u32[]{:S(2)}) collective-permute-start(f32[264,512]{1,0:T(8,128)S(1)} %copy-done.19), channel_id=1, source_target_pairs={{0,4},{4,0},{8,12},{12,8},{16,20},{20,16},{24,28},{28,24},{1,5},{5... | collective-permute-start | bytes 1622024 | tf_op jit(solution)/shard_map/ppermute | solution.py:523
  26.1 6.4 %pairs_grads.1 = (f32[1024,128]{1,0:T(8,128)}, f32[1024,128]{1,0:T(8,128)}) custom-call(bf16[1024,2048]{1,0:T(8,128)(2,1)} %get-tuple-element.60.xs_ref.refs_1_, bf16[1024,2048]{1,0:T(8,128)(2,1)} %get-tuple-element.61.ys_ref.refs_2_, bf16[1024,128]{1,0:T(8,128)(2,1)} %bitcast.44, bf16[1024,128]{1,0:T(8,128)(2,1)} %bitcast.51), custom_call_target="tpu_custom_call" | custom-call | flops 1073741824 | bytes 8388608 | tf_op jit(solution)/shard_map/pairs_grads/pallas_call | solution.py:274
  32.6 0.2 broadcast_select_fusion.4
  32.8 0.0 copy-start
  32.8 0.0 copy-start.2
  32.9 0.0 copy-start.7
  33.0 1.6 %collective-permute-start.5 = (f32[128,512]{1,0:T(8,128)S(1)}, f32[128,512]{1,0:T(8,128)S(1)}, u32[]{:S(2)}, u32[]{:S(2)}) collective-permute-start(f32[128,512]{1,0:T(8,128)S(1)} %get-tuple-element.139), channel_id=1, source_target_pairs={{8,24},{12,28},{16,0},{20,4},{9,25},{13,29},{17,1},{21,5},{10,26},... | collective-permute-start | bytes 786440 | tf_op jit(solution)/shard_map/ppermute | solution.py:536
  34.5 0.8 collective-permute-start.4
  35.4 2.4 %collective-permute-start.8 = (f32[128,512]{1,0:T(8,128)S(1)}, f32[128,512]{1,0:T(8,128)S(1)}, u32[]{:S(2)}, u32[]{:S(2)}) collective-permute-start(f32[128,512]{1,0:T(8,128)S(1)} %get-tuple-element.137), channel_id=1, source_target_pairs={{0,4},{8,12},{12,8},{16,20},{20,16},{28,24},{1,5},{9,13},{13,9},{1... | collective-permute-start | bytes 786440 | tf_op jit(solution)/shard_map/ppermute | solution.py:540
  37.8 0.1 add_select_fusion.8
  38.0 5.4 %collective-permute-start.3 = (f32[136,512]{1,0:T(8,128)S(1)}, f32[136,512]{1,0:T(8,128)S(1)}, u32[]{:S(2)}, u32[]{:S(2)}) collective-permute-start(f32[136,512]{1,0:T(8,128)S(1)} %pad_maximum_fusion.1), channel_id=1, source_target_pairs={{0,8},{4,12},{8,0},{12,4},{16,24},{20,28},{24,16},{28,20},{1,9},{5... | collective-permute-start | bytes 835592 | tf_op jit(solution)/shard_map/ppermute | solution.py:531
  43.4 1.9 %collective-permute-done.5 = f32[128,512]{1,0:T(8,128)S(1)} collective-permute-done((f32[128,512]{1,0:T(8,128)S(1)}, f32[128,512]{1,0:T(8,128)S(1)}, u32[]{:S(2)}, u32[]{:S(2)}) %collective-permute-start.5) | collective-permute-done | bytes 262176 | tf_op jit(solution)/shard_map/ppermute | solution.py:536
  45.3 0.1 broadcast_select_fusion.3
  45.4 0.1 broadcast_select_fusion.6
  45.5 0.6 collective-permute-start.9
  46.1 3.4 %collective-permute-done.3 = f32[136,512]{1,0:T(8,128)S(1)} collective-permute-done((f32[136,512]{1,0:T(8,128)S(1)}, f32[136,512]{1,0:T(8,128)S(1)}, u32[]{:S(2)}, u32[]{:S(2)}) %collective-permute-start.3) | collective-permute-done | bytes 278560 | tf_op jit(solution)/shard_map/ppermute | solution.py:531
  49.5 0.2 broadcast_select_fusion.2
  49.8 1.3 %collective-permute-start.7 = (f32[128,512]{1,0:T(8,128)S(1)}, f32[128,512]{1,0:T(8,128)S(1)}, u32[]{:S(2)}, u32[]{:S(2)}) collective-permute-start(f32[128,512]{1,0:T(8,128)S(1)} %get-tuple-element.138), channel_id=1, source_target_pairs={{8,24},{12,28},{16,0},{20,4},{9,25},{13,29},{17,1},{21,5},{10,26},... | collective-permute-start | bytes 786440 | tf_op jit(solution)/shard_map/ppermute | solution.py:536
  51.1 0.7 collective-permute-start.6
  51.7 0.1 pad_add_fusion.refs_0_
  51.8 3.1 %collective-permute-start.10 = (f32[128,512]{1,0:T(8,128)S(1)}, f32[128,512]{1,0:T(8,128)S(1)}, u32[]{:S(2)}, u32[]{:S(2)}) collective-permute-start(f32[128,512]{1,0:T(8,128)S(1)} %get-tuple-element.134), channel_id=1, source_target_pairs={{0,4},{8,12},{12,8},{16,20},{20,16},{28,24},{1,5},{9,13},{13,9},{1... | collective-permute-start | bytes 786440 | tf_op jit(solution)/shard_map/ppermute | solution.py:540
  55.1 7.3 %local_grads.3 = (bf16[1024,2048]{1,0:T(8,128)(2,1)}, f32[1024,128]{1,0:T(8,128)S(1)}, f32[1024,128]{1,0:T(8,128)S(1)}, f32[4,8,1024]{2,1,0:T(8,128)}, f32[8,128]{1,0:T(8,128)S(1)}) custom-call(s32[2]{0:T(128)S(1)} %pad_add_fusion.refs_0_, bf16[1024,2048]{1,0:T(8,128)(2,1)S(1)} %copy-done, bf16[1024,2048]{1,0:T(8,128)(2,1)} %get-tuple-element.61.ys_ref.refs_2_, ...), custom_call_target="tpu_custom_call" | custom-call | flops 2415919104 | bytes 3145728 | tf_op jit(solution)/shard_map/local_grads/pallas_call | solution.py:442
  62.4 0.1 broadcast_select_fusion
  62.6 0.1 collective-permute-start.11
  62.6 7.6 %local_grads.4 = (bf16[1024,2048]{1,0:T(8,128)(2,1)}, f32[1024,128]{1,0:T(8,128)S(1)}, f32[1024,128]{1,0:T(8,128)S(1)}, f32[4,8,1024]{2,1,0:T(8,128)}, f32[8,128]{1,0:T(8,128)S(1)}) custom-call(s32[2]{0:T(128)S(1)} %pad_add_fusion.refs_0_, bf16[1024,2048]{1,0:T(8,128)(2,1)S(1)} %copy-done, ...), custom_call_target="tpu_custom_call", output_to_operand_aliasing={{0}: (24, {}), {3}: (25, {})} | custom-call | flops 2415919104 | bytes 3145728 | tf_op jit(solution)/shard_map/local_grads/pallas_call | solution.py:442
  70.2 0.1 broadcast_select_fusion.1.refs_18_
  70.4 11.6 %local_grads.5 = (bf16[1024,2048]{1,0:T(8,128)(2,1)}, f32[1024,128]{1,0:T(8,128)}, f32[1024,128]{1,0:T(8,128)}, f32[4,8,1024]{2,1,0:T(8,128)}, f32[8,128]{1,0:T(8,128)S(1)}) custom-call(s32[2]{0:T(128)S(1)} %pad_add_fusion.refs_0_, bf16[1024,2048]{1,0:T(8,128)(2,1)S(1)} %copy-done, ...), custom_call_target="tpu_custom_call", output_to_operand_aliasing={{0}: (24, {}), {3}: (25, {})} | custom-call | flops 4831838208 | bytes 6291456 | tf_op jit(solution)/shard_map/local_grads/pallas_call | solution.py:442
  82.0 0.1 collective-permute-start.14
  82.0 1.6 %collective-permute-start.13 = (f32[8,128]{1,0:T(8,128)S(1)}, f32[8,128]{1,0:T(8,128)S(1)}, u32[]{:S(2)}, u32[]{:S(2)}) collective-permute-start(f32[8,128]{1,0:T(8,128)S(1)} %get-tuple-element.97), channel_id=1, source_target_pairs={{0,2},{1,3},{2,0},{3,1},{4,6},{5,7},{6,4},{7,5},{8,10},{9,11},{10,... | collective-permute-start | bytes 12296 | tf_op jit(solution)/shard_map/ppermute | solution.py:485
  83.6 0.3 collective-permute-start.12
  83.9 1.2 %collective-permute-done.14 = f32[8,128]{1,0:T(8,128)S(1)} collective-permute-done((f32[8,128]{1,0:T(8,128)S(1)}, f32[8,128]{1,0:T(8,128)S(1)}, u32[]{:S(2)}, u32[]{:S(2)}) %collective-permute-start.14) | collective-permute-done | bytes 4128 | tf_op jit(solution)/shard_map/ppermute | solution.py:485
  85.1 0.7 collective-permute-done.13
  85.7 6.8 %collective-permute-start.17 = (f32[8,128]{1,0:T(8,128)S(1)}, f32[8,128]{1,0:T(8,128)S(1)}, u32[]{:S(2)}, u32[]{:S(2)}) collective-permute-start(f32[8,128]{1,0:T(8,128)S(1)} %add_add_fusion.1), channel_id=1, source_target_pairs={{0,12},{4,8},{8,4},{12,0},{16,28},{20,24},{24,20},{28,16},{1,13},{... | collective-permute-start | bytes 12296 | tf_op jit(solution)/shard_map/ppermute | solution.py:485
  92.5 1.0 collective-permute-start.15
  93.5 0.6 collective-permute-done.17
  94.1 2.0 %collective-permute-done.16 = f32[8,128]{1,0:T(8,128)S(1)} collective-permute-done((f32[8,128]{1,0:T(8,128)S(1)}, f32[8,128]{1,0:T(8,128)S(1)}, u32[]{:S(2)}, u32[]{:S(2)}) %collective-permute-start.16) | collective-permute-done | bytes 4128 | tf_op jit(solution)/shard_map/ppermute | solution.py:485
  96.1 3.0 %collective-permute-start.18 = (f32[8,128]{1,0:T(8,128)S(1)}, f32[8,128]{1,0:T(8,128)S(1)}, u32[]{:S(2)}, u32[]{:S(2)}) collective-permute-start(f32[8,128]{1,0:T(8,128)S(1)} %add_add_fusion), channel_id=1, source_target_pairs={{0,16},{4,20},{8,24},{12,28},{16,0},{20,4},{24,8},{28,12},{1,17},{... | collective-permute-start | bytes 12296 | tf_op jit(solution)/shard_map/ppermute | solution.py:485
  99.2 1.6 %collective-permute-done.18 = f32[8,128]{1,0:T(8,128)S(1)} collective-permute-done((f32[8,128]{1,0:T(8,128)S(1)}, f32[8,128]{1,0:T(8,128)S(1)}, u32[]{:S(2)}, u32[]{:S(2)}) %collective-permute-start.18) | collective-permute-done | bytes 4128 | tf_op jit(solution)/shard_map/ppermute | solution.py:485
  100.8 0.5 slice_bitcast_fusion
  101.3 0.6 slice.150
  (59 shorter events, 0.2 us)
Async XLA Ops:
  5.2 15.5 %collective-permute-start.1 = (f32[264,512]{1,0:T(8,128)}, f32[264,512]{1,0:T(8,128)S(1)}, u32[]{:S(2)}, u32[]{:S(2)}) collective-permute-start(f32[264,512]{1,0:T(8,128)} %get-tuple-element.69), channel_id=1, source_target_pairs={{0,4},{4,0},{8,12},{12,8},{16,20},{20,16},{24,28},{28,24},{1,5},{5... | collective-permute-start | bytes 1622024 | tf_op jit(solution)/shard_map/ppermute | solution.py:523
  12.0 12.6 %copy-start.19 = (f32[264,512]{1,0:T(8,128)S(1)}, f32[264,512]{1,0:T(8,128)}, u32[]{:S(2)}) copy-start(f32[264,512]{1,0:T(8,128)} %get-tuple-element.67) | copy-start | bytes 1622020
  22.8 9.8 %collective-permute-start.2 = (f32[136,512]{1,0:T(8,128)S(1)}, f32[136,512]{1,0:T(8,128)S(1)}, u32[]{:S(2)}, u32[]{:S(2)}) collective-permute-start(f32[136,512]{1,0:T(8,128)S(1)} %pad_maximum_fusion), channel_id=1, source_target_pairs={{0,8},{4,12},{8,0},{12,4},{16,24},{20,28},{24,16},{28,20},{1,9},{5... | collective-permute-start | bytes 835592 | tf_op jit(solution)/shard_map/ppermute | solution.py:531
  24.6 13.2 %collective-permute-start = (f32[264,512]{1,0:T(8,128)S(1)}, f32[264,512]{1,0:T(8,128)S(1)}, u32[]{:S(2)}, u32[]{:S(2)}) collective-permute-start(f32[264,512]{1,0:T(8,128)S(1)} %copy-done.19), channel_id=1, source_target_pairs={{0,4},{4,0},{8,12},{12,8},{16,20},{20,16},{24,28},{28,24},{1,5},{5... | collective-permute-start | bytes 1622024 | tf_op jit(solution)/shard_map/ppermute | solution.py:523
  26.1 6.4 %copy-start.18 = (f32[264,512]{1,0:T(8,128)S(1)}, f32[264,512]{1,0:T(8,128)}, u32[]{:S(2)}) copy-start(f32[264,512]{1,0:T(8,128)} %get-tuple-element.68) | copy-start | bytes 1622020
  26.1 11.7 %copy-start.17 = (f32[264,512]{1,0:T(8,128)S(1)}, f32[264,512]{1,0:T(8,128)}, u32[]{:S(2)}) copy-start(f32[264,512]{1,0:T(8,128)} %get-tuple-element.75) | copy-start | bytes 1622020
  32.6 22.4 %copy-start.14 = (f32[1024,128]{1,0:T(8,128)S(1)}, f32[1024,128]{1,0:T(8,128)}, u32[]{:S(2)}) copy-start(f32[1024,128]{1,0:T(8,128)} %get-tuple-element.79.refs_22_) | copy-start | bytes 1572868
  32.8 22.2 %copy-start = (bf16[1024,2048]{1,0:T(8,128)(2,1)S(1)}, bf16[1024,2048]{1,0:T(8,128)(2,1)}, u32[]{:S(2)}) copy-start(bf16[1024,2048]{1,0:T(8,128)(2,1)} %get-tuple-element.60.xs_ref.refs_1_) | copy-start | bytes 12582916
  32.8 22.2 %copy-start.2 = (bf16[1,1024,128]{2,1,0:T(8,128)(2,1)S(1)}, bf16[1,1024,128]{2,1,0:T(8,128)(2,1)}, u32[]{:S(2)}) copy-start(bf16[1,1024,128]{2,1,0:T(8,128)(2,1)} %param.12) | copy-start | bytes 786436
  32.8 22.2 %copy-start.3 = (bf16[1,1024,128]{2,1,0:T(8,128)(2,1)S(1)}, bf16[1,1024,128]{2,1,0:T(8,128)(2,1)}, u32[]{:S(2)}) copy-start(bf16[1,1024,128]{2,1,0:T(8,128)(2,1)} %param.13) | copy-start | bytes 786436
  32.8 22.2 %copy-start.4 = (bf16[1024,128]{1,0:T(8,128)(2,1)S(1)}, bf16[1024,128]{1,0:T(8,128)(2,1)}, u32[]{:S(2)}) copy-start(bf16[1024,128]{1,0:T(8,128)(2,1)} %get-tuple-element.52.refs_5_.refs_7_) | copy-start | bytes 786436
  32.9 22.2 %copy-start.5 = (bf16[4,256,256]{2,1,0:T(8,128)(2,1)S(1)}, bf16[4,256,256]{2,1,0:T(8,128)(2,1)}, u32[]{:S(2)}) copy-start(bf16[4,256,256]{2,1,0:T(8,128)(2,1)} %get-tuple-element.65.refs_14_) | copy-start | bytes 1572868
  32.9 22.2 %copy-start.6 = (bf16[4,256,256]{2,1,0:T(8,128)(2,1)S(1)}, bf16[4,256,256]{2,1,0:T(8,128)(2,1)}, u32[]{:S(2)}) copy-start(bf16[4,256,256]{2,1,0:T(8,128)(2,1)} %get-tuple-element.66.refs_15_) | copy-start | bytes 1572868
  32.9 22.2 %copy-start.7 = (bf16[1536,128]{1,0:T(8,128)(2,1)S(1)}, bf16[1536,128]{1,0:T(8,128)(2,1)}, u32[]{:S(2)}) copy-start(bf16[1536,128]{1,0:T(8,128)(2,1)} %constant.44.clone.refs_16_) | copy-start | bytes 1179652
  32.9 22.2 %copy-start.8 = (f32[16,2048]{1,0:T(8,128)S(1)}, f32[16,2048]{1,0:T(8,128)}, u32[]{:S(2)}) copy-start(f32[16,2048]{1,0:T(8,128)} %get-tuple-element.53.refs_6_.refs_8_) | copy-start | bytes 393220
  32.9 22.2 %copy-start.9 = (bf16[128,1024]{1,0:T(8,128)(2,1)S(1)}, bf16[128,1024]{1,0:T(8,128)(2,1)}, u32[]{:S(2)}) copy-start(bf16[128,1024]{1,0:T(8,128)(2,1)} %get-tuple-element.63.refs_12_) | copy-start | bytes 786436
  32.9 22.2 %copy-start.10 = (bf16[128,1024]{1,0:T(8,128)(2,1)S(1)}, bf16[128,1024]{1,0:T(8,128)(2,1)}, u32[]{:S(2)}) copy-start(bf16[128,1024]{1,0:T(8,128)(2,1)} %get-tuple-element.64.refs_13_) | copy-start | bytes 786436
  32.9 22.2 %copy-start.11 = (f32[1,32,1024]{2,1,0:T(8,128)S(1)}, f32[1,32,1024]{2,1,0:T(8,128)}, u32[]{:S(2)}) copy-start(f32[1,32,1024]{2,1,0:T(8,128)} %refs_5_.1) | copy-start | bytes 393220
  32.9 22.1 %copy-start.12 = (f32[8,2048]{1,0:T(8,128)S(1)}, f32[8,2048]{1,0:T(8,128)}, u32[]{:S(2)}) copy-start(f32[8,2048]{1,0:T(8,128)} %get-tuple-element.62.refs_4_) | copy-start | bytes 196612
  32.9 22.1 %copy-start.13 = (f32[1024,128]{1,0:T(8,128)S(1)}, f32[1024,128]{1,0:T(8,128)}, u32[]{:S(2)}) copy-start(f32[1024,128]{1,0:T(8,128)} %get-tuple-element.72.refs_21_) | copy-start | bytes 1572868
  33.0 22.1 %copy-start.15 = (f32[32]{0:T(128)S(1)}, f32[32]{0:T(128)}, u32[]{:S(2)}) copy-start(f32[32]{0:T(128)} %param.15) | copy-start | bytes 388
  33.0 22.1 %copy-start.16 = (f32[32]{0:T(128)S(1)}, f32[32]{0:T(128)}, u32[]{:S(2)}) copy-start(f32[32]{0:T(128)} %param.16) | copy-start | bytes 388
  33.0 12.3 %collective-permute-start.5 = (f32[128,512]{1,0:T(8,128)S(1)}, f32[128,512]{1,0:T(8,128)S(1)}, u32[]{:S(2)}, u32[]{:S(2)}) collective-permute-start(f32[128,512]{1,0:T(8,128)S(1)} %get-tuple-element.139), channel_id=1, source_target_pairs={{8,24},{12,28},{16,0},{20,4},{9,25},{13,29},{17,1},{21,5},{10,26},... | collective-permute-start | bytes 786440 | tf_op jit(solution)/shard_map/ppermute | solution.py:536
  34.5 10.8 %collective-permute-start.4 = (f32[128,512]{1,0:T(8,128)S(1)}, f32[128,512]{1,0:T(8,128)S(1)}, u32[]{:S(2)}, u32[]{:S(2)}) collective-permute-start(f32[128,512]{1,0:T(8,128)S(1)} %get-tuple-element.139), channel_id=1, source_target_pairs={{8,16},{12,20},{16,8},{20,12},{9,17},{13,21},{17,9},{21,13},{10,18... | collective-permute-start | bytes 786440 | tf_op jit(solution)/shard_map/ppermute | solution.py:535
  35.4 19.6 %collective-permute-start.8 = (f32[128,512]{1,0:T(8,128)S(1)}, f32[128,512]{1,0:T(8,128)S(1)}, u32[]{:S(2)}, u32[]{:S(2)}) collective-permute-start(f32[128,512]{1,0:T(8,128)S(1)} %get-tuple-element.137), channel_id=1, source_target_pairs={{0,4},{8,12},{12,8},{16,20},{20,16},{28,24},{1,5},{9,13},{13,9},{1... | collective-permute-start | bytes 786440 | tf_op jit(solution)/shard_map/ppermute | solution.py:540
  38.0 11.5 %collective-permute-start.3 = (f32[136,512]{1,0:T(8,128)S(1)}, f32[136,512]{1,0:T(8,128)S(1)}, u32[]{:S(2)}, u32[]{:S(2)}) collective-permute-start(f32[136,512]{1,0:T(8,128)S(1)} %pad_maximum_fusion.1), channel_id=1, source_target_pairs={{0,8},{4,12},{8,0},{12,4},{16,24},{20,28},{24,16},{28,20},{1,9},{5... | collective-permute-start | bytes 835592 | tf_op jit(solution)/shard_map/ppermute | solution.py:531
  45.5 9.4 %collective-permute-start.9 = (f32[128,512]{1,0:T(8,128)S(1)}, f32[128,512]{1,0:T(8,128)S(1)}, u32[]{:S(2)}, u32[]{:S(2)}) collective-permute-start(f32[128,512]{1,0:T(8,128)S(1)} %broadcast_select_fusion.6), channel_id=1, source_target_pairs={{0,4},{4,0},{8,12},{12,8},{16,20},{20,16},{24,28},{28,24},{1,5},{5... | collective-permute-start | bytes 786440 | tf_op jit(solution)/shard_map/ppermute | solution.py:545
  49.8 12.6 %collective-permute-start.7 = (f32[128,512]{1,0:T(8,128)S(1)}, f32[128,512]{1,0:T(8,128)S(1)}, u32[]{:S(2)}, u32[]{:S(2)}) collective-permute-start(f32[128,512]{1,0:T(8,128)S(1)} %get-tuple-element.138), channel_id=1, source_target_pairs={{8,24},{12,28},{16,0},{20,4},{9,25},{13,29},{17,1},{21,5},{10,26},... | collective-permute-start | bytes 786440 | tf_op jit(solution)/shard_map/ppermute | solution.py:536
  51.1 11.3 %collective-permute-start.6 = (f32[128,512]{1,0:T(8,128)S(1)}, f32[128,512]{1,0:T(8,128)S(1)}, u32[]{:S(2)}, u32[]{:S(2)}) collective-permute-start(f32[128,512]{1,0:T(8,128)S(1)} %get-tuple-element.138), channel_id=1, source_target_pairs={{8,16},{12,20},{16,8},{20,12},{9,17},{13,21},{17,9},{21,13},{10,18... | collective-permute-start | bytes 786440 | tf_op jit(solution)/shard_map/ppermute | solution.py:535
  51.8 18.5 %collective-permute-start.10 = (f32[128,512]{1,0:T(8,128)S(1)}, f32[128,512]{1,0:T(8,128)S(1)}, u32[]{:S(2)}, u32[]{:S(2)}) collective-permute-start(f32[128,512]{1,0:T(8,128)S(1)} %get-tuple-element.134), channel_id=1, source_target_pairs={{0,4},{8,12},{12,8},{16,20},{20,16},{28,24},{1,5},{9,13},{13,9},{1... | collective-permute-start | bytes 786440 | tf_op jit(solution)/shard_map/ppermute | solution.py:540
  62.6 7.8 %collective-permute-start.11 = (f32[128,512]{1,0:T(8,128)S(1)}, f32[128,512]{1,0:T(8,128)S(1)}, u32[]{:S(2)}, u32[]{:S(2)}) collective-permute-start(f32[128,512]{1,0:T(8,128)S(1)} %get-tuple-element.98), channel_id=1, source_target_pairs={{0,4},{4,0},{8,12},{12,8},{16,20},{20,16},{24,28},{28,24},{1,5},{5... | collective-permute-start | bytes 786440 | tf_op jit(solution)/shard_map/ppermute | solution.py:545
  62.6 7.7 %copy-start.1 = (bf16[1024,2048]{1,0:T(8,128)(2,1)S(1)}, bf16[1024,2048]{1,0:T(8,128)(2,1)}, u32[]{:S(2)}) copy-start(bf16[1024,2048]{1,0:T(8,128)(2,1)} %get-tuple-element.61.ys_ref.refs_2_) | copy-start | bytes 12582916
  82.0 3.1 %collective-permute-start.14 = (f32[8,128]{1,0:T(8,128)S(1)}, f32[8,128]{1,0:T(8,128)S(1)}, u32[]{:S(2)}, u32[]{:S(2)}) collective-permute-start(f32[8,128]{1,0:T(8,128)S(1)} %get-tuple-element.97), channel_id=1, source_target_pairs={{0,3},{1,2},{2,1},{3,0},{4,7},{5,6},{6,5},{7,4},{8,11},{9,10},{10,... | collective-permute-start | bytes 12296 | tf_op jit(solution)/shard_map/ppermute | solution.py:485
  82.0 3.7 %collective-permute-start.13 = (f32[8,128]{1,0:T(8,128)S(1)}, f32[8,128]{1,0:T(8,128)S(1)}, u32[]{:S(2)}, u32[]{:S(2)}) collective-permute-start(f32[8,128]{1,0:T(8,128)S(1)} %get-tuple-element.97), channel_id=1, source_target_pairs={{0,2},{1,3},{2,0},{3,1},{4,6},{5,7},{6,4},{7,5},{8,10},{9,11},{10,... | collective-permute-start | bytes 12296 | tf_op jit(solution)/shard_map/ppermute | solution.py:485
  83.6 2.1 %collective-permute-start.12 = (f32[8,128]{1,0:T(8,128)S(1)}, f32[8,128]{1,0:T(8,128)S(1)}, u32[]{:S(2)}, u32[]{:S(2)}) collective-permute-start(f32[8,128]{1,0:T(8,128)S(1)} %get-tuple-element.97), channel_id=1, source_target_pairs={{0,1},{1,0},{2,3},{3,2},{4,5},{5,4},{6,7},{7,6},{8,9},{9,8},{10,11... | collective-permute-start | bytes 12296 | tf_op jit(solution)/shard_map/ppermute | solution.py:485
  85.7 8.4 %collective-permute-start.17 = (f32[8,128]{1,0:T(8,128)S(1)}, f32[8,128]{1,0:T(8,128)S(1)}, u32[]{:S(2)}, u32[]{:S(2)}) collective-permute-start(f32[8,128]{1,0:T(8,128)S(1)} %add_add_fusion.1), channel_id=1, source_target_pairs={{0,12},{4,8},{8,4},{12,0},{16,28},{20,24},{24,20},{28,16},{1,13},{... | collective-permute-start | bytes 12296 | tf_op jit(solution)/shard_map/ppermute | solution.py:485
  92.5 3.6 %collective-permute-start.16 = (f32[8,128]{1,0:T(8,128)S(1)}, f32[8,128]{1,0:T(8,128)S(1)}, u32[]{:S(2)}, u32[]{:S(2)}) collective-permute-start(f32[8,128]{1,0:T(8,128)S(1)} %add_add_fusion.1), channel_id=1, source_target_pairs={{0,8},{4,12},{8,0},{12,4},{16,24},{20,28},{24,16},{28,20},{1,9},{5... | collective-permute-start | bytes 12296 | tf_op jit(solution)/shard_map/ppermute | solution.py:485
  92.5 3.6 %collective-permute-start.15 = (f32[8,128]{1,0:T(8,128)S(1)}, f32[8,128]{1,0:T(8,128)S(1)}, u32[]{:S(2)}, u32[]{:S(2)}) collective-permute-start(f32[8,128]{1,0:T(8,128)S(1)} %add_add_fusion.1), channel_id=1, source_target_pairs={{0,4},{4,0},{8,12},{12,8},{16,20},{20,16},{24,28},{28,24},{1,5},{5... | collective-permute-start | bytes 12296 | tf_op jit(solution)/shard_map/ppermute | solution.py:485
  96.1 4.6 %collective-permute-start.18 = (f32[8,128]{1,0:T(8,128)S(1)}, f32[8,128]{1,0:T(8,128)S(1)}, u32[]{:S(2)}, u32[]{:S(2)}) collective-permute-start(f32[8,128]{1,0:T(8,128)S(1)} %add_add_fusion), channel_id=1, source_target_pairs={{0,16},{4,20},{8,24},{12,28},{16,0},{20,4},{24,8},{28,12},{1,17},{... | collective-permute-start | bytes 12296 | tf_op jit(solution)/shard_map/ppermute | solution.py:485
